TPU v7x, 32 devices: a whole 2x2x4 slice. The times are simulated.
32 devices in a mesh: row: 8 (over z, core), col: 4 (over y, x).
Axes of the slice: x: 2, y: 2, z: 4, core: 2. Of those that a mesh axis runs over, the one named last changes fastest.
Arguments:
- new_velocity: float32 [3, 160, 160, 160], P(None, 'row', 'col'), may hold values from -6 to 6
- stored_velocity: float32 [6, 3, 256, 256, 256], P(None, None, 'row', 'col'), may hold values from -6 to 6
- stored_vorticity: float32 [6, 3, 256, 256, 256], P(None, None, 'row', 'col'), may hold values from -6 to 6
Outputs:
- next_velocity: float32 [3, 160, 160, 160], P(None, 'row', 'col')
All inputs are finite; a program needn't handle non-finite values.
Results may differ from a plain program's by a relative error of at most 0.00007.
Values sent between devices are 32-bit elements; how exact they have to be, the bound alone decides.
No kernel may reach another device: no remote copies, remote signals or barrier semaphores. Data moves between devices by JAX's collectives and lax.ppermute only.
A program may use at most 256 MiB of HBM per device.

v0:
```python
import math

import jax
import jax.numpy as jnp
from jax import lax
from jax.sharding import PartitionSpec as P

N = 256
MODES = 160
ORDERS = 6
KMAX = 79


highest = lax.Precision.HIGHEST


def synth_table(grid_len, mode_count):
    points = jnp.arange(grid_len, dtype=jnp.int32)[:, None]
    mode_index = jnp.arange(mode_count, dtype=jnp.int32)[None, :]
    wave_index = jnp.where(mode_index == 1, grid_len // 2, mode_index // 2)
    angles = (points * wave_index % grid_len).astype(jnp.float32) * (2.0 * math.pi / grid_len)
    trig_values = jnp.where(
        (mode_index % 2 == 0) | (mode_index == 1), jnp.cos(angles), jnp.sin(angles)
    )
    weight = jnp.where(mode_index < 2, 1.0, 2.0).astype(jnp.float32) / grid_len
    return trig_values * jnp.sqrt(weight)


def slope_table(grid_len, mode_count):
    paired = synth_table(grid_len, mode_count).reshape(grid_len, mode_count // 2, 2)
    wavenum = jnp.arange(mode_count // 2, dtype=jnp.int32).astype(jnp.float32) / KMAX
    return jnp.stack([-wavenum * paired[:, :, 1], wavenum * paired[:, :, 0]], -1).reshape(
        grid_len, mode_count
    )


def keep_modes(mode_index):
    return (mode_index != 1).astype(jnp.float32)


def pair_slope(spectra, axis_pos, wavenum):
    full_shape = spectra.shape
    half_len = full_shape[axis_pos] // 2
    paired = spectra.reshape(full_shape[:axis_pos] + (half_len, 2) + full_shape[axis_pos + 1 :])
    pair_view = [1] * (len(full_shape) + 1)
    pair_view[axis_pos] = half_len
    scaled = wavenum.reshape(tuple(pair_view))
    even_part = lax.slice_in_dim(paired, 0, 1, axis=axis_pos + 1)
    odd_part = lax.slice_in_dim(paired, 1, 2, axis=axis_pos + 1)
    return jnp.concatenate([scaled * odd_part, -scaled * even_part], axis=axis_pos + 1).reshape(
        full_shape
    )


def cross_prod(left, right):
    return jnp.stack(
        [
            left[1] * right[2] - left[2] * right[1],
            left[2] * right[0] - left[0] * right[2],
            left[0] * right[1] - left[1] * right[0],
        ]
    )


def shards(new_velocity, stored_velocity, stored_vorticity):
    row_count = lax.axis_size("row")
    col_count = lax.axis_size("col")
    ky_len = new_velocity.shape[1]
    kz_len = new_velocity.shape[2]
    x_len = N // row_count
    y_len = N // col_count
    ky_index = jnp.arange(ky_len, dtype=jnp.int32) + lax.axis_index("row") * ky_len
    kz_index = jnp.arange(kz_len, dtype=jnp.int32) + lax.axis_index("col") * kz_len
    kx_index = jnp.arange(MODES, dtype=jnp.int32)
    wave_y = (ky_index[0::2] // 2).astype(jnp.float32) / KMAX
    wave_z = (kz_index[0::2] // 2).astype(jnp.float32) / KMAX
    wave_x = (kx_index[0::2] // 2).astype(jnp.float32) / KMAX
    keep_mask = (
        keep_modes(ky_index)[:, None, None]
        * keep_modes(kz_index)[None, :, None]
        * keep_modes(kx_index)[None, None, :]
    )
    basis_table = synth_table(N, MODES)
    coeffs = new_velocity * keep_mask
    coef_x, coef_y, coef_z = (coeffs[0], coeffs[1], coeffs[2])

    def second_synth(fields, matrix):
        return jnp.einsum("cxmz,ym->cyxz", fields, matrix, precision=highest)

    def third_synth(fields, matrix):
        return jnp.einsum(
            "cyaxb,zab->cxyz", fields, matrix.reshape(N, col_count, kz_len), precision=highest
        )

    deriv_matrix = slope_table(N, MODES)
    fields = jnp.stack(
        [coef_x, coef_y, coef_z, pair_slope(coef_y, 2, wave_x), pair_slope(coef_z, 2, wave_x)]
    )
    field_count = fields.shape[0]
    spread = jnp.einsum("cyzm,xm->cxyz", fields, basis_table, precision=highest).reshape(
        field_count, N, ky_len * kz_len
    )
    received = lax.all_to_all(spread, "row", split_axis=1, concat_axis=2, tiled=True)
    section_first = received.reshape(field_count, x_len, MODES, kz_len)
    plain_second = second_synth(section_first, basis_table)
    sloped_second = second_synth(jnp.stack([section_first[0], section_first[2]]), deriv_matrix)
    section_middle = jnp.stack(
        [
            plain_second[0],
            plain_second[1],
            plain_second[2],
            plain_second[3] - sloped_second[0],
            sloped_second[1],
            -plain_second[4],
        ]
    )
    field_count = section_middle.shape[0]
    spread = section_middle.reshape(field_count, N, x_len * kz_len)
    received = lax.all_to_all(spread, "col", split_axis=1, concat_axis=2, tiled=True)
    section_last = received.reshape(field_count, y_len, col_count, x_len, kz_len)
    plain_third = third_synth(section_last, basis_table)
    sloped_third = third_synth(jnp.stack([section_last[0], section_last[1]]), deriv_matrix)
    velocity_new = plain_third[0:3]
    vorticity_new = jnp.stack(
        [plain_third[4] - sloped_third[1], sloped_third[0] + plain_third[5], plain_third[3]]
    )
    cauchy_sum = cross_prod(velocity_new, stored_vorticity[0]) + cross_prod(
        stored_velocity[0], vorticity_new
    )
    for order_idx in range(1, ORDERS):
        cauchy_sum = cauchy_sum + cross_prod(
            stored_velocity[order_idx], stored_vorticity[ORDERS - order_idx]
        )
    spread = jnp.einsum("cxyz,zm->cmxy", cauchy_sum, basis_table, precision=highest).reshape(
        3, MODES, x_len * y_len
    )
    arrived = lax.all_to_all(spread, "col", split_axis=1, concat_axis=2, tiled=True)
    item_count = arrived.shape[0]
    blocks = arrived.reshape(item_count, kz_len, col_count, x_len, y_len)
    mixed = jnp.einsum(
        "cmaxb,abk->ckmx", blocks, basis_table.reshape(col_count, y_len, MODES), precision=highest
    )
    mixed = mixed.reshape(item_count, MODES, kz_len * x_len)
    arrived = lax.all_to_all(mixed, "row", split_axis=1, concat_axis=2, tiled=True)
    item_count = arrived.shape[0]
    blocks = arrived.reshape(item_count, ky_len, row_count, kz_len, x_len)
    spectral = (
        jnp.einsum(
            "ckazb,abj->ckzj",
            blocks,
            basis_table.reshape(row_count, x_len, MODES),
            precision=highest,
        )
        * keep_mask
    )
    wave_my = (ky_index // 2).astype(jnp.float32) / KMAX
    wave_mz = (kz_index // 2).astype(jnp.float32) / KMAX
    wave_mx = (kx_index // 2).astype(jnp.float32) / KMAX
    wave_square = (
        wave_my[:, None, None] ** 2 + wave_mz[None, :, None] ** 2 + wave_mx[None, None, :] ** 2
    )
    divergence = (
        pair_slope(spectral[0], 2, wave_x)
        + pair_slope(spectral[1], 0, wave_y)
        + pair_slope(spectral[2], 1, wave_z)
    )
    potential = jnp.where(
        wave_square > 0, divergence / jnp.where(wave_square > 0, wave_square, 1.0), 0.0
    )
    result = jnp.stack(
        [
            spectral[0] + pair_slope(potential, 2, wave_x),
            spectral[1] + pair_slope(potential, 0, wave_y),
            spectral[2] + pair_slope(potential, 1, wave_z),
        ]
    )
    return result / (ORDERS + 1)


def solution(mesh):
    return jax.shard_map(
        shards,
        mesh=mesh,
        in_specs=(
            P(None, "row", "col", None),
            P(None, None, "row", "col", None),
            P(None, None, "row", "col", None),
        ),
        out_specs=P(None, "row", "col", None),
        check_vma=False,
    )
```

profile of v0, /device:TPU:0, one launch (start us, length us, event | category | flops | bytes accessed | tf_op | source)
XLA Modules:
  0.0 827.3 jit_solution(10441455343804986989)
XLA Ops:
  23.5 7.2 fusion.47
  30.7 7.2 copy.183
  37.9 17.8 %all-to-all-start = ((f32[5,256,800]{2,0,1:T(8,128)}), f32[5,256,800]{2,0,1:T(8,128)}, u32[]{:S(2)}, u32[]{:S(2)}) async-start(f32[5,256,800]{2,0,1:T(8,128)} %copy.183), calls=%async_computation | async-start | bytes 14680064 | tf_op jit(solution)/shard_map/all_to_all | solution.py:103
  60.3 156.8 %all-to-all-done = f32[5,256,800]{2,0,1:T(8,128)} async-done(((f32[5,256,800]{2,0,1:T(8,128)}), f32[5,256,800]{2,0,1:T(8,128)}, u32[]{:S(2)}, u32[]{:S(2)}) %all-to-all-start) | async-done | bytes 4096032 | tf_op jit(solution)/shard_map/all_to_all | solution.py:103
  217.1 7.9 copy.185
  225.0 10.6 %reshape.1257 = f32[5,32,160,40]{3,2,1,0:T(8,128)} reshape(f32[5,32,8,800]{3,2,1,0:T(8,128)} %copy.185) | data formatting | bytes 8192000 | tf_op jit(solution)/shard_map/reshape | solution.py:104
  235.6 27.6 %convolution_bitcast_fusion.1 = f32[5,256,32,40]{1,3,2,0:T(8,128)} fusion(f32[5,32,160,40]{3,2,1,0:T(8,128)} %reshape.1257, f32[160]{0:T(256)S(1)} %fusion.177, s32[160]{0:T(256)S(1)} %fusion.174, pred[160]{0:T(512)(128)(4,1)S(1)} %compare_or_fusion.1), kind=kOutput, calls=%fused_computation.62 | convolution fusion | flops 3146383360 | bytes 10651040 | tf_op jit(solution)/shard_map/cxmz,ym->cyxz/dot_general | solution.py:88
  296.9 6.6 copy.194
  303.5 9.9 %pad_maximum_fusion = f32[6,256,1280]{2,0,1:T(8,128)} fusion(f32[1,256,1280]{2,0,1:T(1,128)} %copy.197, f32[1,256,1280]{2,0,1:T(1,128)S(1)} %copy.196, f32[1,256,1280]{2,0,1:T(1,128)S(1)} %copy.195, f32[3,256,1280]{2,0,1:T(4,128)} %copy.194), kind=kLoop, calls=%fused_computation | loop fusion | flops 5898240 | bytes 15728640 | tf_op jit(solution)/shard_map/stack | solution.py:107
  313.4 6.3 all-to-all-start.1
  319.9 9.4 %subtract_bitcast_fusion.14 = (f32[1,32,64,256]{3,2,1,0:T(8,128)}, f32[1,32,64,256]{3,2,1,0:T(8,128)}, f32[1,32,64,256]{3,2,1,0:T(8,128)}) fusion(f32[6,3,32,64,256]{4,3,2,1,0:T(8,128)} %param.5, f32[6,3,32,64,256]{4,3,2,1,0:T(8,128)} %param.4), kind=kLoop, calls=%fused_computation.107 | loop fusion | flops 4718592 | bytes 18874368 | tf_op jit(solution)/shard_map/sub | solution.py:58
  329.3 13.1 %subtract_bitcast_fusion.2 = (f32[1,32,64,256]{3,2,1,0:T(8,128)}, f32[1,32,64,256]{3,2,1,0:T(8,128)}, f32[1,32,64,256]{3,2,1,0:T(8,128)}, f32[1,32,64,256]{3,2,1,0:T(8,128)}) fusion(f32[6,3,32,64,256]{4,3,2,1,0:T(8,128)} %param.5, f32[6,3,32,64,256]{4,3,2,1,0:T(8,128)} %param.4), kind=kLoop, calls=%fused_computation.95 | loop fusion | flops 6291456 | bytes 33554432 | tf_op jit(solution)/shard_map/sub | solution.py:58
  342.5 11.8 %subtract_bitcast_fusion.6 = (f32[1,32,64,256]{3,2,1,0:T(8,128)}, f32[1,32,64,256]{3,2,1,0:T(8,128)}, f32[1,32,64,256]{3,2,1,0:T(8,128)}, f32[1,32,64,256]{3,2,1,0:T(8,128)}) fusion(f32[6,3,32,64,256]{4,3,2,1,0:T(8,128)} %param.4, f32[6,3,32,64,256]{4,3,2,1,0:T(8,128)} %param.5), kind=kLoop, calls=%fused_computation.99 | loop fusion | flops 6291456 | bytes 29360128 | tf_op jit(solution)/shard_map/sub | solution.py:60
  354.3 14.3 %subtract_bitcast_fusion.1 = (f32[1,32,64,256]{3,2,1,0:T(8,128)}, f32[1,32,64,256]{3,2,1,0:T(8,128)}, f32[1,32,64,256]{3,2,1,0:T(8,128)}, f32[1,32,64,256]{3,2,1,0:T(8,128)}) fusion(f32[6,3,32,64,256]{4,3,2,1,0:T(8,128)} %param.4, f32[6,3,32,64,256]{4,3,2,1,0:T(8,128)} %param.5), kind=kLoop, calls=%fused_computation.94 | loop fusion | flops 6291456 | bytes 37748736 | tf_op jit(solution)/shard_map/sub | solution.py:59
  368.6 66.0 %all-to-all-done.1 = f32[6,256,1280]{2,0,1:T(8,128)} async-done(((f32[6,256,1280]{2,0,1:T(8,128)}), f32[6,256,1280]{2,0,1:T(8,128)}, u32[]{:S(2)}, u32[]{:S(2)}) %all-to-all-start.1) | async-done | bytes 7864352 | tf_op jit(solution)/shard_map/all_to_all | solution.py:119
  434.6 6.5 copy.198
  447.9 13.7 %copy.199 = f32[6,64,4,1280]{1,3,2,0:T(8,128)} copy(f32[6,64,4,1280]{3,0,1,2:T(8,128)} %bitcast.27) | data formatting | bytes 15728640 | tf_op jit(solution)/shard_map/all_to_all | solution.py:119
  461.6 35.8 %convolution_bitcast_fusion = f32[6,32,64,256]{3,2,1,0:T(8,128)S(1)} fusion(f32[6,64,4,32,40]{1,4,3,2,0:T(8,128)} %bitcast.199, f32[4,40]{1,0:T(4,128)S(1)} %multiply_sqrt_fusion, s32[4,40]{1,0:T(4,128)S(1)} %fusion.165, pred[4,40]{1,0:T(4,128)(4,1)S(1)} %fusion.173), kind=kOutput, calls=%fused_computation.50 | convolution fusion | flops 6040453120 | bytes 20448672 | tf_op jit(solution)/shard_map/cyaxb,zab->cxyz/dot_general | solution.py:91
  497.4 7.4 fusion.67
  504.8 10.3 %fusion.59 = f32[2,32,64,256]{3,2,1,0:T(8,128)S(1)} fusion(f32[1,64,4,32,40]{1,4,3,2,0:T(8,128)S(1)} %bitcast.212, f32[1,64,4,32,40]{1,4,3,2,0:T(8,128)S(1)} %bitcast.211, f32[256,4,40,1,1]{0,2,1,3,4:T(8,128)S(1)} %reshape.1277), kind=kOutput, calls=%fused_computation.72 | convolution fusion | flops 2013921280 | bytes 6979584 | tf_op jit(solution)/shard_map/cyaxb,zab->cxyz/dot_general | solution.py:91
  515.2 6.4 fusion.64
  521.5 19.5 %fusion.7 = f32[160,3,32,64]{0,3,2,1:T(8,128)} fusion(f32[1,32,64,256]{3,2,1,0:T(8,128)} %get-tuple-element.31, f32[1,32,64,256]{3,2,1,0:T(8,128)} %get-tuple-element.30, f32[1,32,64,256]{3,2,1,0:T(8,128)} %get-tuple-element.29, f32[1,32,64,256]{3,2,1,0:T(8,128)} %get-tuple-element.28, f32[1,32,64,256]{3,2,1,0:T(8,128)} %get-tuple-element.27, ...), kind=kOutput, calls=%fused_computation.9 | convolution fusion | flops 3052011520 | bytes 47973792 | tf_op jit(solution)/shard_map/cxyz,zm->cmxy/dot_general | solution.py:134
  541.0 7.8 copy.205
  548.9 5.1 all-to-all-start.2
  554.0 58.1 %all-to-all-done.2 = f32[3,160,2048]{2,0,1:T(4,128)} async-done(((f32[3,160,2048]{2,0,1:T(4,128)}), f32[3,160,2048]{2,0,1:T(4,128)}, u32[]{:S(2)}, u32[]{:S(2)}) %all-to-all-start.2) | async-done | bytes 3932192 | tf_op jit(solution)/shard_map/all_to_all | solution.py:137
  612.1 6.7 copy.206
  618.8 7.6 reshape.1261
  626.4 12.8 %fusion.68 = f32[3,160,40,32]{1,2,3,0:T(8,128)S(1)} fusion(f32[3,40,4,32,64]{4,3,1,2,0:T(8,128)} %reshape.1261, f32[160]{0:T(256)S(1)} %fusion.177, s32[160]{0:T(256)S(1)} %fusion.174, s32[4,64]{1,0:T(4,128)S(1)} %multiply_add_fusion.2, pred[160]{0:T(512)(128)(4,1)S(1)} %compare_or_fusion.1), kind=kOutput, calls=%fused_computation.108 | convolution fusion | flops 1888092160 | bytes 6392224 | tf_op jit(solution)/shard_map/cmaxb,abk->ckmx/dot_general | solution.py:140
  642.2 5.4 copy.209
  652.4 73.5 %all-to-all-done.3 = f32[3,160,1280]{2,0,1:T(4,128)S(1)} async-done(((f32[3,160,1280]{2,0,1:T(4,128)}), f32[3,160,1280]{2,0,1:T(4,128)S(1)}, u32[]{:S(2)}, u32[]{:S(2)}) %all-to-all-start.3) | async-done | bytes 2457632 | tf_op jit(solution)/shard_map/all_to_all | solution.py:144
  728.8 7.1 reshape.1263
  736.0 10.3 %bitcast_multiply_fusion = f32[3,20,40,160]{3,2,1,0:T(8,128)S(1)} fusion(f32[3,20,8,40,32]{4,3,2,1,0:T(8,128)} %reshape.1263, f32[20,40,160]{2,1,0:T(8,128)S(1)} %copy-done.3, f32[160]{0:T(256)S(1)} %fusion.177, s32[160]{0:T(256)S(1)} %fusion.174, s32[8,32]{1,0:T(8,128)S(1)} %multiply_add_fusion, pred[160]{0:T(512)(128)(4,1)S(1)} %compare_or_fusion.1), kind=kOutput, calls=%fused_computation.68 | convolution fusion | flops 1180687360 | bytes 4508064 | tf_op jit(solution)/shard_map/ckazb,abj->ckzj/dot_general | solution.py:148
  (156 shorter events, 159.8 us)
Async XLA Ops:
  0.3 2.3 copy-start.2
  8.4 5.0 copy-start.20
  8.4 5.0 copy-start.22
  37.9 179.2 %all-to-all-start = ((f32[5,256,800]{2,0,1:T(8,128)}), f32[5,256,800]{2,0,1:T(8,128)}, u32[]{:S(2)}, u32[]{:S(2)}) async-start(f32[5,256,800]{2,0,1:T(8,128)} %copy.183), calls=%async_computation | async-start | bytes 14680064 | tf_op jit(solution)/shard_map/all_to_all | solution.py:103
  59.5 165.5 %copy-start.17 = (f32[256,80,2]{0,2,1:T(2,128)}, f32[256,80,2]{0,2,1:T(2,128)S(1)}, u32[]{:S(2)}) copy-start(f32[256,80,2]{0,2,1:T(2,128)S(1)} %pad_maximum_fusion.9) | copy-start | bytes 491524
  279.2 4.4 copy-start.13
  279.2 4.4 copy-start.14
  279.2 4.4 copy-start.19
  313.4 6.3 copy-start.18
  313.4 121.2 %all-to-all-start.1 = ((f32[6,256,1280]{2,0,1:T(8,128)}), f32[6,256,1280]{2,0,1:T(8,128)}, u32[]{:S(2)}, u32[]{:S(2)}) async-start(f32[6,256,1280]{2,0,1:T(8,128)} %pad_maximum_fusion), calls=%async_computation.1 | async-start | bytes 20971520 | tf_op jit(solution)/shard_map/all_to_all | solution.py:119
  497.4 7.4 copy-start.8
  515.2 6.4 copy-start.16
  548.9 63.2 %all-to-all-start.2 = ((f32[3,160,2048]{2,0,1:T(4,128)}), f32[3,160,2048]{2,0,1:T(4,128)}, u32[]{:S(2)}, u32[]{:S(2)}) async-start(f32[3,160,2048]{2,0,1:T(4,128)} %copy.205), calls=%async_computation.2 | async-start | bytes 10485760 | tf_op jit(solution)/shard_map/all_to_all | solution.py:137
  647.6 78.3 %all-to-all-start.3 = ((f32[3,160,1280]{2,0,1:T(4,128)}), f32[3,160,1280]{2,0,1:T(4,128)S(1)}, u32[]{:S(2)}, u32[]{:S(2)}) async-start(f32[3,160,1280]{2,0,1:T(4,128)} %copy.209), calls=%async_computation.3 | async-start | bytes 6553600 | tf_op jit(solution)/shard_map/all_to_all | solution.py:144
  728.8 7.2 copy-start.3
  746.3 1.7 copy-start
  748.8 0.9 copy-start.9
  749.7 0.9 copy-start.10
  750.7 6.1 copy-start.4
  756.9 0.6 copy-start.21
  756.9 0.6 copy-start.23
  758.9 0.9 copy-start.11
  758.9 1.1 copy-start.12
  761.9 4.7 copy-start.5
  769.6 1.9 copy-start.6
  769.6 2.9 copy-start.7
  817.6 6.1 copy-start.1
  817.6 6.1 copy-start.15
where the time goes:
time: 832 us; the launch traced here: 827 us
  waiting for transfers between devices  354 us (43%)
  local copies, waits for them, and re-layouts  190 us (23%)
  matrix products  126 us (15%)
  other arithmetic  123 us (15%)
  starting transfers between devices  33.2 us (4%)
    all_to_all x1, waiting for transfers between devices, shards(): lax.all_to_all(spread, 'row', split_axis=1, concat_axis=2, tiled=True)  157 us
    all_to_all x2, waiting for transfers between devices, shards(): lax.all_to_all(spread, 'col', split_axis=1, concat_axis=2, tiled=True)  124 us
    all_to_all x1, waiting for transfers between devices, shards(): lax.all_to_all(mixed, 'row', split_axis=1, concat_axis=2, tiled=True)  73.5 us
    dot_general x2, matrix products, third_synth(): jnp.einsum('cyaxb,zab->cxyz', fields, matrix.reshape(N, col_count, kz_len...  46.2 us
    sub x4, other arithmetic, cross_prod(): left[1] * right[2] - left[2] * right[1]  36.3 us
    dot_general x2, matrix products, second_synth(): return jnp.einsum('cxmz,ym->cyxz', fields, matrix, precision=highest)  29.8 us
    all_to_all x3, local copies, waits for them, and re-layouts, shards(): lax.all_to_all(spread, 'col', split_axis=1, concat_axis=2, tiled=True)  26.9 us
    reshape x7, local copies, waits for them, and re-layouts, pair_slope(): jnp.concatenate([scaled * odd_part, -scaled * even_part], axis=axis_pos + 1)  21.1 us
  transfers between devices with their start and end apart: 4, of which 4 were waited for; matrix products, arithmetic and copies ran while one was open for 7% of the time, Pallas kernels for 0%

commit v1 on v0

v1 whole, which is shorter than its diff:
```python
import functools
import math

import jax
import jax.numpy as jnp
import ml_dtypes
import numpy as np
from jax import lax
from jax.experimental import pallas as pl
from jax.experimental.pallas import tpu as pltpu
from jax.sharding import PartitionSpec as P

LANES = 128
XC = 8
BF16 = jnp.bfloat16
F32 = jnp.float32
NN = (((1,), (0,)), ((), ()))
NT = (((1,), (1,)), ((), ()))


def round_up(value, step):
    return -(-value // step) * step


def synth_np(grid_len, mode_count):
    points = np.arange(grid_len)[:, None]
    mode_index = np.arange(mode_count)[None, :]
    wave_index = np.where(mode_index == 1, grid_len // 2, mode_index // 2)
    angles = (points * wave_index % grid_len) * (2.0 * math.pi / grid_len)
    trig = np.where((mode_index % 2 == 0) | (mode_index == 1), np.cos(angles), np.sin(angles))
    weight = np.where(mode_index < 2, 1.0, 2.0) / grid_len
    return np.where(mode_index == 1, 0.0, trig * np.sqrt(weight))


def slope_np(table, kmax):
    paired = table.reshape(table.shape[0], -1, 2)
    wavenum = np.arange(paired.shape[1]) / kmax
    return np.stack([-wavenum * paired[:, :, 1], wavenum * paired[:, :, 0]], -1).reshape(table.shape)


def halves(table):
    high = table.astype(ml_dtypes.bfloat16)
    low = (table - high.astype(np.float64)).astype(ml_dtypes.bfloat16)
    return jnp.asarray(high), jnp.asarray(low)


def pieces_of(values):
    high = values.astype(BF16)
    return high, (values - high.astype(F32)).astype(BF16)


def dot(left, right, dims):
    return lax.dot_general(left, right, dims, preferred_element_type=F32)


def dot_data_left(values, high, low, dims=NN):
    top, rest = pieces_of(values)
    return dot(top, high, dims) + (dot(top, low, dims) + dot(rest, high, dims))


def dot_data_right(high, low, values, dims=NT):
    top, rest = pieces_of(values)
    return dot(high, top, dims) + (dot(low, top, dims) + dot(high, rest, dims))


def turn(values, shift):
    shift = shift % values.shape[-1]
    return values if shift == 0 else pltpu.roll(values, shift, axis=values.ndim - 1)


def lane_pack(parts, width, source_lane=0):
    tiles = []
    lane = lax.broadcasted_iota(jnp.int32, parts[0].shape, 1)
    for tile in range(-(-len(parts) * width // LANES)):
        start = tile * LANES
        acc = None
        for idx in range(start // width, min(len(parts) - 1, (start + LANES - 1) // width) + 1):
            moved = turn(parts[idx], idx * width - source_lane)
            acc = moved if acc is None else jnp.where(lane >= idx * width - start, moved, acc)
        tiles.append(acc)
    return tiles


def params(kind):
    return pltpu.CompilerParams(
        dimension_semantics=(kind,), vmem_limit_bytes=40 * 1024 * 1024
    )


def whole(array):
    rank = len(array.shape)
    return pl.BlockSpec(array.shape, lambda *_: (0,) * rank)


def first_synth_kernel(dims, x_ref, high_ref, low_ref, wave_ref, *rest):
    chunks, dests, xc = dims
    outs, rows = rest[:chunks], rest[chunks]
    _, ky_len, kz_len, modes = x_ref.shape
    group = 5 * kz_len
    wide = rows.shape[1]
    tail = modes // LANES * LANES
    if tail < wide:
        rows[:, tail:] = jnp.zeros((rows.shape[0], wide - tail), F32)
    if ky_len * group < rows.shape[0]:
        rows[ky_len * group :, :] = jnp.zeros((rows.shape[0] - ky_len * group, wide), F32)
    even = lax.broadcasted_iota(jnp.int32, (kz_len, wide), 1) % 2 == 0
    wave = wave_ref[0:1, :]

    def fill(ky, carry):
        base = ky * group
        for comp in range(3):
            start = pl.multiple_of(base + comp * kz_len, 8)
            rows[pl.ds(start, kz_len), 0:modes] = x_ref[comp, ky]
            if comp:
                value = rows[pl.ds(start, kz_len), :]
                swapped = jnp.where(even, turn(value, -1), -turn(value, 1)) * wave
                rows[pl.ds(pl.multiple_of(start + 2 * kz_len, 8), kz_len), :] = swapped
        return carry

    lax.fori_loop(0, ky_len, fill, 0)
    step = 256
    tiles = rows.shape[0] // LANES

    def mult(blk, carry):
        start = pl.multiple_of(blk * step, step)
        result = dot_data_right(high_ref[...], low_ref[...], rows[pl.ds(start, step), :])
        for idx in range(chunks):
            for dest in range(dests):
                at = (idx * dests + dest) * xc
                for tile in range(step // LANES):
                    spot = pl.multiple_of((dest * tiles + blk * (step // LANES) + tile) * xc, 8)
                    outs[idx][pl.ds(spot, xc), :] = result[
                        at : at + xc, tile * LANES : (tile + 1) * LANES
                    ]
        return carry

    lax.fori_loop(0, rows.shape[0] // step, mult, 0)


def first_synth(coeffs, table, wave, dims, lanes):
    chunks = dims[0]
    grid_len = table[0].shape[0]
    height = grid_len // chunks * (lanes // LANES)
    return pl.pallas_call(
        functools.partial(first_synth_kernel, dims),
        out_shape=[jax.ShapeDtypeStruct((height, LANES), F32)] * chunks,
        scratch_shapes=[pltpu.VMEM((lanes, table[0].shape[1]), F32)],
        compiler_params=pltpu.CompilerParams(vmem_limit_bytes=40 * 1024 * 1024),
        cost_estimate=pl.CostEstimate(
            flops=6 * grid_len * lanes * 256, bytes_accessed=4 * grid_len * lanes, transcendentals=0
        ),
        name="first_synth",
    )(coeffs, table[0], table[1], wave)


def second_synth_kernel(dims, a_ref, high_ref, low_ref, shigh_ref, slow_ref, out_ref):
    rows, xc, ky_len, kz_len, cols, y_len, pack = dims
    group = 5 * kz_len
    wide = round_up(group, LANES)
    at = pl.program_id(0)
    turned = []
    for part in range(pack):
        tiles = a_ref.shape[0] // (rows * xc)
        line = [
            a_ref[pl.ds(tile * xc + at * pack + part, rows, stride=tiles * xc), :]
            for tile in range(tiles)
        ]
        found = []
        for ky in range(ky_len):
            start = ky * group
            low, off = divmod(start, LANES)
            window = line[low : low + (wide // LANES) + (1 if off else 0)]
            found.append(turn(jnp.concatenate(window, axis=1), -off)[:, :wide])
        turned.append(jnp.concatenate(found, axis=0).T[:group])
    plain = dot_data_left(jnp.concatenate(turned, axis=0), high_ref[...], low_ref[...])
    slope_in = [t[c * kz_len : (c + 1) * kz_len] for t in turned for c in (0, 2)]
    slope = dot_data_left(jnp.concatenate(slope_in, axis=0), shigh_ref[...], slow_ref[...])
    fields = []
    for part in range(pack):
        own = plain[part * group : (part + 1) * group]
        sl = slope[part * 2 * kz_len : (part + 1) * 2 * kz_len]
        fields.append(
            jnp.concatenate(
                [
                    own[: 3 * kz_len],
                    own[3 * kz_len : 4 * kz_len] - sl[:kz_len],
                    sl[kz_len:],
                    -own[4 * kz_len :],
                ],
                axis=0,
            )
        )
    for dest in range(cols):
        tile, off = divmod(dest * y_len, LANES)
        out_ref[dest, 0] = lane_pack(
            [f[:, tile * LANES : (tile + 1) * LANES] for f in fields], y_len, off
        )[0]


def second_synth(arrived, table, slopes, dims):
    rows, xc, ky_len, kz_len, cols, y_len, pack = dims
    packs = xc // pack
    return pl.pallas_call(
        functools.partial(second_synth_kernel, dims),
        grid=(packs,),
        in_specs=[whole(a) for a in (arrived, *table, *slopes)],
        out_specs=pl.BlockSpec((cols, 1, 6 * kz_len, LANES), lambda i: (0, i, 0, 0)),
        out_shape=jax.ShapeDtypeStruct((cols, packs, 6 * kz_len, LANES), F32),
        compiler_params=params("arbitrary"),
        cost_estimate=pl.CostEstimate(
            flops=6 * xc * 7 * kz_len * 256 * 256 * 2,
            bytes_accessed=4 * arrived.size + 4 * cols * packs * 6 * kz_len * LANES,
            transcendentals=0,
        ),
        name="second_synth",
    )(arrived, *table, *slopes)


def cross(left, right):
    return [
        left[1] * right[2] - left[2] * right[1],
        left[2] * right[0] - left[0] * right[2],
        left[0] * right[1] - left[1] * right[0],
    ]


def earlier_kernel(count, *refs):
    vels, vorts, out_ref = refs[:count], refs[count : 2 * count], refs[2 * count]
    pack, y_len = out_ref.shape[1:3]
    for part in range(pack):
        def body(step, carry):
            at = pl.ds(pl.multiple_of(step * 8, 8), 8)
            total = None
            for vel, vort in zip(vels, vorts):
                term = cross(
                    [vel[0, c, part, at, :] for c in range(3)],
                    [vort[0, c, part, at, :] for c in range(3)],
                )
                total = term if total is None else [a + b for a, b in zip(total, term)]
            for comp in range(3):
                out_ref[comp, part, at, :] = total[comp]
            return carry

        lax.fori_loop(0, y_len // 8, body, 0, unroll=2)


def earlier(velocity, vorticity, chunk, xc, pack):
    orders, _, _, y_len, grid_len = velocity.shape
    packs = xc // pack
    block = (1, 3, pack, y_len, grid_len)

    def at(order):
        return pl.BlockSpec(block, lambda i: (order, 0, chunk * packs + i, 0, 0))

    specs = [at(k) for k in range(1, orders)] + [at(orders - k) for k in range(1, orders)]
    size = xc * y_len * grid_len
    return pl.pallas_call(
        functools.partial(earlier_kernel, orders - 1),
        grid=(packs,),
        in_specs=specs,
        out_specs=pl.BlockSpec((3, pack, y_len, grid_len), lambda i: (0, i, 0, 0)),
        out_shape=jax.ShapeDtypeStruct((3, xc, y_len, grid_len), F32),
        compiler_params=params("arbitrary"),
        cost_estimate=pl.CostEstimate(
            flops=size * 9 * 2 * orders, bytes_accessed=4 * size * (6 * orders - 3), transcendentals=0
        ),
        name="earlier_orders",
    )(*[velocity] * (orders - 1), *[vorticity] * (orders - 1))


def third_kernel(dims, b_ref, vel_ref, vort_ref, base_ref, high_ref, low_ref, shigh_ref, slow_ref, out_ref):
    kz_len, cols, y_len, pack = dims
    grid_len = high_ref.shape[1]

    def stack(field):
        return jnp.concatenate(
            [b_ref[src, 0, field * kz_len : (field + 1) * kz_len, :] for src in range(cols)], axis=0
        ).T

    lines = jnp.concatenate([stack(field) for field in range(6)], axis=0)
    plain = dot_data_left(lines, high_ref[...], low_ref[...])
    slope = dot_data_left(lines[: 2 * LANES], shigh_ref[...], slow_ref[...])
    at = [plain[f * LANES : (f + 1) * LANES] for f in range(6)]
    vel_new = at[:3]
    vort_new = [at[4] - slope[LANES:], slope[:LANES] + at[5], at[3]]
    flat = (pack * y_len, grid_len)
    vel = [vel_ref[0, c].reshape(flat) for c in range(3)]
    vort = [vort_ref[0, c].reshape(flat) for c in range(3)]
    one, two = cross(vel_new, vort), cross(vel, vort_new)
    total = [one[c] + two[c] + base_ref[c].reshape(flat) for c in range(3)]
    result = dot_data_right(high_ref[...], low_ref[...], jnp.concatenate(total, axis=0))
    for dest in range(cols):
        for comp in range(3):
            out_ref[dest, 0, comp * kz_len : (comp + 1) * kz_len, :] = result[
                dest * kz_len : (dest + 1) * kz_len, comp * LANES : (comp + 1) * LANES
            ]


def third(arrived, velocity, vorticity, base, table, slopes, chunk, dims):
    kz_len, cols, y_len, pack = dims
    packs = arrived.shape[1]
    grid_len = velocity.shape[-1]
    stored = pl.BlockSpec((1, 3, pack, y_len, grid_len), lambda i: (0, 0, chunk * packs + i, 0, 0))
    return pl.pallas_call(
        functools.partial(third_kernel, dims),
        grid=(packs,),
        in_specs=[
            pl.BlockSpec((cols, 1, 6 * kz_len, LANES), lambda i: (0, i, 0, 0)),
            stored,
            stored,
            pl.BlockSpec((3, pack, y_len, grid_len), lambda i: (0, i, 0, 0)),
            *[whole(a) for a in (*table, *slopes)],
        ],
        out_specs=pl.BlockSpec((cols, 1, 3 * kz_len, LANES), lambda i: (0, i, 0, 0)),
        out_shape=jax.ShapeDtypeStruct((cols, packs, 3 * kz_len, LANES), F32),
        compiler_params=params("arbitrary"),
        cost_estimate=pl.CostEstimate(
            flops=6 * packs * LANES * 11 * 256 * 256 * 2,
            bytes_accessed=4 * (arrived.size * 3 // 2 + packs * LANES * grid_len * 9),
            transcendentals=0,
        ),
        name="third_dimension",
    )(arrived, velocity, vorticity, base, *table, *slopes)


def second_back_kernel(dims, c_ref, high_ref, low_ref, out_ref):
    rows, xc, ky_len, kz_len, cols, y_len, pack = dims
    width = 3 * kz_len
    high_pad = round_up(width, LANES)
    lines = []
    for part in range(pack):
        tiles = lane_pack([c_ref[src, 0] for src in range(cols)], y_len, part * y_len)
        lines.append(jnp.concatenate(tiles, axis=1))
        if high_pad > width:
            lines.append(jnp.zeros((high_pad - width, cols * y_len), F32))
    result = dot_data_right(high_ref[...], low_ref[...], jnp.concatenate(lines, axis=0))
    for part in range(pack):
        own = result[:, part * high_pad : (part + 1) * high_pad]
        tiles = lane_pack([own[ky * rows : (ky + 1) * rows] for ky in range(ky_len)], width)
        at = pl.program_id(0) * pack + part
        for idx, tile in enumerate(tiles):
            out_ref[pl.ds(idx * xc + at, rows, stride=len(tiles) * xc), :] = tile


def second_back(arrived, table, dims):
    rows, xc, ky_len, kz_len, cols, y_len, pack = dims
    packs = xc // pack
    lanes = round_up(ky_len * 3 * kz_len, LANES)
    return pl.pallas_call(
        functools.partial(second_back_kernel, dims),
        grid=(packs,),
        in_specs=[
            pl.BlockSpec((cols, 1, 3 * kz_len, LANES), lambda i: (0, i, 0, 0)),
            *[whole(a) for a in table],
        ],
        out_specs=pl.BlockSpec((rows * xc * lanes // LANES, LANES), lambda i: (0, 0)),
        out_shape=jax.ShapeDtypeStruct((rows * xc * lanes // LANES, LANES), F32),
        compiler_params=params("arbitrary"),
        cost_estimate=pl.CostEstimate(
            flops=6 * xc * LANES * 256 * 256 * 2,
            bytes_accessed=4 * (arrived.size + rows * xc * lanes),
            transcendentals=0,
        ),
        name="second_back",
    )(arrived, *table)


def last_kernel(dims, *refs):
    chunks, xc, kz_len, modes, scale = dims
    wave_y_ref = refs[0]
    parts = refs[1 : 1 + chunks]
    high_ref, low_ref, wave_x_ref, wave_z_ref, out_ref, rows = refs[1 + chunks :]
    pair = 2 * 3 * kz_len
    at = pl.program_id(0)

    @pl.when(at == 0)
    def _():
        tiles = rows.shape[0] // LANES
        for tile in range(tiles):
            found = [
                part[(src * tiles + tile) * xc : (src * tiles + tile + 1) * xc, :]
                for part in parts
                for src in range(part.shape[0] // (tiles * xc))
            ]
            rows[tile * LANES : (tile + 1) * LANES, :] = jnp.concatenate(found, axis=0).T

    data = rows[pl.ds(pl.multiple_of(at * pair, 8), pair), :]
    spec = dot_data_left(data, high_ref[...], low_ref[...])
    wide = spec.shape[1]
    wave_x = jnp.broadcast_to(wave_x_ref[0:1, :], (kz_len, wide))
    wave_z = wave_z_ref[...]
    wave_y = wave_y_ref[at]
    even_x = lax.broadcasted_iota(jnp.int32, (kz_len, wide), 1) % 2 == 0
    even_z = lax.broadcasted_iota(jnp.int32, (kz_len, wide), 0) % 2 == 0

    def slope_x(value):
        return jnp.where(even_x, turn(value, -1), -turn(value, 1)) * wave_x

    def slope_z(value):
        return (
            jnp.where(
                even_z,
                pltpu.roll(value, kz_len - 1, axis=0),
                -pltpu.roll(value, 1, axis=0),
            )
            * wave_z
        )

    s = [
        [spec[(y * 3 + c) * kz_len : (y * 3 + c + 1) * kz_len] for c in range(3)] for y in range(2)
    ]
    square = wave_x * wave_x + wave_z * wave_z + wave_y * wave_y
    positive = square > 0
    safe = jnp.where(positive, square, 1.0)
    potential = []
    for y in range(2):
        along_y = s[1 - y][1] * (wave_y if y == 0 else -wave_y)
        divergence = slope_x(s[y][0]) + along_y + slope_z(s[y][2])
        potential.append(jnp.where(positive, divergence / safe, 0.0))
    for y in range(2):
        along_y = potential[1 - y] * (wave_y if y == 0 else -wave_y)
        found = [
            s[y][0] + slope_x(potential[y]),
            s[y][1] + along_y,
            s[y][2] + slope_z(potential[y]),
        ]
        for comp in range(3):
            out_ref[comp, y] = (found[comp] * scale)[:, :modes]


def last(parts, table, wave_y, wave_x, wave_z, xc, ky_len, kz_len, modes, scale):
    chunks = len(parts)
    grid_len = table[0].shape[0]
    lanes = parts[0].size * chunks // grid_len
    return pl.pallas_call(
        functools.partial(last_kernel, (chunks, xc, kz_len, modes, scale)),
        grid=(ky_len // 2,),
        in_specs=[
            pl.BlockSpec(memory_space=pltpu.SMEM),
            *[whole(a) for a in (*parts, *table, wave_x, wave_z)],
        ],
        out_specs=pl.BlockSpec((3, 2, kz_len, modes), lambda i: (0, i, 0, 0)),
        out_shape=jax.ShapeDtypeStruct((3, ky_len, kz_len, modes), F32),
        scratch_shapes=[pltpu.VMEM((lanes, grid_len), F32)],
        compiler_params=params("arbitrary"),
        cost_estimate=pl.CostEstimate(
            flops=6 * lanes * 256 * 256,
            bytes_accessed=4 * (grid_len * lanes + 3 * ky_len * kz_len * modes),
            transcendentals=0,
        ),
        name="last_projection",
    )(wave_y, *parts, *table, wave_x, wave_z)


def shards(new_velocity, stored_velocity, stored_vorticity):
    rows = lax.axis_size("row")
    cols = lax.axis_size("col")
    _, ky_len, kz_own, modes = new_velocity.shape
    orders, _, x_len, y_len, grid_len = stored_velocity.shape
    kz_len = round_up(kz_own, 8)
    kmax = modes // 2 - 1
    xc = min(XC, x_len)
    chunks = x_len // xc
    pack = LANES // y_len
    packs = xc // pack
    wide = round_up(modes, LANES)
    group = 5 * kz_len
    lanes = round_up(ky_len * group, 256)

    basis = synth_np(grid_len, modes)
    slope = slope_np(basis, kmax)
    x_order = (
        np.arange(rows)[None, :, None] * x_len
        + np.arange(chunks)[:, None, None] * xc
        + np.arange(xc)[None, None, :]
    ).reshape(-1)
    y_order = (np.arange(rows)[None, :] * ky_len + np.arange(ky_len)[:, None]).reshape(-1)

    def spread_z(table):
        parts = table.T.reshape(cols, kz_own, grid_len)
        return np.pad(parts, ((0, 0), (0, kz_len - kz_own), (0, 0))).reshape(cols * kz_len, grid_len)

    table_x = halves(np.pad(basis[x_order], ((0, 0), (0, wide - modes))))
    table_y, slope_y = halves(basis.T[y_order]), halves(slope.T[y_order])
    table_z, slope_z = halves(spread_z(basis)), halves(spread_z(slope))

    def wave_of(index):
        return (index // 2).astype(F32) / kmax

    mode = jnp.arange(wide, dtype=jnp.int32)
    wave_x = jnp.broadcast_to(jnp.where(mode < modes, wave_of(mode), 0.0)[None, :], (8, wide))
    ky_first = lax.axis_index("row") * ky_len + 2 * jnp.arange(ky_len // 2, dtype=jnp.int32)
    wave_y = wave_of(ky_first)
    kz = lax.axis_index("col") * kz_own + jnp.arange(kz_len, dtype=jnp.int32)
    wave_z = jnp.broadcast_to(wave_of(kz)[:, None], (kz_len, wide))

    coeffs = new_velocity
    if kz_len > kz_own:
        coeffs = jnp.pad(coeffs, ((0, 0), (0, 0), (0, kz_len - kz_own), (0, 0)))

    def swap(value, axis):
        return lax.all_to_all(value, axis, split_axis=0, concat_axis=0, tiled=True)

    dims = (rows, xc, ky_len, kz_len, cols, y_len, pack)
    sent = first_synth(coeffs, table_x, wave_x, (chunks, rows, xc), lanes)
    back = []
    for chunk in range(chunks):
        arrived = swap(sent[chunk], "row")
        base = earlier(stored_velocity, stored_vorticity, chunk, xc, pack)
        arrived = swap(second_synth(arrived, table_y, slope_y, dims), "col")
        found = third(
            arrived, stored_velocity, stored_vorticity, base, table_z, slope_z, chunk, dims[3:]
        )
        found = second_back(swap(found, "col"), table_y, dims)
        back.append(swap(found, "row"))
    result = last(
        back, table_x, wave_y, wave_x, wave_z, xc, ky_len, kz_len, modes, 1.0 / (orders + 1)
    )
    return result[:, :, :kz_own] if kz_len > kz_own else result


def solution(mesh):
    return jax.shard_map(
        shards,
        mesh=mesh,
        in_specs=(
            P(None, "row", "col", None),
            P(None, None, "row", "col", None),
            P(None, None, "row", "col", None),
        ),
        out_specs=P(None, "row", "col", None),
        check_vma=False,
    )
```

time: 832 us -> 408 us (0.49)
  waiting for transfers between devices: 354 us -> 151 us
  local copies, waits for them, and re-layouts: 190 us -> 16.1 us
  matrix products: 126 us -> 0 us
  other arithmetic: 123 us -> 0.03 us
  Pallas kernels: 0 us -> 98.7 us
  blocking collectives: 0 us -> 92.2 us
  starting transfers between devices: 33.2 us -> 48.5 us
    all_to_all x4 -> x13, waiting for transfers between devices: 354 us -> 151 us  [swap(): return lax.all_to_all(value, axis, split_axis=0, concat_axis=0, tiled=True)]
    dot_general x8 -> x0, matrix products: 126 us -> none  [the longest x2 46.2 us: third_synth(): jnp.einsum('cyaxb,zab->cxyz', fields, matrix.reshape(N, col_count, kz_len...]
    pallas_call x0 -> x18, Pallas kernels: none -> 98.7 us  [the longest x4 28.2 us: third(): pl.pallas_call(functools.partial(third_kernel, dims), grid=(packs,), in_s...]
    all_to_all x0 -> x3, blocking collectives: none -> 92.2 us  [swap(): return lax.all_to_all(value, axis, split_axis=0, concat_axis=0, tiled=True)]
    reshape x14 -> x0, local copies, waits for them, and re-layouts: 67.7 us -> none  [the longest x7 21.1 us: pair_slope(): jnp.concatenate([scaled * odd_part, -scaled * even_part], axis=axis_pos + 1)]
    sub x7 -> x0, other arithmetic: 66.1 us -> none  [the longest x4 36.3 us: cross_prod(): left[1] * right[2] - left[2] * right[1]]
    all_to_all x6 -> x0, local copies, waits for them, and re-layouts: 41.6 us -> none  [the longest x3 26.9 us: shards(): lax.all_to_all(spread, 'col', split_axis=1, concat_axis=2, tiled=True)]
    slice x20 -> x0, local copies, waits for them, and re-layouts: 31.1 us -> none  [the longest x4 6.28 us: shards(): section_first[0]]
  transfers between devices with their start and end apart: 4 -> 13, of which waited for: 4 -> 10; matrix products, arithmetic and copies ran while one was open for 7% -> 0% of each run, Pallas kernels for 0% -> 20%
where the time goes in v1:
time: 408 us; the launch traced here: 407 us
  waiting for transfers between devices  151 us (37%)
  Pallas kernels  98.7 us (24%)
  blocking collectives  92.2 us (23%)
  starting transfers between devices  48.5 us (12%)
  local copies, waits for them, and re-layouts  16.1 us (4%)
    all_to_all x13, waiting for transfers between devices, swap(): return lax.all_to_all(value, axis, split_axis=0, concat_axis=0, tiled=True)  151 us
    all_to_all x3, blocking collectives, swap(): return lax.all_to_all(value, axis, split_axis=0, concat_axis=0, tiled=True)  92.2 us
    all_to_all x13, starting transfers between devices, swap(): return lax.all_to_all(value, axis, split_axis=0, concat_axis=0, tiled=True)  48.5 us
    pallas_call x4, Pallas kernels, third(): pl.pallas_call(functools.partial(third_kernel, dims), grid=(packs,), in_s...  28.2 us
    pallas_call x4, Pallas kernels, earlier(): pl.pallas_call(functools.partial(earlier_kernel, orders - 1), grid=(packs...  26.2 us
    unnamed x62, local copies, waits for them, and re-layouts  16 us
    pallas_call x4, Pallas kernels, second_back(): pl.pallas_call(functools.partial(second_back_kernel, dims), grid=(packs,)...  13.9 us
    pallas_call x4, Pallas kernels, second_synth(): pl.pallas_call(functools.partial(second_synth_kernel, dims), grid=(packs,...  13.4 us
  transfers between devices with their start and end apart: 13, of which 10 were waited for; matrix products, arithmetic and copies ran while one was open for 0% of the time, Pallas kernels for 20%

profile of v1, /device:TPU:0, one launch (start us, length us, event | category | flops | bytes accessed | tf_op | source)
XLA Modules:
  0.0 406.7 jit_solution(12705009241506285958)
XLA Ops:
  3.5 9.8 %first_synth.1 = (f32[2048,128]{1,0:T(8,128)S(1)}, f32[2048,128]{1,0:T(8,128)}, f32[2048,128]{1,0:T(8,128)S(1)}, f32[2048,128]{1,0:T(8,128)S(1)}) custom-call(f32[3,20,40,160]{3,2,1,0:T(8,128)S(1)} %copy-done.24, bf16[256,256]{1,0:T(8,128)(2,1)S(1)} %copy-done.18, bf16[256,256]{1,0:T(8,128)(2,1)S(1)} %copy-done.20, ...), custom_call_target="tpu_custom_call" | custom-call | flops 1610612736 | bytes 4194304 | tf_op jit(solution)/shard_map/first_synth/pallas_call | solution.py:144
  13.3 32.7 %all_to_all.128 = f32[8,256,128]{2,1,0:T(8,128)S(1)} all-to-all(f32[8,256,128]{2,1,0:T(8,128)S(1)} %bitcast.26), channel_id=1, replica_groups=mesh['row'=8,'col'=4] {'row'}, dimensions={0} | all-to-all | bytes 2097152 | tf_op jit(solution)/shard_map/all_to_all | solution.py:502
  46.0 29.7 %all_to_all.129 = f32[8,256,128]{2,1,0:T(8,128)} all-to-all(f32[8,256,128]{2,1,0:T(8,128)S(1)} %bitcast.25), channel_id=1, replica_groups=mesh['row'=8,'col'=4] {'row'}, dimensions={0} | all-to-all | bytes 2097152 | tf_op jit(solution)/shard_map/all_to_all | solution.py:502
  75.7 29.8 %all_to_all.130 = f32[8,256,128]{2,1,0:T(8,128)} all-to-all(f32[8,256,128]{2,1,0:T(8,128)S(1)} %bitcast.24), channel_id=1, replica_groups=mesh['row'=8,'col'=4] {'row'}, dimensions={0} | all-to-all | bytes 2097152 | tf_op jit(solution)/shard_map/all_to_all | solution.py:502
  113.8 21.8 %all-to-all-done.4 = f32[8,256,128]{2,1,0:T(8,128)S(1)} async-done(((f32[8,256,128]{2,1,0:T(8,128)}), f32[8,256,128]{2,1,0:T(8,128)S(1)}, u32[]{:S(2)}, u32[]{:S(2)}) %all-to-all-start.4) | async-done | bytes 1048608 | tf_op jit(solution)/shard_map/all_to_all | solution.py:502
  135.6 3.7 all-to-all-start.9
  145.2 17.5 %all-to-all-done.9.b_ref = f32[4,4,240,128]{3,2,1,0:T(8,128)S(1)} async-done(((f32[4,4,240,128]{3,2,1,0:T(8,128)}), f32[4,4,240,128]{3,2,1,0:T(8,128)S(1)}, u32[]{:S(2)}, u32[]{:S(2)}) %all-to-all-start.9) | async-done | bytes 1966112 | tf_op jit(solution)/shard_map/all_to_all | solution.py:502
  164.0 3.6 all-to-all-start.13
  173.5 17.0 %all-to-all-done.13.b_ref = f32[4,4,240,128]{3,2,1,0:T(8,128)S(1)} async-done(((f32[4,4,240,128]{3,2,1,0:T(8,128)}), f32[4,4,240,128]{3,2,1,0:T(8,128)S(1)}, u32[]{:S(2)}, u32[]{:S(2)}) %all-to-all-start.13) | async-done | bytes 1966112 | tf_op jit(solution)/shard_map/all_to_all | solution.py:502
  191.8 3.6 all-to-all-start.1
  200.1 18.2 %all-to-all-done.1.b_ref = f32[4,4,240,128]{3,2,1,0:T(8,128)S(1)} async-done(((f32[4,4,240,128]{3,2,1,0:T(8,128)}), f32[4,4,240,128]{3,2,1,0:T(8,128)S(1)}, u32[]{:S(2)}, u32[]{:S(2)}) %all-to-all-start.1) | async-done | bytes 1966112 | tf_op jit(solution)/shard_map/all_to_all | solution.py:502
  219.5 3.6 all-to-all-start.5
  223.2 6.8 %earlier_orders.6.base_ref = f32[3,8,64,256]{3,2,1,0:T(8,128)S(1)} custom-call(f32[6,3,32,64,256]{4,3,2,1,0:T(8,128)} %vel_ref.7, f32[6,3,32,64,256]{4,3,2,1,0:T(8,128)} %vel_ref.7, f32[6,3,32,64,256]{4,3,2,1,0:T(8,128)} %vel_ref.7, f32[6,3,32,64,256]{4,3,2,1,0:T(8,128)} %vel_ref.7, f32[6,3,32,64,256]{4,3,2,1,0:T(8,128)} %vel_ref.7, ...), custom_call_target="tpu_custom_call" | custom-call | flops 14155776 | bytes 17301504 | tf_op jit(solution)/shard_map/earlier_orders/pallas_call | solution.py:257
  230.0 7.1 %third_dimension.6 = f32[4,4,120,128]{3,2,1,0:T(8,128)} custom-call(f32[4,4,240,128]{3,2,1,0:T(8,128)S(1)} %copy-done.5, f32[6,3,32,64,256]{4,3,2,1,0:T(8,128)} %vel_ref.7, f32[6,3,32,64,256]{4,3,2,1,0:T(8,128)} %vort_ref.7, f32[3,8,64,256]{3,2,1,0:T(8,128)S(1)} %earlier_orders.6.base_ref, bf16[160,256]{1,0:T(8,128)(2,1)S(1)} %copy-done.10, ...), custom_call_target="tpu_custom_call" | custom-call | flops 4429185024 | bytes 7667712 | tf_op jit(solution)/shard_map/third_dimension/pallas_call | solution.py:304
  237.1 8.9 %all-to-all-done.5.b_ref = f32[4,4,240,128]{3,2,1,0:T(8,128)S(1)} async-done(((f32[4,4,240,128]{3,2,1,0:T(8,128)}), f32[4,4,240,128]{3,2,1,0:T(8,128)S(1)}, u32[]{:S(2)}, u32[]{:S(2)}) %all-to-all-start.5) | async-done | bytes 1966112 | tf_op jit(solution)/shard_map/all_to_all | solution.py:502
  249.6 6.5 %earlier_orders.7.base_ref = f32[3,8,64,256]{3,2,1,0:T(8,128)S(1)} custom-call(f32[6,3,32,64,256]{4,3,2,1,0:T(8,128)} %vel_ref.7, f32[6,3,32,64,256]{4,3,2,1,0:T(8,128)} %vel_ref.7, f32[6,3,32,64,256]{4,3,2,1,0:T(8,128)} %vel_ref.7, f32[6,3,32,64,256]{4,3,2,1,0:T(8,128)} %vel_ref.7, f32[6,3,32,64,256]{4,3,2,1,0:T(8,128)} %vel_ref.7, ...), custom_call_target="tpu_custom_call" | custom-call | flops 14155776 | bytes 17301504 | tf_op jit(solution)/shard_map/earlier_orders/pallas_call | solution.py:257
  256.1 7.1 %third_dimension.7 = f32[4,4,120,128]{3,2,1,0:T(8,128)} custom-call(f32[4,4,240,128]{3,2,1,0:T(8,128)S(1)} %copy-done.3, f32[6,3,32,64,256]{4,3,2,1,0:T(8,128)} %vel_ref.7, f32[6,3,32,64,256]{4,3,2,1,0:T(8,128)} %vort_ref.7, f32[3,8,64,256]{3,2,1,0:T(8,128)S(1)} %earlier_orders.7.base_ref, bf16[160,256]{1,0:T(8,128)(2,1)S(1)} %copy-done.10, ...), custom_call_target="tpu_custom_call" | custom-call | flops 4429185024 | bytes 7667712 | tf_op jit(solution)/shard_map/third_dimension/pallas_call | solution.py:304
  263.1 4.2 %all-to-all-start.14 = ((f32[4,4,120,128]{3,2,1,0:T(8,128)}), f32[4,4,120,128]{3,2,1,0:T(8,128)}, u32[]{:S(2)}, u32[]{:S(2)}) async-start(f32[4,4,120,128]{3,2,1,0:T(8,128)} %third_dimension.7), calls=%async_computation.14 | async-start | bytes 1966080 | tf_op jit(solution)/shard_map/all_to_all | solution.py:502
  267.4 6.5 %earlier_orders.4.base_ref = f32[3,8,64,256]{3,2,1,0:T(8,128)S(1)} custom-call(f32[6,3,32,64,256]{4,3,2,1,0:T(8,128)} %vel_ref.7, f32[6,3,32,64,256]{4,3,2,1,0:T(8,128)} %vel_ref.7, f32[6,3,32,64,256]{4,3,2,1,0:T(8,128)} %vel_ref.7, f32[6,3,32,64,256]{4,3,2,1,0:T(8,128)} %vel_ref.7, f32[6,3,32,64,256]{4,3,2,1,0:T(8,128)} %vel_ref.7, ...), custom_call_target="tpu_custom_call" | custom-call | flops 14155776 | bytes 17301504 | tf_op jit(solution)/shard_map/earlier_orders/pallas_call | solution.py:257
  273.9 7.0 %third_dimension.4 = f32[4,4,120,128]{3,2,1,0:T(8,128)} custom-call(f32[4,4,240,128]{3,2,1,0:T(8,128)S(1)} %copy-done.1, f32[6,3,32,64,256]{4,3,2,1,0:T(8,128)} %vel_ref.7, f32[6,3,32,64,256]{4,3,2,1,0:T(8,128)} %vort_ref.7, f32[3,8,64,256]{3,2,1,0:T(8,128)S(1)} %earlier_orders.4.base_ref, bf16[160,256]{1,0:T(8,128)(2,1)S(1)} %copy-done.10, ...), custom_call_target="tpu_custom_call" | custom-call | flops 4429185024 | bytes 7667712 | tf_op jit(solution)/shard_map/third_dimension/pallas_call | solution.py:304
  280.9 4.2 %all-to-all-start.2 = ((f32[4,4,120,128]{3,2,1,0:T(8,128)}), f32[4,4,120,128]{3,2,1,0:T(8,128)}, u32[]{:S(2)}, u32[]{:S(2)}) async-start(f32[4,4,120,128]{3,2,1,0:T(8,128)} %third_dimension.4), calls=%async_computation.2 | async-start | bytes 1966080 | tf_op jit(solution)/shard_map/all_to_all | solution.py:502
  285.2 6.4 %earlier_orders.5.base_ref = f32[3,8,64,256]{3,2,1,0:T(8,128)S(1)} custom-call(f32[6,3,32,64,256]{4,3,2,1,0:T(8,128)} %vel_ref.7, f32[6,3,32,64,256]{4,3,2,1,0:T(8,128)} %vel_ref.7, f32[6,3,32,64,256]{4,3,2,1,0:T(8,128)} %vel_ref.7, f32[6,3,32,64,256]{4,3,2,1,0:T(8,128)} %vel_ref.7, f32[6,3,32,64,256]{4,3,2,1,0:T(8,128)} %vel_ref.7, ...), custom_call_target="tpu_custom_call" | custom-call | flops 14155776 | bytes 17301504 | tf_op jit(solution)/shard_map/earlier_orders/pallas_call | solution.py:257
  291.6 7.1 %third_dimension.5 = f32[4,4,120,128]{3,2,1,0:T(8,128)} custom-call(f32[4,4,240,128]{3,2,1,0:T(8,128)S(1)} %all-to-all-done.5.b_ref, f32[6,3,32,64,256]{4,3,2,1,0:T(8,128)} %vel_ref.7, f32[6,3,32,64,256]{4,3,2,1,0:T(8,128)} %vort_ref.7, f32[3,8,64,256]{3,2,1,0:T(8,128)S(1)} %earlier_orders.5.base_ref, bf16[160,256]{1,0:T(8,128)(2,1)S(1)} %copy-done.10, ...), custom_call_target="tpu_custom_call" | custom-call | flops 4429185024 | bytes 7667712 | tf_op jit(solution)/shard_map/third_dimension/pallas_call | solution.py:304
  298.6 4.3 %all-to-all-start.6 = ((f32[4,4,120,128]{3,2,1,0:T(8,128)}), f32[4,4,120,128]{3,2,1,0:T(8,128)S(1)}, u32[]{:S(2)}, u32[]{:S(2)}) async-start(f32[4,4,120,128]{3,2,1,0:T(8,128)} %third_dimension.5), calls=%async_computation.6 | async-start | bytes 1966080 | tf_op jit(solution)/shard_map/all_to_all | solution.py:502
  305.7 9.0 %all-to-all-done.6.c_ref = f32[4,4,120,128]{3,2,1,0:T(8,128)S(1)} async-done(((f32[4,4,120,128]{3,2,1,0:T(8,128)}), f32[4,4,120,128]{3,2,1,0:T(8,128)S(1)}, u32[]{:S(2)}, u32[]{:S(2)}) %all-to-all-start.6) | async-done | bytes 983072 | tf_op jit(solution)/shard_map/all_to_all | solution.py:502
  319.2 4.2 %second_back.7 = f32[1216,128]{1,0:T(8,128)} custom-call(f32[4,4,120,128]{3,2,1,0:T(8,128)} %all-to-all-done.14.c_ref, bf16[160,256]{1,0:T(8,128)(2,1)S(1)} %copy-done.26, bf16[160,256]{1,0:T(8,128)(2,1)S(1)} %copy-done.28), custom_call_target="tpu_custom_call" | custom-call | flops 805306368 | bytes 1605632 | tf_op jit(solution)/shard_map/second_back/pallas_call | solution.py:349
  323.4 13.2 %all-to-all-done.11 = f32[8,152,128]{2,1,0:T(8,128)S(1)} async-done(((f32[8,152,128]{2,1,0:T(8,128)}), f32[8,152,128]{2,1,0:T(8,128)S(1)}, u32[]{:S(2)}, u32[]{:S(2)}) %all-to-all-start.11) | async-done | bytes 622624 | tf_op jit(solution)/shard_map/all_to_all | solution.py:502
  340.2 4.2 %second_back.4 = f32[1216,128]{1,0:T(8,128)} custom-call(f32[4,4,120,128]{3,2,1,0:T(8,128)} %all-to-all-done.2.c_ref, bf16[160,256]{1,0:T(8,128)(2,1)S(1)} %copy-done.26, bf16[160,256]{1,0:T(8,128)(2,1)S(1)} %copy-done.28), custom_call_target="tpu_custom_call" | custom-call | flops 805306368 | bytes 1605632 | tf_op jit(solution)/shard_map/second_back/pallas_call | solution.py:349
  344.4 13.1 %all-to-all-done.15 = f32[8,152,128]{2,1,0:T(8,128)S(1)} async-done(((f32[8,152,128]{2,1,0:T(8,128)}), f32[8,152,128]{2,1,0:T(8,128)S(1)}, u32[]{:S(2)}, u32[]{:S(2)}) %all-to-all-start.15) | async-done | bytes 622624 | tf_op jit(solution)/shard_map/all_to_all | solution.py:502
  363.9 14.6 %all-to-all-done.3 = f32[8,152,128]{2,1,0:T(8,128)S(1)} async-done(((f32[8,152,128]{2,1,0:T(8,128)}), f32[8,152,128]{2,1,0:T(8,128)S(1)}, u32[]{:S(2)}, u32[]{:S(2)}) %all-to-all-start.3) | async-done | bytes 622624 | tf_op jit(solution)/shard_map/all_to_all | solution.py:502
  382.1 17.3 %all-to-all-done.7 = f32[8,152,128]{2,1,0:T(8,128)S(1)} async-done(((f32[8,152,128]{2,1,0:T(8,128)}), f32[8,152,128]{2,1,0:T(8,128)S(1)}, u32[]{:S(2)}, u32[]{:S(2)}) %all-to-all-start.7) | async-done | bytes 622624 | tf_op jit(solution)/shard_map/all_to_all | solution.py:502
  399.5 7.3 %last_projection.1 = f32[3,20,40,160]{3,2,1,0:T(8,128)} custom-call(f32[10]{0:T(128)S(1)} %convert_multiply_fusion.1.refs_0_, f32[1216,128]{1,0:T(8,128)S(1)} %bitcast.18, f32[1216,128]{1,0:T(8,128)S(1)} %bitcast.19, f32[1216,128]{1,0:T(8,128)S(1)} %bitcast.16, f32[1216,128]{1,0:T(8,128)S(1)} %bitcast.17, bf16[256,256]{1,0:T(8,128)(2,1)S(1)} %copy-done.19, ...), custom_call_target="tpu_custom_call" | custom-call | flops 956301312 | bytes 4026368 | tf_op jit(solution)/shard_map/last_projection/pallas_call | solution.py:435
  (82 shorter events, 56.3 us)
Async XLA Ops:
  1.8 1.7 copy-start.24
  3.5 9.8 %copy-start.22 = (f32[8,256]{1,0:T(8,128)}, f32[8,256]{1,0:T(8,128)S(1)}, u32[]{:S(2)}) copy-start(f32[8,256]{1,0:T(8,128)S(1)} %broadcast_in_dim.19.wave_ref.refs_7_) | copy-start | bytes 24580
  75.7 33.4 %copy-start.25 = (bf16[160,256]{1,0:T(8,128)(2,1)S(1)}, bf16[160,256]{1,0:T(8,128)(2,1)}, u32[]{:S(2)}) copy-start(bf16[160,256]{1,0:T(8,128)(2,1)} %constant.82.clone.high_ref) | copy-start | bytes 245764
  75.7 33.4 %copy-start.27 = (bf16[160,256]{1,0:T(8,128)(2,1)S(1)}, bf16[160,256]{1,0:T(8,128)(2,1)}, u32[]{:S(2)}) copy-start(bf16[160,256]{1,0:T(8,128)(2,1)} %constant.83.clone.low_ref) | copy-start | bytes 245764
  75.7 33.4 %copy-start.29 = (bf16[160,256]{1,0:T(8,128)(2,1)S(1)}, bf16[160,256]{1,0:T(8,128)(2,1)}, u32[]{:S(2)}) copy-start(bf16[160,256]{1,0:T(8,128)(2,1)} %constant.84.clone.shigh_ref) | copy-start | bytes 245764
  75.7 33.4 %copy-start.30 = (bf16[160,256]{1,0:T(8,128)(2,1)S(1)}, bf16[160,256]{1,0:T(8,128)(2,1)}, u32[]{:S(2)}) copy-start(bf16[160,256]{1,0:T(8,128)(2,1)} %constant.85.clone.slow_ref) | copy-start | bytes 245764
  105.5 30.1 %all-to-all-start.4 = ((f32[8,256,128]{2,1,0:T(8,128)}), f32[8,256,128]{2,1,0:T(8,128)S(1)}, u32[]{:S(2)}, u32[]{:S(2)}) async-start(f32[8,256,128]{2,1,0:T(8,128)} %bitcast.4), calls=%async_computation.4 | async-start | bytes 2097152 | tf_op jit(solution)/shard_map/all_to_all | solution.py:502
  135.6 27.1 %all-to-all-start.9 = ((f32[4,4,240,128]{3,2,1,0:T(8,128)}), f32[4,4,240,128]{3,2,1,0:T(8,128)S(1)}, u32[]{:S(2)}, u32[]{:S(2)}) async-start(f32[4,4,240,128]{3,2,1,0:T(8,128)} %copy-done.8), calls=%async_computation.9 | async-start | bytes 3932160 | tf_op jit(solution)/shard_map/all_to_all | solution.py:502
  164.0 26.5 %all-to-all-start.13 = ((f32[4,4,240,128]{3,2,1,0:T(8,128)}), f32[4,4,240,128]{3,2,1,0:T(8,128)S(1)}, u32[]{:S(2)}, u32[]{:S(2)}) async-start(f32[4,4,240,128]{3,2,1,0:T(8,128)} %copy-done.9), calls=%async_computation.13 | async-start | bytes 3932160 | tf_op jit(solution)/shard_map/all_to_all | solution.py:502
  191.8 26.5 %all-to-all-start.1 = ((f32[4,4,240,128]{3,2,1,0:T(8,128)}), f32[4,4,240,128]{3,2,1,0:T(8,128)S(1)}, u32[]{:S(2)}, u32[]{:S(2)}) async-start(f32[4,4,240,128]{3,2,1,0:T(8,128)} %copy-done.7), calls=%async_computation.1 | async-start | bytes 3932160 | tf_op jit(solution)/shard_map/all_to_all | solution.py:502
  219.5 26.5 %all-to-all-start.5 = ((f32[4,4,240,128]{3,2,1,0:T(8,128)}), f32[4,4,240,128]{3,2,1,0:T(8,128)S(1)}, u32[]{:S(2)}, u32[]{:S(2)}) async-start(f32[4,4,240,128]{3,2,1,0:T(8,128)} %copy-done.6), calls=%async_computation.5 | async-start | bytes 3932160 | tf_op jit(solution)/shard_map/all_to_all | solution.py:502
  223.2 6.9 %copy-start.5 = (f32[4,4,240,128]{3,2,1,0:T(8,128)S(1)}, f32[4,4,240,128]{3,2,1,0:T(8,128)}, u32[]{:S(2)}) copy-start(f32[4,4,240,128]{3,2,1,0:T(8,128)} %copy-done.4) | copy-start | bytes 5898244
  223.2 6.9 %copy-start.10 = (bf16[160,256]{1,0:T(8,128)(2,1)S(1)}, bf16[160,256]{1,0:T(8,128)(2,1)}, u32[]{:S(2)}) copy-start(bf16[160,256]{1,0:T(8,128)(2,1)} %constant.86.clone.high_ref) | copy-start | bytes 245764
  223.2 6.8 %copy-start.11 = (bf16[160,256]{1,0:T(8,128)(2,1)S(1)}, bf16[160,256]{1,0:T(8,128)(2,1)}, u32[]{:S(2)}) copy-start(bf16[160,256]{1,0:T(8,128)(2,1)} %constant.87.clone.low_ref) | copy-start | bytes 245764
  223.2 6.8 %copy-start.12 = (bf16[160,256]{1,0:T(8,128)(2,1)S(1)}, bf16[160,256]{1,0:T(8,128)(2,1)}, u32[]{:S(2)}) copy-start(bf16[160,256]{1,0:T(8,128)(2,1)} %constant.88.clone.shigh_ref) | copy-start | bytes 245764
  223.2 6.8 %copy-start.13 = (bf16[160,256]{1,0:T(8,128)(2,1)S(1)}, bf16[160,256]{1,0:T(8,128)(2,1)}, u32[]{:S(2)}) copy-start(bf16[160,256]{1,0:T(8,128)(2,1)} %constant.89.clone.slow_ref) | copy-start | bytes 245764
  246.0 17.1 %all-to-all-start.10 = ((f32[4,4,120,128]{3,2,1,0:T(8,128)}), f32[4,4,120,128]{3,2,1,0:T(8,128)S(1)}, u32[]{:S(2)}, u32[]{:S(2)}) async-start(f32[4,4,120,128]{3,2,1,0:T(8,128)} %third_dimension.6), calls=%async_computation.10 | async-start | bytes 1966080 | tf_op jit(solution)/shard_map/all_to_all | solution.py:502
  249.5 6.5 %copy-start.3 = (f32[4,4,240,128]{3,2,1,0:T(8,128)S(1)}, f32[4,4,240,128]{3,2,1,0:T(8,128)}, u32[]{:S(2)}) copy-start(f32[4,4,240,128]{3,2,1,0:T(8,128)} %copy-done.2) | copy-start | bytes 5898244
  263.1 17.8 %all-to-all-start.14 = ((f32[4,4,120,128]{3,2,1,0:T(8,128)}), f32[4,4,120,128]{3,2,1,0:T(8,128)}, u32[]{:S(2)}, u32[]{:S(2)}) async-start(f32[4,4,120,128]{3,2,1,0:T(8,128)} %third_dimension.7), calls=%async_computation.14 | async-start | bytes 1966080 | tf_op jit(solution)/shard_map/all_to_all | solution.py:502
  267.4 6.5 %copy-start.1 = (f32[4,4,240,128]{3,2,1,0:T(8,128)S(1)}, f32[4,4,240,128]{3,2,1,0:T(8,128)}, u32[]{:S(2)}) copy-start(f32[4,4,240,128]{3,2,1,0:T(8,128)} %copy-done) | copy-start | bytes 5898244
  280.9 17.7 %all-to-all-start.2 = ((f32[4,4,120,128]{3,2,1,0:T(8,128)}), f32[4,4,120,128]{3,2,1,0:T(8,128)}, u32[]{:S(2)}, u32[]{:S(2)}) async-start(f32[4,4,120,128]{3,2,1,0:T(8,128)} %third_dimension.4), calls=%async_computation.2 | async-start | bytes 1966080 | tf_op jit(solution)/shard_map/all_to_all | solution.py:502
  298.6 4.3 %copy-start.26 = (bf16[160,256]{1,0:T(8,128)(2,1)S(1)}, bf16[160,256]{1,0:T(8,128)(2,1)}, u32[]{:S(2)}) copy-start(bf16[160,256]{1,0:T(8,128)(2,1)} %constant.82.clone.high_ref) | copy-start | bytes 245764
  298.6 4.3 %copy-start.28 = (bf16[160,256]{1,0:T(8,128)(2,1)S(1)}, bf16[160,256]{1,0:T(8,128)(2,1)}, u32[]{:S(2)}) copy-start(bf16[160,256]{1,0:T(8,128)(2,1)} %constant.83.clone.low_ref) | copy-start | bytes 245764
  298.6 16.1 %all-to-all-start.6 = ((f32[4,4,120,128]{3,2,1,0:T(8,128)}), f32[4,4,120,128]{3,2,1,0:T(8,128)S(1)}, u32[]{:S(2)}, u32[]{:S(2)}) async-start(f32[4,4,120,128]{3,2,1,0:T(8,128)} %third_dimension.5), calls=%async_computation.6 | async-start | bytes 1966080 | tf_op jit(solution)/shard_map/all_to_all | solution.py:502
  315.7 20.9 %all-to-all-start.11 = ((f32[8,152,128]{2,1,0:T(8,128)}), f32[8,152,128]{2,1,0:T(8,128)S(1)}, u32[]{:S(2)}, u32[]{:S(2)}) async-start(f32[8,152,128]{2,1,0:T(8,128)} %bitcast.10), calls=%async_computation.11 | async-start | bytes 1245184 | tf_op jit(solution)/shard_map/all_to_all | solution.py:502
  336.6 20.9 %all-to-all-start.15 = ((f32[8,152,128]{2,1,0:T(8,128)}), f32[8,152,128]{2,1,0:T(8,128)S(1)}, u32[]{:S(2)}, u32[]{:S(2)}) async-start(f32[8,152,128]{2,1,0:T(8,128)} %bitcast.14), calls=%async_computation.15 | async-start | bytes 1245184 | tf_op jit(solution)/shard_map/all_to_all | solution.py:502
  340.1 20.9 %copy-start.17 = (f32[4,4,120,128]{3,2,1,0:T(8,128)S(1)}, f32[4,4,120,128]{3,2,1,0:T(8,128)}, u32[]{:S(2)}) copy-start(f32[4,4,120,128]{3,2,1,0:T(8,128)} %copy-done.16) | copy-start | bytes 2949124
  357.5 20.9 %all-to-all-start.3 = ((f32[8,152,128]{2,1,0:T(8,128)}), f32[8,152,128]{2,1,0:T(8,128)S(1)}, u32[]{:S(2)}, u32[]{:S(2)}) async-start(f32[8,152,128]{2,1,0:T(8,128)} %bitcast.2), calls=%async_computation.3 | async-start | bytes 1245184 | tf_op jit(solution)/shard_map/all_to_all | solution.py:502
  361.1 38.4 %copy-start.19 = (bf16[256,256]{1,0:T(8,128)(2,1)S(1)}, bf16[256,256]{1,0:T(8,128)(2,1)}, u32[]{:S(2)}) copy-start(bf16[256,256]{1,0:T(8,128)(2,1)} %constant.80.clone.high_ref.refs_5_) | copy-start | bytes 393220
  361.1 38.4 %copy-start.21 = (bf16[256,256]{1,0:T(8,128)(2,1)S(1)}, bf16[256,256]{1,0:T(8,128)(2,1)}, u32[]{:S(2)}) copy-start(bf16[256,256]{1,0:T(8,128)(2,1)} %constant.81.clone.low_ref.refs_6_) | copy-start | bytes 393220
  361.1 38.4 %copy-start.23 = (f32[8,256]{1,0:T(8,128)S(1)}, f32[8,256]{1,0:T(8,128)}, u32[]{:S(2)}) copy-start(f32[8,256]{1,0:T(8,128)} %copy-done.22) | copy-start | bytes 24580
  378.5 20.9 %all-to-all-start.7 = ((f32[8,152,128]{2,1,0:T(8,128)}), f32[8,152,128]{2,1,0:T(8,128)S(1)}, u32[]{:S(2)}, u32[]{:S(2)}) async-start(f32[8,152,128]{2,1,0:T(8,128)} %bitcast.6), calls=%async_computation.7 | async-start | bytes 1245184 | tf_op jit(solution)/shard_map/all_to_all | solution.py:502
  (12 other events, 14.3 us)

commit v2 on v1

--- a/solution.py
+++ b/solution.py
@@ -41,7 +41,7 @@
 def halves(table):
     high = table.astype(ml_dtypes.bfloat16)
     low = (table - high.astype(np.float64)).astype(ml_dtypes.bfloat16)
-    return jnp.asarray(high), jnp.asarray(low)
+    return high, low
 
 
 def pieces_of(values):
@@ -138,6 +138,7 @@
 
 
 def first_synth(coeffs, table, wave, dims, lanes):
+    table = [jnp.asarray(part) for part in table]
     chunks = dims[0]
     grid_len = table[0].shape[0]
     height = grid_len // chunks * (lanes // LANES)
@@ -153,7 +154,7 @@
     )(coeffs, table[0], table[1], wave)
 
 
-def second_synth_kernel(dims, a_ref, high_ref, low_ref, shigh_ref, slow_ref, out_ref):
+def second_synth_kernel(dims, a_ref, table_ref, *out_refs):
     rows, xc, ky_len, kz_len, cols, y_len, pack = dims
     group = 5 * kz_len
     wide = round_up(group, LANES)
@@ -172,9 +173,9 @@
             window = line[low : low + (wide // LANES) + (1 if off else 0)]
             found.append(turn(jnp.concatenate(window, axis=1), -off)[:, :wide])
         turned.append(jnp.concatenate(found, axis=0).T[:group])
-    plain = dot_data_left(jnp.concatenate(turned, axis=0), high_ref[...], low_ref[...])
+    plain = dot_data_left(jnp.concatenate(turned, axis=0), table_ref[0], table_ref[1])
     slope_in = [t[c * kz_len : (c + 1) * kz_len] for t in turned for c in (0, 2)]
-    slope = dot_data_left(jnp.concatenate(slope_in, axis=0), shigh_ref[...], slow_ref[...])
+    slope = dot_data_left(jnp.concatenate(slope_in, axis=0), table_ref[2], table_ref[3])
     fields = []
     for part in range(pack):
         own = plain[part * group : (part + 1) * group]
@@ -192,20 +193,20 @@
         )
     for dest in range(cols):
         tile, off = divmod(dest * y_len, LANES)
-        out_ref[dest, 0] = lane_pack(
+        out_refs[dest][0] = lane_pack(
             [f[:, tile * LANES : (tile + 1) * LANES] for f in fields], y_len, off
         )[0]
 
 
-def second_synth(arrived, table, slopes, dims):
+def second_synth(arrived, table, dims):
     rows, xc, ky_len, kz_len, cols, y_len, pack = dims
     packs = xc // pack
     return pl.pallas_call(
         functools.partial(second_synth_kernel, dims),
         grid=(packs,),
-        in_specs=[whole(a) for a in (arrived, *table, *slopes)],
-        out_specs=pl.BlockSpec((cols, 1, 6 * kz_len, LANES), lambda i: (0, i, 0, 0)),
-        out_shape=jax.ShapeDtypeStruct((cols, packs, 6 * kz_len, LANES), F32),
+        in_specs=[whole(arrived), whole(table)],
+        out_specs=[pl.BlockSpec((1, 6 * kz_len, LANES), lambda i: (i, 0, 0))] * cols,
+        out_shape=[jax.ShapeDtypeStruct((packs, 6 * kz_len, LANES), F32)] * cols,
         compiler_params=params("arbitrary"),
         cost_estimate=pl.CostEstimate(
             flops=6 * xc * 7 * kz_len * 256 * 256 * 2,
@@ -213,7 +214,7 @@
             transcendentals=0,
         ),
         name="second_synth",
-    )(arrived, *table, *slopes)
+    )(arrived, table)
 
 
 def cross(left, right):
@@ -268,18 +269,20 @@
     )(*[velocity] * (orders - 1), *[vorticity] * (orders - 1))
 
 
-def third_kernel(dims, b_ref, vel_ref, vort_ref, base_ref, high_ref, low_ref, shigh_ref, slow_ref, out_ref):
+def third_kernel(dims, *refs):
     kz_len, cols, y_len, pack = dims
-    grid_len = high_ref.shape[1]
+    b_refs, out_refs = refs[:cols], refs[cols + 4 :]
+    vel_ref, vort_ref, base_ref, table_ref = refs[cols : cols + 4]
+    grid_len = table_ref.shape[2]
 
     def stack(field):
         return jnp.concatenate(
-            [b_ref[src, 0, field * kz_len : (field + 1) * kz_len, :] for src in range(cols)], axis=0
+            [b_ref[0, field * kz_len : (field + 1) * kz_len, :] for b_ref in b_refs], axis=0
         ).T
 
     lines = jnp.concatenate([stack(field) for field in range(6)], axis=0)
-    plain = dot_data_left(lines, high_ref[...], low_ref[...])
-    slope = dot_data_left(lines[: 2 * LANES], shigh_ref[...], slow_ref[...])
+    plain = dot_data_left(lines, table_ref[0], table_ref[1])
+    slope = dot_data_left(lines[: 2 * LANES], table_ref[2], table_ref[3])
     at = [plain[f * LANES : (f + 1) * LANES] for f in range(6)]
     vel_new = at[:3]
     vort_new = [at[4] - slope[LANES:], slope[:LANES] + at[5], at[3]]
@@ -288,52 +291,53 @@
     vort = [vort_ref[0, c].reshape(flat) for c in range(3)]
     one, two = cross(vel_new, vort), cross(vel, vort_new)
     total = [one[c] + two[c] + base_ref[c].reshape(flat) for c in range(3)]
-    result = dot_data_right(high_ref[...], low_ref[...], jnp.concatenate(total, axis=0))
+    result = dot_data_right(table_ref[0], table_ref[1], jnp.concatenate(total, axis=0))
     for dest in range(cols):
         for comp in range(3):
-            out_ref[dest, 0, comp * kz_len : (comp + 1) * kz_len, :] = result[
+            out_refs[dest][0, comp * kz_len : (comp + 1) * kz_len, :] = result[
                 dest * kz_len : (dest + 1) * kz_len, comp * LANES : (comp + 1) * LANES
             ]
 
 
-def third(arrived, velocity, vorticity, base, table, slopes, chunk, dims):
+def third(arrived, velocity, vorticity, base, table, chunk, dims):
     kz_len, cols, y_len, pack = dims
-    packs = arrived.shape[1]
+    packs = arrived[0].shape[0]
     grid_len = velocity.shape[-1]
     stored = pl.BlockSpec((1, 3, pack, y_len, grid_len), lambda i: (0, 0, chunk * packs + i, 0, 0))
     return pl.pallas_call(
         functools.partial(third_kernel, dims),
         grid=(packs,),
         in_specs=[
-            pl.BlockSpec((cols, 1, 6 * kz_len, LANES), lambda i: (0, i, 0, 0)),
+            *[pl.BlockSpec((1, 6 * kz_len, LANES), lambda i: (i, 0, 0))] * cols,
             stored,
             stored,
             pl.BlockSpec((3, pack, y_len, grid_len), lambda i: (0, i, 0, 0)),
-            *[whole(a) for a in (*table, *slopes)],
+            whole(table),
         ],
-        out_specs=pl.BlockSpec((cols, 1, 3 * kz_len, LANES), lambda i: (0, i, 0, 0)),
-        out_shape=jax.ShapeDtypeStruct((cols, packs, 3 * kz_len, LANES), F32),
+        out_specs=[pl.BlockSpec((1, 3 * kz_len, LANES), lambda i: (i, 0, 0))] * cols,
+        out_shape=[jax.ShapeDtypeStruct((packs, 3 * kz_len, LANES), F32)] * cols,
         compiler_params=params("arbitrary"),
         cost_estimate=pl.CostEstimate(
             flops=6 * packs * LANES * 11 * 256 * 256 * 2,
-            bytes_accessed=4 * (arrived.size * 3 // 2 + packs * LANES * grid_len * 9),
+            bytes_accessed=4 * (cols * arrived[0].size * 3 // 2 + packs * LANES * grid_len * 9),
             transcendentals=0,
         ),
         name="third_dimension",
-    )(arrived, velocity, vorticity, base, *table, *slopes)
-
-
-def second_back_kernel(dims, c_ref, high_ref, low_ref, out_ref):
+    )(*arrived, velocity, vorticity, base, table)
+
+
+def second_back_kernel(dims, *refs):
     rows, xc, ky_len, kz_len, cols, y_len, pack = dims
+    c_refs, table_ref, out_ref = refs[:cols], refs[cols], refs[cols + 1]
     width = 3 * kz_len
     high_pad = round_up(width, LANES)
     lines = []
     for part in range(pack):
-        tiles = lane_pack([c_ref[src, 0] for src in range(cols)], y_len, part * y_len)
+        tiles = lane_pack([c_ref[0] for c_ref in c_refs], y_len, part * y_len)
         lines.append(jnp.concatenate(tiles, axis=1))
         if high_pad > width:
             lines.append(jnp.zeros((high_pad - width, cols * y_len), F32))
-    result = dot_data_right(high_ref[...], low_ref[...], jnp.concatenate(lines, axis=0))
+    result = dot_data_right(table_ref[0], table_ref[1], jnp.concatenate(lines, axis=0))
     for part in range(pack):
         own = result[:, part * high_pad : (part + 1) * high_pad]
         tiles = lane_pack([own[ky * rows : (ky + 1) * rows] for ky in range(ky_len)], width)
@@ -350,19 +354,19 @@
         functools.partial(second_back_kernel, dims),
         grid=(packs,),
         in_specs=[
-            pl.BlockSpec((cols, 1, 3 * kz_len, LANES), lambda i: (0, i, 0, 0)),
-            *[whole(a) for a in table],
+            *[pl.BlockSpec((1, 3 * kz_len, LANES), lambda i: (i, 0, 0))] * cols,
+            whole(table),
         ],
         out_specs=pl.BlockSpec((rows * xc * lanes // LANES, LANES), lambda i: (0, 0)),
         out_shape=jax.ShapeDtypeStruct((rows * xc * lanes // LANES, LANES), F32),
         compiler_params=params("arbitrary"),
         cost_estimate=pl.CostEstimate(
             flops=6 * xc * LANES * 256 * 256 * 2,
-            bytes_accessed=4 * (arrived.size + rows * xc * lanes),
+            bytes_accessed=4 * (cols * arrived[0].size + rows * xc * lanes),
             transcendentals=0,
         ),
         name="second_back",
-    )(arrived, *table)
+    )(*arrived, table)
 
 
 def last_kernel(dims, *refs):
@@ -430,6 +434,7 @@
 
 def last(parts, table, wave_y, wave_x, wave_z, xc, ky_len, kz_len, modes, scale):
     chunks = len(parts)
+    table = [jnp.asarray(part) for part in table]
     grid_len = table[0].shape[0]
     lanes = parts[0].size * chunks // grid_len
     return pl.pallas_call(
@@ -476,13 +481,27 @@
     ).reshape(-1)
     y_order = (np.arange(rows)[None, :] * ky_len + np.arange(ky_len)[:, None]).reshape(-1)
 
-    def spread_z(table):
-        parts = table.T.reshape(cols, kz_own, grid_len)
-        return np.pad(parts, ((0, 0), (0, kz_len - kz_own), (0, 0))).reshape(cols * kz_len, grid_len)
+    def own_table(stack):
+        return lax.dynamic_index_in_dim(jnp.asarray(stack), lax.axis_index("col"), 0, False)
+
+    def halves_of(plain, sloped):
+        return np.stack([part for table in (plain, sloped) for part in halves(table)])
+
+    def y_table(col):
+        points = np.concatenate([(col ^ k) * y_len + np.arange(y_len) for k in range(cols)])
+        return halves_of(basis[points].T[y_order], slope[points].T[y_order])
+
+    def z_table(col):
+        def spread(table):
+            parts = table.T.reshape(cols, kz_own, grid_len)[[col ^ k for k in range(cols)]]
+            parts = np.pad(parts, ((0, 0), (0, kz_len - kz_own), (0, 0)))
+            return parts.reshape(cols * kz_len, grid_len)
+
+        return halves_of(spread(basis), spread(slope))
 
     table_x = halves(np.pad(basis[x_order], ((0, 0), (0, wide - modes))))
-    table_y, slope_y = halves(basis.T[y_order]), halves(slope.T[y_order])
-    table_z, slope_z = halves(spread_z(basis)), halves(spread_z(slope))
+    table_y = own_table(np.stack([y_table(col) for col in range(cols)]))
+    table_z = own_table(np.stack([z_table(col) for col in range(cols)]))
 
     def wave_of(index):
         return (index // 2).astype(F32) / kmax
@@ -498,21 +517,42 @@
     if kz_len > kz_own:
         coeffs = jnp.pad(coeffs, ((0, 0), (0, 0), (0, kz_len - kz_own), (0, 0)))
 
-    def swap(value, axis):
-        return lax.all_to_all(value, axis, split_axis=0, concat_axis=0, tiled=True)
+    def row_swap(value):
+        return lax.all_to_all(value, "row", split_axis=0, concat_axis=0, tiled=True)
+
+    def col_swap(values):
+        return [
+            lax.ppermute(value, "col", [(src, src ^ k) for src in range(cols)]) if k else value
+            for k, value in enumerate(values)
+        ]
 
     dims = (rows, xc, ky_len, kz_len, cols, y_len, pack)
-    sent = first_synth(coeffs, table_x, wave_x, (chunks, rows, xc), lanes)
-    back = []
-    for chunk in range(chunks):
-        arrived = swap(sent[chunk], "row")
-        base = earlier(stored_velocity, stored_vorticity, chunk, xc, pack)
-        arrived = swap(second_synth(arrived, table_y, slope_y, dims), "col")
-        found = third(
-            arrived, stored_velocity, stored_vorticity, base, table_z, slope_z, chunk, dims[3:]
-        )
-        found = second_back(swap(found, "col"), table_y, dims)
-        back.append(swap(found, "row"))
+    sent = list(first_synth(coeffs, table_x, wave_x, (chunks, rows, xc), lanes))
+    sent, *stored = lax.optimization_barrier((sent, stored_velocity, stored_vorticity))
+    base = [earlier(*stored, k, xc, pack) for k in range(chunks)]
+    first, second, middle, back = {}, {}, {}, {}
+    for step in range(chunks + 3):
+        live = {}
+        if step < chunks:
+            live["first", step] = row_swap(sent[step])
+        if 0 <= step - 1 < chunks:
+            live["second", step - 1] = col_swap(second_synth(first[step - 1], table_y, dims))
+        if 0 <= step - 2 < chunks:
+            at = step - 2
+            live["middle", at] = col_swap(
+                third(second[at], stored_velocity, stored_vorticity, base[at], table_z, at, dims[3:])
+            )
+        if 0 <= step - 3 < chunks:
+            live["back", step - 3] = row_swap(second_back(middle[step - 3], table_y, dims))
+        ready = {k: base[k] for k in range(chunks) if max(k - 1, 0) == step}
+        later = sent[step + 1 :]
+        live, ready, later = lax.optimization_barrier((live, ready, later))
+        sent[step + 1 :] = later
+        for k, value in ready.items():
+            base[k] = value
+        for (kind, at), value in live.items():
+            {"first": first, "second": second, "middle": middle, "back": back}[kind][at] = value
+    back = [back[k] for k in range(chunks)]
     result = last(
         back, table_x, wave_y, wave_x, wave_z, xc, ky_len, kz_len, modes, 1.0 / (orders + 1)
     )

time: 408 us -> 375 us (0.919)
  blocking collectives: 92.2 us -> 22.1 us
  local copies, waits for them, and re-layouts: 16.1 us -> 57 us
  waiting for transfers between devices: 151 us -> 136 us
  starting transfers between devices: 48.5 us -> 62 us
    all_to_all x13 -> x7, waiting for transfers between devices: 151 us -> 30.2 us  [row_swap(): return lax.all_to_all(value, 'row', split_axis=0, concat_axis=0, tiled=True)]
    ppermute x0 -> x24, waiting for transfers between devices: none -> 105 us  [col_swap(): lax.ppermute(value, 'col', [(src, src ^ k) for src in range(cols)])]
    all_to_all x3 -> x1, blocking collectives: 92.2 us -> 22.1 us  [row_swap(): return lax.all_to_all(value, 'row', split_axis=0, concat_axis=0, tiled=True)]
    unnamed x62 -> x150, local copies, waits for them, and re-layouts: 16 us -> 55.8 us
    ppermute x0 -> x24, starting transfers between devices: none -> 28.2 us  [col_swap(): lax.ppermute(value, 'col', [(src, src ^ k) for src in range(cols)])]
    all_to_all x13 -> x7, starting transfers between devices: 48.5 us -> 33.8 us  [row_swap(): return lax.all_to_all(value, 'row', split_axis=0, concat_axis=0, tiled=True)]
    pallas_call x4, Pallas kernels: 13.9 us -> 9.1 us  [second_back(): pl.pallas_call(functools.partial(second_back_kernel, dims), grid=(packs,)...]
    pallas_call x4, Pallas kernels: 13.4 us -> 17.9 us  [second_synth(): pl.pallas_call(functools.partial(second_synth_kernel, dims), grid=(packs,...]
  transfers between devices with their start and end apart: 13 -> 31, of which waited for: 10 -> 10; matrix products, arithmetic and copies ran while one was open for 0% -> 0% of each run, Pallas kernels for 20% -> 18%
where the time goes in v2:
time: 375 us; the launch traced here: 373 us
  waiting for transfers between devices  136 us (36%)
  Pallas kernels  95.4 us (25%)
  starting transfers between devices  62 us (17%)
  local copies, waits for them, and re-layouts  57 us (15%)
  blocking collectives  22.1 us (6%)
    ppermute x24, waiting for transfers between devices, col_swap(): lax.ppermute(value, 'col', [(src, src ^ k) for src in range(cols)])  105 us
    unnamed x150, local copies, waits for them, and re-layouts  55.8 us
    all_to_all x7, starting transfers between devices, row_swap(): return lax.all_to_all(value, 'row', split_axis=0, concat_axis=0, tiled=True)  33.8 us
    all_to_all x7, waiting for transfers between devices, row_swap(): return lax.all_to_all(value, 'row', split_axis=0, concat_axis=0, tiled=True)  30.2 us
    ppermute x24, starting transfers between devices, col_swap(): lax.ppermute(value, 'col', [(src, src ^ k) for src in range(cols)])  28.2 us
    pallas_call x4, Pallas kernels, earlier(): pl.pallas_call(functools.partial(earlier_kernel, orders - 1), grid=(packs...  25.5 us
    pallas_call x4, Pallas kernels, third(): pl.pallas_call(functools.partial(third_kernel, dims), grid=(packs,), in_s...  25 us
    all_to_all x1, blocking collectives, row_swap(): return lax.all_to_all(value, 'row', split_axis=0, concat_axis=0, tiled=True)  22.1 us
  transfers between devices with their start and end apart: 31, of which 10 were waited for; matrix products, arithmetic and copies ran while one was open for 0% of the time, Pallas kernels for 18%

profile of v2, /device:TPU:0, one launch (start us, length us, event | category | flops | bytes accessed | tf_op | source)
XLA Modules:
  0.0 372.5 jit_solution(1309836889680131487)
XLA Ops:
  3.5 10.1 %first_synth.1 = (f32[2048,128]{1,0:T(8,128)}, f32[2048,128]{1,0:T(8,128)}, f32[2048,128]{1,0:T(8,128)S(1)}, f32[2048,128]{1,0:T(8,128)S(1)}) custom-call(f32[3,20,40,160]{3,2,1,0:T(8,128)S(1)} %copy-done.48, bf16[256,256]{1,0:T(8,128)(2,1)S(1)} %copy-done.42, bf16[256,256]{1,0:T(8,128)(2,1)S(1)} %copy-done.44, f32[8,256]{1,0:T(8,128)S(1)} %broadcast_in_dim.19.wave_ref.refs_7_), custom_call_target="tpu_custom_call" | custom-call | flops 1610612736 | bytes 4194304 | tf_op jit(solution)/shard_map/first_synth/pallas_call | solution.py:145
  15.6 6.3 %all-to-all-start = ((f32[8,256,128]{2,1,0:T(8,128)}), f32[8,256,128]{2,1,0:T(8,128)}, u32[]{:S(2)}, u32[]{:S(2)}) async-start(f32[8,256,128]{2,1,0:T(8,128)} %bitcast), calls=%async_computation | async-start | bytes 2097152 | tf_op jit(solution)/shard_map/all_to_all | solution.py:521
  21.9 6.4 %earlier_orders.4.refs_6_ = f32[3,8,64,256]{3,2,1,0:T(8,128)S(1)} custom-call(f32[6,3,32,64,256]{4,3,2,1,0:T(8,128)} %refs_4_.11, f32[6,3,32,64,256]{4,3,2,1,0:T(8,128)} %refs_4_.11, f32[6,3,32,64,256]{4,3,2,1,0:T(8,128)} %refs_4_.11, f32[6,3,32,64,256]{4,3,2,1,0:T(8,128)} %refs_4_.11, f32[6,3,32,64,256]{4,3,2,1,0:T(8,128)} %refs_4_.11, ...), custom_call_target="tpu_custom_call" | custom-call | flops 14155776 | bytes 17301504 | tf_op jit(solution)/shard_map/earlier_orders/pallas_call | solution.py:258
  28.3 6.4 %earlier_orders.5.refs_6_ = f32[3,8,64,256]{3,2,1,0:T(8,128)S(1)} custom-call(f32[6,3,32,64,256]{4,3,2,1,0:T(8,128)} %refs_4_.11, f32[6,3,32,64,256]{4,3,2,1,0:T(8,128)} %refs_4_.11, f32[6,3,32,64,256]{4,3,2,1,0:T(8,128)} %refs_4_.11, f32[6,3,32,64,256]{4,3,2,1,0:T(8,128)} %refs_4_.11, f32[6,3,32,64,256]{4,3,2,1,0:T(8,128)} %refs_4_.11, ...), custom_call_target="tpu_custom_call" | custom-call | flops 14155776 | bytes 17301504 | tf_op jit(solution)/shard_map/earlier_orders/pallas_call | solution.py:258
  35.8 12.7 %all-to-all-done = f32[8,256,128]{2,1,0:T(8,128)} async-done(((f32[8,256,128]{2,1,0:T(8,128)}), f32[8,256,128]{2,1,0:T(8,128)}, u32[]{:S(2)}, u32[]{:S(2)}) %all-to-all-start) | async-done | bytes 1048608 | tf_op jit(solution)/shard_map/all_to_all | solution.py:521
  48.6 4.2 %all-to-all-start.1 = ((f32[8,256,128]{2,1,0:T(8,128)}), f32[8,256,128]{2,1,0:T(8,128)}, u32[]{:S(2)}, u32[]{:S(2)}) async-start(f32[8,256,128]{2,1,0:T(8,128)} %bitcast.2), calls=%async_computation.1 | async-start | bytes 2097152 | tf_op jit(solution)/shard_map/all_to_all | solution.py:521
  54.0 4.6 %second_synth.4 = (f32[4,240,128]{2,1,0:T(8,128)S(1)}, f32[4,240,128]{2,1,0:T(8,128)S(1)}, f32[4,240,128]{2,1,0:T(8,128)S(1)}, f32[4,240,128]{2,1,0:T(8,128)S(1)}) custom-call(f32[2048,128]{1,0:T(8,128)} %bitcast.1.a_ref, bf16[4,160,256]{2,1,0:T(8,128)(2,1)S(1)} %get-tuple-element.188.table_ref.refs_4_), custom_call_target="tpu_custom_call" | custom-call | flops 1761607680 | bytes 3014656 | tf_op jit(solution)/shard_map/second_synth/pallas_call | solution.py:204
  62.2 6.4 %earlier_orders.6.refs_6_ = f32[3,8,64,256]{3,2,1,0:T(8,128)S(1)} custom-call(f32[6,3,32,64,256]{4,3,2,1,0:T(8,128)} %refs_4_.11, f32[6,3,32,64,256]{4,3,2,1,0:T(8,128)} %refs_4_.11, f32[6,3,32,64,256]{4,3,2,1,0:T(8,128)} %refs_4_.11, f32[6,3,32,64,256]{4,3,2,1,0:T(8,128)} %refs_4_.11, f32[6,3,32,64,256]{4,3,2,1,0:T(8,128)} %refs_4_.11, ...), custom_call_target="tpu_custom_call" | custom-call | flops 14155776 | bytes 17301504 | tf_op jit(solution)/shard_map/earlier_orders/pallas_call | solution.py:258
  68.5 4.2 %collective-permute-done.refs_1_ = f32[4,240,128]{2,1,0:T(8,128)S(1)} collective-permute-done((f32[4,240,128]{2,1,0:T(8,128)S(1)}, f32[4,240,128]{2,1,0:T(8,128)S(1)}, u32[]{:S(2)}, u32[]{:S(2)}) %collective-permute-start) | collective-permute-done | bytes 491552 | tf_op jit(solution)/shard_map/ppermute | solution.py:525
  73.5 10.4 %collective-permute-done.1.refs_2_ = f32[4,240,128]{2,1,0:T(8,128)S(1)} collective-permute-done((f32[4,240,128]{2,1,0:T(8,128)S(1)}, f32[4,240,128]{2,1,0:T(8,128)S(1)}, u32[]{:S(2)}, u32[]{:S(2)}) %collective-permute-start.1) | collective-permute-done | bytes 491552 | tf_op jit(solution)/shard_map/ppermute | solution.py:525
  85.5 4.8 %all-to-all-start.2 = ((f32[8,256,128]{2,1,0:T(8,128)}), f32[8,256,128]{2,1,0:T(8,128)}, u32[]{:S(2)}, u32[]{:S(2)}) async-start(f32[8,256,128]{2,1,0:T(8,128)} %bitcast.24), calls=%async_computation.2 | async-start | bytes 2097152 | tf_op jit(solution)/shard_map/all_to_all | solution.py:521
  94.4 6.2 %third_dimension.4 = (f32[4,120,128]{2,1,0:T(8,128)S(1)}, f32[4,120,128]{2,1,0:T(8,128)S(1)}, f32[4,120,128]{2,1,0:T(8,128)S(1)}, f32[4,120,128]{2,1,0:T(8,128)S(1)}) custom-call(f32[4,240,128]{2,1,0:T(8,128)S(1)} %copy-done.27, f32[4,240,128]{2,1,0:T(8,128)S(1)} %copy-done.29, f32[4,240,128]{2,1,0:T(8,128)S(1)} %copy-done.31, ...), custom_call_target="tpu_custom_call" | custom-call | flops 4429185024 | bytes 7667712 | tf_op jit(solution)/shard_map/third_dimension/pallas_call | solution.py:307
  101.7 4.5 %second_synth.5 = (f32[4,240,128]{2,1,0:T(8,128)S(1)}, f32[4,240,128]{2,1,0:T(8,128)S(1)}, f32[4,240,128]{2,1,0:T(8,128)S(1)}, f32[4,240,128]{2,1,0:T(8,128)S(1)}) custom-call(f32[2048,128]{1,0:T(8,128)} %bitcast.3.a_ref, bf16[4,160,256]{2,1,0:T(8,128)(2,1)S(1)} %copy-done.35), custom_call_target="tpu_custom_call" | custom-call | flops 1761607680 | bytes 3014656 | tf_op jit(solution)/shard_map/second_synth/pallas_call | solution.py:204
  112.8 6.4 %earlier_orders.7.refs_6_ = f32[3,8,64,256]{3,2,1,0:T(8,128)S(1)} custom-call(f32[6,3,32,64,256]{4,3,2,1,0:T(8,128)} %refs_4_.11, f32[6,3,32,64,256]{4,3,2,1,0:T(8,128)} %refs_4_.11, f32[6,3,32,64,256]{4,3,2,1,0:T(8,128)} %refs_4_.11, f32[6,3,32,64,256]{4,3,2,1,0:T(8,128)} %refs_4_.11, f32[6,3,32,64,256]{4,3,2,1,0:T(8,128)} %refs_4_.11, ...), custom_call_target="tpu_custom_call" | custom-call | flops 14155776 | bytes 17301504 | tf_op jit(solution)/shard_map/earlier_orders/pallas_call | solution.py:258
  119.2 22.8 %collective-permute-done.4.refs_2_ = f32[4,120,128]{2,1,0:T(8,128)S(1)} collective-permute-done((f32[4,120,128]{2,1,0:T(8,128)S(1)}, f32[4,120,128]{2,1,0:T(8,128)S(1)}, u32[]{:S(2)}, u32[]{:S(2)}) %collective-permute-start.4) | collective-permute-done | bytes 245792 | tf_op jit(solution)/shard_map/ppermute | solution.py:525
  152.5 22.1 %all_to_all.96 = f32[8,152,128]{2,1,0:T(8,128)} all-to-all(f32[8,152,128]{2,1,0:T(8,128)S(1)} %bitcast.26), channel_id=1, replica_groups=mesh['row'=8,'col'=4] {'row'}, dimensions={0} | all-to-all | bytes 1245184 | tf_op jit(solution)/shard_map/all_to_all | solution.py:521
  174.6 4.3 %all-to-all-start.4 = ((f32[8,256,128]{2,1,0:T(8,128)}), f32[8,256,128]{2,1,0:T(8,128)}, u32[]{:S(2)}, u32[]{:S(2)}) async-start(f32[8,256,128]{2,1,0:T(8,128)} %bitcast.23), calls=%async_computation.4 | async-start | bytes 2097152 | tf_op jit(solution)/shard_map/all_to_all | solution.py:521
  184.4 6.3 %third_dimension.5 = (f32[4,120,128]{2,1,0:T(8,128)S(1)}, f32[4,120,128]{2,1,0:T(8,128)S(1)}, f32[4,120,128]{2,1,0:T(8,128)S(1)}, f32[4,120,128]{2,1,0:T(8,128)S(1)}) custom-call(f32[4,240,128]{2,1,0:T(8,128)S(1)} %copy-done.7, f32[4,240,128]{2,1,0:T(8,128)S(1)} %copy-done.11, f32[4,240,128]{2,1,0:T(8,128)S(1)} %copy-done.13, f32[4,240,128]{2,1,0:T(8,128)S(1)} %copy-done.19, ...), custom_call_target="tpu_custom_call" | custom-call | flops 4429185024 | bytes 7667712 | tf_op jit(solution)/shard_map/third_dimension/pallas_call | solution.py:307
  191.2 4.5 %second_synth.6 = (f32[4,240,128]{2,1,0:T(8,128)S(1)}, f32[4,240,128]{2,1,0:T(8,128)S(1)}, f32[4,240,128]{2,1,0:T(8,128)S(1)}, f32[4,240,128]{2,1,0:T(8,128)S(1)}) custom-call(f32[2048,128]{1,0:T(8,128)} %bitcast.6.a_ref, bf16[4,160,256]{2,1,0:T(8,128)(2,1)S(1)} %copy-done.37), custom_call_target="tpu_custom_call" | custom-call | flops 1761607680 | bytes 3014656 | tf_op jit(solution)/shard_map/second_synth/pallas_call | solution.py:204
  203.7 28.4 %collective-permute-done.10.refs_2_ = f32[4,120,128]{2,1,0:T(8,128)S(1)} collective-permute-done((f32[4,120,128]{2,1,0:T(8,128)S(1)}, f32[4,120,128]{2,1,0:T(8,128)S(1)}, u32[]{:S(2)}, u32[]{:S(2)}) %collective-permute-start.10) | collective-permute-done | bytes 245792 | tf_op jit(solution)/shard_map/ppermute | solution.py:525
  243.2 4.8 %all-to-all-start.5 = ((f32[8,152,128]{2,1,0:T(8,128)}), f32[8,152,128]{2,1,0:T(8,128)}, u32[]{:S(2)}, u32[]{:S(2)}) async-start(f32[8,152,128]{2,1,0:T(8,128)} %bitcast.25), calls=%async_computation.5 | async-start | bytes 1245184 | tf_op jit(solution)/shard_map/all_to_all | solution.py:521
  252.1 6.2 %third_dimension.6 = (f32[4,120,128]{2,1,0:T(8,128)S(1)}, f32[4,120,128]{2,1,0:T(8,128)S(1)}, f32[4,120,128]{2,1,0:T(8,128)S(1)}, f32[4,120,128]{2,1,0:T(8,128)S(1)}) custom-call(f32[4,240,128]{2,1,0:T(8,128)S(1)} %copy-done.9, f32[4,240,128]{2,1,0:T(8,128)S(1)} %copy-done.15, f32[4,240,128]{2,1,0:T(8,128)S(1)} %copy-done.21, f32[4,240,128]{2,1,0:T(8,128)S(1)} %copy-done.25, ...), custom_call_target="tpu_custom_call" | custom-call | flops 4429185024 | bytes 7667712 | tf_op jit(solution)/shard_map/third_dimension/pallas_call | solution.py:307
  259.5 4.4 %second_synth.7 = (f32[4,240,128]{2,1,0:T(8,128)S(1)}, f32[4,240,128]{2,1,0:T(8,128)S(1)}, f32[4,240,128]{2,1,0:T(8,128)S(1)}, f32[4,240,128]{2,1,0:T(8,128)S(1)}) custom-call(f32[2048,128]{1,0:T(8,128)} %bitcast.11.a_ref, bf16[4,160,256]{2,1,0:T(8,128)(2,1)S(1)} %copy-done.39), custom_call_target="tpu_custom_call" | custom-call | flops 1761607680 | bytes 3014656 | tf_op jit(solution)/shard_map/second_synth/pallas_call | solution.py:204
  271.3 28.5 %collective-permute-done.16.refs_2_ = f32[4,120,128]{2,1,0:T(8,128)S(1)} collective-permute-done((f32[4,120,128]{2,1,0:T(8,128)S(1)}, f32[4,120,128]{2,1,0:T(8,128)S(1)}, u32[]{:S(2)}, u32[]{:S(2)}) %collective-permute-start.16) | collective-permute-done | bytes 245792 | tf_op jit(solution)/shard_map/ppermute | solution.py:525
  309.5 4.7 %all-to-all-start.6 = ((f32[8,152,128]{2,1,0:T(8,128)}), f32[8,152,128]{2,1,0:T(8,128)S(1)}, u32[]{:S(2)}, u32[]{:S(2)}) async-start(f32[8,152,128]{2,1,0:T(8,128)} %bitcast.14), calls=%async_computation.6 | async-start | bytes 1245184 | tf_op jit(solution)/shard_map/all_to_all | solution.py:521
  316.3 6.2 %third_dimension.7 = (f32[4,120,128]{2,1,0:T(8,128)S(1)}, f32[4,120,128]{2,1,0:T(8,128)S(1)}, f32[4,120,128]{2,1,0:T(8,128)S(1)}, f32[4,120,128]{2,1,0:T(8,128)S(1)}) custom-call(f32[4,240,128]{2,1,0:T(8,128)S(1)} %get-tuple-element.173.refs_0_, f32[4,240,128]{2,1,0:T(8,128)S(1)} %collective-permute-done.18.refs_1_, f32[4,240,128]{2,1,0:T(8,128)S(1)} %copy-done.17, ...), custom_call_target="tpu_custom_call" | custom-call | flops 4429185024 | bytes 7667712 | tf_op jit(solution)/shard_map/third_dimension/pallas_call | solution.py:307
  326.7 5.3 %collective-permute-done.21.refs_1_ = f32[4,120,128]{2,1,0:T(8,128)S(1)} collective-permute-done((f32[4,120,128]{2,1,0:T(8,128)S(1)}, f32[4,120,128]{2,1,0:T(8,128)S(1)}, u32[]{:S(2)}, u32[]{:S(2)}) %collective-permute-start.21) | collective-permute-done | bytes 245792 | tf_op jit(solution)/shard_map/ppermute | solution.py:525
  331.9 4.2 %collective-permute-done.22.refs_2_ = f32[4,120,128]{2,1,0:T(8,128)S(1)} collective-permute-done((f32[4,120,128]{2,1,0:T(8,128)S(1)}, f32[4,120,128]{2,1,0:T(8,128)S(1)}, u32[]{:S(2)}, u32[]{:S(2)}) %collective-permute-start.22) | collective-permute-done | bytes 245792 | tf_op jit(solution)/shard_map/ppermute | solution.py:525
  339.7 2.7 second_back.7
  342.4 4.7 %all-to-all-start.7 = ((f32[8,152,128]{2,1,0:T(8,128)}), f32[8,152,128]{2,1,0:T(8,128)S(1)}, u32[]{:S(2)}, u32[]{:S(2)}) async-start(f32[8,152,128]{2,1,0:T(8,128)} %bitcast.16), calls=%async_computation.7 | async-start | bytes 1245184 | tf_op jit(solution)/shard_map/all_to_all | solution.py:521
  347.2 17.4 %all-to-all-done.7 = f32[8,152,128]{2,1,0:T(8,128)S(1)} async-done(((f32[8,152,128]{2,1,0:T(8,128)}), f32[8,152,128]{2,1,0:T(8,128)S(1)}, u32[]{:S(2)}, u32[]{:S(2)}) %all-to-all-start.7) | async-done | bytes 622624 | tf_op jit(solution)/shard_map/all_to_all | solution.py:521
  364.7 7.8 %last_projection.1 = f32[3,20,40,160]{3,2,1,0:T(8,128)} custom-call(f32[10]{0:T(128)S(1)} %convert_multiply_fusion.1.refs_0_, f32[1216,128]{1,0:T(8,128)S(1)} %bitcast.20, f32[1216,128]{1,0:T(8,128)} %bitcast.13.refs_2_, f32[1216,128]{1,0:T(8,128)S(1)} %bitcast.21, f32[1216,128]{1,0:T(8,128)S(1)} %bitcast.22, bf16[256,256]{1,0:T(8,128)(2,1)S(1)} %copy-done.43, ...), custom_call_target="tpu_custom_call" | custom-call | flops 956301312 | bytes 4026368 | tf_op jit(solution)/shard_map/last_projection/pallas_call | solution.py:440
  (205 shorter events, 93.3 us)
Async XLA Ops:
  15.6 33.0 %all-to-all-start = ((f32[8,256,128]{2,1,0:T(8,128)}), f32[8,256,128]{2,1,0:T(8,128)}, u32[]{:S(2)}, u32[]{:S(2)}) async-start(f32[8,256,128]{2,1,0:T(8,128)} %bitcast), calls=%async_computation | async-start | bytes 2097152 | tf_op jit(solution)/shard_map/all_to_all | solution.py:521
  48.6 36.9 %all-to-all-start.1 = ((f32[8,256,128]{2,1,0:T(8,128)}), f32[8,256,128]{2,1,0:T(8,128)}, u32[]{:S(2)}, u32[]{:S(2)}) async-start(f32[8,256,128]{2,1,0:T(8,128)} %bitcast.2), calls=%async_computation.1 | async-start | bytes 2097152 | tf_op jit(solution)/shard_map/all_to_all | solution.py:521
  58.6 14.1 %collective-permute-start = (f32[4,240,128]{2,1,0:T(8,128)S(1)}, f32[4,240,128]{2,1,0:T(8,128)S(1)}, u32[]{:S(2)}, u32[]{:S(2)}) collective-permute-start(f32[4,240,128]{2,1,0:T(8,128)S(1)} %get-tuple-element.109), channel_id=1, source_target_pairs={{0,1},{1,0},{2,3},{3,2},{4,5},{5,4},{6,7},{7,6},{8,9},{9,8},{10,11... | collective-permute-start | bytes 1474568 | tf_op jit(solution)/shard_map/ppermute | solution.py:525
  60.2 23.7 %collective-permute-start.1 = (f32[4,240,128]{2,1,0:T(8,128)S(1)}, f32[4,240,128]{2,1,0:T(8,128)S(1)}, u32[]{:S(2)}, u32[]{:S(2)}) collective-permute-start(f32[4,240,128]{2,1,0:T(8,128)S(1)} %get-tuple-element.110), channel_id=1, source_target_pairs={{0,2},{1,3},{2,0},{3,1},{4,6},{5,7},{6,4},{7,5},{8,10},{9,11},{10,... | collective-permute-start | bytes 1474568 | tf_op jit(solution)/shard_map/ppermute | solution.py:525
  61.7 23.0 %collective-permute-start.2 = (f32[4,240,128]{2,1,0:T(8,128)S(1)}, f32[4,240,128]{2,1,0:T(8,128)S(1)}, u32[]{:S(2)}, u32[]{:S(2)}) collective-permute-start(f32[4,240,128]{2,1,0:T(8,128)S(1)} %get-tuple-element.111), channel_id=1, source_target_pairs={{0,3},{1,2},{2,1},{3,0},{4,7},{5,6},{6,5},{7,4},{8,11},{9,10},{10,... | collective-permute-start | bytes 1474568 | tf_op jit(solution)/shard_map/ppermute | solution.py:525
  85.5 60.4 %all-to-all-start.2 = ((f32[8,256,128]{2,1,0:T(8,128)}), f32[8,256,128]{2,1,0:T(8,128)}, u32[]{:S(2)}, u32[]{:S(2)}) async-start(f32[8,256,128]{2,1,0:T(8,128)} %bitcast.24), calls=%async_computation.2 | async-start | bytes 2097152 | tf_op jit(solution)/shard_map/all_to_all | solution.py:521
  101.3 10.1 %collective-permute-start.3 = (f32[4,120,128]{2,1,0:T(8,128)S(1)}, f32[4,120,128]{2,1,0:T(8,128)S(1)}, u32[]{:S(2)}, u32[]{:S(2)}) collective-permute-start(f32[4,120,128]{2,1,0:T(8,128)S(1)} %get-tuple-element.121), channel_id=1, source_target_pairs={{0,1},{1,0},{2,3},{3,2},{4,5},{5,4},{6,7},{7,6},{8,9},{9,8},{10,11... | collective-permute-start | bytes 737288 | tf_op jit(solution)/shard_map/ppermute | solution.py:525
  106.2 37.3 %collective-permute-start.6 = (f32[4,240,128]{2,1,0:T(8,128)S(1)}, f32[4,240,128]{2,1,0:T(8,128)S(1)}, u32[]{:S(2)}, u32[]{:S(2)}) collective-permute-start(f32[4,240,128]{2,1,0:T(8,128)S(1)} %get-tuple-element.126), channel_id=1, source_target_pairs={{0,1},{1,0},{2,3},{3,2},{4,5},{5,4},{6,7},{7,6},{8,9},{9,8},{10,11... | collective-permute-start | bytes 1474568 | tf_op jit(solution)/shard_map/ppermute | solution.py:525
  107.9 36.4 %collective-permute-start.7 = (f32[4,240,128]{2,1,0:T(8,128)S(1)}, f32[4,240,128]{2,1,0:T(8,128)S(1)}, u32[]{:S(2)}, u32[]{:S(2)}) collective-permute-start(f32[4,240,128]{2,1,0:T(8,128)S(1)} %get-tuple-element.127), channel_id=1, source_target_pairs={{0,2},{1,3},{2,0},{3,1},{4,6},{5,7},{6,4},{7,5},{8,10},{9,11},{10,... | collective-permute-start | bytes 1474568 | tf_op jit(solution)/shard_map/ppermute | solution.py:525
  109.4 35.7 %collective-permute-start.8 = (f32[4,240,128]{2,1,0:T(8,128)S(1)}, f32[4,240,128]{2,1,0:T(8,128)S(1)}, u32[]{:S(2)}, u32[]{:S(2)}) collective-permute-start(f32[4,240,128]{2,1,0:T(8,128)S(1)} %get-tuple-element.128), channel_id=1, source_target_pairs={{0,3},{1,2},{2,1},{3,0},{4,7},{5,6},{6,5},{7,4},{8,11},{9,10},{10,... | collective-permute-start | bytes 1474568 | tf_op jit(solution)/shard_map/ppermute | solution.py:525
  109.8 32.2 %collective-permute-start.4 = (f32[4,120,128]{2,1,0:T(8,128)S(1)}, f32[4,120,128]{2,1,0:T(8,128)S(1)}, u32[]{:S(2)}, u32[]{:S(2)}) collective-permute-start(f32[4,120,128]{2,1,0:T(8,128)S(1)} %get-tuple-element.122), channel_id=1, source_target_pairs={{0,2},{1,3},{2,0},{3,1},{4,6},{5,7},{6,4},{7,5},{8,10},{9,11},{10,... | collective-permute-start | bytes 737288 | tf_op jit(solution)/shard_map/ppermute | solution.py:525
  111.4 31.3 %collective-permute-start.5 = (f32[4,120,128]{2,1,0:T(8,128)S(1)}, f32[4,120,128]{2,1,0:T(8,128)S(1)}, u32[]{:S(2)}, u32[]{:S(2)}) collective-permute-start(f32[4,120,128]{2,1,0:T(8,128)S(1)} %get-tuple-element.123), channel_id=1, source_target_pairs={{0,3},{1,2},{2,1},{3,0},{4,7},{5,6},{6,5},{7,4},{8,11},{9,10},{10,... | collective-permute-start | bytes 737288 | tf_op jit(solution)/shard_map/ppermute | solution.py:525
  174.6 61.2 %all-to-all-start.4 = ((f32[8,256,128]{2,1,0:T(8,128)}), f32[8,256,128]{2,1,0:T(8,128)}, u32[]{:S(2)}, u32[]{:S(2)}) async-start(f32[8,256,128]{2,1,0:T(8,128)} %bitcast.23), calls=%async_computation.4 | async-start | bytes 2097152 | tf_op jit(solution)/shard_map/all_to_all | solution.py:521
  190.6 10.9 %collective-permute-start.9 = (f32[4,120,128]{2,1,0:T(8,128)S(1)}, f32[4,120,128]{2,1,0:T(8,128)S(1)}, u32[]{:S(2)}, u32[]{:S(2)}) collective-permute-start(f32[4,120,128]{2,1,0:T(8,128)S(1)} %get-tuple-element.141), channel_id=1, source_target_pairs={{0,1},{1,0},{2,3},{3,2},{4,5},{5,4},{6,7},{7,6},{8,9},{9,8},{10,11... | collective-permute-start | bytes 737288 | tf_op jit(solution)/shard_map/ppermute | solution.py:525
  196.4 37.0 %collective-permute-start.12 = (f32[4,240,128]{2,1,0:T(8,128)S(1)}, f32[4,240,128]{2,1,0:T(8,128)S(1)}, u32[]{:S(2)}, u32[]{:S(2)}) collective-permute-start(f32[4,240,128]{2,1,0:T(8,128)S(1)} %get-tuple-element.146), channel_id=1, source_target_pairs={{0,1},{1,0},{2,3},{3,2},{4,5},{5,4},{6,7},{7,6},{8,9},{9,8},{10,11... | collective-permute-start | bytes 1474568 | tf_op jit(solution)/shard_map/ppermute | solution.py:525
  198.0 36.2 %collective-permute-start.13 = (f32[4,240,128]{2,1,0:T(8,128)S(1)}, f32[4,240,128]{2,1,0:T(8,128)S(1)}, u32[]{:S(2)}, u32[]{:S(2)}) collective-permute-start(f32[4,240,128]{2,1,0:T(8,128)S(1)} %get-tuple-element.147), channel_id=1, source_target_pairs={{0,2},{1,3},{2,0},{3,1},{4,6},{5,7},{6,4},{7,5},{8,10},{9,11},{10,... | collective-permute-start | bytes 1474568 | tf_op jit(solution)/shard_map/ppermute | solution.py:525
  199.5 35.5 %collective-permute-start.14 = (f32[4,240,128]{2,1,0:T(8,128)S(1)}, f32[4,240,128]{2,1,0:T(8,128)S(1)}, u32[]{:S(2)}, u32[]{:S(2)}) collective-permute-start(f32[4,240,128]{2,1,0:T(8,128)S(1)} %get-tuple-element.148), channel_id=1, source_target_pairs={{0,3},{1,2},{2,1},{3,0},{4,7},{5,6},{6,5},{7,4},{8,11},{9,10},{10,... | collective-permute-start | bytes 1474568 | tf_op jit(solution)/shard_map/ppermute | solution.py:525
  199.9 32.1 %collective-permute-start.10 = (f32[4,120,128]{2,1,0:T(8,128)S(1)}, f32[4,120,128]{2,1,0:T(8,128)S(1)}, u32[]{:S(2)}, u32[]{:S(2)}) collective-permute-start(f32[4,120,128]{2,1,0:T(8,128)S(1)} %get-tuple-element.142), channel_id=1, source_target_pairs={{0,2},{1,3},{2,0},{3,1},{4,6},{5,7},{6,4},{7,5},{8,10},{9,11},{10,... | collective-permute-start | bytes 737288 | tf_op jit(solution)/shard_map/ppermute | solution.py:525
  202.2 30.5 %collective-permute-start.11 = (f32[4,120,128]{2,1,0:T(8,128)S(1)}, f32[4,120,128]{2,1,0:T(8,128)S(1)}, u32[]{:S(2)}, u32[]{:S(2)}) collective-permute-start(f32[4,120,128]{2,1,0:T(8,128)S(1)} %get-tuple-element.143), channel_id=1, source_target_pairs={{0,3},{1,2},{2,1},{3,0},{4,7},{5,6},{6,5},{7,4},{8,11},{9,10},{10,... | collective-permute-start | bytes 737288 | tf_op jit(solution)/shard_map/ppermute | solution.py:525
  243.2 58.8 %all-to-all-start.5 = ((f32[8,152,128]{2,1,0:T(8,128)}), f32[8,152,128]{2,1,0:T(8,128)}, u32[]{:S(2)}, u32[]{:S(2)}) async-start(f32[8,152,128]{2,1,0:T(8,128)} %bitcast.25), calls=%async_computation.5 | async-start | bytes 1245184 | tf_op jit(solution)/shard_map/all_to_all | solution.py:521
  259.1 10.1 %collective-permute-start.15 = (f32[4,120,128]{2,1,0:T(8,128)S(1)}, f32[4,120,128]{2,1,0:T(8,128)S(1)}, u32[]{:S(2)}, u32[]{:S(2)}) collective-permute-start(f32[4,120,128]{2,1,0:T(8,128)S(1)} %get-tuple-element.160), channel_id=1, source_target_pairs={{0,1},{1,0},{2,3},{3,2},{4,5},{5,4},{6,7},{7,6},{8,9},{9,8},{10,11... | collective-permute-start | bytes 737288 | tf_op jit(solution)/shard_map/ppermute | solution.py:525
  264.0 37.2 %collective-permute-start.18 = (f32[4,240,128]{2,1,0:T(8,128)S(1)}, f32[4,240,128]{2,1,0:T(8,128)S(1)}, u32[]{:S(2)}, u32[]{:S(2)}) collective-permute-start(f32[4,240,128]{2,1,0:T(8,128)S(1)} %get-tuple-element.165), channel_id=1, source_target_pairs={{0,1},{1,0},{2,3},{3,2},{4,5},{5,4},{6,7},{7,6},{8,9},{9,8},{10,11... | collective-permute-start | bytes 1474568 | tf_op jit(solution)/shard_map/ppermute | solution.py:525
  265.6 35.5 %collective-permute-start.19 = (f32[4,240,128]{2,1,0:T(8,128)S(1)}, f32[4,240,128]{2,1,0:T(8,128)S(1)}, u32[]{:S(2)}, u32[]{:S(2)}) collective-permute-start(f32[4,240,128]{2,1,0:T(8,128)S(1)} %get-tuple-element.166), channel_id=1, source_target_pairs={{0,2},{1,3},{2,0},{3,1},{4,6},{5,7},{6,4},{7,5},{8,10},{9,11},{10,... | collective-permute-start | bytes 1474568 | tf_op jit(solution)/shard_map/ppermute | solution.py:525
  267.2 34.0 %collective-permute-start.20 = (f32[4,240,128]{2,1,0:T(8,128)S(1)}, f32[4,240,128]{2,1,0:T(8,128)S(1)}, u32[]{:S(2)}, u32[]{:S(2)}) collective-permute-start(f32[4,240,128]{2,1,0:T(8,128)S(1)} %get-tuple-element.167), channel_id=1, source_target_pairs={{0,3},{1,2},{2,1},{3,0},{4,7},{5,6},{6,5},{7,4},{8,11},{9,10},{10,... | collective-permute-start | bytes 1474568 | tf_op jit(solution)/shard_map/ppermute | solution.py:525
  267.5 32.3 %collective-permute-start.16 = (f32[4,120,128]{2,1,0:T(8,128)S(1)}, f32[4,120,128]{2,1,0:T(8,128)S(1)}, u32[]{:S(2)}, u32[]{:S(2)}) collective-permute-start(f32[4,120,128]{2,1,0:T(8,128)S(1)} %get-tuple-element.161), channel_id=1, source_target_pairs={{0,2},{1,3},{2,0},{3,1},{4,6},{5,7},{6,4},{7,5},{8,10},{9,11},{10,... | collective-permute-start | bytes 737288 | tf_op jit(solution)/shard_map/ppermute | solution.py:525
  269.9 30.6 %collective-permute-start.17 = (f32[4,120,128]{2,1,0:T(8,128)S(1)}, f32[4,120,128]{2,1,0:T(8,128)S(1)}, u32[]{:S(2)}, u32[]{:S(2)}) collective-permute-start(f32[4,120,128]{2,1,0:T(8,128)S(1)} %get-tuple-element.162), channel_id=1, source_target_pairs={{0,3},{1,2},{2,1},{3,0},{4,7},{5,6},{6,5},{7,4},{8,11},{9,10},{10,... | collective-permute-start | bytes 737288 | tf_op jit(solution)/shard_map/ppermute | solution.py:525
  309.5 28.3 %all-to-all-start.6 = ((f32[8,152,128]{2,1,0:T(8,128)}), f32[8,152,128]{2,1,0:T(8,128)S(1)}, u32[]{:S(2)}, u32[]{:S(2)}) async-start(f32[8,152,128]{2,1,0:T(8,128)} %bitcast.14), calls=%async_computation.6 | async-start | bytes 1245184 | tf_op jit(solution)/shard_map/all_to_all | solution.py:521
  323.2 8.7 %collective-permute-start.21 = (f32[4,120,128]{2,1,0:T(8,128)S(1)}, f32[4,120,128]{2,1,0:T(8,128)S(1)}, u32[]{:S(2)}, u32[]{:S(2)}) collective-permute-start(f32[4,120,128]{2,1,0:T(8,128)S(1)} %get-tuple-element.179), channel_id=1, source_target_pairs={{0,1},{1,0},{2,3},{3,2},{4,5},{5,4},{6,7},{7,6},{8,9},{9,8},{10,11... | collective-permute-start | bytes 737288 | tf_op jit(solution)/shard_map/ppermute | solution.py:525
  323.6 12.5 %collective-permute-start.22 = (f32[4,120,128]{2,1,0:T(8,128)S(1)}, f32[4,120,128]{2,1,0:T(8,128)S(1)}, u32[]{:S(2)}, u32[]{:S(2)}) collective-permute-start(f32[4,120,128]{2,1,0:T(8,128)S(1)} %get-tuple-element.180), channel_id=1, source_target_pairs={{0,2},{1,3},{2,0},{3,1},{4,6},{5,7},{6,4},{7,5},{8,10},{9,11},{10,... | collective-permute-start | bytes 737288 | tf_op jit(solution)/shard_map/ppermute | solution.py:525
  325.2 12.5 %collective-permute-start.23 = (f32[4,120,128]{2,1,0:T(8,128)S(1)}, f32[4,120,128]{2,1,0:T(8,128)S(1)}, u32[]{:S(2)}, u32[]{:S(2)}) collective-permute-start(f32[4,120,128]{2,1,0:T(8,128)S(1)} %get-tuple-element.181), channel_id=1, source_target_pairs={{0,3},{1,2},{2,1},{3,0},{4,7},{5,6},{6,5},{7,4},{8,11},{9,10},{10,... | collective-permute-start | bytes 737288 | tf_op jit(solution)/shard_map/ppermute | solution.py:525
  339.7 25.0 %copy-start.47 = (f32[8,256]{1,0:T(8,128)S(1)}, f32[8,256]{1,0:T(8,128)}, u32[]{:S(2)}) copy-start(f32[8,256]{1,0:T(8,128)} %copy-done.46) | copy-start | bytes 24580
  342.4 22.2 %all-to-all-start.7 = ((f32[8,152,128]{2,1,0:T(8,128)}), f32[8,152,128]{2,1,0:T(8,128)S(1)}, u32[]{:S(2)}, u32[]{:S(2)}) async-start(f32[8,152,128]{2,1,0:T(8,128)} %bitcast.16), calls=%async_computation.7 | async-start | bytes 1245184 | tf_op jit(solution)/shard_map/all_to_all | solution.py:521
  (74 other events, 211.2 us)

commit v3 on v2

--- a/solution.py
+++ b/solution.py
@@ -81,10 +81,30 @@
     return tiles
 
 
-def params(kind):
-    return pltpu.CompilerParams(
-        dimension_semantics=(kind,), vmem_limit_bytes=40 * 1024 * 1024
-    )
+VMEM_LIMIT = 32 * 1024 * 1024
+SHORT = pl.CostEstimate(flops=1024, bytes_accessed=1024, transcendentals=0)
+HBM = pl.BlockSpec(memory_space=pl.ANY)
+SMEM = pl.BlockSpec(memory_space=pltpu.SMEM)
+
+
+def params():
+    return pltpu.CompilerParams(dimension_semantics=("arbitrary",), vmem_limit_bytes=VMEM_LIMIT)
+
+
+def fetch(sources, buffers, sem):
+    at = pl.program_id(0)
+
+    def copy(k, step):
+        return pltpu.make_async_copy(sources[k].at[step], buffers.at[k, step], sem.at[k, step])
+
+    @pl.when(at == 0)
+    def _():
+        for step in range(buffers.shape[1]):
+            for k in range(len(sources)):
+                copy(k, step).start()
+
+    for k in range(len(sources)):
+        copy(k, at).wait()
 
 
 def whole(array):
@@ -92,70 +112,89 @@
     return pl.BlockSpec(array.shape, lambda *_: (0,) * rank)
 
 
-def first_synth_kernel(dims, x_ref, high_ref, low_ref, wave_ref, *rest):
+def first_synth_kernel(dims, place_ref, own_ref, other_ref, table_ref, wave_ref, *rest):
     chunks, dests, xc = dims
-    outs, rows = rest[:chunks], rest[chunks]
-    _, ky_len, kz_len, modes = x_ref.shape
+    outs, rows = rest[: chunks * dests], rest[chunks * dests]
+    _, ky_len, kz_len, modes = own_ref.shape
     group = 5 * kz_len
-    wide = rows.shape[1]
+    half, wide = rows.shape[0] // 2, rows.shape[1]
     tail = modes // LANES * LANES
     if tail < wide:
-        rows[:, tail:] = jnp.zeros((rows.shape[0], wide - tail), F32)
-    if ky_len * group < rows.shape[0]:
-        rows[ky_len * group :, :] = jnp.zeros((rows.shape[0] - ky_len * group, wide), F32)
+        rows[:, tail:] = jnp.zeros((2 * half, wide - tail), F32)
+    if ky_len * group < half:
+        for core in range(2):
+            rows[core * half + ky_len * group : (core + 1) * half, :] = jnp.zeros(
+                (half - ky_len * group, wide), F32
+            )
     even = lax.broadcasted_iota(jnp.int32, (kz_len, wide), 1) % 2 == 0
     wave = wave_ref[0:1, :]
+    core = place_ref[1]
 
     def fill(ky, carry):
-        base = ky * group
-        for comp in range(3):
-            start = pl.multiple_of(base + comp * kz_len, 8)
-            rows[pl.ds(start, kz_len), 0:modes] = x_ref[comp, ky]
-            if comp:
-                value = rows[pl.ds(start, kz_len), :]
-                swapped = jnp.where(even, turn(value, -1), -turn(value, 1)) * wave
-                rows[pl.ds(pl.multiple_of(start + 2 * kz_len, 8), kz_len), :] = swapped
+        for ref, side in ((own_ref, core), (other_ref, 1 - core)):
+            base = side * half + ky * group
+            for comp in range(3):
+                start = pl.multiple_of(base + comp * kz_len, 8)
+                rows[pl.ds(start, kz_len), 0:modes] = ref[comp, ky]
+                if comp:
+                    value = rows[pl.ds(start, kz_len), :]
+                    swapped = jnp.where(even, turn(value, -1), -turn(value, 1)) * wave
+                    rows[pl.ds(pl.multiple_of(start + 2 * kz_len, 8), kz_len), :] = swapped
         return carry
 
     lax.fori_loop(0, ky_len, fill, 0)
     step = 256
-    tiles = rows.shape[0] // LANES
+    points = table_ref.shape[0] // 2
 
     def mult(blk, carry):
         start = pl.multiple_of(blk * step, step)
-        result = dot_data_right(high_ref[...], low_ref[...], rows[pl.ds(start, step), :])
-        for idx in range(chunks):
-            for dest in range(dests):
-                at = (idx * dests + dest) * xc
-                for tile in range(step // LANES):
-                    spot = pl.multiple_of((dest * tiles + blk * (step // LANES) + tile) * xc, 8)
-                    outs[idx][pl.ds(spot, xc), :] = result[
-                        at : at + xc, tile * LANES : (tile + 1) * LANES
-                    ]
+        high, low = pieces_of(rows[pl.ds(start, step), :])
+        both = dot(table_ref[...], high, NT)
+        result = both[:points] + (both[points:] + dot(table_ref[:points], low, NT))
+        for idx, out in enumerate(outs):
+            for tile in range(step // LANES):
+                spot = pl.multiple_of((blk * (step // LANES) + tile) * xc, 8)
+                out[pl.ds(spot, xc), :] = result[
+                    idx * xc : (idx + 1) * xc, tile * LANES : (tile + 1) * LANES
+                ]
         return carry
 
-    lax.fori_loop(0, rows.shape[0] // step, mult, 0)
-
-
-def first_synth(coeffs, table, wave, dims, lanes):
-    table = [jnp.asarray(part) for part in table]
-    chunks = dims[0]
-    grid_len = table[0].shape[0]
-    height = grid_len // chunks * (lanes // LANES)
-    return pl.pallas_call(
+    lax.fori_loop(0, 2 * half // step, mult, 0)
+
+
+def first_synth(place, own, other, table, wave, dims, lanes):
+    chunks, dests, xc = dims
+    out = jax.ShapeDtypeStruct((2 * lanes // LANES * xc, LANES), F32)
+    found = pl.pallas_call(
         functools.partial(first_synth_kernel, dims),
-        out_shape=[jax.ShapeDtypeStruct((height, LANES), F32)] * chunks,
-        scratch_shapes=[pltpu.VMEM((lanes, table[0].shape[1]), F32)],
-        compiler_params=pltpu.CompilerParams(vmem_limit_bytes=40 * 1024 * 1024),
-        cost_estimate=pl.CostEstimate(
-            flops=6 * grid_len * lanes * 256, bytes_accessed=4 * grid_len * lanes, transcendentals=0
-        ),
+        in_specs=[SMEM] + [pl.BlockSpec(memory_space=pltpu.VMEM)] * 4,
+        out_shape=[out] * (chunks * dests),
+        scratch_shapes=[pltpu.VMEM((2 * lanes, table.shape[1]), F32)],
+        compiler_params=pltpu.CompilerParams(vmem_limit_bytes=VMEM_LIMIT),
+        cost_estimate=SHORT,
         name="first_synth",
-    )(coeffs, table[0], table[1], wave)
-
-
-def second_synth_kernel(dims, a_ref, table_ref, *out_refs):
+    )(place, own, other, table, wave)
+    return [list(found[k * dests : (k + 1) * dests]) for k in range(chunks)]
+
+
+def second_synth_kernel(dims, place_ref, *refs):
     rows, xc, ky_len, kz_len, cols, y_len, pack = dims
+    groups = rows // 2
+    parts, table_ref, out_refs = refs[:groups], refs[groups], refs[groups + 1 : -2]
+    a_ref, sem = refs[-2:]
+    size = a_ref.shape[0] // groups
+
+    @pl.when(pl.program_id(0) == 0)
+    def _():
+        copies = []
+        for k, part in enumerate(parts):
+            spot = pl.multiple_of((place_ref[0] ^ k) * size, 8)
+            copies.append(pltpu.make_async_copy(part, a_ref.at[pl.ds(spot, size), :], sem.at[k]))
+        for copy in copies:
+            copy.start()
+        for copy in copies:
+            copy.wait()
+
     group = 5 * kz_len
     wide = round_up(group, LANES)
     at = pl.program_id(0)
@@ -198,23 +237,23 @@
         )[0]
 
 
-def second_synth(arrived, table, dims):
+def second_synth(place, arrived, table, dims):
     rows, xc, ky_len, kz_len, cols, y_len, pack = dims
     packs = xc // pack
     return pl.pallas_call(
         functools.partial(second_synth_kernel, dims),
         grid=(packs,),
-        in_specs=[whole(arrived), whole(table)],
+        in_specs=[SMEM] + [HBM] * len(arrived) + [whole(table)],
         out_specs=[pl.BlockSpec((1, 6 * kz_len, LANES), lambda i: (i, 0, 0))] * cols,
         out_shape=[jax.ShapeDtypeStruct((packs, 6 * kz_len, LANES), F32)] * cols,
-        compiler_params=params("arbitrary"),
-        cost_estimate=pl.CostEstimate(
-            flops=6 * xc * 7 * kz_len * 256 * 256 * 2,
-            bytes_accessed=4 * arrived.size + 4 * cols * packs * 6 * kz_len * LANES,
-            transcendentals=0,
-        ),
+        scratch_shapes=[
+            pltpu.VMEM((len(arrived) * arrived[0].shape[0], LANES), F32),
+            pltpu.SemaphoreType.DMA((len(arrived),)),
+        ],
+        compiler_params=params(),
+        cost_estimate=SHORT,
         name="second_synth",
-    )(arrived, table)
+    )(place, *arrived, table)
 
 
 def cross(left, right):
@@ -261,31 +300,32 @@
         in_specs=specs,
         out_specs=pl.BlockSpec((3, pack, y_len, grid_len), lambda i: (0, i, 0, 0)),
         out_shape=jax.ShapeDtypeStruct((3, xc, y_len, grid_len), F32),
-        compiler_params=params("arbitrary"),
-        cost_estimate=pl.CostEstimate(
-            flops=size * 9 * 2 * orders, bytes_accessed=4 * size * (6 * orders - 3), transcendentals=0
-        ),
+        compiler_params=params(),
+        cost_estimate=SHORT,
         name="earlier_orders",
     )(*[velocity] * (orders - 1), *[vorticity] * (orders - 1))
 
 
 def third_kernel(dims, *refs):
     kz_len, cols, y_len, pack = dims
-    b_refs, out_refs = refs[:cols], refs[cols + 4 :]
+    b_refs, out_refs = refs[:cols], refs[cols + 4 : -2]
+    buffers, sem = refs[-2:]
+    fetch(b_refs, buffers, sem)
+    at = pl.program_id(0)
     vel_ref, vort_ref, base_ref, table_ref = refs[cols : cols + 4]
     grid_len = table_ref.shape[2]
 
     def stack(field):
         return jnp.concatenate(
-            [b_ref[0, field * kz_len : (field + 1) * kz_len, :] for b_ref in b_refs], axis=0
+            [buffers[src, at, field * kz_len : (field + 1) * kz_len, :] for src in range(cols)], axis=0
         ).T
 
     lines = jnp.concatenate([stack(field) for field in range(6)], axis=0)
     plain = dot_data_left(lines, table_ref[0], table_ref[1])
     slope = dot_data_left(lines[: 2 * LANES], table_ref[2], table_ref[3])
-    at = [plain[f * LANES : (f + 1) * LANES] for f in range(6)]
-    vel_new = at[:3]
-    vort_new = [at[4] - slope[LANES:], slope[:LANES] + at[5], at[3]]
+    new = [plain[f * LANES : (f + 1) * LANES] for f in range(6)]
+    vel_new = new[:3]
+    vort_new = [new[4] - slope[LANES:], slope[:LANES] + new[5], new[3]]
     flat = (pack * y_len, grid_len)
     vel = [vel_ref[0, c].reshape(flat) for c in range(3)]
     vort = [vort_ref[0, c].reshape(flat) for c in range(3)]
@@ -308,7 +348,7 @@
         functools.partial(third_kernel, dims),
         grid=(packs,),
         in_specs=[
-            *[pl.BlockSpec((1, 6 * kz_len, LANES), lambda i: (i, 0, 0))] * cols,
+            *[HBM] * cols,
             stored,
             stored,
             pl.BlockSpec((3, pack, y_len, grid_len), lambda i: (0, i, 0, 0)),
@@ -316,24 +356,27 @@
         ],
         out_specs=[pl.BlockSpec((1, 3 * kz_len, LANES), lambda i: (i, 0, 0))] * cols,
         out_shape=[jax.ShapeDtypeStruct((packs, 3 * kz_len, LANES), F32)] * cols,
-        compiler_params=params("arbitrary"),
-        cost_estimate=pl.CostEstimate(
-            flops=6 * packs * LANES * 11 * 256 * 256 * 2,
-            bytes_accessed=4 * (cols * arrived[0].size * 3 // 2 + packs * LANES * grid_len * 9),
-            transcendentals=0,
-        ),
+        scratch_shapes=[
+            pltpu.VMEM((cols, packs, 6 * kz_len, LANES), F32),
+            pltpu.SemaphoreType.DMA((cols, packs)),
+        ],
+        compiler_params=params(),
+        cost_estimate=SHORT,
         name="third_dimension",
     )(*arrived, velocity, vorticity, base, table)
 
 
-def second_back_kernel(dims, *refs):
+def second_back_kernel(dims, place_ref, *refs):
     rows, xc, ky_len, kz_len, cols, y_len, pack = dims
-    c_refs, table_ref, out_ref = refs[:cols], refs[cols], refs[cols + 1]
+    c_refs, table_ref, out_refs = refs[:cols], refs[cols], refs[cols + 1 : -4]
+    out_ref, sem, buffers, fetch_sem = refs[-4:]
+    fetch(c_refs, buffers, fetch_sem)
+    at = pl.program_id(0)
     width = 3 * kz_len
     high_pad = round_up(width, LANES)
     lines = []
     for part in range(pack):
-        tiles = lane_pack([c_ref[0] for c_ref in c_refs], y_len, part * y_len)
+        tiles = lane_pack([buffers[src, at] for src in range(cols)], y_len, part * y_len)
         lines.append(jnp.concatenate(tiles, axis=1))
         if high_pad > width:
             lines.append(jnp.zeros((high_pad - width, cols * y_len), F32))
@@ -341,55 +384,99 @@
     for part in range(pack):
         own = result[:, part * high_pad : (part + 1) * high_pad]
         tiles = lane_pack([own[ky * rows : (ky + 1) * rows] for ky in range(ky_len)], width)
-        at = pl.program_id(0) * pack + part
+        spot = at * pack + part
         for idx, tile in enumerate(tiles):
-            out_ref[pl.ds(idx * xc + at, rows, stride=len(tiles) * xc), :] = tile
-
-
-def second_back(arrived, table, dims):
+            out_ref[pl.ds(idx * xc + spot, rows, stride=len(tiles) * xc), :] = tile
+
+    @pl.when(pl.program_id(0) == pl.num_programs(0) - 1)
+    def _():
+        size = out_ref.shape[0] // len(out_refs)
+        copies = []
+        for k, out in enumerate(out_refs):
+            spot = pl.multiple_of((place_ref[0] ^ k) * size, 8)
+            copies.append(pltpu.make_async_copy(out_ref.at[pl.ds(spot, size), :], out, sem.at[k]))
+        for copy in copies:
+            copy.start()
+        for copy in copies:
+            copy.wait()
+
+
+def second_back(place, arrived, table, dims):
     rows, xc, ky_len, kz_len, cols, y_len, pack = dims
     packs = xc // pack
-    lanes = round_up(ky_len * 3 * kz_len, LANES)
+    size = round_up(ky_len * 3 * kz_len, LANES) // LANES * xc
+    groups = rows // 2
     return pl.pallas_call(
         functools.partial(second_back_kernel, dims),
         grid=(packs,),
         in_specs=[
-            *[pl.BlockSpec((1, 3 * kz_len, LANES), lambda i: (i, 0, 0))] * cols,
+            SMEM,
+            *[HBM] * cols,
             whole(table),
         ],
-        out_specs=pl.BlockSpec((rows * xc * lanes // LANES, LANES), lambda i: (0, 0)),
-        out_shape=jax.ShapeDtypeStruct((rows * xc * lanes // LANES, LANES), F32),
-        compiler_params=params("arbitrary"),
-        cost_estimate=pl.CostEstimate(
-            flops=6 * xc * LANES * 256 * 256 * 2,
-            bytes_accessed=4 * (cols * arrived[0].size + rows * xc * lanes),
-            transcendentals=0,
-        ),
+        out_specs=[HBM] * groups,
+        out_shape=[jax.ShapeDtypeStruct((2 * size, LANES), F32)] * groups,
+        scratch_shapes=[
+            pltpu.VMEM((rows * size, LANES), F32),
+            pltpu.SemaphoreType.DMA((groups,)),
+            pltpu.VMEM((cols, packs, 3 * kz_len, LANES), F32),
+            pltpu.SemaphoreType.DMA((cols, packs)),
+        ],
+        compiler_params=params(),
+        cost_estimate=SHORT,
         name="second_back",
-    )(*arrived, table)
+    )(place, *arrived, table)
+
+
+def first_back_kernel(dims, place_ref, *refs):
+    count, xc, own = dims
+    parts, table_ref, out_ref = refs[:count], refs[count], refs[count + 1]
+    data, sem = refs[-2:]
+    size = data.shape[1]
+    core = place_ref[1] if own else 1 - place_ref[1]
+    spot = pl.multiple_of(core * size, 8)
+    copies = [
+        pltpu.make_async_copy(part.at[pl.ds(spot, size), :], data.at[k], sem.at[k])
+        for k, part in enumerate(parts)
+    ]
+    for copy in copies:
+        copy.start()
+    for copy in copies:
+        copy.wait()
+    for tile in range(size // xc):
+        found = jnp.concatenate([data[k, tile * xc : (tile + 1) * xc, :] for k in range(count)], axis=0)
+        out_ref[:, tile * LANES : (tile + 1) * LANES] = dot_data_right(
+            table_ref[0], table_ref[1], found, NN
+        )
+
+
+def first_back(place, parts, table, xc, own):
+    count = len(parts)
+    size = parts[0].shape[0] // 2
+    return pl.pallas_call(
+        functools.partial(first_back_kernel, (count, xc, own)),
+        in_specs=[SMEM] + [HBM] * count + [pl.BlockSpec(memory_space=pltpu.VMEM)],
+        out_shape=jax.ShapeDtypeStruct((table.shape[1], size // xc * LANES), F32),
+        scratch_shapes=[pltpu.VMEM((count, size, LANES), F32), pltpu.SemaphoreType.DMA((count,))],
+        compiler_params=pltpu.CompilerParams(vmem_limit_bytes=VMEM_LIMIT),
+        cost_estimate=SHORT,
+        name="first_back",
+    )(place, *parts, table)
 
 
 def last_kernel(dims, *refs):
-    chunks, xc, kz_len, modes, scale = dims
-    wave_y_ref = refs[0]
-    parts = refs[1 : 1 + chunks]
-    high_ref, low_ref, wave_x_ref, wave_z_ref, out_ref, rows = refs[1 + chunks :]
+    kz_len, modes, scale = dims
+    wave_y_ref, own_ref, other_ref, wave_x_ref, wave_z_ref, out_ref, rows = refs
     pair = 2 * 3 * kz_len
     at = pl.program_id(0)
 
     @pl.when(at == 0)
     def _():
-        tiles = rows.shape[0] // LANES
-        for tile in range(tiles):
-            found = [
-                part[(src * tiles + tile) * xc : (src * tiles + tile + 1) * xc, :]
-                for part in parts
-                for src in range(part.shape[0] // (tiles * xc))
-            ]
-            rows[tile * LANES : (tile + 1) * LANES, :] = jnp.concatenate(found, axis=0).T
-
-    data = rows[pl.ds(pl.multiple_of(at * pair, 8), pair), :]
-    spec = dot_data_left(data, high_ref[...], low_ref[...])
+        for tile in range(rows.shape[0] // LANES):
+            lanes = slice(tile * LANES, (tile + 1) * LANES)
+            rows[lanes, 0:modes] = (own_ref[:, lanes] + other_ref[:, lanes]).T
+
+    spec = rows[pl.ds(pl.multiple_of(at * pair, 8), pair), :]
     wide = spec.shape[1]
     wave_x = jnp.broadcast_to(wave_x_ref[0:1, :], (kz_len, wide))
     wave_z = wave_z_ref[...]
@@ -432,29 +519,23 @@
             out_ref[comp, y] = (found[comp] * scale)[:, :modes]
 
 
-def last(parts, table, wave_y, wave_x, wave_z, xc, ky_len, kz_len, modes, scale):
-    chunks = len(parts)
-    table = [jnp.asarray(part) for part in table]
-    grid_len = table[0].shape[0]
-    lanes = parts[0].size * chunks // grid_len
+def last(own, other, wave_y, wave_x, wave_z, ky_len, kz_len, scale):
+    modes, lanes = own.shape
     return pl.pallas_call(
-        functools.partial(last_kernel, (chunks, xc, kz_len, modes, scale)),
+        functools.partial(last_kernel, (kz_len, modes, scale)),
         grid=(ky_len // 2,),
-        in_specs=[
-            pl.BlockSpec(memory_space=pltpu.SMEM),
-            *[whole(a) for a in (*parts, *table, wave_x, wave_z)],
-        ],
+        in_specs=[SMEM, *[whole(a) for a in (own, other, wave_x, wave_z)]],
         out_specs=pl.BlockSpec((3, 2, kz_len, modes), lambda i: (0, i, 0, 0)),
         out_shape=jax.ShapeDtypeStruct((3, ky_len, kz_len, modes), F32),
-        scratch_shapes=[pltpu.VMEM((lanes, grid_len), F32)],
-        compiler_params=params("arbitrary"),
-        cost_estimate=pl.CostEstimate(
-            flops=6 * lanes * 256 * 256,
-            bytes_accessed=4 * (grid_len * lanes + 3 * ky_len * kz_len * modes),
-            transcendentals=0,
-        ),
+        scratch_shapes=[pltpu.VMEM((lanes, wave_x.shape[1]), F32)],
+        compiler_params=params(),
+        cost_estimate=SHORT,
         name="last_projection",
-    )(wave_y, *parts, *table, wave_x, wave_z)
+    )(wave_y, own, other, wave_x, wave_z)
+
+
+def after(value, *earlier_values):
+    return lax.optimization_barrier((value, earlier_values))[0]
 
 
 def shards(new_velocity, stored_velocity, stored_vorticity):
@@ -474,15 +555,21 @@
 
     basis = synth_np(grid_len, modes)
     slope = slope_np(basis, kmax)
-    x_order = (
-        np.arange(rows)[None, :, None] * x_len
-        + np.arange(chunks)[:, None, None] * xc
-        + np.arange(xc)[None, None, :]
-    ).reshape(-1)
     y_order = (np.arange(rows)[None, :] * ky_len + np.arange(ky_len)[:, None]).reshape(-1)
 
-    def own_table(stack):
-        return lax.dynamic_index_in_dim(jnp.asarray(stack), lax.axis_index("col"), 0, False)
+    groups = rows // 2
+    place = jnp.stack([lax.axis_index("row") // 2, lax.axis_index("row") % 2]).astype(jnp.int32)
+
+    def own_table(tables, axis):
+        return lax.dynamic_index_in_dim(jnp.asarray(np.stack(tables)), lax.axis_index(axis), 0, False)
+
+    def x_points(row):
+        owner = np.array([row ^ (2 * k) for k in range(groups)])
+        return (
+            owner[None, :, None] * x_len
+            + np.arange(chunks)[:, None, None] * xc
+            + np.arange(xc)[None, None, :]
+        ).reshape(-1)
 
     def halves_of(plain, sloped):
         return np.stack([part for table in (plain, sloped) for part in halves(table)])
@@ -499,9 +586,16 @@
 
         return halves_of(spread(basis), spread(slope))
 
-    table_x = halves(np.pad(basis[x_order], ((0, 0), (0, wide - modes))))
-    table_y = own_table(np.stack([y_table(col) for col in range(cols)]))
-    table_z = own_table(np.stack([z_table(col) for col in range(cols)]))
+    def x_table(row):
+        points = np.pad(basis[x_points(row)], ((0, 0), (0, wide - modes)))
+        return np.concatenate(halves(points), axis=0)
+
+    table_x = own_table([x_table(row) for row in range(rows)], "row")
+    table_x_back = own_table(
+        [np.stack(halves(basis[x_points(row)].T)) for row in range(rows)], "row"
+    )
+    table_y = own_table([y_table(col) for col in range(cols)], "col")
+    table_z = own_table([z_table(col) for col in range(cols)], "col")
 
     def wave_of(index):
         return (index // 2).astype(F32) / kmax
@@ -517,45 +611,65 @@
     if kz_len > kz_own:
         coeffs = jnp.pad(coeffs, ((0, 0), (0, 0), (0, kz_len - kz_own), (0, 0)))
 
-    def row_swap(value):
-        return lax.all_to_all(value, "row", split_axis=0, concat_axis=0, tiled=True)
-
-    def col_swap(values):
+    def exchange(values, axis, shift, size):
         return [
-            lax.ppermute(value, "col", [(src, src ^ k) for src in range(cols)]) if k else value
+            lax.ppermute(value, axis, [(src, src ^ (k << shift)) for src in range(size)]) if k else value
             for k, value in enumerate(values)
         ]
 
+    def core_swap(value):
+        return lax.ppermute(value, "row", [(src, src ^ 1) for src in range(rows)])
+
     dims = (rows, xc, ky_len, kz_len, cols, y_len, pack)
-    sent = list(first_synth(coeffs, table_x, wave_x, (chunks, rows, xc), lanes))
-    sent, *stored = lax.optimization_barrier((sent, stored_velocity, stored_vorticity))
-    base = [earlier(*stored, k, xc, pack) for k in range(chunks)]
-    first, second, middle, back = {}, {}, {}, {}
-    for step in range(chunks + 3):
-        live = {}
+    sent = first_synth(
+        place, coeffs, core_swap(coeffs), table_x, wave_x, (chunks, groups, xc), lanes
+    )
+    latest = sent[0][0]
+
+    def ordered(kernel, operands, *others):
+        nonlocal latest
+        operands = after(operands, latest)
+        found = kernel(operands, *others)
+        latest = found[0] if isinstance(found, (list, tuple)) else found
+        return found
+
+    stored = (stored_velocity, stored_vorticity)
+
+    def run_earlier(chunk):
+        return ordered(lambda values: earlier(*values, chunk, xc, pack), stored)
+
+    first, second, middle, back, base = {}, {}, {}, {}, {}
+    for chunk in range(chunks):
+        values = sent[chunk]
+        if chunk:
+            values = [values[0]] + [
+                after(value, first[chunk - 1][k]) for k, value in enumerate(values) if k
+            ]
+        first[chunk] = exchange(values, "row", 1, rows)
+    base[0] = run_earlier(0)
+    for step in range(chunks + 2):
+        if step + 1 < chunks:
+            base[step + 1] = run_earlier(step + 1)
         if step < chunks:
-            live["first", step] = row_swap(sent[step])
-        if 0 <= step - 1 < chunks:
-            live["second", step - 1] = col_swap(second_synth(first[step - 1], table_y, dims))
-        if 0 <= step - 2 < chunks:
-            at = step - 2
-            live["middle", at] = col_swap(
-                third(second[at], stored_velocity, stored_vorticity, base[at], table_z, at, dims[3:])
+            found = ordered(lambda values: second_synth(place, values, table_y, dims), first[step])
+            second[step] = exchange(found, "col", 0, cols)
+        at = step - 1
+        if 0 <= at < chunks:
+            found = ordered(
+                lambda values: third(values, *stored, base[at], table_z, at, dims[3:]), second[at]
             )
-        if 0 <= step - 3 < chunks:
-            live["back", step - 3] = row_swap(second_back(middle[step - 3], table_y, dims))
-        ready = {k: base[k] for k in range(chunks) if max(k - 1, 0) == step}
-        later = sent[step + 1 :]
-        live, ready, later = lax.optimization_barrier((live, ready, later))
-        sent[step + 1 :] = later
-        for k, value in ready.items():
-            base[k] = value
-        for (kind, at), value in live.items():
-            {"first": first, "second": second, "middle": middle, "back": back}[kind][at] = value
-    back = [back[k] for k in range(chunks)]
-    result = last(
-        back, table_x, wave_y, wave_x, wave_z, xc, ky_len, kz_len, modes, 1.0 / (orders + 1)
-    )
+            middle[at] = exchange(found, "col", 0, cols)
+        at = step - 2
+        if 0 <= at < chunks:
+            values = middle[at]
+            if at:
+                values = after(values, back[at - 1])
+            found = ordered(lambda values: second_back(place, values, table_y, dims), values)
+            back[at] = exchange(found, "row", 1, rows)
+    parts = [value for chunk in range(chunks) for value in back[chunk]]
+    away = first_back(place, parts, table_x_back, xc, False)
+    home = first_back(place, after(parts, away), table_x_back, xc, True)
+    result = last(home, core_swap(away), wave_y, wave_x, wave_z, ky_len, kz_len, 1.0 / (orders + 1))
     return result[:, :, :kz_own] if kz_len > kz_own else result
 
 

time: 375 us -> 324 us (0.86)
  waiting for transfers between devices: 136 us -> 102 us
  Pallas kernels: 95.4 us -> 129 us
  local copies, waits for them, and re-layouts: 57 us -> 23.9 us
  blocking collectives: 22.1 us -> 0 us
  starting transfers between devices: 62 us -> 67 us
    ppermute x24 -> x50, starting transfers between devices: 28.2 us -> 67 us  [the longest x48 66.4 us: exchange(): lax.ppermute(value, axis, [(src, src ^ k << shift) for src in range(size)])]
    unnamed x150 -> x102, local copies, waits for them, and re-layouts: 55.8 us -> 20.9 us
    all_to_all x7 -> x0, starting transfers between devices: 33.8 us -> none  [row_swap(): return lax.all_to_all(value, 'row', split_axis=0, concat_axis=0, tiled=True)]
    all_to_all x7 -> x0, waiting for transfers between devices: 30.2 us -> none  [row_swap(): return lax.all_to_all(value, 'row', split_axis=0, concat_axis=0, tiled=True)]
    all_to_all x1 -> x0, blocking collectives: 22.1 us -> none  [row_swap(): return lax.all_to_all(value, 'row', split_axis=0, concat_axis=0, tiled=True)]
    pallas_call x2 -> x4, Pallas kernels: 17.9 us -> 30 us  [the longest x1 17.6 us: first_synth(): pl.pallas_call(functools.partial(first_synth_kernel, dims), in_specs=[SME...]
    pallas_call x4, Pallas kernels: 25 us -> 36.9 us  [third(): pl.pallas_call(functools.partial(third_kernel, dims), grid=(packs,), in_s...]
    pallas_call x4, Pallas kernels: 9.1 us -> 19 us  [second_back(): pl.pallas_call(functools.partial(second_back_kernel, dims), grid=(packs,)...]
  transfers between devices with their start and end apart: 31 -> 50, of which waited for: 10 -> 15; matrix products, arithmetic and copies ran while one was open for 0% -> 1% of each run, Pallas kernels for 18% -> 22%
where the time goes in v3:
time: 324 us; the launch traced here: 323 us
  Pallas kernels  129 us (40%)
  waiting for transfers between devices  102 us (31%)
  starting transfers between devices  67 us (21%)
  local copies, waits for them, and re-layouts  23.9 us (7%)
    ppermute x48, waiting for transfers between devices, exchange(): lax.ppermute(value, axis, [(src, src ^ k << shift) for src in range(size)])  98.4 us
    ppermute x48, starting transfers between devices, exchange(): lax.ppermute(value, axis, [(src, src ^ k << shift) for src in range(size)])  66.4 us
    pallas_call x4, Pallas kernels, third(): pl.pallas_call(functools.partial(third_kernel, dims), grid=(packs,), in_s...  36.9 us
    pallas_call x4, Pallas kernels, earlier(): pl.pallas_call(functools.partial(earlier_kernel, orders - 1), grid=(packs...  25.7 us
    unnamed x102, local copies, waits for them, and re-layouts  20.9 us
    pallas_call x4, Pallas kernels, second_back(): pl.pallas_call(functools.partial(second_back_kernel, dims), grid=(packs,)...  19 us
    pallas_call x4, Pallas kernels, second_synth(): pl.pallas_call(functools.partial(second_synth_kernel, dims), grid=(packs,...  17.6 us
    pallas_call x1, Pallas kernels, first_synth(): pl.pallas_call(functools.partial(first_synth_kernel, dims), in_specs=[SME...  17.6 us
  transfers between devices with their start and end apart: 50, of which 15 were waited for; matrix products, arithmetic and copies ran while one was open for 1% of the time, Pallas kernels for 22%

profile of v3, /device:TPU:0, one launch (start us, length us, event | category | flops | bytes accessed | tf_op | source)
XLA Modules:
  0.0 322.8 jit_solution(5790527680338794695)
XLA Ops:
  1.5 3.5 %collective-permute-done.other_ref = f32[3,20,40,160]{3,2,1,0:T(8,128)S(1)} collective-permute-done((f32[3,20,40,160]{3,2,1,0:T(8,128)}, f32[3,20,40,160]{3,2,1,0:T(8,128)S(1)}, u32[]{:S(2)}, u32[]{:S(2)}) %collective-permute-start) | collective-permute-done | bytes 1536032 | tf_op jit(solution)/shard_map/ppermute | solution.py:621
  6.7 17.6 %first_synth.1 = (f32[512,128]{1,0:T(8,128)S(1)}, f32[512,128]{1,0:T(8,128)S(1)}, f32[512,128]{1,0:T(8,128)}, f32[512,128]{1,0:T(8,128)}, f32[512,128]{1,0:T(8,1...) custom-call(s32[2]{0:T(128)S(1)} %pad_add_fusion.place_ref, ...), custom_call_target="tpu_custom_call" | custom-call | flops 1024 | bytes 1024 | tf_op jit(solution)/shard_map/first_synth/pallas_call | solution.py:168
  35.4 8.9 %collective-permute-done.1.refs_1_ = f32[512,128]{1,0:T(8,128)S(1)} collective-permute-done((f32[512,128]{1,0:T(8,128)S(1)}, f32[512,128]{1,0:T(8,128)S(1)}, u32[]{:S(2)}, u32[]{:S(2)}) %collective-permute-start.1) | collective-permute-done | bytes 262176 | tf_op jit(solution)/shard_map/ppermute | solution.py:616
  46.2 6.4 %earlier_orders.4.refs_6_ = f32[3,8,64,256]{3,2,1,0:T(8,128)S(1)} custom-call(f32[6,3,32,64,256]{4,3,2,1,0:T(8,128)} %refs_4_.11, f32[6,3,32,64,256]{4,3,2,1,0:T(8,128)} %refs_4_.11, f32[6,3,32,64,256]{4,3,2,1,0:T(8,128)} %refs_4_.11, f32[6,3,32,64,256]{4,3,2,1,0:T(8,128)} %refs_4_.11, f32[6,3,32,64,256]{4,3,2,1,0:T(8,128)} %refs_4_.11, ...), custom_call_target="tpu_custom_call" | custom-call | flops 1024 | bytes 1024 | tf_op jit(solution)/shard_map/earlier_orders/pallas_call | solution.py:297
  52.7 6.5 %earlier_orders.5.refs_6_ = f32[3,8,64,256]{3,2,1,0:T(8,128)S(1)} custom-call(f32[6,3,32,64,256]{4,3,2,1,0:T(8,128)} %refs_4_.11, f32[6,3,32,64,256]{4,3,2,1,0:T(8,128)} %refs_4_.11, f32[6,3,32,64,256]{4,3,2,1,0:T(8,128)} %refs_4_.11, f32[6,3,32,64,256]{4,3,2,1,0:T(8,128)} %refs_4_.11, f32[6,3,32,64,256]{4,3,2,1,0:T(8,128)} %refs_4_.11, ...), custom_call_target="tpu_custom_call" | custom-call | flops 1024 | bytes 1024 | tf_op jit(solution)/shard_map/earlier_orders/pallas_call | solution.py:297
  59.2 4.9 %second_synth.4 = (f32[4,240,128]{2,1,0:T(8,128)S(1)}, f32[4,240,128]{2,1,0:T(8,128)S(1)}, f32[4,240,128]{2,1,0:T(8,128)S(1)}, f32[4,240,128]{2,1,0:T(8,128)S(1)}) custom-call(s32[2]{0:T(128)S(1)} %copy-done.34, f32[512,128]{1,0:T(8,128)S(1)} %get-tuple-element.170.refs_0_, f32[512,128]{1,0:T(8,128)S(1)} %copy-done.30, ...), custom_call_target="tpu_custom_call" | custom-call | flops 1024 | bytes 1024 | tf_op jit(solution)/shard_map/second_synth/pallas_call | solution.py:243
  67.7 3.6 %collective-permute-start.8 = (f32[512,128]{1,0:T(8,128)S(1)}, f32[512,128]{1,0:T(8,128)S(1)}, u32[]{:S(2)}, u32[]{:S(2)}) collective-permute-start(f32[512,128]{1,0:T(8,128)S(1)} %copy-done.50), channel_id=1, source_target_pairs={{0,16},{4,20},{8,24},{12,28},{16,0},{20,4},{24,8},{28,12},{1,17},{... | collective-permute-start | bytes 786440 | tf_op jit(solution)/shard_map/ppermute | solution.py:616
  72.1 16.2 %collective-permute-done.8.refs_2_ = f32[512,128]{1,0:T(8,128)S(1)} collective-permute-done((f32[512,128]{1,0:T(8,128)S(1)}, f32[512,128]{1,0:T(8,128)S(1)}, u32[]{:S(2)}, u32[]{:S(2)}) %collective-permute-start.8) | collective-permute-done | bytes 262176 | tf_op jit(solution)/shard_map/ppermute | solution.py:616
  88.3 6.1 %collective-permute-start.17 = (f32[512,128]{1,0:T(8,128)S(1)}, f32[512,128]{1,0:T(8,128)S(1)}, u32[]{:S(2)}, u32[]{:S(2)}) collective-permute-start(f32[512,128]{1,0:T(8,128)S(1)} %copy-done.44), channel_id=1, source_target_pairs={{0,16},{4,20},{8,24},{12,28},{16,0},{20,4},{24,8},{28,12},{1,17},{... | collective-permute-start | bytes 786440 | tf_op jit(solution)/shard_map/ppermute | solution.py:616
  94.4 6.4 %earlier_orders.6.refs_6_ = f32[3,8,64,256]{3,2,1,0:T(8,128)S(1)} custom-call(f32[6,3,32,64,256]{4,3,2,1,0:T(8,128)} %refs_4_.11, f32[6,3,32,64,256]{4,3,2,1,0:T(8,128)} %refs_4_.11, f32[6,3,32,64,256]{4,3,2,1,0:T(8,128)} %refs_4_.11, f32[6,3,32,64,256]{4,3,2,1,0:T(8,128)} %refs_4_.11, f32[6,3,32,64,256]{4,3,2,1,0:T(8,128)} %refs_4_.11, ...), custom_call_target="tpu_custom_call" | custom-call | flops 1024 | bytes 1024 | tf_op jit(solution)/shard_map/earlier_orders/pallas_call | solution.py:297
  100.8 4.8 %second_synth.5 = (f32[4,240,128]{2,1,0:T(8,128)S(1)}, f32[4,240,128]{2,1,0:T(8,128)S(1)}, f32[4,240,128]{2,1,0:T(8,128)S(1)}, f32[4,240,128]{2,1,0:T(8,128)S(1)}) custom-call(s32[2]{0:T(128)S(1)} %copy-done.34, f32[512,128]{1,0:T(8,128)S(1)} %get-tuple-element.187.refs_0_, f32[512,128]{1,0:T(8,128)} %collective-permute-done.7.refs_1_, ...), custom_call_target="tpu_custom_call" | custom-call | flops 1024 | bytes 1024 | tf_op jit(solution)/shard_map/second_synth/pallas_call | solution.py:243
  110.7 9.0 %third_dimension.4 = (f32[4,120,128]{2,1,0:T(8,128)S(1)}, f32[4,120,128]{2,1,0:T(8,128)S(1)}, f32[4,120,128]{2,1,0:T(8,128)S(1)}, f32[4,120,128]{2,1,0:T(8,128)S(1)}) custom-call(f32[4,240,128]{2,1,0:T(8,128)S(1)} %get-tuple-element.192.refs_0_, f32[4,240,128]{2,1,0:T(8,128)S(1)} %collective-permute-done.4.refs_1_, ...), custom_call_target="tpu_custom_call" | custom-call | flops 1024 | bytes 1024 | tf_op jit(solution)/shard_map/third_dimension/pallas_call | solution.py:347
  122.8 10.4 %collective-permute-done.10.refs_1_ = f32[4,120,128]{2,1,0:T(8,128)S(1)} collective-permute-done((f32[4,120,128]{2,1,0:T(8,128)S(1)}, f32[4,120,128]{2,1,0:T(8,128)S(1)}, u32[]{:S(2)}, u32[]{:S(2)}) %collective-permute-start.10) | collective-permute-done | bytes 245792 | tf_op jit(solution)/shard_map/ppermute | solution.py:616
  140.0 6.4 %earlier_orders.7.refs_6_ = f32[3,8,64,256]{3,2,1,0:T(8,128)S(1)} custom-call(f32[6,3,32,64,256]{4,3,2,1,0:T(8,128)} %refs_4_.11, f32[6,3,32,64,256]{4,3,2,1,0:T(8,128)} %refs_4_.11, f32[6,3,32,64,256]{4,3,2,1,0:T(8,128)} %refs_4_.11, f32[6,3,32,64,256]{4,3,2,1,0:T(8,128)} %refs_4_.11, f32[6,3,32,64,256]{4,3,2,1,0:T(8,128)} %refs_4_.11, ...), custom_call_target="tpu_custom_call" | custom-call | flops 1024 | bytes 1024 | tf_op jit(solution)/shard_map/earlier_orders/pallas_call | solution.py:297
  146.4 3.9 %second_synth.6 = (f32[4,240,128]{2,1,0:T(8,128)S(1)}, f32[4,240,128]{2,1,0:T(8,128)S(1)}, f32[4,240,128]{2,1,0:T(8,128)S(1)}, f32[4,240,128]{2,1,0:T(8,128)S(1)}) custom-call(s32[2]{0:T(128)S(1)} %copy-done.34, f32[512,128]{1,0:T(8,128)S(1)} %get-tuple-element.212.refs_0_, f32[512,128]{1,0:T(8,128)S(1)} %collective-permute-done.16.refs_1_, ...), custom_call_target="tpu_custom_call" | custom-call | flops 1024 | bytes 1024 | tf_op jit(solution)/shard_map/second_synth/pallas_call | solution.py:243
  150.4 9.3 %third_dimension.5 = (f32[4,120,128]{2,1,0:T(8,128)S(1)}, f32[4,120,128]{2,1,0:T(8,128)S(1)}, f32[4,120,128]{2,1,0:T(8,128)S(1)}, f32[4,120,128]{2,1,0:T(8,128)S(1)}) custom-call(f32[4,240,128]{2,1,0:T(8,128)S(1)} %get-tuple-element.217.refs_0_, f32[4,240,128]{2,1,0:T(8,128)S(1)} %collective-permute-done.13.refs_1_, ...), custom_call_target="tpu_custom_call" | custom-call | flops 1024 | bytes 1024 | tf_op jit(solution)/shard_map/third_dimension/pallas_call | solution.py:347
  159.7 4.7 %second_back.4 = (f32[304,128]{1,0:T(8,128)S(1)}, f32[304,128]{1,0:T(8,128)S(1)}, f32[304,128]{1,0:T(8,128)S(1)}, f32[304,128]{1,0:T(8,128)S(1)}) custom-call(s32[2]{0:T(128)S(1)} %copy-done.34, f32[4,120,128]{2,1,0:T(8,128)S(1)} %get-tuple-element.222.refs_0_, f32[4,120,128]{2,1,0:T(8,128)S(1)} %collective-permute-done.10.refs_1_, ...), custom_call_target="tpu_custom_call" | custom-call | flops 1024 | bytes 1024 | tf_op jit(solution)/shard_map/second_back/pallas_call | solution.py:409
  171.6 3.1 collective-permute-done.20.refs_2_
  176.5 5.3 %collective-permute-done.21.refs_3_ = f32[304,128]{1,0:T(8,128)S(1)} collective-permute-done((f32[304,128]{1,0:T(8,128)S(1)}, f32[304,128]{1,0:T(8,128)S(1)}, u32[]{:S(2)}, u32[]{:S(2)}) %collective-permute-start.21) | collective-permute-done | bytes 155680 | tf_op jit(solution)/shard_map/ppermute | solution.py:616
  183.8 3.9 %second_synth.7 = (f32[4,240,128]{2,1,0:T(8,128)S(1)}, f32[4,240,128]{2,1,0:T(8,128)S(1)}, f32[4,240,128]{2,1,0:T(8,128)S(1)}, f32[4,240,128]{2,1,0:T(8,128)S(1)}) custom-call(s32[2]{0:T(128)S(1)} %copy-done.34, f32[512,128]{1,0:T(8,128)S(1)} %get-tuple-element.247.refs_0_, f32[512,128]{1,0:T(8,128)S(1)} %collective-permute-done.28.refs_1_, ...), custom_call_target="tpu_custom_call" | custom-call | flops 1024 | bytes 1024 | tf_op jit(solution)/shard_map/second_synth/pallas_call | solution.py:243
  187.7 11.9 %collective-permute-done.23.refs_2_ = f32[4,120,128]{2,1,0:T(8,128)S(1)} collective-permute-done((f32[4,120,128]{2,1,0:T(8,128)S(1)}, f32[4,120,128]{2,1,0:T(8,128)S(1)}, u32[]{:S(2)}, u32[]{:S(2)}) %collective-permute-start.23) | collective-permute-done | bytes 245792 | tf_op jit(solution)/shard_map/ppermute | solution.py:616
  199.7 9.3 %third_dimension.6 = (f32[4,120,128]{2,1,0:T(8,128)S(1)}, f32[4,120,128]{2,1,0:T(8,128)S(1)}, f32[4,120,128]{2,1,0:T(8,128)S(1)}, f32[4,120,128]{2,1,0:T(8,128)S(1)}) custom-call(f32[4,240,128]{2,1,0:T(8,128)S(1)} %get-tuple-element.252.refs_0_, f32[4,240,128]{2,1,0:T(8,128)S(1)} %collective-permute-done.25.refs_1_, ...), custom_call_target="tpu_custom_call" | custom-call | flops 1024 | bytes 1024 | tf_op jit(solution)/shard_map/third_dimension/pallas_call | solution.py:347
  209.0 4.9 %second_back.5 = (f32[304,128]{1,0:T(8,128)S(1)}, f32[304,128]{1,0:T(8,128)S(1)}, f32[304,128]{1,0:T(8,128)S(1)}, f32[304,128]{1,0:T(8,128)S(1)}) custom-call(s32[2]{0:T(128)S(1)} %copy-done.34, f32[4,120,128]{2,1,0:T(8,128)S(1)} %get-tuple-element.257.refs_0_, f32[4,120,128]{2,1,0:T(8,128)S(1)} %collective-permute-done.22.refs_1_, ...), custom_call_target="tpu_custom_call" | custom-call | flops 1024 | bytes 1024 | tf_op jit(solution)/shard_map/second_back/pallas_call | solution.py:409
  223.9 5.8 %collective-permute-done.33.refs_7_ = f32[304,128]{1,0:T(8,128)S(1)} collective-permute-done((f32[304,128]{1,0:T(8,128)S(1)}, f32[304,128]{1,0:T(8,128)S(1)}, u32[]{:S(2)}, u32[]{:S(2)}) %collective-permute-start.33) | collective-permute-done | bytes 155680 | tf_op jit(solution)/shard_map/ppermute | solution.py:616
  232.3 15.6 %collective-permute-done.35.refs_2_ = f32[4,120,128]{2,1,0:T(8,128)S(1)} collective-permute-done((f32[4,120,128]{2,1,0:T(8,128)S(1)}, f32[4,120,128]{2,1,0:T(8,128)S(1)}, u32[]{:S(2)}, u32[]{:S(2)}) %collective-permute-start.35) | collective-permute-done | bytes 245792 | tf_op jit(solution)/shard_map/ppermute | solution.py:616
  247.9 9.3 %third_dimension.7 = (f32[4,120,128]{2,1,0:T(8,128)S(1)}, f32[4,120,128]{2,1,0:T(8,128)S(1)}, f32[4,120,128]{2,1,0:T(8,128)S(1)}, f32[4,120,128]{2,1,0:T(8,128)S(1)}) custom-call(f32[4,240,128]{2,1,0:T(8,128)S(1)} %get-tuple-element.275.refs_0_, f32[4,240,128]{2,1,0:T(8,128)S(1)} %collective-permute-done.37.refs_1_, ...), custom_call_target="tpu_custom_call" | custom-call | flops 1024 | bytes 1024 | tf_op jit(solution)/shard_map/third_dimension/pallas_call | solution.py:347
  257.2 4.7 %second_back.6 = (f32[304,128]{1,0:T(8,128)S(1)}, f32[304,128]{1,0:T(8,128)S(1)}, f32[304,128]{1,0:T(8,128)S(1)}, f32[304,128]{1,0:T(8,128)S(1)}) custom-call(s32[2]{0:T(128)S(1)} %copy-done.34, f32[4,120,128]{2,1,0:T(8,128)S(1)} %get-tuple-element.280.refs_0_, f32[4,120,128]{2,1,0:T(8,128)S(1)} %collective-permute-done.34.refs_1_, ...), custom_call_target="tpu_custom_call" | custom-call | flops 1024 | bytes 1024 | tf_op jit(solution)/shard_map/second_back/pallas_call | solution.py:409
  270.9 6.9 %collective-permute-done.41.refs_10_ = f32[304,128]{1,0:T(8,128)S(1)} collective-permute-done((f32[304,128]{1,0:T(8,128)S(1)}, f32[304,128]{1,0:T(8,128)S(1)}, u32[]{:S(2)}, u32[]{:S(2)}) %collective-permute-start.41) | collective-permute-done | bytes 155680 | tf_op jit(solution)/shard_map/ppermute | solution.py:616
  277.8 4.7 %second_back.7 = (f32[304,128]{1,0:T(8,128)S(1)}, f32[304,128]{1,0:T(8,128)S(1)}, f32[304,128]{1,0:T(8,128)S(1)}, f32[304,128]{1,0:T(8,128)S(1)}) custom-call(s32[2]{0:T(128)S(1)} %copy-done.34, f32[4,120,128]{2,1,0:T(8,128)S(1)} %get-tuple-element.295.refs_0_, f32[4,120,128]{2,1,0:T(8,128)S(1)} %collective-permute-done.43.refs_1_, ...), custom_call_target="tpu_custom_call" | custom-call | flops 1024 | bytes 1024 | tf_op jit(solution)/shard_map/second_back/pallas_call | solution.py:409
  289.4 7.8 %collective-permute-done.47.refs_14_ = f32[304,128]{1,0:T(8,128)S(1)} collective-permute-done((f32[304,128]{1,0:T(8,128)S(1)}, f32[304,128]{1,0:T(8,128)S(1)}, u32[]{:S(2)}, u32[]{:S(2)}) %collective-permute-start.47) | collective-permute-done | bytes 155680 | tf_op jit(solution)/shard_map/ppermute | solution.py:616
  297.2 3.1 first_back.2
  316.5 6.2 %last_projection.1 = f32[3,20,40,160]{3,2,1,0:T(8,128)} custom-call(f32[10]{0:T(128)S(1)} %convert_multiply_fusion.1.refs_0_, f32[160,2432]{1,0:T(8,128)S(1)} %first_back.3.refs_1_, f32[160,2432]{1,0:T(8,128)S(1)} %collective-permute-done.49.refs_2_, f32[8,256]{1,0:T(8,128)S(1)} %copy-done.32, f32[40,256]{1,0:T(8,128)S(1)} %broadcast_in_dim.20.refs_4_), custom_call_target="tpu_custom_call" | custom-call | flops 1024 | bytes 1024 | tf_op jit(solution)/shard_map/last_projection/pallas_call | solution.py:524
  (199 shorter events, 90.8 us)
Async XLA Ops:
  32.8 26.4 %collective-permute-start.2 = (f32[512,128]{1,0:T(8,128)}, f32[512,128]{1,0:T(8,128)}, u32[]{:S(2)}, u32[]{:S(2)}) collective-permute-start(f32[512,128]{1,0:T(8,128)} %get-tuple-element.164), channel_id=1, source_target_pairs={{0,16},{4,20},{8,24},{12,28},{16,0},{20,4},{24,8},{28,12},{1,17},{... | collective-permute-start | bytes 786440 | tf_op jit(solution)/shard_map/ppermute | solution.py:616
  35.4 23.8 %collective-permute-start.3 = (f32[512,128]{1,0:T(8,128)}, f32[512,128]{1,0:T(8,128)}, u32[]{:S(2)}, u32[]{:S(2)}) collective-permute-start(f32[512,128]{1,0:T(8,128)} %get-tuple-element.165), channel_id=1, source_target_pairs={{0,24},{4,28},{8,16},{12,20},{16,8},{20,12},{24,0},{28,4},{1,25},{... | collective-permute-start | bytes 786440 | tf_op jit(solution)/shard_map/ppermute | solution.py:616
  45.1 26.2 %collective-permute-start.7 = (f32[512,128]{1,0:T(8,128)}, f32[512,128]{1,0:T(8,128)}, u32[]{:S(2)}, u32[]{:S(2)}) collective-permute-start(f32[512,128]{1,0:T(8,128)} %get-tuple-element.180), channel_id=1, source_target_pairs={{0,8},{4,12},{8,0},{12,4},{16,24},{20,28},{24,16},{28,20},{1,9},{5... | collective-permute-start | bytes 786440 | tf_op jit(solution)/shard_map/ppermute | solution.py:616
  64.2 41.5 %collective-permute-start.4 = (f32[4,240,128]{2,1,0:T(8,128)S(1)}, f32[4,240,128]{2,1,0:T(8,128)S(1)}, u32[]{:S(2)}, u32[]{:S(2)}) collective-permute-start(f32[4,240,128]{2,1,0:T(8,128)S(1)} %get-tuple-element.175), channel_id=1, source_target_pairs={{0,1},{1,0},{2,3},{3,2},{4,5},{5,4},{6,7},{7,6},{8,9},{9,8},{10,11... | collective-permute-start | bytes 1474568 | tf_op jit(solution)/shard_map/ppermute | solution.py:616
  65.9 41.3 %collective-permute-start.5 = (f32[4,240,128]{2,1,0:T(8,128)S(1)}, f32[4,240,128]{2,1,0:T(8,128)S(1)}, u32[]{:S(2)}, u32[]{:S(2)}) collective-permute-start(f32[4,240,128]{2,1,0:T(8,128)S(1)} %get-tuple-element.176), channel_id=1, source_target_pairs={{0,2},{1,3},{2,0},{3,1},{4,6},{5,7},{6,4},{7,5},{8,10},{9,11},{10,... | collective-permute-start | bytes 1474568 | tf_op jit(solution)/shard_map/ppermute | solution.py:616
  67.4 41.3 %collective-permute-start.6 = (f32[4,240,128]{2,1,0:T(8,128)S(1)}, f32[4,240,128]{2,1,0:T(8,128)S(1)}, u32[]{:S(2)}, u32[]{:S(2)}) collective-permute-start(f32[4,240,128]{2,1,0:T(8,128)S(1)} %get-tuple-element.177), channel_id=1, source_target_pairs={{0,3},{1,2},{2,1},{3,0},{4,7},{5,6},{6,5},{7,4},{8,11},{9,10},{10,... | collective-permute-start | bytes 1474568 | tf_op jit(solution)/shard_map/ppermute | solution.py:616
  67.7 20.6 %collective-permute-start.8 = (f32[512,128]{1,0:T(8,128)S(1)}, f32[512,128]{1,0:T(8,128)S(1)}, u32[]{:S(2)}, u32[]{:S(2)}) collective-permute-start(f32[512,128]{1,0:T(8,128)S(1)} %copy-done.50), channel_id=1, source_target_pairs={{0,16},{4,20},{8,24},{12,28},{16,0},{20,4},{24,8},{28,12},{1,17},{... | collective-permute-start | bytes 786440 | tf_op jit(solution)/shard_map/ppermute | solution.py:616
  71.3 17.0 %collective-permute-start.9 = (f32[512,128]{1,0:T(8,128)S(1)}, f32[512,128]{1,0:T(8,128)S(1)}, u32[]{:S(2)}, u32[]{:S(2)}) collective-permute-start(f32[512,128]{1,0:T(8,128)S(1)} %copy-done.48), channel_id=1, source_target_pairs={{0,24},{4,28},{8,16},{12,20},{16,8},{20,12},{24,0},{28,4},{1,25},{... | collective-permute-start | bytes 786440 | tf_op jit(solution)/shard_map/ppermute | solution.py:616
  88.3 20.9 %collective-permute-start.16 = (f32[512,128]{1,0:T(8,128)S(1)}, f32[512,128]{1,0:T(8,128)S(1)}, u32[]{:S(2)}, u32[]{:S(2)}) collective-permute-start(f32[512,128]{1,0:T(8,128)S(1)} %copy-done.46), channel_id=1, source_target_pairs={{0,8},{4,12},{8,0},{12,4},{16,24},{20,28},{24,16},{28,20},{1,9},{5... | collective-permute-start | bytes 786440 | tf_op jit(solution)/shard_map/ppermute | solution.py:616
  88.3 31.3 %collective-permute-start.17 = (f32[512,128]{1,0:T(8,128)S(1)}, f32[512,128]{1,0:T(8,128)S(1)}, u32[]{:S(2)}, u32[]{:S(2)}) collective-permute-start(f32[512,128]{1,0:T(8,128)S(1)} %copy-done.44), channel_id=1, source_target_pairs={{0,16},{4,20},{8,24},{12,28},{16,0},{20,4},{24,8},{28,12},{1,17},{... | collective-permute-start | bytes 786440 | tf_op jit(solution)/shard_map/ppermute | solution.py:616
  105.7 30.0 %collective-permute-start.13 = (f32[4,240,128]{2,1,0:T(8,128)S(1)}, f32[4,240,128]{2,1,0:T(8,128)S(1)}, u32[]{:S(2)}, u32[]{:S(2)}) collective-permute-start(f32[4,240,128]{2,1,0:T(8,128)S(1)} %get-tuple-element.200), channel_id=1, source_target_pairs={{0,1},{1,0},{2,3},{3,2},{4,5},{5,4},{6,7},{7,6},{8,9},{9,8},{10,11... | collective-permute-start | bytes 1474568 | tf_op jit(solution)/shard_map/ppermute | solution.py:616
  107.2 28.4 %collective-permute-start.14 = (f32[4,240,128]{2,1,0:T(8,128)S(1)}, f32[4,240,128]{2,1,0:T(8,128)S(1)}, u32[]{:S(2)}, u32[]{:S(2)}) collective-permute-start(f32[4,240,128]{2,1,0:T(8,128)S(1)} %get-tuple-element.201), channel_id=1, source_target_pairs={{0,2},{1,3},{2,0},{3,1},{4,6},{5,7},{6,4},{7,5},{8,10},{9,11},{10,... | collective-permute-start | bytes 1474568 | tf_op jit(solution)/shard_map/ppermute | solution.py:616
  108.7 29.4 %collective-permute-start.15 = (f32[4,240,128]{2,1,0:T(8,128)S(1)}, f32[4,240,128]{2,1,0:T(8,128)S(1)}, u32[]{:S(2)}, u32[]{:S(2)}) collective-permute-start(f32[4,240,128]{2,1,0:T(8,128)S(1)} %get-tuple-element.202), channel_id=1, source_target_pairs={{0,3},{1,2},{2,1},{3,0},{4,7},{5,6},{6,5},{7,4},{8,11},{9,10},{10,... | collective-permute-start | bytes 1474568 | tf_op jit(solution)/shard_map/ppermute | solution.py:616
  121.3 38.4 %collective-permute-start.11 = (f32[4,120,128]{2,1,0:T(8,128)S(1)}, f32[4,120,128]{2,1,0:T(8,128)S(1)}, u32[]{:S(2)}, u32[]{:S(2)}) collective-permute-start(f32[4,120,128]{2,1,0:T(8,128)S(1)} %get-tuple-element.198), channel_id=1, source_target_pairs={{0,2},{1,3},{2,0},{3,1},{4,6},{5,7},{6,4},{7,5},{8,10},{9,11},{10,... | collective-permute-start | bytes 737288 | tf_op jit(solution)/shard_map/ppermute | solution.py:616
  133.2 26.5 %collective-permute-start.12 = (f32[4,120,128]{2,1,0:T(8,128)S(1)}, f32[4,120,128]{2,1,0:T(8,128)S(1)}, u32[]{:S(2)}, u32[]{:S(2)}) collective-permute-start(f32[4,120,128]{2,1,0:T(8,128)S(1)} %get-tuple-element.199), channel_id=1, source_target_pairs={{0,3},{1,2},{2,1},{3,0},{4,7},{5,6},{6,5},{7,4},{8,11},{9,10},{10,... | collective-permute-start | bytes 737288 | tf_op jit(solution)/shard_map/ppermute | solution.py:616
  135.6 31.4 %collective-permute-start.28 = (f32[512,128]{1,0:T(8,128)S(1)}, f32[512,128]{1,0:T(8,128)S(1)}, u32[]{:S(2)}, u32[]{:S(2)}) collective-permute-start(f32[512,128]{1,0:T(8,128)S(1)} %copy-done.40), channel_id=1, source_target_pairs={{0,8},{4,12},{8,0},{12,4},{16,24},{20,28},{24,16},{28,20},{1,9},{5... | collective-permute-start | bytes 786440 | tf_op jit(solution)/shard_map/ppermute | solution.py:616
  135.7 31.9 %collective-permute-start.29 = (f32[512,128]{1,0:T(8,128)S(1)}, f32[512,128]{1,0:T(8,128)S(1)}, u32[]{:S(2)}, u32[]{:S(2)}) collective-permute-start(f32[512,128]{1,0:T(8,128)S(1)} %copy-done.38), channel_id=1, source_target_pairs={{0,16},{4,20},{8,24},{12,28},{16,0},{20,4},{24,8},{28,12},{1,17},{... | collective-permute-start | bytes 786440 | tf_op jit(solution)/shard_map/ppermute | solution.py:616
  138.2 30.9 %collective-permute-start.30 = (f32[512,128]{1,0:T(8,128)S(1)}, f32[512,128]{1,0:T(8,128)S(1)}, u32[]{:S(2)}, u32[]{:S(2)}) collective-permute-start(f32[512,128]{1,0:T(8,128)S(1)} %copy-done.36), channel_id=1, source_target_pairs={{0,24},{4,28},{8,16},{12,20},{16,8},{20,12},{24,0},{28,4},{1,25},{... | collective-permute-start | bytes 786440 | tf_op jit(solution)/shard_map/ppermute | solution.py:616
  167.0 15.3 %collective-permute-start.22 = (f32[4,120,128]{2,1,0:T(8,128)S(1)}, f32[4,120,128]{2,1,0:T(8,128)S(1)}, u32[]{:S(2)}, u32[]{:S(2)}) collective-permute-start(f32[4,120,128]{2,1,0:T(8,128)S(1)} %get-tuple-element.230), channel_id=1, source_target_pairs={{0,1},{1,0},{2,3},{3,2},{4,5},{5,4},{6,7},{7,6},{8,9},{9,8},{10,11... | collective-permute-start | bytes 737288 | tf_op jit(solution)/shard_map/ppermute | solution.py:616
  167.6 32.1 %collective-permute-start.25 = (f32[4,240,128]{2,1,0:T(8,128)S(1)}, f32[4,240,128]{2,1,0:T(8,128)S(1)}, u32[]{:S(2)}, u32[]{:S(2)}) collective-permute-start(f32[4,240,128]{2,1,0:T(8,128)S(1)} %get-tuple-element.237), channel_id=1, source_target_pairs={{0,1},{1,0},{2,3},{3,2},{4,5},{5,4},{6,7},{7,6},{8,9},{9,8},{10,11... | collective-permute-start | bytes 1474568 | tf_op jit(solution)/shard_map/ppermute | solution.py:616
  169.0 30.6 %collective-permute-start.26 = (f32[4,240,128]{2,1,0:T(8,128)S(1)}, f32[4,240,128]{2,1,0:T(8,128)S(1)}, u32[]{:S(2)}, u32[]{:S(2)}) collective-permute-start(f32[4,240,128]{2,1,0:T(8,128)S(1)} %get-tuple-element.238), channel_id=1, source_target_pairs={{0,2},{1,3},{2,0},{3,1},{4,6},{5,7},{6,4},{7,5},{8,10},{9,11},{10,... | collective-permute-start | bytes 1474568 | tf_op jit(solution)/shard_map/ppermute | solution.py:616
  170.9 28.8 %collective-permute-start.27 = (f32[4,240,128]{2,1,0:T(8,128)S(1)}, f32[4,240,128]{2,1,0:T(8,128)S(1)}, u32[]{:S(2)}, u32[]{:S(2)}) collective-permute-start(f32[4,240,128]{2,1,0:T(8,128)S(1)} %get-tuple-element.239), channel_id=1, source_target_pairs={{0,3},{1,2},{2,1},{3,0},{4,7},{5,6},{6,5},{7,4},{8,11},{9,10},{10,... | collective-permute-start | bytes 1474568 | tf_op jit(solution)/shard_map/ppermute | solution.py:616
  181.8 17.9 %collective-permute-start.23 = (f32[4,120,128]{2,1,0:T(8,128)S(1)}, f32[4,120,128]{2,1,0:T(8,128)S(1)}, u32[]{:S(2)}, u32[]{:S(2)}) collective-permute-start(f32[4,120,128]{2,1,0:T(8,128)S(1)} %get-tuple-element.231), channel_id=1, source_target_pairs={{0,2},{1,3},{2,0},{3,1},{4,6},{5,7},{6,4},{7,5},{8,10},{9,11},{10,... | collective-permute-start | bytes 737288 | tf_op jit(solution)/shard_map/ppermute | solution.py:616
  182.3 17.4 %collective-permute-start.24 = (f32[4,120,128]{2,1,0:T(8,128)S(1)}, f32[4,120,128]{2,1,0:T(8,128)S(1)}, u32[]{:S(2)}, u32[]{:S(2)}) collective-permute-start(f32[4,120,128]{2,1,0:T(8,128)S(1)} %get-tuple-element.232), channel_id=1, source_target_pairs={{0,3},{1,2},{2,1},{3,0},{4,7},{5,6},{6,5},{7,4},{8,11},{9,10},{10,... | collective-permute-start | bytes 737288 | tf_op jit(solution)/shard_map/ppermute | solution.py:616
  215.8 16.5 %collective-permute-start.34 = (f32[4,120,128]{2,1,0:T(8,128)S(1)}, f32[4,120,128]{2,1,0:T(8,128)S(1)}, u32[]{:S(2)}, u32[]{:S(2)}) collective-permute-start(f32[4,120,128]{2,1,0:T(8,128)S(1)} %get-tuple-element.265), channel_id=1, source_target_pairs={{0,1},{1,0},{2,3},{3,2},{4,5},{5,4},{6,7},{7,6},{8,9},{9,8},{10,11... | collective-permute-start | bytes 737288 | tf_op jit(solution)/shard_map/ppermute | solution.py:616
  216.4 31.5 %collective-permute-start.37 = (f32[4,240,128]{2,1,0:T(8,128)S(1)}, f32[4,240,128]{2,1,0:T(8,128)S(1)}, u32[]{:S(2)}, u32[]{:S(2)}) collective-permute-start(f32[4,240,128]{2,1,0:T(8,128)S(1)} %get-tuple-element.272), channel_id=1, source_target_pairs={{0,1},{1,0},{2,3},{3,2},{4,5},{5,4},{6,7},{7,6},{8,9},{9,8},{10,11... | collective-permute-start | bytes 1474568 | tf_op jit(solution)/shard_map/ppermute | solution.py:616
  217.9 30.0 %collective-permute-start.38 = (f32[4,240,128]{2,1,0:T(8,128)S(1)}, f32[4,240,128]{2,1,0:T(8,128)S(1)}, u32[]{:S(2)}, u32[]{:S(2)}) collective-permute-start(f32[4,240,128]{2,1,0:T(8,128)S(1)} %get-tuple-element.273), channel_id=1, source_target_pairs={{0,2},{1,3},{2,0},{3,1},{4,6},{5,7},{6,4},{7,5},{8,10},{9,11},{10,... | collective-permute-start | bytes 1474568 | tf_op jit(solution)/shard_map/ppermute | solution.py:616
  221.6 26.3 %collective-permute-start.39 = (f32[4,240,128]{2,1,0:T(8,128)S(1)}, f32[4,240,128]{2,1,0:T(8,128)S(1)}, u32[]{:S(2)}, u32[]{:S(2)}) collective-permute-start(f32[4,240,128]{2,1,0:T(8,128)S(1)} %get-tuple-element.274), channel_id=1, source_target_pairs={{0,3},{1,2},{2,1},{3,0},{4,7},{5,6},{6,5},{7,4},{8,11},{9,10},{10,... | collective-permute-start | bytes 1474568 | tf_op jit(solution)/shard_map/ppermute | solution.py:616
  229.7 18.2 %collective-permute-start.35 = (f32[4,120,128]{2,1,0:T(8,128)S(1)}, f32[4,120,128]{2,1,0:T(8,128)S(1)}, u32[]{:S(2)}, u32[]{:S(2)}) collective-permute-start(f32[4,120,128]{2,1,0:T(8,128)S(1)} %get-tuple-element.266), channel_id=1, source_target_pairs={{0,2},{1,3},{2,0},{3,1},{4,6},{5,7},{6,4},{7,5},{8,10},{9,11},{10,... | collective-permute-start | bytes 737288 | tf_op jit(solution)/shard_map/ppermute | solution.py:616
  232.3 15.6 %collective-permute-start.36 = (f32[4,120,128]{2,1,0:T(8,128)S(1)}, f32[4,120,128]{2,1,0:T(8,128)S(1)}, u32[]{:S(2)}, u32[]{:S(2)}) collective-permute-start(f32[4,120,128]{2,1,0:T(8,128)S(1)} %get-tuple-element.267), channel_id=1, source_target_pairs={{0,3},{1,2},{2,1},{3,0},{4,7},{5,6},{6,5},{7,4},{8,11},{9,10},{10,... | collective-permute-start | bytes 737288 | tf_op jit(solution)/shard_map/ppermute | solution.py:616
  262.5 15.3 %collective-permute-start.43 = (f32[4,120,128]{2,1,0:T(8,128)S(1)}, f32[4,120,128]{2,1,0:T(8,128)S(1)}, u32[]{:S(2)}, u32[]{:S(2)}) collective-permute-start(f32[4,120,128]{2,1,0:T(8,128)S(1)} %get-tuple-element.288), channel_id=1, source_target_pairs={{0,1},{1,0},{2,3},{3,2},{4,5},{5,4},{6,7},{7,6},{8,9},{9,8},{10,11... | collective-permute-start | bytes 737288 | tf_op jit(solution)/shard_map/ppermute | solution.py:616
  300.4 16.0 %collective-permute-start.49 = (f32[160,2432]{1,0:T(8,128)S(1)}, f32[160,2432]{1,0:T(8,128)S(1)}, u32[]{:S(2)}, u32[]{:S(2)}) collective-permute-start(f32[160,2432]{1,0:T(8,128)S(1)} %first_back.2), channel_id=1, source_target_pairs={{0,4},{4,0},{8,12},{12,8},{16,20},{20,16},{24,28},{28,24},{1,5},{5... | collective-permute-start | bytes 4669448 | tf_op jit(solution)/shard_map/ppermute | solution.py:621
  (69 other events, 1143.6 us)

commit v4 on v3

v4 whole, which is shorter than its diff:
```python
import functools
import math

import jax
import jax.numpy as jnp
import ml_dtypes
import numpy as np
from jax import lax
from jax.experimental import pallas as pl
from jax.experimental.pallas import tpu as pltpu
from jax.sharding import PartitionSpec as P

LANES = 128
XC = 8
BF16 = jnp.bfloat16
F32 = jnp.float32
NN = (((1,), (0,)), ((), ()))
NT = (((1,), (1,)), ((), ()))


def round_up(value, step):
    return -(-value // step) * step


def synth_np(grid_len, mode_count):
    points = np.arange(grid_len)[:, None]
    mode_index = np.arange(mode_count)[None, :]
    wave_index = np.where(mode_index == 1, grid_len // 2, mode_index // 2)
    angles = (points * wave_index % grid_len) * (2.0 * math.pi / grid_len)
    trig = np.where((mode_index % 2 == 0) | (mode_index == 1), np.cos(angles), np.sin(angles))
    weight = np.where(mode_index < 2, 1.0, 2.0) / grid_len
    return np.where(mode_index == 1, 0.0, trig * np.sqrt(weight))


def slope_np(table, kmax):
    paired = table.reshape(table.shape[0], -1, 2)
    wavenum = np.arange(paired.shape[1]) / kmax
    return np.stack([-wavenum * paired[:, :, 1], wavenum * paired[:, :, 0]], -1).reshape(table.shape)


def halves(table):
    high = table.astype(ml_dtypes.bfloat16)
    low = (table - high.astype(np.float64)).astype(ml_dtypes.bfloat16)
    return high, low


def pieces_of(values):
    high = values.astype(BF16)
    return high, (values - high.astype(F32)).astype(BF16)


def dot(left, right, dims):
    return lax.dot_general(left, right, dims, preferred_element_type=F32)


def dot_data_left(values, high, low, dims=NN):
    top, rest = pieces_of(values)
    return dot(top, high, dims) + (dot(top, low, dims) + dot(rest, high, dims))


def dot_data_right(high, low, values, dims=NT):
    top, rest = pieces_of(values)
    return dot(high, top, dims) + (dot(low, top, dims) + dot(high, rest, dims))


def turn(values, shift):
    shift = shift % values.shape[-1]
    return values if shift == 0 else pltpu.roll(values, shift, axis=values.ndim - 1)


def lane_pack(parts, width, source_lane=0):
    tiles = []
    lane = lax.broadcasted_iota(jnp.int32, parts[0].shape, 1)
    for tile in range(-(-len(parts) * width // LANES)):
        start = tile * LANES
        acc = None
        for idx in range(start // width, min(len(parts) - 1, (start + LANES - 1) // width) + 1):
            moved = turn(parts[idx], idx * width - source_lane)
            acc = moved if acc is None else jnp.where(lane >= idx * width - start, moved, acc)
        tiles.append(acc)
    return tiles


VMEM_LIMIT = 24 * 1024 * 1024
SHORT = pl.CostEstimate(flops=1024, bytes_accessed=1024, transcendentals=0)
HBM = pl.BlockSpec(memory_space=pl.ANY)
SMEM = pl.BlockSpec(memory_space=pltpu.SMEM)
VMEM = pl.BlockSpec(memory_space=pltpu.VMEM)


def params():
    return pltpu.CompilerParams(dimension_semantics=("arbitrary",), vmem_limit_bytes=VMEM_LIMIT)


def still():
    return pltpu.CompilerParams(vmem_limit_bytes=VMEM_LIMIT)


def both_passes(values, high_low, high):
    top, rest = pieces_of(values)
    wide = dot(top, high_low, NN)
    half = high.shape[1]
    return wide[:, :half] + (wide[:, half:] + dot(rest, high, NN))


def whole(array):
    rank = len(array.shape)
    return pl.BlockSpec(array.shape, lambda *_: (0,) * rank)


def first_synth_kernel(dims, place_ref, own_ref, other_ref, table_ref, *rest):
    chunks, dests, xc = dims
    outs = rest[: chunks * dests]
    own_data, other_data, rows, sem = rest[chunks * dests :]
    _, ky_len, kz_len, _ = own_data.shape
    group = 5 * kz_len
    half = rows.shape[0] // 2
    copies = [
        pltpu.make_async_copy(ref.at[comp], data.at[comp], sem.at[side, comp])
        for side, (ref, data) in enumerate(((own_ref, own_data), (other_ref, other_data)))
        for comp in range(3)
    ]
    for copy in copies:
        copy.start()
    if ky_len * group < half:
        for core in range(2):
            rows[core * half + ky_len * group : (core + 1) * half, :] = jnp.zeros(
                (half - ky_len * group, LANES), F32
            )
    plain = jnp.concatenate([table_ref[0], table_ref[1]], axis=1)
    slope = jnp.concatenate([table_ref[2], table_ref[3]], axis=1)
    step = 4 if ky_len % 4 == 0 else 2

    for side, data in enumerate((own_data, other_data)):
        for copy in copies[3 * side : 3 * side + 3]:
            copy.wait()
        core = place_ref[1] if side == 0 else 1 - place_ref[1]

        def body(idx, carry):
            first = idx * step
            lines = [[data[comp, first + k] for comp in range(3)] for k in range(step)]
            found = both_passes(
                jnp.concatenate([v for line in lines for v in line], axis=0), plain, table_ref[0]
            )
            sloped = both_passes(
                jnp.concatenate([v for line in lines for v in line[1:]], axis=0), slope, table_ref[2]
            )
            for k in range(step):
                base = core * half + (first + k) * group
                rows[pl.ds(pl.multiple_of(base, 8), 3 * kz_len), :] = found[
                    3 * k * kz_len : 3 * (k + 1) * kz_len
                ]
                rows[pl.ds(pl.multiple_of(base + 3 * kz_len, 8), 2 * kz_len), :] = sloped[
                    2 * k * kz_len : 2 * (k + 1) * kz_len
                ]
            return carry

        lax.fori_loop(0, ky_len // step, body, 0)

    def flip(tile, carry):
        found = rows[pl.ds(pl.multiple_of(tile * LANES, LANES), LANES), :].T
        for idx, out in enumerate(outs):
            out[pl.ds(pl.multiple_of(tile * xc, 8), xc), :] = found[idx * xc : (idx + 1) * xc]
        return carry

    lax.fori_loop(0, 2 * half // LANES, flip, 0, unroll=2)


def first_synth(place, own, other, table, dims, lanes):
    chunks, dests, xc = dims
    out = jax.ShapeDtypeStruct((2 * lanes // LANES * xc, LANES), F32)
    found = pl.pallas_call(
        functools.partial(first_synth_kernel, dims),
        in_specs=[SMEM, HBM, HBM, VMEM],
        out_specs=[VMEM] * (chunks * dests),
        out_shape=[out] * (chunks * dests),
        scratch_shapes=[
            pltpu.VMEM(own.shape, F32),
            pltpu.VMEM(own.shape, F32),
            pltpu.VMEM((2 * lanes, LANES), F32),
            pltpu.SemaphoreType.DMA((2, 3)),
        ],
        compiler_params=still(),
        cost_estimate=SHORT,
        name="first_synth",
    )(place, own, other, table)
    return [list(found[k * dests : (k + 1) * dests]) for k in range(chunks)]


def second_synth_kernel(dims, place_ref, *refs):
    rows, xc, ky_len, kz_len, cols, y_len, pack = dims
    groups = rows // 2
    parts, table_ref, out_ref, a_ref = refs[:groups], refs[groups], refs[groups + 1], refs[groups + 2]
    size = a_ref.shape[0] // groups
    for k, part in enumerate(parts):
        a_ref[pl.ds(pl.multiple_of((place_ref[0] ^ k) * size, 8), size), :] = part[...]
    group = 5 * kz_len
    wide = round_up(group, LANES)
    tiles = a_ref.shape[0] // (rows * xc)

    def body(at, carry):
        turned = []
        for part in range(pack):
            line = [
                a_ref[pl.ds(tile * xc + at * pack + part, rows, stride=tiles * xc), :]
                for tile in range(tiles)
            ]
            found = []
            for ky in range(ky_len):
                start = ky * group
                low, off = divmod(start, LANES)
                window = line[low : low + (wide // LANES) + (1 if off else 0)]
                found.append(turn(jnp.concatenate(window, axis=1), -off)[:, :wide])
            turned.append(jnp.concatenate(found, axis=0).T[:group])
        plain = dot_data_left(jnp.concatenate(turned, axis=0), table_ref[0], table_ref[1])
        slope_in = [t[c * kz_len : (c + 1) * kz_len] for t in turned for c in (0, 2)]
        slope = dot_data_left(jnp.concatenate(slope_in, axis=0), table_ref[2], table_ref[3])
        fields = []
        for part in range(pack):
            own = plain[part * group : (part + 1) * group]
            sl = slope[part * 2 * kz_len : (part + 1) * 2 * kz_len]
            fields.append(
                jnp.concatenate(
                    [
                        own[: 3 * kz_len],
                        own[3 * kz_len : 4 * kz_len] - sl[:kz_len],
                        sl[kz_len:],
                        -own[4 * kz_len :],
                    ],
                    axis=0,
                )
            )
        for dest in range(cols):
            tile, off = divmod(dest * y_len, LANES)
            out_ref[place_ref[2] ^ dest, at] = lane_pack(
                [f[:, tile * LANES : (tile + 1) * LANES] for f in fields], y_len, off
            )[0]
        return carry

    lax.fori_loop(0, xc // pack, body, 0)


def second_synth(place, arrived, table, dims):
    rows, xc, ky_len, kz_len, cols, y_len, pack = dims
    packs = xc // pack
    return pl.pallas_call(
        functools.partial(second_synth_kernel, dims),
        in_specs=[SMEM] + [VMEM] * (len(arrived) + 1),
        out_specs=VMEM,
        out_shape=jax.ShapeDtypeStruct((cols, packs, 6 * kz_len, LANES), F32),
        scratch_shapes=[pltpu.VMEM((len(arrived) * arrived[0].shape[0], LANES), F32)],
        compiler_params=still(),
        cost_estimate=SHORT,
        name="second_synth",
    )(place, *arrived, table)


def cross(left, right):
    return [
        left[1] * right[2] - left[2] * right[1],
        left[2] * right[0] - left[0] * right[2],
        left[0] * right[1] - left[1] * right[0],
    ]


def earlier_kernel(count, *refs):
    vels, vorts, out_ref = refs[:count], refs[count : 2 * count], refs[2 * count]
    pack, y_len = out_ref.shape[1:3]
    for part in range(pack):
        def body(step, carry):
            at = pl.ds(pl.multiple_of(step * 8, 8), 8)
            total = None
            for vel, vort in zip(vels, vorts):
                term = cross(
                    [vel[0, c, part, at, :] for c in range(3)],
                    [vort[0, c, part, at, :] for c in range(3)],
                )
                total = term if total is None else [a + b for a, b in zip(total, term)]
            for comp in range(3):
                out_ref[comp, part, at, :] = total[comp]
            return carry

        lax.fori_loop(0, y_len // 8, body, 0, unroll=2)


def earlier(velocity, vorticity, chunk, xc, pack):
    orders, _, _, y_len, grid_len = velocity.shape
    packs = xc // pack
    block = (1, 3, pack, y_len, grid_len)

    def at(order):
        return pl.BlockSpec(block, lambda i: (order, 0, chunk * packs + i, 0, 0))

    specs = [at(k) for k in range(1, orders)] + [at(orders - k) for k in range(1, orders)]
    size = xc * y_len * grid_len
    return pl.pallas_call(
        functools.partial(earlier_kernel, orders - 1),
        grid=(packs,),
        in_specs=specs,
        out_specs=pl.BlockSpec((3, pack, y_len, grid_len), lambda i: (0, i, 0, 0)),
        out_shape=jax.ShapeDtypeStruct((3, xc, y_len, grid_len), F32),
        compiler_params=params(),
        cost_estimate=SHORT,
        name="earlier_orders",
    )(*[velocity] * (orders - 1), *[vorticity] * (orders - 1))


def third_kernel(dims, place_ref, *refs):
    chunk, kz_len, cols, y_len, pack = dims
    b_ref, stored_refs = refs[0], refs[1:4]
    table_ref, out_ref, data, sem = refs[4:]
    grid_len = table_ref.shape[2]
    xc = data.shape[2]
    packs = xc // pack

    def copies(at):
        spot = pl.ds(at * pack, pack)
        far = pl.ds(chunk * xc + at * pack, pack)
        sources = [ref.at[0, :, far] for ref in stored_refs[:2]] + [stored_refs[2].at[:, spot]]
        return [
            pltpu.make_async_copy(source, data.at[idx, :, spot], sem.at[idx, at])
            for idx, source in enumerate(sources)
        ]

    for at in range(packs):
        for copy in copies(at):
            copy.start()

    def body(at, carry):
        def stack(field):
            return jnp.concatenate(
                [
                    b_ref[place_ref[2] ^ k, at, field * kz_len : (field + 1) * kz_len, :]
                    for k in range(cols)
                ],
                axis=0,
            ).T

        lines = jnp.concatenate([stack(field) for field in range(6)], axis=0)
        plain = dot_data_left(lines, table_ref[0], table_ref[1])
        slope = dot_data_left(lines[: 2 * LANES], table_ref[2], table_ref[3])
        new = [plain[f * LANES : (f + 1) * LANES] for f in range(6)]
        vel_new = new[:3]
        vort_new = [new[4] - slope[LANES:], slope[:LANES] + new[5], new[3]]
        for copy in copies(at):
            copy.wait()
        spot = pl.ds(at * pack, pack)
        flat = (pack * y_len, grid_len)
        vel, vort, base = [[data[idx, c, spot].reshape(flat) for c in range(3)] for idx in range(3)]
        one, two = cross(vel_new, vort), cross(vel, vort_new)
        total = [one[c] + two[c] + base[c] for c in range(3)]
        result = dot_data_right(table_ref[0], table_ref[1], jnp.concatenate(total, axis=0))
        for k in range(cols):
            for comp in range(3):
                out_ref[place_ref[2] ^ k, at, comp * kz_len : (comp + 1) * kz_len, :] = result[
                    k * kz_len : (k + 1) * kz_len, comp * LANES : (comp + 1) * LANES
                ]
        return carry

    lax.fori_loop(0, packs, body, 0)


def third(place, arrived, velocity, vorticity, base, table, chunk, dims):
    kz_len, cols, y_len, pack = dims
    packs = arrived.shape[1]
    grid_len = velocity.shape[-1]
    return pl.pallas_call(
        functools.partial(third_kernel, (chunk, *dims)),
        in_specs=[SMEM, VMEM] + [HBM] * 3 + [VMEM],
        out_specs=VMEM,
        out_shape=jax.ShapeDtypeStruct((cols, packs, 3 * kz_len, LANES), F32),
        scratch_shapes=[
            pltpu.VMEM((3, 3, packs * pack, y_len, grid_len), F32),
            pltpu.SemaphoreType.DMA((3, packs)),
        ],
        compiler_params=still(),
        cost_estimate=SHORT,
        name="third_dimension",
    )(place, arrived, velocity, vorticity, base, table)


def second_back_kernel(dims, place_ref, c_ref, table_ref, *refs):
    rows, xc, ky_len, kz_len, cols, y_len, pack = dims
    outs, all_ref = refs[:-1], refs[-1]
    width = 3 * kz_len
    high_pad = round_up(width, LANES)

    def body(at, carry):
        lines = []
        for part in range(pack):
            tiles = lane_pack(
                [c_ref[place_ref[2] ^ k, at] for k in range(cols)], y_len, part * y_len
            )
            lines.append(jnp.concatenate(tiles, axis=1))
            if high_pad > width:
                lines.append(jnp.zeros((high_pad - width, cols * y_len), F32))
        result = dot_data_right(table_ref[0], table_ref[1], jnp.concatenate(lines, axis=0))
        for part in range(pack):
            own = result[:, part * high_pad : (part + 1) * high_pad]
            tiles = lane_pack([own[ky * rows : (ky + 1) * rows] for ky in range(ky_len)], width)
            for idx, tile in enumerate(tiles):
                spot = idx * xc + at * pack + part
                all_ref[pl.ds(spot, rows, stride=len(tiles) * xc), :] = tile
        return carry

    lax.fori_loop(0, xc // pack, body, 0)
    size = all_ref.shape[0] // len(outs)
    for k, out in enumerate(outs):
        out[...] = all_ref[pl.ds(pl.multiple_of((place_ref[0] ^ k) * size, 8), size), :]


def second_back(place, arrived, table, dims):
    rows, xc, ky_len, kz_len, cols, y_len, pack = dims
    size = round_up(ky_len * 3 * kz_len, LANES) // LANES * xc
    groups = rows // 2
    return pl.pallas_call(
        functools.partial(second_back_kernel, dims),
        in_specs=[SMEM, VMEM, VMEM],
        out_specs=[VMEM] * groups,
        out_shape=[jax.ShapeDtypeStruct((2 * size, LANES), F32)] * groups,
        scratch_shapes=[pltpu.VMEM((rows * size, LANES), F32)],
        compiler_params=still(),
        cost_estimate=SHORT,
        name="second_back",
    )(place, arrived, table)


def first_back_kernel(dims, place_ref, *refs):
    count, xc, own = dims
    parts, table_ref, out_ref = refs[:count], refs[count], refs[count + 1]
    size = parts[0].shape[0] // 2
    core = place_ref[1] if own else 1 - place_ref[1]
    for tile in range(size // xc):
        spot = pl.ds(pl.multiple_of(core * size + tile * xc, 8), xc)
        found = jnp.concatenate([part[spot, :] for part in parts], axis=0)
        out_ref[:, tile * LANES : (tile + 1) * LANES] = dot_data_right(
            table_ref[0], table_ref[1], found, NN
        )


def first_back(place, parts, table, xc, own):
    count = len(parts)
    size = parts[0].shape[0] // 2
    return pl.pallas_call(
        functools.partial(first_back_kernel, (count, xc, own)),
        in_specs=[SMEM] + [VMEM] * (count + 1),
        out_specs=VMEM,
        out_shape=jax.ShapeDtypeStruct((table.shape[1], size // xc * LANES), F32),
        compiler_params=still(),
        cost_estimate=SHORT,
        name="first_back",
    )(place, *parts, table)


def last_kernel(dims, *refs):
    kz_len, modes, scale = dims
    wave_y_ref, own_ref, other_ref, wave_x_ref, wave_z_ref, out_ref, rows = refs
    pair = 2 * 3 * kz_len
    at = pl.program_id(0)

    @pl.when(at == 0)
    def _():
        for tile in range(rows.shape[0] // LANES):
            lanes = slice(tile * LANES, (tile + 1) * LANES)
            rows[lanes, 0:modes] = (own_ref[:, lanes] + other_ref[:, lanes]).T

    spec = rows[pl.ds(pl.multiple_of(at * pair, 8), pair), :]
    wide = spec.shape[1]
    wave_x = jnp.broadcast_to(wave_x_ref[0:1, :], (kz_len, wide))
    wave_z = wave_z_ref[...]
    wave_y = wave_y_ref[at]
    even_x = lax.broadcasted_iota(jnp.int32, (kz_len, wide), 1) % 2 == 0
    even_z = lax.broadcasted_iota(jnp.int32, (kz_len, wide), 0) % 2 == 0

    def slope_x(value):
        return jnp.where(even_x, turn(value, -1), -turn(value, 1)) * wave_x

    def slope_z(value):
        return (
            jnp.where(
                even_z,
                pltpu.roll(value, kz_len - 1, axis=0),
                -pltpu.roll(value, 1, axis=0),
            )
            * wave_z
        )

    s = [
        [spec[(y * 3 + c) * kz_len : (y * 3 + c + 1) * kz_len] for c in range(3)] for y in range(2)
    ]
    square = wave_x * wave_x + wave_z * wave_z + wave_y * wave_y
    positive = square > 0
    safe = jnp.where(positive, square, 1.0)
    potential = []
    for y in range(2):
        along_y = s[1 - y][1] * (wave_y if y == 0 else -wave_y)
        divergence = slope_x(s[y][0]) + along_y + slope_z(s[y][2])
        potential.append(jnp.where(positive, divergence / safe, 0.0))
    for y in range(2):
        along_y = potential[1 - y] * (wave_y if y == 0 else -wave_y)
        found = [
            s[y][0] + slope_x(potential[y]),
            s[y][1] + along_y,
            s[y][2] + slope_z(potential[y]),
        ]
        for comp in range(3):
            out_ref[comp, y] = (found[comp] * scale)[:, :modes]


def last(own, other, wave_y, wave_x, wave_z, ky_len, kz_len, scale):
    modes, lanes = own.shape
    return pl.pallas_call(
        functools.partial(last_kernel, (kz_len, modes, scale)),
        grid=(ky_len // 2,),
        in_specs=[SMEM, *[whole(a) for a in (own, other, wave_x, wave_z)]],
        out_specs=pl.BlockSpec((3, 2, kz_len, modes), lambda i: (0, i, 0, 0)),
        out_shape=jax.ShapeDtypeStruct((3, ky_len, kz_len, modes), F32),
        scratch_shapes=[pltpu.VMEM((lanes, wave_x.shape[1]), F32)],
        compiler_params=params(),
        cost_estimate=SHORT,
        name="last_projection",
    )(wave_y, own, other, wave_x, wave_z)


def after(value, *earlier_values):
    return lax.optimization_barrier((value, earlier_values))[0]


def shards(new_velocity, stored_velocity, stored_vorticity):
    rows = lax.axis_size("row")
    cols = lax.axis_size("col")
    _, ky_len, kz_own, modes = new_velocity.shape
    orders, _, x_len, y_len, grid_len = stored_velocity.shape
    kz_len = round_up(kz_own, 8)
    kmax = modes // 2 - 1
    xc = min(XC, x_len)
    chunks = x_len // xc
    pack = LANES // y_len
    packs = xc // pack
    wide = round_up(modes, LANES)
    group = 5 * kz_len
    lanes = round_up(ky_len * group, 256)

    basis = synth_np(grid_len, modes)
    slope = slope_np(basis, kmax)
    y_order = (np.arange(rows)[None, :] * ky_len + np.arange(ky_len)[:, None]).reshape(-1)

    groups = rows // 2
    row, col = lax.axis_index("row"), lax.axis_index("col")
    place = jnp.stack([row // 2, row % 2, col]).astype(jnp.int32)

    def own_table(tables, axis):
        return lax.dynamic_index_in_dim(jnp.asarray(np.stack(tables)), lax.axis_index(axis), 0, False)

    def x_points(row):
        owner = np.array([row ^ (2 * k) for k in range(groups)])
        return (
            owner[None, :, None] * x_len
            + np.arange(chunks)[:, None, None] * xc
            + np.arange(xc)[None, None, :]
        ).reshape(-1)

    def halves_of(plain, sloped):
        return np.stack([part for table in (plain, sloped) for part in halves(table)])

    def y_table(col):
        points = np.concatenate([(col ^ k) * y_len + np.arange(y_len) for k in range(cols)])
        return halves_of(basis[points].T[y_order], slope[points].T[y_order])

    def z_table(col):
        def spread(table):
            parts = table.T.reshape(cols, kz_own, grid_len)[[col ^ k for k in range(cols)]]
            parts = np.pad(parts, ((0, 0), (0, kz_len - kz_own), (0, 0)))
            return parts.reshape(cols * kz_len, grid_len)

        return halves_of(spread(basis), spread(slope))

    table_x = own_table(
        [halves_of(basis[x_points(row)].T, slope[x_points(row)].T) for row in range(rows)], "row"
    )
    table_y = own_table([y_table(col) for col in range(cols)], "col")
    table_z = own_table([z_table(col) for col in range(cols)], "col")

    def wave_of(index):
        return (index // 2).astype(F32) / kmax

    mode = jnp.arange(wide, dtype=jnp.int32)
    wave_x = jnp.broadcast_to(jnp.where(mode < modes, wave_of(mode), 0.0)[None, :], (8, wide))
    ky_first = lax.axis_index("row") * ky_len + 2 * jnp.arange(ky_len // 2, dtype=jnp.int32)
    wave_y = wave_of(ky_first)
    kz = lax.axis_index("col") * kz_own + jnp.arange(kz_len, dtype=jnp.int32)
    wave_z = jnp.broadcast_to(wave_of(kz)[:, None], (kz_len, wide))

    coeffs = new_velocity
    if kz_len > kz_own:
        coeffs = jnp.pad(coeffs, ((0, 0), (0, 0), (0, kz_len - kz_own), (0, 0)))

    def col_swap(value):
        return lax.all_to_all(value, "col", split_axis=0, concat_axis=0, tiled=True)

    def core_swap(value):
        return lax.ppermute(value, "row", [(src, src ^ 1) for src in range(rows)])

    dims = (rows, xc, ky_len, kz_len, cols, y_len, pack)
    sent = first_synth(place, coeffs, core_swap(coeffs), table_x, (chunks, groups, xc), lanes)
    latest = sent[0][0]

    def ordered(kernel, operands, *others):
        nonlocal latest
        operands = after(operands, latest)
        found = kernel(operands, *others)
        latest = found[0] if isinstance(found, (list, tuple)) else found
        return found

    stored = (stored_velocity, stored_vorticity)

    def run_earlier(chunk):
        return ordered(lambda values: earlier(*values, chunk, xc, pack), stored)

    def z_exchange(values, *gates):
        found = [values[0]]
        for k in range(1, groups):
            value = after(values[k], *gates) if gates else values[k]
            found.append(lax.ppermute(value, "row", [(src, src ^ (2 * k)) for src in range(rows)]))
        return found

    first, second, middle, back, base = {}, {}, {}, {}, {}
    first[0] = z_exchange(sent[0])
    for chunk in range(min(2, chunks)):
        base[chunk] = run_earlier(chunk)
    z_last = first[0]
    for step in range(chunks + 2):
        if step + 1 < chunks:
            z_last = first[step + 1] = z_exchange(sent[step + 1], z_last)
        if step < chunks:
            found = ordered(lambda values: second_synth(place, values, table_y, dims), first[step])
            second[step] = col_swap(found)
        at = step - 1
        if 0 <= at < chunks:
            found = ordered(
                lambda values: third(place, values, *stored, base[at], table_z, at, dims[3:]),
                second[at],
            )
            middle[at] = col_swap(found)
        if step + 2 < chunks:
            base[step + 2] = run_earlier(step + 2)
        at = step - 2
        if 0 <= at < chunks:
            found = ordered(lambda values: second_back(place, values, table_y, dims), middle[at])
            z_last = back[at] = z_exchange(found, z_last)
    parts = [value for chunk in range(chunks) for value in back[chunk]]
    away = first_back(place, parts, table_x, xc, False)
    home = first_back(place, parts, after(table_x, away), xc, True)
    result = last(home, core_swap(away), wave_y, wave_x, wave_z, ky_len, kz_len, 1.0 / (orders + 1))
    return result[:, :, :kz_own] if kz_len > kz_own else result


def solution(mesh):
    return jax.shard_map(
        shards,
        mesh=mesh,
        in_specs=(
            P(None, "row", "col", None),
            P(None, None, "row", "col", None),
            P(None, None, "row", "col", None),
        ),
        out_specs=P(None, "row", "col", None),
        check_vma=False,
    )
```

time: 324 us -> 337 us (1.040)
  Pallas kernels: 129 us -> 100 us
  local copies, waits for them, and re-layouts: 23.9 us -> 46.3 us
  starting transfers between devices: 67 us -> 82.6 us
  blocking collectives: 0 us -> 14.1 us
  waiting for transfers between devices: 102 us -> 91.5 us
    all_to_all x0 -> x7, starting transfers between devices: none -> 27.9 us  [col_swap(): return lax.all_to_all(value, 'col', split_axis=0, concat_axis=0, tiled=True)]
    ppermute x48 -> x24, waiting for transfers between devices: 98.4 us -> 72.7 us  [z_exchange(): lax.ppermute(value, 'row', [(src, src ^ 2 * k) for src in range(rows)])]
    unnamed x102 -> x126, local copies, waits for them, and re-layouts: 20.9 us -> 43.3 us
    pallas_call x12, Pallas kernels: 73.5 us -> 55.1 us  [the longest x4 25.9 us: third(): pl.pallas_call(functools.partial(third_kernel, (chunk, *dims)), in_specs=...]
    all_to_all x0 -> x7, waiting for transfers between devices: none -> 15.3 us  [col_swap(): return lax.all_to_all(value, 'col', split_axis=0, concat_axis=0, tiled=True)]
    all_to_all x0 -> x1, blocking collectives: none -> 14.1 us  [col_swap(): return lax.all_to_all(value, 'col', split_axis=0, concat_axis=0, tiled=True)]
    ppermute x48 -> x24, starting transfers between devices: 66.4 us -> 54.2 us  [z_exchange(): lax.ppermute(value, 'row', [(src, src ^ 2 * k) for src in range(rows)])]
    pallas_call x1, Pallas kernels: 17.6 us -> 9.36 us  [first_synth(): pl.pallas_call(functools.partial(first_synth_kernel, dims), in_specs=[SME...]
  transfers between devices with their start and end apart: 50 -> 33, of which waited for: 15 -> 15; matrix products, arithmetic and copies ran while one was open for 1% -> 1% of each run, Pallas kernels for 22% -> 23%
where the time goes in v4:
time: 337 us; the launch traced here: 335 us
  Pallas kernels  100 us (30%)
  waiting for transfers between devices  91.5 us (27%)
  starting transfers between devices  82.6 us (25%)
  local copies, waits for them, and re-layouts  46.3 us (14%)
  blocking collectives  14.1 us (4%)
    ppermute x24, waiting for transfers between devices, z_exchange(): lax.ppermute(value, 'row', [(src, src ^ 2 * k) for src in range(rows)])  72.7 us
    ppermute x24, starting transfers between devices, z_exchange(): lax.ppermute(value, 'row', [(src, src ^ 2 * k) for src in range(rows)])  54.2 us
    unnamed x126, local copies, waits for them, and re-layouts  43.3 us
    all_to_all x7, starting transfers between devices, col_swap(): return lax.all_to_all(value, 'col', split_axis=0, concat_axis=0, tiled=True)  27.9 us
    pallas_call x4, Pallas kernels, third(): pl.pallas_call(functools.partial(third_kernel, (chunk, *dims)), in_specs=...  25.9 us
    pallas_call x4, Pallas kernels, earlier(): pl.pallas_call(functools.partial(earlier_kernel, orders - 1), grid=(packs...  25.6 us
    pallas_call x4, Pallas kernels, second_synth(): pl.pallas_call(functools.partial(second_synth_kernel, dims), in_specs=[SM...  17.4 us
    all_to_all x7, waiting for transfers between devices, col_swap(): return lax.all_to_all(value, 'col', split_axis=0, concat_axis=0, tiled=True)  15.3 us
  transfers between devices with their start and end apart: 33, of which 15 were waited for; matrix products, arithmetic and copies ran while one was open for 1% of the time, Pallas kernels for 23%

profile of v4, /device:TPU:0, one launch (start us, length us, event | category | flops | bytes accessed | tf_op | source)
XLA Modules:
  0.0 335.0 jit_solution(333844130467220100)
XLA Ops:
  6.7 9.4 %first_synth.1 = (f32[512,128]{1,0:T(8,128)S(1)}, f32[512,128]{1,0:T(8,128)}, f32[512,128]{1,0:T(8,128)}, f32[512,128]{1,0:T(8,128)}, f32[512,128]{1,0:T(8,128)S...) custom-call(s32[3]{0:T(128)S(1)} %pad_add_fusion.place_ref, ...), custom_call_target="tpu_custom_call" | custom-call | flops 1024 | bytes 1024 | tf_op jit(solution)/shard_map/first_synth/pallas_call | solution.py:172
  28.2 6.4 %earlier_orders.4.refs_3_ = f32[3,8,64,256]{3,2,1,0:T(8,128)S(1)} custom-call(f32[6,3,32,64,256]{4,3,2,1,0:T(8,128)} %refs_1_.11, f32[6,3,32,64,256]{4,3,2,1,0:T(8,128)} %refs_1_.11, f32[6,3,32,64,256]{4,3,2,1,0:T(8,128)} %refs_1_.11, f32[6,3,32,64,256]{4,3,2,1,0:T(8,128)} %refs_1_.11, f32[6,3,32,64,256]{4,3,2,1,0:T(8,128)} %refs_1_.11, ...), custom_call_target="tpu_custom_call" | custom-call | flops 1024 | bytes 1024 | tf_op jit(solution)/shard_map/earlier_orders/pallas_call | solution.py:296
  35.9 6.4 %earlier_orders.5.refs_3_ = f32[3,8,64,256]{3,2,1,0:T(8,128)S(1)} custom-call(f32[6,3,32,64,256]{4,3,2,1,0:T(8,128)} %refs_1_.11, f32[6,3,32,64,256]{4,3,2,1,0:T(8,128)} %refs_1_.11, f32[6,3,32,64,256]{4,3,2,1,0:T(8,128)} %refs_1_.11, f32[6,3,32,64,256]{4,3,2,1,0:T(8,128)} %refs_1_.11, f32[6,3,32,64,256]{4,3,2,1,0:T(8,128)} %refs_1_.11, ...), custom_call_target="tpu_custom_call" | custom-call | flops 1024 | bytes 1024 | tf_op jit(solution)/shard_map/earlier_orders/pallas_call | solution.py:296
  46.3 4.5 %second_synth.4 = f32[4,4,240,128]{3,2,1,0:T(8,128)S(1)} custom-call(s32[3]{0:T(128)S(1)} %copy-done.51, f32[512,128]{1,0:T(8,128)S(1)} %copy-done.49, f32[512,128]{1,0:T(8,128)} %collective-permute-done.1.refs_1_, f32[512,128]{1,0:T(8,128)} %collective-permute-done.2.refs_2_, f32[512,128]{1,0:T(8,128)} %collective-permute-done.3.refs_3_, ...), custom_call_target="tpu_custom_call" | custom-call | flops 1024 | bytes 1024 | tf_op jit(solution)/shard_map/second_synth/pallas_call | solution.py:246
  55.7 5.1 %collective-permute-start.4 = (f32[512,128]{1,0:T(8,128)}, f32[512,128]{1,0:T(8,128)S(1)}, u32[]{:S(2)}, u32[]{:S(2)}) collective-permute-start(f32[512,128]{1,0:T(8,128)} %copy-done.57), channel_id=1, source_target_pairs={{0,8},{4,12},{8,0},{12,4},{16,24},{20,28},{24,16},{28,20},{1,9},{5... | collective-permute-start | bytes 786440 | tf_op jit(solution)/shard_map/ppermute | solution.py:624
  63.3 6.4 %earlier_orders.6.refs_3_ = f32[3,8,64,256]{3,2,1,0:T(8,128)S(1)} custom-call(f32[6,3,32,64,256]{4,3,2,1,0:T(8,128)} %refs_1_.11, f32[6,3,32,64,256]{4,3,2,1,0:T(8,128)} %refs_1_.11, f32[6,3,32,64,256]{4,3,2,1,0:T(8,128)} %refs_1_.11, f32[6,3,32,64,256]{4,3,2,1,0:T(8,128)} %refs_1_.11, f32[6,3,32,64,256]{4,3,2,1,0:T(8,128)} %refs_1_.11, ...), custom_call_target="tpu_custom_call" | custom-call | flops 1024 | bytes 1024 | tf_op jit(solution)/shard_map/earlier_orders/pallas_call | solution.py:296
  70.9 11.5 %collective-permute-done.5.refs_2_ = f32[512,128]{1,0:T(8,128)S(1)} collective-permute-done((f32[512,128]{1,0:T(8,128)}, f32[512,128]{1,0:T(8,128)S(1)}, u32[]{:S(2)}, u32[]{:S(2)}) %collective-permute-start.5) | collective-permute-done | bytes 262176 | tf_op jit(solution)/shard_map/ppermute | solution.py:624
  82.4 3.9 %second_synth.5 = f32[4,4,240,128]{3,2,1,0:T(8,128)S(1)} custom-call(s32[3]{0:T(128)S(1)} %copy-done.51, f32[512,128]{1,0:T(8,128)S(1)} %copy-done.47, f32[512,128]{1,0:T(8,128)S(1)} %collective-permute-done.4.refs_1_, f32[512,128]{1,0:T(8,128)S(1)} %collective-permute-done.5.refs_2_, f32[512,128]{1,0:T(8,128)S(1)} %collective-permute-done.6.refs_3_, ...), custom_call_target="tpu_custom_call" | custom-call | flops 1024 | bytes 1024 | tf_op jit(solution)/shard_map/second_synth/pallas_call | solution.py:246
  88.8 4.2 %all-to-all-start.2 = ((f32[4,4,240,128]{3,2,1,0:T(8,128)}), f32[4,4,240,128]{3,2,1,0:T(8,128)S(1)}, u32[]{:S(2)}, u32[]{:S(2)}) async-start(f32[4,4,240,128]{3,2,1,0:T(8,128)} %copy-done.3), calls=%async_computation.2 | async-start | bytes 3932160 | tf_op jit(solution)/shard_map/all_to_all | solution.py:599
  97.0 6.2 %third_dimension.4 = f32[4,4,120,128]{3,2,1,0:T(8,128)S(1)} custom-call(s32[3]{0:T(128)S(1)} %copy-done.51, f32[4,4,240,128]{3,2,1,0:T(8,128)S(1)} %copy-done.1, f32[6,3,32,64,256]{4,3,2,1,0:T(8,128)} %refs_1_.11, f32[6,3,32,64,256]{4,3,2,1,0:T(8,128)} %refs_2_.11, f32[3,8,64,256]{3,2,1,0:T(8,128)S(1)} %copy-done.12, ...), custom_call_target="tpu_custom_call" | custom-call | flops 1024 | bytes 1024 | tf_op jit(solution)/shard_map/third_dimension/pallas_call | solution.py:367
  104.2 7.6 %all-to-all-done.2.refs_0_ = f32[4,4,240,128]{3,2,1,0:T(8,128)S(1)} async-done(((f32[4,4,240,128]{3,2,1,0:T(8,128)}), f32[4,4,240,128]{3,2,1,0:T(8,128)S(1)}, u32[]{:S(2)}, u32[]{:S(2)}) %all-to-all-start.2) | async-done | bytes 1966112 | tf_op jit(solution)/shard_map/all_to_all | solution.py:599
  111.9 4.2 %all-to-all-start.1 = ((f32[4,4,120,128]{3,2,1,0:T(8,128)}), f32[4,4,120,128]{3,2,1,0:T(8,128)}, u32[]{:S(2)}, u32[]{:S(2)}) async-start(f32[4,4,120,128]{3,2,1,0:T(8,128)} %copy-done.15), calls=%async_computation.1 | async-start | bytes 1966080 | tf_op jit(solution)/shard_map/all_to_all | solution.py:599
  116.1 6.3 %collective-permute-start.7 = (f32[512,128]{1,0:T(8,128)}, f32[512,128]{1,0:T(8,128)S(1)}, u32[]{:S(2)}, u32[]{:S(2)}) collective-permute-start(f32[512,128]{1,0:T(8,128)} %copy-done.54), channel_id=1, source_target_pairs={{0,8},{4,12},{8,0},{12,4},{16,24},{20,28},{24,16},{28,20},{1,9},{5... | collective-permute-start | bytes 786440 | tf_op jit(solution)/shard_map/ppermute | solution.py:624
  124.9 6.4 %earlier_orders.7.refs_3_ = f32[3,8,64,256]{3,2,1,0:T(8,128)S(1)} custom-call(f32[6,3,32,64,256]{4,3,2,1,0:T(8,128)} %refs_1_.11, f32[6,3,32,64,256]{4,3,2,1,0:T(8,128)} %refs_1_.11, f32[6,3,32,64,256]{4,3,2,1,0:T(8,128)} %refs_1_.11, f32[6,3,32,64,256]{4,3,2,1,0:T(8,128)} %refs_1_.11, f32[6,3,32,64,256]{4,3,2,1,0:T(8,128)} %refs_1_.11, ...), custom_call_target="tpu_custom_call" | custom-call | flops 1024 | bytes 1024 | tf_op jit(solution)/shard_map/earlier_orders/pallas_call | solution.py:296
  132.5 11.5 %collective-permute-done.8.refs_2_ = f32[512,128]{1,0:T(8,128)S(1)} collective-permute-done((f32[512,128]{1,0:T(8,128)}, f32[512,128]{1,0:T(8,128)S(1)}, u32[]{:S(2)}, u32[]{:S(2)}) %collective-permute-start.8) | collective-permute-done | bytes 262176 | tf_op jit(solution)/shard_map/ppermute | solution.py:624
  144.0 5.2 %second_synth.6 = f32[4,4,240,128]{3,2,1,0:T(8,128)} custom-call(s32[3]{0:T(128)S(1)} %copy-done.51, f32[512,128]{1,0:T(8,128)S(1)} %get-tuple-element.126.refs_0_, f32[512,128]{1,0:T(8,128)S(1)} %collective-permute-done.7.refs_1_, f32[512,128]{1,0:T(8,128)S(1)} %collective-permute-done.8.refs_2_, f32[512,128]{1,0:T(8,128)S(1)} %collective-permute-done.9.refs_3_, ...), custom_call_target="tpu_custom_call" | custom-call | flops 1024 | bytes 1024 | tf_op jit(solution)/shard_map/second_synth/pallas_call | solution.py:246
  149.2 6.2 %third_dimension.5 = f32[4,4,120,128]{3,2,1,0:T(8,128)S(1)} custom-call(s32[3]{0:T(128)S(1)} %copy-done.51, f32[4,4,240,128]{3,2,1,0:T(8,128)S(1)} %all-to-all-done.2.refs_0_, f32[6,3,32,64,256]{4,3,2,1,0:T(8,128)} %refs_1_.11, f32[6,3,32,64,256]{4,3,2,1,0:T(8,128)} %refs_2_.11, f32[3,8,64,256]{3,2,1,0:T(8,128)S(1)} %copy-done.8, ...), custom_call_target="tpu_custom_call" | custom-call | flops 1024 | bytes 1024 | tf_op jit(solution)/shard_map/third_dimension/pallas_call | solution.py:367
  156.4 14.1 %all_to_all.40.c_ref = f32[4,4,120,128]{3,2,1,0:T(8,128)} all-to-all(f32[4,4,120,128]{3,2,1,0:T(8,128)} %copy-done.17), channel_id=1, replica_groups=mesh['row'=8,'col'=4] {'col'}, dimensions={0} | all-to-all | bytes 1966080 | tf_op jit(solution)/shard_map/all_to_all | solution.py:599
  174.1 6.1 %collective-permute-start.10 = (f32[512,128]{1,0:T(8,128)}, f32[512,128]{1,0:T(8,128)S(1)}, u32[]{:S(2)}, u32[]{:S(2)}) collective-permute-start(f32[512,128]{1,0:T(8,128)} %get-tuple-element.136), channel_id=1, source_target_pairs={{0,8},{4,12},{8,0},{12,4},{16,24},{20,28},{24,16},{28,20},{1,9},{5... | collective-permute-start | bytes 786440 | tf_op jit(solution)/shard_map/ppermute | solution.py:624
  187.3 12.5 %collective-permute-done.11.refs_2_ = f32[512,128]{1,0:T(8,128)S(1)} collective-permute-done((f32[512,128]{1,0:T(8,128)}, f32[512,128]{1,0:T(8,128)S(1)}, u32[]{:S(2)}, u32[]{:S(2)}) %collective-permute-start.11) | collective-permute-done | bytes 262176 | tf_op jit(solution)/shard_map/ppermute | solution.py:624
  199.8 3.9 %second_synth.7 = f32[4,4,240,128]{3,2,1,0:T(8,128)S(1)} custom-call(s32[3]{0:T(128)S(1)} %copy-done.51, f32[512,128]{1,0:T(8,128)S(1)} %get-tuple-element.146.refs_0_, f32[512,128]{1,0:T(8,128)S(1)} %collective-permute-done.10.refs_1_, f32[512,128]{1,0:T(8,128)S(1)} %collective-permute-done.11.refs_2_, f32[512,128]{1,0:T(8,128)S(1)} %collective-permute-done.12.refs_3_, ...), custom_call_target="tpu_custom_call" | custom-call | flops 1024 | bytes 1024 | tf_op jit(solution)/shard_map/second_synth/pallas_call | solution.py:246
  205.0 4.4 %all-to-all-start.6 = ((f32[4,4,240,128]{3,2,1,0:T(8,128)}), f32[4,4,240,128]{3,2,1,0:T(8,128)}, u32[]{:S(2)}, u32[]{:S(2)}) async-start(f32[4,4,240,128]{3,2,1,0:T(8,128)} %copy-done.4), calls=%async_computation.6 | async-start | bytes 3932160 | tf_op jit(solution)/shard_map/all_to_all | solution.py:599
  210.8 6.2 %third_dimension.6 = f32[4,4,120,128]{3,2,1,0:T(8,128)S(1)} custom-call(s32[3]{0:T(128)S(1)} %copy-done.51, f32[4,4,240,128]{3,2,1,0:T(8,128)S(1)} %all-to-all-done.4.refs_0_, f32[6,3,32,64,256]{4,3,2,1,0:T(8,128)} %refs_1_.11, f32[6,3,32,64,256]{4,3,2,1,0:T(8,128)} %refs_2_.11, f32[3,8,64,256]{3,2,1,0:T(8,128)S(1)} %copy-done.6, ...), custom_call_target="tpu_custom_call" | custom-call | flops 1024 | bytes 1024 | tf_op jit(solution)/shard_map/third_dimension/pallas_call | solution.py:367
  218.0 7.6 %all-to-all-done.6.refs_0_ = f32[4,4,240,128]{3,2,1,0:T(8,128)} async-done(((f32[4,4,240,128]{3,2,1,0:T(8,128)}), f32[4,4,240,128]{3,2,1,0:T(8,128)}, u32[]{:S(2)}, u32[]{:S(2)}) %all-to-all-start.6) | async-done | bytes 1966112 | tf_op jit(solution)/shard_map/all_to_all | solution.py:599
  234.9 7.2 %third_dimension.7 = f32[4,4,120,128]{3,2,1,0:T(8,128)S(1)} custom-call(s32[3]{0:T(128)S(1)} %copy-done.51, f32[4,4,240,128]{3,2,1,0:T(8,128)} %all-to-all-done.6.refs_0_, f32[6,3,32,64,256]{4,3,2,1,0:T(8,128)} %refs_1_.11, f32[6,3,32,64,256]{4,3,2,1,0:T(8,128)} %refs_2_.11, f32[3,8,64,256]{3,2,1,0:T(8,128)S(1)} %copy-done.10, ...), custom_call_target="tpu_custom_call" | custom-call | flops 1024 | bytes 1024 | tf_op jit(solution)/shard_map/third_dimension/pallas_call | solution.py:367
  243.1 4.1 %all-to-all-start.7 = ((f32[4,4,120,128]{3,2,1,0:T(8,128)}), f32[4,4,120,128]{3,2,1,0:T(8,128)S(1)}, u32[]{:S(2)}, u32[]{:S(2)}) async-start(f32[4,4,120,128]{3,2,1,0:T(8,128)} %copy-done.14), calls=%async_computation.7 | async-start | bytes 1966080 | tf_op jit(solution)/shard_map/all_to_all | solution.py:599
  248.7 8.4 %collective-permute-start.14 = (f32[304,128]{1,0:T(8,128)}, f32[304,128]{1,0:T(8,128)S(1)}, u32[]{:S(2)}, u32[]{:S(2)}) collective-permute-start(f32[304,128]{1,0:T(8,128)} %get-tuple-element.143), channel_id=1, source_target_pairs={{0,16},{4,20},{8,24},{12,28},{16,0},{20,4},{24,8},{28,12},{1,17},{... | collective-permute-start | bytes 466952 | tf_op jit(solution)/shard_map/ppermute | solution.py:624
  257.6 9.1 %collective-permute-done.14.refs_2_ = f32[304,128]{1,0:T(8,128)S(1)} collective-permute-done((f32[304,128]{1,0:T(8,128)}, f32[304,128]{1,0:T(8,128)S(1)}, u32[]{:S(2)}, u32[]{:S(2)}) %collective-permute-start.14) | collective-permute-done | bytes 155680 | tf_op jit(solution)/shard_map/ppermute | solution.py:624
  275.7 5.4 %collective-permute-done.17.refs_6_ = f32[304,128]{1,0:T(8,128)S(1)} collective-permute-done((f32[304,128]{1,0:T(8,128)}, f32[304,128]{1,0:T(8,128)S(1)}, u32[]{:S(2)}, u32[]{:S(2)}) %collective-permute-start.17) | collective-permute-done | bytes 155680 | tf_op jit(solution)/shard_map/ppermute | solution.py:624
  289.3 7.3 %collective-permute-done.20.refs_10_ = f32[304,128]{1,0:T(8,128)S(1)} collective-permute-done((f32[304,128]{1,0:T(8,128)}, f32[304,128]{1,0:T(8,128)S(1)}, u32[]{:S(2)}, u32[]{:S(2)}) %collective-permute-start.20) | collective-permute-done | bytes 155680 | tf_op jit(solution)/shard_map/ppermute | solution.py:624
  303.4 8.8 %collective-permute-done.23.refs_14_ = f32[304,128]{1,0:T(8,128)S(1)} collective-permute-done((f32[304,128]{1,0:T(8,128)S(1)}, f32[304,128]{1,0:T(8,128)S(1)}, u32[]{:S(2)}, u32[]{:S(2)}) %collective-permute-start.23) | collective-permute-done | bytes 155680 | tf_op jit(solution)/shard_map/ppermute | solution.py:624
  328.8 6.2 %last_projection.1 = f32[3,20,40,160]{3,2,1,0:T(8,128)} custom-call(f32[10]{0:T(128)S(1)} %convert_multiply_fusion.1.refs_0_, f32[160,2432]{1,0:T(8,128)S(1)} %first_back.3.refs_1_, f32[160,2432]{1,0:T(8,128)S(1)} %collective-permute-done.25.refs_2_, f32[8,256]{1,0:T(8,128)S(1)} %broadcast_in_dim.9.refs_3_, f32[40,256]{1,0:T(8,128)S(1)} %broadcast_in_dim.18.refs_4_), custom_call_target="tpu_custom_call" | custom-call | flops 1024 | bytes 1024 | tf_op jit(solution)/shard_map/last_projection/pallas_call | solution.py:512
  (190 shorter events, 111.8 us)
Async XLA Ops:
  21.7 21.8 %collective-permute-start.1 = (f32[512,128]{1,0:T(8,128)}, f32[512,128]{1,0:T(8,128)}, u32[]{:S(2)}, u32[]{:S(2)}) collective-permute-start(f32[512,128]{1,0:T(8,128)} %get-tuple-element.92), channel_id=1, source_target_pairs={{0,8},{4,12},{8,0},{12,4},{16,24},{20,28},{24,16},{28,20},{1,9},{5... | collective-permute-start | bytes 786440 | tf_op jit(solution)/shard_map/ppermute | solution.py:624
  24.6 21.6 %collective-permute-start.2 = (f32[512,128]{1,0:T(8,128)}, f32[512,128]{1,0:T(8,128)}, u32[]{:S(2)}, u32[]{:S(2)}) collective-permute-start(f32[512,128]{1,0:T(8,128)} %get-tuple-element.93), channel_id=1, source_target_pairs={{0,16},{4,20},{8,24},{12,28},{16,0},{20,4},{24,8},{28,12},{1,17},{... | collective-permute-start | bytes 786440 | tf_op jit(solution)/shard_map/ppermute | solution.py:624
  27.2 19.1 %collective-permute-start.3 = (f32[512,128]{1,0:T(8,128)}, f32[512,128]{1,0:T(8,128)}, u32[]{:S(2)}, u32[]{:S(2)}) collective-permute-start(f32[512,128]{1,0:T(8,128)} %get-tuple-element.94), channel_id=1, source_target_pairs={{0,24},{4,28},{8,16},{12,20},{16,8},{20,12},{24,0},{28,4},{1,25},{... | collective-permute-start | bytes 786440 | tf_op jit(solution)/shard_map/ppermute | solution.py:624
  52.0 35.6 %all-to-all-start = ((f32[4,4,240,128]{3,2,1,0:T(8,128)}), f32[4,4,240,128]{3,2,1,0:T(8,128)S(1)}, u32[]{:S(2)}, u32[]{:S(2)}) async-start(f32[4,4,240,128]{3,2,1,0:T(8,128)} %copy-done.2), calls=%async_computation | async-start | bytes 3932160 | tf_op jit(solution)/shard_map/all_to_all | solution.py:599
  55.7 15.2 %collective-permute-start.4 = (f32[512,128]{1,0:T(8,128)}, f32[512,128]{1,0:T(8,128)S(1)}, u32[]{:S(2)}, u32[]{:S(2)}) collective-permute-start(f32[512,128]{1,0:T(8,128)} %copy-done.57), channel_id=1, source_target_pairs={{0,8},{4,12},{8,0},{12,4},{16,24},{20,28},{24,16},{28,20},{1,9},{5... | collective-permute-start | bytes 786440 | tf_op jit(solution)/shard_map/ppermute | solution.py:624
  60.8 21.6 %collective-permute-start.5 = (f32[512,128]{1,0:T(8,128)}, f32[512,128]{1,0:T(8,128)S(1)}, u32[]{:S(2)}, u32[]{:S(2)}) collective-permute-start(f32[512,128]{1,0:T(8,128)} %copy-done.56), channel_id=1, source_target_pairs={{0,16},{4,20},{8,24},{12,28},{16,0},{20,4},{24,8},{28,12},{1,17},{... | collective-permute-start | bytes 786440 | tf_op jit(solution)/shard_map/ppermute | solution.py:624
  61.9 20.5 %collective-permute-start.6 = (f32[512,128]{1,0:T(8,128)}, f32[512,128]{1,0:T(8,128)S(1)}, u32[]{:S(2)}, u32[]{:S(2)}) collective-permute-start(f32[512,128]{1,0:T(8,128)} %copy-done.55), channel_id=1, source_target_pairs={{0,24},{4,28},{8,16},{12,20},{16,8},{20,12},{24,0},{28,4},{1,25},{... | collective-permute-start | bytes 786440 | tf_op jit(solution)/shard_map/ppermute | solution.py:624
  88.8 23.0 %all-to-all-start.2 = ((f32[4,4,240,128]{3,2,1,0:T(8,128)}), f32[4,4,240,128]{3,2,1,0:T(8,128)S(1)}, u32[]{:S(2)}, u32[]{:S(2)}) async-start(f32[4,4,240,128]{3,2,1,0:T(8,128)} %copy-done.3), calls=%async_computation.2 | async-start | bytes 3932160 | tf_op jit(solution)/shard_map/all_to_all | solution.py:599
  111.9 44.5 %all-to-all-start.1 = ((f32[4,4,120,128]{3,2,1,0:T(8,128)}), f32[4,4,120,128]{3,2,1,0:T(8,128)}, u32[]{:S(2)}, u32[]{:S(2)}) async-start(f32[4,4,120,128]{3,2,1,0:T(8,128)} %copy-done.15), calls=%async_computation.1 | async-start | bytes 1966080 | tf_op jit(solution)/shard_map/all_to_all | solution.py:599
  116.1 16.4 %collective-permute-start.7 = (f32[512,128]{1,0:T(8,128)}, f32[512,128]{1,0:T(8,128)S(1)}, u32[]{:S(2)}, u32[]{:S(2)}) collective-permute-start(f32[512,128]{1,0:T(8,128)} %copy-done.54), channel_id=1, source_target_pairs={{0,8},{4,12},{8,0},{12,4},{16,24},{20,28},{24,16},{28,20},{1,9},{5... | collective-permute-start | bytes 786440 | tf_op jit(solution)/shard_map/ppermute | solution.py:624
  122.4 21.6 %collective-permute-start.8 = (f32[512,128]{1,0:T(8,128)}, f32[512,128]{1,0:T(8,128)S(1)}, u32[]{:S(2)}, u32[]{:S(2)}) collective-permute-start(f32[512,128]{1,0:T(8,128)} %copy-done.53), channel_id=1, source_target_pairs={{0,16},{4,20},{8,24},{12,28},{16,0},{20,4},{24,8},{28,12},{1,17},{... | collective-permute-start | bytes 786440 | tf_op jit(solution)/shard_map/ppermute | solution.py:624
  123.4 20.6 %collective-permute-start.9 = (f32[512,128]{1,0:T(8,128)}, f32[512,128]{1,0:T(8,128)S(1)}, u32[]{:S(2)}, u32[]{:S(2)}) collective-permute-start(f32[512,128]{1,0:T(8,128)} %copy-done.52), channel_id=1, source_target_pairs={{0,24},{4,28},{8,16},{12,20},{16,8},{20,12},{24,0},{28,4},{1,25},{... | collective-permute-start | bytes 786440 | tf_op jit(solution)/shard_map/ppermute | solution.py:624
  170.5 34.5 %all-to-all-start.4 = ((f32[4,4,240,128]{3,2,1,0:T(8,128)}), f32[4,4,240,128]{3,2,1,0:T(8,128)S(1)}, u32[]{:S(2)}, u32[]{:S(2)}) async-start(f32[4,4,240,128]{3,2,1,0:T(8,128)} %second_synth.6), calls=%async_computation.4 | async-start | bytes 3932160 | tf_op jit(solution)/shard_map/all_to_all | solution.py:599
  174.1 13.2 %collective-permute-start.10 = (f32[512,128]{1,0:T(8,128)}, f32[512,128]{1,0:T(8,128)S(1)}, u32[]{:S(2)}, u32[]{:S(2)}) collective-permute-start(f32[512,128]{1,0:T(8,128)} %get-tuple-element.136), channel_id=1, source_target_pairs={{0,8},{4,12},{8,0},{12,4},{16,24},{20,28},{24,16},{28,20},{1,9},{5... | collective-permute-start | bytes 786440 | tf_op jit(solution)/shard_map/ppermute | solution.py:624
  180.2 19.6 %collective-permute-start.11 = (f32[512,128]{1,0:T(8,128)}, f32[512,128]{1,0:T(8,128)S(1)}, u32[]{:S(2)}, u32[]{:S(2)}) collective-permute-start(f32[512,128]{1,0:T(8,128)} %get-tuple-element.138), channel_id=1, source_target_pairs={{0,16},{4,20},{8,24},{12,28},{16,0},{20,4},{24,8},{28,12},{1,17},{... | collective-permute-start | bytes 786440 | tf_op jit(solution)/shard_map/ppermute | solution.py:624
  181.1 18.6 %collective-permute-start.12 = (f32[512,128]{1,0:T(8,128)}, f32[512,128]{1,0:T(8,128)S(1)}, u32[]{:S(2)}, u32[]{:S(2)}) collective-permute-start(f32[512,128]{1,0:T(8,128)} %get-tuple-element.140), channel_id=1, source_target_pairs={{0,24},{4,28},{8,16},{12,20},{16,8},{20,12},{24,0},{28,4},{1,25},{... | collective-permute-start | bytes 786440 | tf_op jit(solution)/shard_map/ppermute | solution.py:624
  205.0 20.6 %all-to-all-start.6 = ((f32[4,4,240,128]{3,2,1,0:T(8,128)}), f32[4,4,240,128]{3,2,1,0:T(8,128)}, u32[]{:S(2)}, u32[]{:S(2)}) async-start(f32[4,4,240,128]{3,2,1,0:T(8,128)} %copy-done.4), calls=%async_computation.6 | async-start | bytes 3932160 | tf_op jit(solution)/shard_map/all_to_all | solution.py:599
  225.6 17.5 %all-to-all-start.5 = ((f32[4,4,120,128]{3,2,1,0:T(8,128)}), f32[4,4,120,128]{3,2,1,0:T(8,128)S(1)}, u32[]{:S(2)}, u32[]{:S(2)}) async-start(f32[4,4,120,128]{3,2,1,0:T(8,128)} %copy-done.16), calls=%async_computation.5 | async-start | bytes 1966080 | tf_op jit(solution)/shard_map/all_to_all | solution.py:599
  243.1 43.8 %all-to-all-start.7 = ((f32[4,4,120,128]{3,2,1,0:T(8,128)}), f32[4,4,120,128]{3,2,1,0:T(8,128)S(1)}, u32[]{:S(2)}, u32[]{:S(2)}) async-start(f32[4,4,120,128]{3,2,1,0:T(8,128)} %copy-done.14), calls=%async_computation.7 | async-start | bytes 1966080 | tf_op jit(solution)/shard_map/all_to_all | solution.py:599
  247.2 10.4 %collective-permute-start.15 = (f32[304,128]{1,0:T(8,128)}, f32[304,128]{1,0:T(8,128)S(1)}, u32[]{:S(2)}, u32[]{:S(2)}) collective-permute-start(f32[304,128]{1,0:T(8,128)} %get-tuple-element.145), channel_id=1, source_target_pairs={{0,24},{4,28},{8,16},{12,20},{16,8},{20,12},{24,0},{28,4},{1,25},{... | collective-permute-start | bytes 466952 | tf_op jit(solution)/shard_map/ppermute | solution.py:624
  248.7 18.0 %collective-permute-start.14 = (f32[304,128]{1,0:T(8,128)}, f32[304,128]{1,0:T(8,128)S(1)}, u32[]{:S(2)}, u32[]{:S(2)}) collective-permute-start(f32[304,128]{1,0:T(8,128)} %get-tuple-element.143), channel_id=1, source_target_pairs={{0,16},{4,20},{8,24},{12,28},{16,0},{20,4},{24,8},{28,12},{1,17},{... | collective-permute-start | bytes 466952 | tf_op jit(solution)/shard_map/ppermute | solution.py:624
  257.1 9.6 %collective-permute-start.13 = (f32[304,128]{1,0:T(8,128)S(1)}, f32[304,128]{1,0:T(8,128)S(1)}, u32[]{:S(2)}, u32[]{:S(2)}) collective-permute-start(f32[304,128]{1,0:T(8,128)S(1)} %copy-done.59), channel_id=1, source_target_pairs={{0,8},{4,12},{8,0},{12,4},{16,24},{20,28},{24,16},{28,20},{1,9},{5... | collective-permute-start | bytes 466952 | tf_op jit(solution)/shard_map/ppermute | solution.py:624
  266.7 9.0 %collective-permute-start.18 = (f32[304,128]{1,0:T(8,128)}, f32[304,128]{1,0:T(8,128)S(1)}, u32[]{:S(2)}, u32[]{:S(2)}) collective-permute-start(f32[304,128]{1,0:T(8,128)} %copy-done.62), channel_id=1, source_target_pairs={{0,24},{4,28},{8,16},{12,20},{16,8},{20,12},{24,0},{28,4},{1,25},{... | collective-permute-start | bytes 466952 | tf_op jit(solution)/shard_map/ppermute | solution.py:624
  269.6 11.5 %collective-permute-start.17 = (f32[304,128]{1,0:T(8,128)}, f32[304,128]{1,0:T(8,128)S(1)}, u32[]{:S(2)}, u32[]{:S(2)}) collective-permute-start(f32[304,128]{1,0:T(8,128)} %copy-done.61), channel_id=1, source_target_pairs={{0,16},{4,20},{8,24},{12,28},{16,0},{20,4},{24,8},{28,12},{1,17},{... | collective-permute-start | bytes 466952 | tf_op jit(solution)/shard_map/ppermute | solution.py:624
  269.6 12.2 %collective-permute-start.16 = (f32[304,128]{1,0:T(8,128)}, f32[304,128]{1,0:T(8,128)S(1)}, u32[]{:S(2)}, u32[]{:S(2)}) collective-permute-start(f32[304,128]{1,0:T(8,128)} %copy-done.60), channel_id=1, source_target_pairs={{0,8},{4,12},{8,0},{12,4},{16,24},{20,28},{24,16},{28,20},{1,9},{5... | collective-permute-start | bytes 466952 | tf_op jit(solution)/shard_map/ppermute | solution.py:624
  282.5 6.8 %collective-permute-start.19 = (f32[304,128]{1,0:T(8,128)}, f32[304,128]{1,0:T(8,128)S(1)}, u32[]{:S(2)}, u32[]{:S(2)}) collective-permute-start(f32[304,128]{1,0:T(8,128)} %get-tuple-element.163), channel_id=1, source_target_pairs={{0,8},{4,12},{8,0},{12,4},{16,24},{20,28},{24,16},{28,20},{1,9},{5... | collective-permute-start | bytes 466952 | tf_op jit(solution)/shard_map/ppermute | solution.py:624
  282.5 14.2 %collective-permute-start.20 = (f32[304,128]{1,0:T(8,128)}, f32[304,128]{1,0:T(8,128)S(1)}, u32[]{:S(2)}, u32[]{:S(2)}) collective-permute-start(f32[304,128]{1,0:T(8,128)} %get-tuple-element.165), channel_id=1, source_target_pairs={{0,16},{4,20},{8,24},{12,28},{16,0},{20,4},{24,8},{28,12},{1,17},{... | collective-permute-start | bytes 466952 | tf_op jit(solution)/shard_map/ppermute | solution.py:624
  284.6 12.1 %collective-permute-start.21 = (f32[304,128]{1,0:T(8,128)}, f32[304,128]{1,0:T(8,128)S(1)}, u32[]{:S(2)}, u32[]{:S(2)}) collective-permute-start(f32[304,128]{1,0:T(8,128)} %get-tuple-element.167), channel_id=1, source_target_pairs={{0,24},{4,28},{8,16},{12,20},{16,8},{20,12},{24,0},{28,4},{1,25},{... | collective-permute-start | bytes 466952 | tf_op jit(solution)/shard_map/ppermute | solution.py:624
  296.7 6.7 %collective-permute-start.22 = (f32[304,128]{1,0:T(8,128)S(1)}, f32[304,128]{1,0:T(8,128)S(1)}, u32[]{:S(2)}, u32[]{:S(2)}) collective-permute-start(f32[304,128]{1,0:T(8,128)S(1)} %get-tuple-element.171), channel_id=1, source_target_pairs={{0,8},{4,12},{8,0},{12,4},{16,24},{20,28},{24,16},{28,20},{1,9},{5... | collective-permute-start | bytes 466952 | tf_op jit(solution)/shard_map/ppermute | solution.py:624
  298.9 13.2 %collective-permute-start.23 = (f32[304,128]{1,0:T(8,128)S(1)}, f32[304,128]{1,0:T(8,128)S(1)}, u32[]{:S(2)}, u32[]{:S(2)}) collective-permute-start(f32[304,128]{1,0:T(8,128)S(1)} %get-tuple-element.173), channel_id=1, source_target_pairs={{0,16},{4,20},{8,24},{12,28},{16,0},{20,4},{24,8},{28,12},{1,17},{... | collective-permute-start | bytes 466952 | tf_op jit(solution)/shard_map/ppermute | solution.py:624
  299.8 12.3 %collective-permute-start.24 = (f32[304,128]{1,0:T(8,128)S(1)}, f32[304,128]{1,0:T(8,128)S(1)}, u32[]{:S(2)}, u32[]{:S(2)}) collective-permute-start(f32[304,128]{1,0:T(8,128)S(1)} %get-tuple-element.175), channel_id=1, source_target_pairs={{0,24},{4,28},{8,16},{12,20},{16,8},{20,12},{24,0},{28,4},{1,25},{... | collective-permute-start | bytes 466952 | tf_op jit(solution)/shard_map/ppermute | solution.py:624
  320.0 8.7 %collective-permute-start.25 = (f32[160,2432]{1,0:T(8,128)}, f32[160,2432]{1,0:T(8,128)S(1)}, u32[]{:S(2)}, u32[]{:S(2)}) collective-permute-start(f32[160,2432]{1,0:T(8,128)} %first_back.2), channel_id=1, source_target_pairs={{0,4},{4,0},{8,12},{12,8},{16,20},{20,16},{24,28},{28,24},{1,5},{5... | collective-permute-start | bytes 4669448 | tf_op jit(solution)/shard_map/ppermute | solution.py:602
  (64 other events, 458.6 us)

commit v5 on v4

--- a/solution.py
+++ b/solution.py
@@ -11,7 +11,7 @@
 from jax.sharding import PartitionSpec as P
 
 LANES = 128
-XC = 8
+XC = 16
 BF16 = jnp.bfloat16
 F32 = jnp.float32
 NN = (((1,), (0,)), ((), ()))
@@ -81,9 +81,11 @@
     return tiles
 
 
-VMEM_LIMIT = 24 * 1024 * 1024
+VMEM_LIMIT = 32 * 1024 * 1024
+VMEM_MOST = 60 * 1024 * 1024
 SHORT = pl.CostEstimate(flops=1024, bytes_accessed=1024, transcendentals=0)
-HBM = pl.BlockSpec(memory_space=pl.ANY)
+ANY = pl.BlockSpec(memory_space=pl.ANY)
+HBM = pl.BlockSpec(memory_space=pltpu.HBM)
 SMEM = pl.BlockSpec(memory_space=pltpu.SMEM)
 VMEM = pl.BlockSpec(memory_space=pltpu.VMEM)
 
@@ -92,8 +94,14 @@
     return pltpu.CompilerParams(dimension_semantics=("arbitrary",), vmem_limit_bytes=VMEM_LIMIT)
 
 
-def still():
-    return pltpu.CompilerParams(vmem_limit_bytes=VMEM_LIMIT)
+def still(limit=VMEM_LIMIT):
+    return pltpu.CompilerParams(vmem_limit_bytes=limit)
+
+
+def finish(held, out_refs, sem):
+    for at in range(held.shape[1]):
+        for k, out in enumerate(out_refs):
+            pltpu.make_async_copy(held.at[k, at], out.at[at], sem.at[k, at]).wait()
 
 
 def both_passes(values, high_low, high):
@@ -111,7 +119,7 @@
 def first_synth_kernel(dims, place_ref, own_ref, other_ref, table_ref, *rest):
     chunks, dests, xc = dims
     outs = rest[: chunks * dests]
-    own_data, other_data, rows, sem = rest[chunks * dests :]
+    own_data, other_data, rows, held, sem, out_sem = rest[chunks * dests :]
     _, ky_len, kz_len, _ = own_data.shape
     group = 5 * kz_len
     half = rows.shape[0] // 2
@@ -159,11 +167,16 @@
 
     def flip(tile, carry):
         found = rows[pl.ds(pl.multiple_of(tile * LANES, LANES), LANES), :].T
-        for idx, out in enumerate(outs):
-            out[pl.ds(pl.multiple_of(tile * xc, 8), xc), :] = found[idx * xc : (idx + 1) * xc]
+        for idx in range(chunks * dests):
+            held[idx, pl.ds(pl.multiple_of(tile * xc, 8), xc), :] = found[idx * xc : (idx + 1) * xc]
         return carry
 
     lax.fori_loop(0, 2 * half // LANES, flip, 0, unroll=2)
+    copies = [pltpu.make_async_copy(held.at[k], out, out_sem.at[k]) for k, out in enumerate(outs)]
+    for copy in copies:
+        copy.start()
+    for copy in copies:
+        copy.wait()
 
 
 def first_synth(place, own, other, table, dims, lanes):
@@ -171,16 +184,18 @@
     out = jax.ShapeDtypeStruct((2 * lanes // LANES * xc, LANES), F32)
     found = pl.pallas_call(
         functools.partial(first_synth_kernel, dims),
-        in_specs=[SMEM, HBM, HBM, VMEM],
-        out_specs=[VMEM] * (chunks * dests),
+        in_specs=[SMEM, ANY, ANY, VMEM],
+        out_specs=[HBM] * (chunks * dests),
         out_shape=[out] * (chunks * dests),
         scratch_shapes=[
             pltpu.VMEM(own.shape, F32),
             pltpu.VMEM(own.shape, F32),
             pltpu.VMEM((2 * lanes, LANES), F32),
+            pltpu.VMEM((chunks * dests, *out.shape), F32),
             pltpu.SemaphoreType.DMA((2, 3)),
+            pltpu.SemaphoreType.DMA((chunks * dests,)),
         ],
-        compiler_params=still(),
+        compiler_params=still(VMEM_MOST),
         cost_estimate=SHORT,
         name="first_synth",
     )(place, own, other, table)
@@ -190,7 +205,8 @@
 def second_synth_kernel(dims, place_ref, *refs):
     rows, xc, ky_len, kz_len, cols, y_len, pack = dims
     groups = rows // 2
-    parts, table_ref, out_ref, a_ref = refs[:groups], refs[groups], refs[groups + 1], refs[groups + 2]
+    parts, table_ref, out_refs = refs[:groups], refs[groups], refs[groups + 1 : -3]
+    a_ref, held, sem = refs[-3:]
     size = a_ref.shape[0] // groups
     for k, part in enumerate(parts):
         a_ref[pl.ds(pl.multiple_of((place_ref[0] ^ k) * size, 8), size), :] = part[...]
@@ -232,12 +248,14 @@
             )
         for dest in range(cols):
             tile, off = divmod(dest * y_len, LANES)
-            out_ref[place_ref[2] ^ dest, at] = lane_pack(
+            held[dest, at] = lane_pack(
                 [f[:, tile * LANES : (tile + 1) * LANES] for f in fields], y_len, off
             )[0]
+            pltpu.make_async_copy(held.at[dest, at], out_refs[dest].at[at], sem.at[dest, at]).start()
         return carry
 
     lax.fori_loop(0, xc // pack, body, 0)
+    finish(held, out_refs, sem)
 
 
 def second_synth(place, arrived, table, dims):
@@ -246,9 +264,13 @@
     return pl.pallas_call(
         functools.partial(second_synth_kernel, dims),
         in_specs=[SMEM] + [VMEM] * (len(arrived) + 1),
-        out_specs=VMEM,
-        out_shape=jax.ShapeDtypeStruct((cols, packs, 6 * kz_len, LANES), F32),
-        scratch_shapes=[pltpu.VMEM((len(arrived) * arrived[0].shape[0], LANES), F32)],
+        out_specs=[HBM] * cols,
+        out_shape=[jax.ShapeDtypeStruct((packs, 6 * kz_len, LANES), F32)] * cols,
+        scratch_shapes=[
+            pltpu.VMEM((len(arrived) * arrived[0].shape[0], LANES), F32),
+            pltpu.VMEM((cols, packs, 6 * kz_len, LANES), F32),
+            pltpu.SemaphoreType.DMA((cols, packs)),
+        ],
         compiler_params=still(),
         cost_estimate=SHORT,
         name="second_synth",
@@ -307,8 +329,9 @@
 
 def third_kernel(dims, place_ref, *refs):
     chunk, kz_len, cols, y_len, pack = dims
-    b_ref, stored_refs = refs[0], refs[1:4]
-    table_ref, out_ref, data, sem = refs[4:]
+    b_refs, stored_refs, table_ref = refs[:cols], refs[cols : cols + 3], refs[cols + 3]
+    data, sem, held, out_sem = refs[-4:]
+    out_refs = refs[-4 - cols : -4]
     grid_len = table_ref.shape[2]
     xc = data.shape[2]
     packs = xc // pack
@@ -329,11 +352,7 @@
     def body(at, carry):
         def stack(field):
             return jnp.concatenate(
-                [
-                    b_ref[place_ref[2] ^ k, at, field * kz_len : (field + 1) * kz_len, :]
-                    for k in range(cols)
-                ],
-                axis=0,
+                [b_refs[k][at, field * kz_len : (field + 1) * kz_len, :] for k in range(cols)], axis=0
             ).T
 
         lines = jnp.concatenate([stack(field) for field in range(6)], axis=0)
@@ -352,36 +371,41 @@
         result = dot_data_right(table_ref[0], table_ref[1], jnp.concatenate(total, axis=0))
         for k in range(cols):
             for comp in range(3):
-                out_ref[place_ref[2] ^ k, at, comp * kz_len : (comp + 1) * kz_len, :] = result[
+                held[k, at, comp * kz_len : (comp + 1) * kz_len, :] = result[
                     k * kz_len : (k + 1) * kz_len, comp * LANES : (comp + 1) * LANES
                 ]
+            pltpu.make_async_copy(held.at[k, at], out_refs[k].at[at], out_sem.at[k, at]).start()
         return carry
 
     lax.fori_loop(0, packs, body, 0)
+    finish(held, out_refs, out_sem)
 
 
 def third(place, arrived, velocity, vorticity, base, table, chunk, dims):
     kz_len, cols, y_len, pack = dims
-    packs = arrived.shape[1]
+    packs = arrived[0].shape[0]
     grid_len = velocity.shape[-1]
     return pl.pallas_call(
         functools.partial(third_kernel, (chunk, *dims)),
-        in_specs=[SMEM, VMEM] + [HBM] * 3 + [VMEM],
-        out_specs=VMEM,
-        out_shape=jax.ShapeDtypeStruct((cols, packs, 3 * kz_len, LANES), F32),
+        in_specs=[SMEM] + [VMEM] * cols + [ANY] * 3 + [VMEM],
+        out_specs=[HBM] * cols,
+        out_shape=[jax.ShapeDtypeStruct((packs, 3 * kz_len, LANES), F32)] * cols,
         scratch_shapes=[
             pltpu.VMEM((3, 3, packs * pack, y_len, grid_len), F32),
             pltpu.SemaphoreType.DMA((3, packs)),
+            pltpu.VMEM((cols, packs, 3 * kz_len, LANES), F32),
+            pltpu.SemaphoreType.DMA((cols, packs)),
         ],
         compiler_params=still(),
         cost_estimate=SHORT,
         name="third_dimension",
-    )(place, arrived, velocity, vorticity, base, table)
-
-
-def second_back_kernel(dims, place_ref, c_ref, table_ref, *refs):
+    )(place, *arrived, velocity, vorticity, base, table)
+
+
+def second_back_kernel(dims, place_ref, *refs):
     rows, xc, ky_len, kz_len, cols, y_len, pack = dims
-    outs, all_ref = refs[:-1], refs[-1]
+    c_refs, table_ref, outs = refs[:cols], refs[cols], refs[cols + 1 : -2]
+    all_ref, sem = refs[-2:]
     width = 3 * kz_len
     high_pad = round_up(width, LANES)
 
@@ -389,7 +413,7 @@
         lines = []
         for part in range(pack):
             tiles = lane_pack(
-                [c_ref[place_ref[2] ^ k, at] for k in range(cols)], y_len, part * y_len
+                [c_ref[at] for c_ref in c_refs], y_len, part * y_len
             )
             lines.append(jnp.concatenate(tiles, axis=1))
             if high_pad > width:
@@ -405,8 +429,14 @@
 
     lax.fori_loop(0, xc // pack, body, 0)
     size = all_ref.shape[0] // len(outs)
+    copies = []
     for k, out in enumerate(outs):
-        out[...] = all_ref[pl.ds(pl.multiple_of((place_ref[0] ^ k) * size, 8), size), :]
+        spot = pl.multiple_of((place_ref[0] ^ k) * size, 8)
+        copies.append(pltpu.make_async_copy(all_ref.at[pl.ds(spot, size), :], out, sem.at[k]))
+    for copy in copies:
+        copy.start()
+    for copy in copies:
+        copy.wait()
 
 
 def second_back(place, arrived, table, dims):
@@ -415,38 +445,45 @@
     groups = rows // 2
     return pl.pallas_call(
         functools.partial(second_back_kernel, dims),
-        in_specs=[SMEM, VMEM, VMEM],
-        out_specs=[VMEM] * groups,
+        in_specs=[SMEM] + [VMEM] * (cols + 1),
+        out_specs=[HBM] * groups,
         out_shape=[jax.ShapeDtypeStruct((2 * size, LANES), F32)] * groups,
-        scratch_shapes=[pltpu.VMEM((rows * size, LANES), F32)],
+        scratch_shapes=[pltpu.VMEM((rows * size, LANES), F32), pltpu.SemaphoreType.DMA((groups,))],
         compiler_params=still(),
         cost_estimate=SHORT,
         name="second_back",
-    )(place, arrived, table)
+    )(place, *arrived, table)
 
 
 def first_back_kernel(dims, place_ref, *refs):
-    count, xc, own = dims
-    parts, table_ref, out_ref = refs[:count], refs[count], refs[count + 1]
-    size = parts[0].shape[0] // 2
-    core = place_ref[1] if own else 1 - place_ref[1]
-    for tile in range(size // xc):
-        spot = pl.ds(pl.multiple_of(core * size + tile * xc, 8), xc)
-        found = jnp.concatenate([part[spot, :] for part in parts], axis=0)
-        out_ref[:, tile * LANES : (tile + 1) * LANES] = dot_data_right(
-            table_ref[0], table_ref[1], found, NN
-        )
-
-
-def first_back(place, parts, table, xc, own):
+    count, xc = dims
+    parts, table_ref, outs = refs[:count], refs[count], refs[count + 1 : count + 3]
+    data, sem = refs[-2:]
+    copies = [pltpu.make_async_copy(part, data.at[k], sem.at[k]) for k, part in enumerate(parts)]
+    for copy in copies:
+        copy.start()
+    for copy in copies:
+        copy.wait()
+    size = data.shape[1] // 2
+    for out_ref, core in zip(outs, (1 - place_ref[1], place_ref[1])):
+        for tile in range(size // xc):
+            spot = pl.ds(pl.multiple_of(core * size + tile * xc, 8), xc)
+            found = jnp.concatenate([data[k, spot, :] for k in range(count)], axis=0)
+            out_ref[:, tile * LANES : (tile + 1) * LANES] = dot_data_right(
+                table_ref[0], table_ref[1], found, NN
+            )
+
+
+def first_back(place, parts, table, xc):
     count = len(parts)
-    size = parts[0].shape[0] // 2
+    size = parts[0].shape[0]
+    out = jax.ShapeDtypeStruct((table.shape[1], size // (2 * xc) * LANES), F32)
     return pl.pallas_call(
-        functools.partial(first_back_kernel, (count, xc, own)),
-        in_specs=[SMEM] + [VMEM] * (count + 1),
-        out_specs=VMEM,
-        out_shape=jax.ShapeDtypeStruct((table.shape[1], size // xc * LANES), F32),
-        compiler_params=still(),
+        functools.partial(first_back_kernel, (count, xc)),
+        in_specs=[SMEM] + [ANY] * count + [VMEM],
+        out_shape=[out, out],
+        scratch_shapes=[pltpu.VMEM((count, size, LANES), F32), pltpu.SemaphoreType.DMA((count,))],
+        compiler_params=still(VMEM_MOST),
         cost_estimate=SHORT,
         name="first_back",
     )(place, *parts, table)
@@ -595,8 +632,11 @@
     if kz_len > kz_own:
         coeffs = jnp.pad(coeffs, ((0, 0), (0, 0), (0, kz_len - kz_own), (0, 0)))
 
-    def col_swap(value):
-        return lax.all_to_all(value, "col", split_axis=0, concat_axis=0, tiled=True)
+    def exchange(values, axis, shift, size):
+        return [
+            lax.ppermute(value, axis, [(src, src ^ (k << shift)) for src in range(size)]) if k else value
+            for k, value in enumerate(values)
+        ]
 
     def core_swap(value):
         return lax.ppermute(value, "row", [(src, src ^ 1) for src in range(rows)])
@@ -626,31 +666,24 @@
 
     first, second, middle, back, base = {}, {}, {}, {}, {}
     first[0] = z_exchange(sent[0])
-    for chunk in range(min(2, chunks)):
+    for chunk in range(chunks):
         base[chunk] = run_earlier(chunk)
-    z_last = first[0]
-    for step in range(chunks + 2):
+    for step in range(chunks):
         if step + 1 < chunks:
-            z_last = first[step + 1] = z_exchange(sent[step + 1], z_last)
-        if step < chunks:
-            found = ordered(lambda values: second_synth(place, values, table_y, dims), first[step])
-            second[step] = col_swap(found)
-        at = step - 1
-        if 0 <= at < chunks:
-            found = ordered(
-                lambda values: third(place, values, *stored, base[at], table_z, at, dims[3:]),
-                second[at],
-            )
-            middle[at] = col_swap(found)
-        if step + 2 < chunks:
-            base[step + 2] = run_earlier(step + 2)
-        at = step - 2
-        if 0 <= at < chunks:
-            found = ordered(lambda values: second_back(place, values, table_y, dims), middle[at])
-            z_last = back[at] = z_exchange(found, z_last)
-    parts = [value for chunk in range(chunks) for value in back[chunk]]
-    away = first_back(place, parts, table_x, xc, False)
-    home = first_back(place, parts, after(table_x, away), xc, True)
+            first[step + 1] = z_exchange(sent[step + 1], first[step])
+        found = ordered(lambda values: second_synth(place, values, table_y, dims), first[step])
+        second[step] = exchange(found, "col", 0, cols)
+    for step in range(chunks):
+        middle[step] = ordered(
+            lambda values: third(place, values, *stored, base[step], table_z, step, dims[3:]),
+            second[step],
+        )
+    for step in range(chunks):
+        found = exchange(middle[step], "col", 0, cols)
+        found = ordered(lambda values: second_back(place, values, table_y, dims), found)
+        back[step] = z_exchange(found, *([back[step - 1]] if step else []))
+    parts = [value for step in range(chunks) for value in back[step]]
+    away, home = first_back(place, parts, table_x, xc)
     result = last(home, core_swap(away), wave_y, wave_x, wave_z, ky_len, kz_len, 1.0 / (orders + 1))
     return result[:, :, :kz_own] if kz_len > kz_own else result
 

time: 337 us -> 289 us (0.86)
  local copies, waits for them, and re-layouts: 46.3 us -> 7.17 us
  starting transfers between devices: 82.6 us -> 52.8 us
  waiting for transfers between devices: 91.5 us -> 110 us
  Pallas kernels: 100 us -> 115 us
  blocking collectives: 14.1 us -> 0 us
    unnamed x126 -> x32, local copies, waits for them, and re-layouts: 43.3 us -> 4.39 us
    ppermute x0 -> x12, waiting for transfers between devices: none -> 28 us  [exchange(): lax.ppermute(value, axis, [(src, src ^ k << shift) for src in range(size)])]
    all_to_all x7 -> x0, starting transfers between devices: 27.9 us -> none  [col_swap(): return lax.all_to_all(value, 'col', split_axis=0, concat_axis=0, tiled=True)]
    ppermute x24 -> x12, starting transfers between devices: 54.2 us -> 37 us  [z_exchange(): lax.ppermute(value, 'row', [(src, src ^ 2 * k) for src in range(rows)])]
    ppermute x0 -> x12, starting transfers between devices: none -> 15.3 us  [exchange(): lax.ppermute(value, axis, [(src, src ^ k << shift) for src in range(size)])]
    all_to_all x7 -> x0, waiting for transfers between devices: 15.3 us -> none  [col_swap(): return lax.all_to_all(value, 'col', split_axis=0, concat_axis=0, tiled=True)]
    all_to_all x1 -> x0, blocking collectives: 14.1 us -> none  [col_swap(): return lax.all_to_all(value, 'col', split_axis=0, concat_axis=0, tiled=True)]
    pallas_call x4 -> x2, Pallas kernels: 17.4 us -> 29.9 us  [second_synth(): pl.pallas_call(functools.partial(second_synth_kernel, dims), in_specs=[SM...]
  transfers between devices with their start and end apart: 33 -> 26, of which waited for: 15 -> 13; matrix products, arithmetic and copies ran while one was open for 1% -> 1% of each run, Pallas kernels for 23% -> 27%
where the time goes in v5:
time: 289 us; the launch traced here: 286 us
  Pallas kernels  115 us (40%)
  waiting for transfers between devices  110 us (38%)
  starting transfers between devices  52.8 us (18%)
  local copies, waits for them, and re-layouts  7.17 us (2%)
    ppermute x12, waiting for transfers between devices, z_exchange(): lax.ppermute(value, 'row', [(src, src ^ 2 * k) for src in range(rows)])  76.3 us
    ppermute x12, starting transfers between devices, z_exchange(): lax.ppermute(value, 'row', [(src, src ^ 2 * k) for src in range(rows)])  37 us
    pallas_call x2, Pallas kernels, second_synth(): pl.pallas_call(functools.partial(second_synth_kernel, dims), in_specs=[SM...  29.9 us
    pallas_call x2, Pallas kernels, third(): pl.pallas_call(functools.partial(third_kernel, (chunk, *dims)), in_specs=...  29.2 us
    ppermute x12, waiting for transfers between devices, exchange(): lax.ppermute(value, axis, [(src, src ^ k << shift) for src in range(size)])  28 us
    pallas_call x2, Pallas kernels, earlier(): pl.pallas_call(functools.partial(earlier_kernel, orders - 1), grid=(packs...  23.6 us
    ppermute x12, starting transfers between devices, exchange(): lax.ppermute(value, axis, [(src, src ^ k << shift) for src in range(size)])  15.3 us
    pallas_call x1, Pallas kernels, first_synth(): pl.pallas_call(functools.partial(first_synth_kernel, dims), in_specs=[SME...  11.6 us
  transfers between devices with their start and end apart: 26, of which 13 were waited for; matrix products, arithmetic and copies ran while one was open for 1% of the time, Pallas kernels for 27%

profile of v5, /device:TPU:0, one launch (start us, length us, event | category | flops | bytes accessed | tf_op | source)
XLA Modules:
  0.0 286.2 jit_solution(8373812175719358710)
XLA Ops:
  1.1 1.6 dynamic-slice_bitcast_fusion.2.table_ref.refs_8_
  2.7 2.3 collective-permute-done.other_ref
  6.4 11.6 %first_synth.1 = (f32[1024,128]{1,0:T(8,128)}, f32[1024,128]{1,0:T(8,128)}, f32[1024,128]{1,0:T(8,128)}, f32[1024,128]{1,0:T(8,128)}, f32[1024,128]{1,0:T(8,128)...) custom-call(s32[3]{0:T(128)} %pad_add_fusion.place_ref, f32[3,20,40,160]{3,2,1,0:T(8,128)} %own_ref.1, ...), custom_call_target="tpu_custom_call" | custom-call | flops 1024 | bytes 1024 | tf_op jit(solution)/shard_map/first_synth/pallas_call | solution.py:185
  18.1 3.0 %collective-permute-start.1 = (f32[1024,128]{1,0:T(8,128)}, f32[1024,128]{1,0:T(8,128)}, u32[]{:S(2)}, u32[]{:S(2)}) collective-permute-start(f32[1024,128]{1,0:T(8,128)} %get-tuple-element.74), channel_id=1, source_target_pairs={{0,8},{4,12},{8,0},{12,4},{16,24},{20,28},{24,16},{28,20},{1,9},{5... | collective-permute-start | bytes 1572872 | tf_op jit(solution)/shard_map/ppermute | solution.py:664
  21.1 2.6 collective-permute-start.2
  24.8 11.8 %earlier_orders.2.refs_6_ = f32[3,16,64,256]{3,2,1,0:T(8,128)S(1)} custom-call(f32[6,3,32,64,256]{4,3,2,1,0:T(8,128)} %refs_4_.5, f32[6,3,32,64,256]{4,3,2,1,0:T(8,128)} %refs_4_.5, f32[6,3,32,64,256]{4,3,2,1,0:T(8,128)} %refs_4_.5, f32[6,3,32,64,256]{4,3,2,1,0:T(8,128)} %refs_4_.5, f32[6,3,32,64,256]{4,3,2,1,0:T(8,128)} %refs_4_.5, ...), custom_call_target="tpu_custom_call" | custom-call | flops 1024 | bytes 1024 | tf_op jit(solution)/shard_map/earlier_orders/pallas_call | solution.py:318
  36.6 11.8 %earlier_orders.3.refs_6_ = f32[3,16,64,256]{3,2,1,0:T(8,128)S(1)} custom-call(f32[6,3,32,64,256]{4,3,2,1,0:T(8,128)} %refs_4_.5, f32[6,3,32,64,256]{4,3,2,1,0:T(8,128)} %refs_4_.5, f32[6,3,32,64,256]{4,3,2,1,0:T(8,128)} %refs_4_.5, f32[6,3,32,64,256]{4,3,2,1,0:T(8,128)} %refs_4_.5, f32[6,3,32,64,256]{4,3,2,1,0:T(8,128)} %refs_4_.5, ...), custom_call_target="tpu_custom_call" | custom-call | flops 1024 | bytes 1024 | tf_op jit(solution)/shard_map/earlier_orders/pallas_call | solution.py:318
  48.4 11.1 %collective-permute-done.2.refs_2_ = f32[1024,128]{1,0:T(8,128)} collective-permute-done((f32[1024,128]{1,0:T(8,128)}, f32[1024,128]{1,0:T(8,128)}, u32[]{:S(2)}, u32[]{:S(2)}) %collective-permute-start.2) | collective-permute-done | bytes 524320 | tf_op jit(solution)/shard_map/ppermute | solution.py:664
  59.6 15.4 %second_synth.2 = (f32[8,240,128]{2,1,0:T(8,128)S(1)}, f32[8,240,128]{2,1,0:T(8,128)S(1)}, f32[8,240,128]{2,1,0:T(8,128)S(1)}, f32[8,240,128]{2,1,0:T(8,128)S(1)}) custom-call(s32[3]{0:T(128)S(1)} %copy-done.5, f32[1024,128]{1,0:T(8,128)S(1)} %copy-done.2, f32[1024,128]{1,0:T(8,128)} %collective-permute-done.1.refs_1_, ...), custom_call_target="tpu_custom_call" | custom-call | flops 1024 | bytes 1024 | tf_op jit(solution)/shard_map/second_synth/pallas_call | solution.py:264
  75.0 1.6 collective-permute-start.4
  76.5 10.7 %collective-permute-start.7 = (f32[1024,128]{1,0:T(8,128)S(1)}, f32[1024,128]{1,0:T(8,128)S(1)}, u32[]{:S(2)}, u32[]{:S(2)}) collective-permute-start(f32[1024,128]{1,0:T(8,128)S(1)} %copy-done.15), channel_id=1, source_target_pairs={{0,8},{4,12},{8,0},{12,4},{16,24},{20,28},{24,16},{28,20},{1,9},{5... | collective-permute-start | bytes 1572872 | tf_op jit(solution)/shard_map/ppermute | solution.py:664
  91.3 16.7 %collective-permute-done.7.refs_1_ = f32[1024,128]{1,0:T(8,128)S(1)} collective-permute-done((f32[1024,128]{1,0:T(8,128)S(1)}, f32[1024,128]{1,0:T(8,128)S(1)}, u32[]{:S(2)}, u32[]{:S(2)}) %collective-permute-start.7) | collective-permute-done | bytes 524320 | tf_op jit(solution)/shard_map/ppermute | solution.py:664
  109.5 16.0 %collective-permute-done.8.refs_2_ = f32[1024,128]{1,0:T(8,128)S(1)} collective-permute-done((f32[1024,128]{1,0:T(8,128)S(1)}, f32[1024,128]{1,0:T(8,128)S(1)}, u32[]{:S(2)}, u32[]{:S(2)}) %collective-permute-start.8) | collective-permute-done | bytes 524320 | tf_op jit(solution)/shard_map/ppermute | solution.py:664
  125.5 14.6 %second_synth.3 = (f32[8,240,128]{2,1,0:T(8,128)S(1)}, f32[8,240,128]{2,1,0:T(8,128)S(1)}, f32[8,240,128]{2,1,0:T(8,128)S(1)}, f32[8,240,128]{2,1,0:T(8,128)S(1)}) custom-call(s32[3]{0:T(128)S(1)} %copy-done.5, f32[1024,128]{1,0:T(8,128)S(1)} %copy-done.1, f32[1024,128]{1,0:T(8,128)S(1)} %collective-permute-done.7.refs_1_, ...), custom_call_target="tpu_custom_call" | custom-call | flops 1024 | bytes 1024 | tf_op jit(solution)/shard_map/second_synth/pallas_call | solution.py:264
  143.6 14.6 %third_dimension.2 = (f32[8,120,128]{2,1,0:T(8,128)S(1)}, f32[8,120,128]{2,1,0:T(8,128)S(1)}, f32[8,120,128]{2,1,0:T(8,128)S(1)}, f32[8,120,128]{2,1,0:T(8,128)S(1)}) custom-call(s32[3]{0:T(128)S(1)} %copy-done.5, f32[8,240,128]{2,1,0:T(8,128)S(1)} %get-tuple-element.101.refs_0_, f32[8,240,128]{2,1,0:T(8,128)S(1)} %collective-permute-done.4.refs_1_, ...), custom_call_target="tpu_custom_call" | custom-call | flops 1024 | bytes 1024 | tf_op jit(solution)/shard_map/third_dimension/pallas_call | solution.py:388
  160.3 4.5 %collective-permute-done.13.refs_1_ = f32[8,240,128]{2,1,0:T(8,128)S(1)} collective-permute-done((f32[8,240,128]{2,1,0:T(8,128)S(1)}, f32[8,240,128]{2,1,0:T(8,128)S(1)}, u32[]{:S(2)}, u32[]{:S(2)}) %collective-permute-start.13) | collective-permute-done | bytes 983072 | tf_op jit(solution)/shard_map/ppermute | solution.py:637
  166.3 16.6 %collective-permute-done.14.refs_2_ = f32[8,240,128]{2,1,0:T(8,128)S(1)} collective-permute-done((f32[8,240,128]{2,1,0:T(8,128)S(1)}, f32[8,240,128]{2,1,0:T(8,128)S(1)}, u32[]{:S(2)}, u32[]{:S(2)}) %collective-permute-start.14) | collective-permute-done | bytes 983072 | tf_op jit(solution)/shard_map/ppermute | solution.py:637
  182.9 4.0 %collective-permute-done.15.refs_3_ = f32[8,240,128]{2,1,0:T(8,128)S(1)} collective-permute-done((f32[8,240,128]{2,1,0:T(8,128)S(1)}, f32[8,240,128]{2,1,0:T(8,128)S(1)}, u32[]{:S(2)}, u32[]{:S(2)}) %collective-permute-start.15) | collective-permute-done | bytes 983072 | tf_op jit(solution)/shard_map/ppermute | solution.py:637
  186.9 14.6 %third_dimension.3 = (f32[8,120,128]{2,1,0:T(8,128)S(1)}, f32[8,120,128]{2,1,0:T(8,128)S(1)}, f32[8,120,128]{2,1,0:T(8,128)S(1)}, f32[8,120,128]{2,1,0:T(8,128)S(1)}) custom-call(s32[3]{0:T(128)S(1)} %copy-done.5, f32[8,240,128]{2,1,0:T(8,128)S(1)} %get-tuple-element.112.refs_0_, f32[8,240,128]{2,1,0:T(8,128)S(1)} %collective-permute-done.13.refs_1_, ...), custom_call_target="tpu_custom_call" | custom-call | flops 1024 | bytes 1024 | tf_op jit(solution)/shard_map/third_dimension/pallas_call | solution.py:388
  202.4 2.7 collective-permute-start.20
  205.1 2.9 %collective-permute-done.12.refs_3_ = f32[8,120,128]{2,1,0:T(8,128)S(1)} collective-permute-done((f32[8,120,128]{2,1,0:T(8,128)S(1)}, f32[8,120,128]{2,1,0:T(8,128)S(1)}, u32[]{:S(2)}, u32[]{:S(2)}) %collective-permute-start.12) | collective-permute-done | bytes 491552 | tf_op jit(solution)/shard_map/ppermute | solution.py:637
  208.0 4.7 %second_back.2 = (f32[608,128]{1,0:T(8,128)S(1)}, f32[608,128]{1,0:T(8,128)S(1)}, f32[608,128]{1,0:T(8,128)S(1)}, f32[608,128]{1,0:T(8,128)S(1)}) custom-call(s32[3]{0:T(128)S(1)} %copy-done.5, f32[8,120,128]{2,1,0:T(8,128)S(1)} %get-tuple-element.117.refs_0_, f32[8,120,128]{2,1,0:T(8,128)S(1)} %collective-permute-done.10.refs_1_, ...), custom_call_target="tpu_custom_call" | custom-call | flops 1024 | bytes 1024 | tf_op jit(solution)/shard_map/second_back/pallas_call | solution.py:446
  212.7 9.3 %collective-permute-start.16 = (f32[608,128]{1,0:T(8,128)S(1)}, f32[608,128]{1,0:T(8,128)S(1)}, u32[]{:S(2)}, u32[]{:S(2)}) collective-permute-start(f32[608,128]{1,0:T(8,128)S(1)} %get-tuple-element.122), channel_id=1, source_target_pairs={{0,8},{4,12},{8,0},{12,4},{16,24},{20,28},{24,16},{28,20},{1,9},{5... | collective-permute-start | bytes 933896 | tf_op jit(solution)/shard_map/ppermute | solution.py:664
  224.5 4.7 %second_back.3 = (f32[608,128]{1,0:T(8,128)S(1)}, f32[608,128]{1,0:T(8,128)S(1)}, f32[608,128]{1,0:T(8,128)S(1)}, f32[608,128]{1,0:T(8,128)S(1)}) custom-call(s32[3]{0:T(128)S(1)} %copy-done.5, f32[8,120,128]{2,1,0:T(8,128)S(1)} %get-tuple-element.128.refs_0_, f32[8,120,128]{2,1,0:T(8,128)S(1)} %collective-permute-done.19.refs_1_, ...), custom_call_target="tpu_custom_call" | custom-call | flops 1024 | bytes 1024 | tf_op jit(solution)/shard_map/second_back/pallas_call | solution.py:446
  229.9 2.0 collective-permute-done.16.refs_1_
  231.9 10.0 %collective-permute-done.17.refs_2_ = f32[608,128]{1,0:T(8,128)S(1)} collective-permute-done((f32[608,128]{1,0:T(8,128)S(1)}, f32[608,128]{1,0:T(8,128)S(1)}, u32[]{:S(2)}, u32[]{:S(2)}) %collective-permute-start.17) | collective-permute-done | bytes 311328 | tf_op jit(solution)/shard_map/ppermute | solution.py:664
  241.9 3.9 %collective-permute-start.22 = (f32[608,128]{1,0:T(8,128)S(1)}, f32[608,128]{1,0:T(8,128)S(1)}, u32[]{:S(2)}, u32[]{:S(2)}) collective-permute-start(f32[608,128]{1,0:T(8,128)S(1)} %get-tuple-element.134), channel_id=1, source_target_pairs={{0,8},{4,12},{8,0},{12,4},{16,24},{20,28},{24,16},{28,20},{1,9},{5... | collective-permute-start | bytes 933896 | tf_op jit(solution)/shard_map/ppermute | solution.py:664
  248.3 5.7 %collective-permute-done.22.refs_5_ = f32[608,128]{1,0:T(8,128)S(1)} collective-permute-done((f32[608,128]{1,0:T(8,128)S(1)}, f32[608,128]{1,0:T(8,128)S(1)}, u32[]{:S(2)}, u32[]{:S(2)}) %collective-permute-start.22) | collective-permute-done | bytes 311328 | tf_op jit(solution)/shard_map/ppermute | solution.py:664
  254.0 14.9 %collective-permute-done.23.refs_6_ = f32[608,128]{1,0:T(8,128)S(1)} collective-permute-done((f32[608,128]{1,0:T(8,128)S(1)}, f32[608,128]{1,0:T(8,128)S(1)}, u32[]{:S(2)}, u32[]{:S(2)}) %collective-permute-start.23) | collective-permute-done | bytes 311328 | tf_op jit(solution)/shard_map/ppermute | solution.py:664
  269.7 5.2 %first_back.1 = (f32[160,2432]{1,0:T(8,128)}, f32[160,2432]{1,0:T(8,128)}) custom-call(s32[3]{0:T(128)} %pad_add_fusion.place_ref, f32[608,128]{1,0:T(8,128)} %copy-done.3, f32[608,128]{1,0:T(8,128)} %copy-done.7, f32[608,128]{1,0:T(8,128)} %copy-done.8, f32[608,128]{1,0:T(8,128)} %copy-done.9, f32[608,128]{1,0:T(8,128)} %copy-done.4, ...), custom_call_target="tpu_custom_call" | custom-call | flops 1024 | bytes 1024 | tf_op jit(solution)/shard_map/first_back/pallas_call | solution.py:481
  275.0 3.5 %collective-permute-done.25.refs_2_ = f32[160,2432]{1,0:T(8,128)S(1)} collective-permute-done((f32[160,2432]{1,0:T(8,128)}, f32[160,2432]{1,0:T(8,128)S(1)}, u32[]{:S(2)}, u32[]{:S(2)}) %collective-permute-start.25) | collective-permute-done | bytes 1556512 | tf_op jit(solution)/shard_map/ppermute | solution.py:642
  280.0 6.2 %last_projection.1 = f32[3,20,40,160]{3,2,1,0:T(8,128)} custom-call(f32[10]{0:T(128)S(1)} %convert_multiply_fusion.1.refs_0_, f32[160,2432]{1,0:T(8,128)S(1)} %copy-done, f32[160,2432]{1,0:T(8,128)S(1)} %collective-permute-done.25.refs_2_, f32[8,256]{1,0:T(8,128)S(1)} %broadcast_in_dim.9.refs_3_, f32[40,256]{1,0:T(8,128)S(1)} %broadcast_in_dim.18.refs_4_), custom_call_target="tpu_custom_call" | custom-call | flops 1024 | bytes 1024 | tf_op jit(solution)/shard_map/last_projection/pallas_call | solution.py:549
  (71 shorter events, 25.4 us)
Async XLA Ops:
  0.0 5.0 %collective-permute-start = (f32[3,20,40,160]{3,2,1,0:T(8,128)}, f32[3,20,40,160]{3,2,1,0:T(8,128)S(1)}, u32[]{:S(2)}, u32[]{:S(2)}) collective-permute-start(f32[3,20,40,160]{3,2,1,0:T(8,128)} %own_ref.1), channel_id=1, source_target_pairs={{0,4},{4,0},{8,12},{12,8},{16,20},{20,16},{24,28},{28,24},{1,5},{5... | collective-permute-start | bytes 4608008 | tf_op jit(solution)/shard_map/ppermute | solution.py:642
  18.1 30.4 %collective-permute-start.1 = (f32[1024,128]{1,0:T(8,128)}, f32[1024,128]{1,0:T(8,128)}, u32[]{:S(2)}, u32[]{:S(2)}) collective-permute-start(f32[1024,128]{1,0:T(8,128)} %get-tuple-element.74), channel_id=1, source_target_pairs={{0,8},{4,12},{8,0},{12,4},{16,24},{20,28},{24,16},{28,20},{1,9},{5... | collective-permute-start | bytes 1572872 | tf_op jit(solution)/shard_map/ppermute | solution.py:664
  21.1 38.5 %collective-permute-start.2 = (f32[1024,128]{1,0:T(8,128)}, f32[1024,128]{1,0:T(8,128)}, u32[]{:S(2)}, u32[]{:S(2)}) collective-permute-start(f32[1024,128]{1,0:T(8,128)} %get-tuple-element.75), channel_id=1, source_target_pairs={{0,16},{4,20},{8,24},{12,28},{16,0},{20,4},{24,8},{28,12},{1,17},{... | collective-permute-start | bytes 1572872 | tf_op jit(solution)/shard_map/ppermute | solution.py:664
  23.7 35.9 %collective-permute-start.3 = (f32[1024,128]{1,0:T(8,128)}, f32[1024,128]{1,0:T(8,128)}, u32[]{:S(2)}, u32[]{:S(2)}) collective-permute-start(f32[1024,128]{1,0:T(8,128)} %get-tuple-element.76), channel_id=1, source_target_pairs={{0,24},{4,28},{8,16},{12,20},{16,8},{20,12},{24,0},{28,4},{1,25},{... | collective-permute-start | bytes 1572872 | tf_op jit(solution)/shard_map/ppermute | solution.py:664
  48.4 28.2 %copy-start.15 = (f32[1024,128]{1,0:T(8,128)S(1)}, f32[1024,128]{1,0:T(8,128)}, u32[]{:S(2)}) copy-start(f32[1024,128]{1,0:T(8,128)} %get-tuple-element.91) | copy-start | bytes 1572868
  48.4 38.9 %copy-start.14 = (f32[1024,128]{1,0:T(8,128)S(1)}, f32[1024,128]{1,0:T(8,128)}, u32[]{:S(2)}) copy-start(f32[1024,128]{1,0:T(8,128)} %get-tuple-element.93) | copy-start | bytes 1572868
  48.4 39.9 %copy-start.13 = (f32[1024,128]{1,0:T(8,128)S(1)}, f32[1024,128]{1,0:T(8,128)}, u32[]{:S(2)}) copy-start(f32[1024,128]{1,0:T(8,128)} %get-tuple-element.95) | copy-start | bytes 1572868
  48.4 77.1 %copy-start.1 = (f32[1024,128]{1,0:T(8,128)S(1)}, f32[1024,128]{1,0:T(8,128)}, u32[]{:S(2)}) copy-start(f32[1024,128]{1,0:T(8,128)} %get-tuple-element.96.refs_0_) | copy-start | bytes 1572868
  75.0 67.2 %collective-permute-start.4 = (f32[8,240,128]{2,1,0:T(8,128)S(1)}, f32[8,240,128]{2,1,0:T(8,128)S(1)}, u32[]{:S(2)}, u32[]{:S(2)}) collective-permute-start(f32[8,240,128]{2,1,0:T(8,128)S(1)} %get-tuple-element.86), channel_id=1, source_target_pairs={{0,1},{1,0},{2,3},{3,2},{4,5},{5,4},{6,7},{7,6},{8,9},{9,8},{10,11... | collective-permute-start | bytes 2949128 | tf_op jit(solution)/shard_map/ppermute | solution.py:637
  76.5 31.5 %collective-permute-start.7 = (f32[1024,128]{1,0:T(8,128)S(1)}, f32[1024,128]{1,0:T(8,128)S(1)}, u32[]{:S(2)}, u32[]{:S(2)}) collective-permute-start(f32[1024,128]{1,0:T(8,128)S(1)} %copy-done.15), channel_id=1, source_target_pairs={{0,8},{4,12},{8,0},{12,4},{16,24},{20,28},{24,16},{28,20},{1,9},{5... | collective-permute-start | bytes 1572872 | tf_op jit(solution)/shard_map/ppermute | solution.py:664
  87.2 38.2 %collective-permute-start.8 = (f32[1024,128]{1,0:T(8,128)S(1)}, f32[1024,128]{1,0:T(8,128)S(1)}, u32[]{:S(2)}, u32[]{:S(2)}) collective-permute-start(f32[1024,128]{1,0:T(8,128)S(1)} %copy-done.14), channel_id=1, source_target_pairs={{0,16},{4,20},{8,24},{12,28},{16,0},{20,4},{24,8},{28,12},{1,17},{... | collective-permute-start | bytes 1572872 | tf_op jit(solution)/shard_map/ppermute | solution.py:664
  88.3 37.1 %collective-permute-start.9 = (f32[1024,128]{1,0:T(8,128)S(1)}, f32[1024,128]{1,0:T(8,128)S(1)}, u32[]{:S(2)}, u32[]{:S(2)}) collective-permute-start(f32[1024,128]{1,0:T(8,128)S(1)} %copy-done.13), channel_id=1, source_target_pairs={{0,24},{4,28},{8,16},{12,20},{16,8},{20,12},{24,0},{28,4},{1,25},{... | collective-permute-start | bytes 1572872 | tf_op jit(solution)/shard_map/ppermute | solution.py:664
  89.8 53.8 %collective-permute-start.5 = (f32[8,240,128]{2,1,0:T(8,128)S(1)}, f32[8,240,128]{2,1,0:T(8,128)S(1)}, u32[]{:S(2)}, u32[]{:S(2)}) collective-permute-start(f32[8,240,128]{2,1,0:T(8,128)S(1)} %get-tuple-element.87), channel_id=1, source_target_pairs={{0,2},{1,3},{2,0},{3,1},{4,6},{5,7},{6,4},{7,5},{8,10},{9,11},{10,... | collective-permute-start | bytes 2949128 | tf_op jit(solution)/shard_map/ppermute | solution.py:637
  108.0 35.6 %collective-permute-start.6 = (f32[8,240,128]{2,1,0:T(8,128)S(1)}, f32[8,240,128]{2,1,0:T(8,128)S(1)}, u32[]{:S(2)}, u32[]{:S(2)}) collective-permute-start(f32[8,240,128]{2,1,0:T(8,128)S(1)} %get-tuple-element.88), channel_id=1, source_target_pairs={{0,3},{1,2},{2,1},{3,0},{4,7},{5,6},{6,5},{7,4},{8,11},{9,10},{10,... | collective-permute-start | bytes 2949128 | tf_op jit(solution)/shard_map/ppermute | solution.py:637
  140.0 24.8 %collective-permute-start.13 = (f32[8,240,128]{2,1,0:T(8,128)S(1)}, f32[8,240,128]{2,1,0:T(8,128)S(1)}, u32[]{:S(2)}, u32[]{:S(2)}) collective-permute-start(f32[8,240,128]{2,1,0:T(8,128)S(1)} %get-tuple-element.109), channel_id=1, source_target_pairs={{0,1},{1,0},{2,3},{3,2},{4,5},{5,4},{6,7},{7,6},{8,9},{9,8},{10,11... | collective-permute-start | bytes 2949128 | tf_op jit(solution)/shard_map/ppermute | solution.py:637
  140.6 42.3 %collective-permute-start.14 = (f32[8,240,128]{2,1,0:T(8,128)S(1)}, f32[8,240,128]{2,1,0:T(8,128)S(1)}, u32[]{:S(2)}, u32[]{:S(2)}) collective-permute-start(f32[8,240,128]{2,1,0:T(8,128)S(1)} %get-tuple-element.110), channel_id=1, source_target_pairs={{0,2},{1,3},{2,0},{3,1},{4,6},{5,7},{6,4},{7,5},{8,10},{9,11},{10,... | collective-permute-start | bytes 2949128 | tf_op jit(solution)/shard_map/ppermute | solution.py:637
  142.2 44.8 %collective-permute-start.15 = (f32[8,240,128]{2,1,0:T(8,128)S(1)}, f32[8,240,128]{2,1,0:T(8,128)S(1)}, u32[]{:S(2)}, u32[]{:S(2)}) collective-permute-start(f32[8,240,128]{2,1,0:T(8,128)S(1)} %get-tuple-element.111), channel_id=1, source_target_pairs={{0,3},{1,2},{2,1},{3,0},{4,7},{5,6},{6,5},{7,4},{8,11},{9,10},{10,... | collective-permute-start | bytes 2949128 | tf_op jit(solution)/shard_map/ppermute | solution.py:637
  158.2 46.8 %collective-permute-start.10 = (f32[8,120,128]{2,1,0:T(8,128)S(1)}, f32[8,120,128]{2,1,0:T(8,128)S(1)}, u32[]{:S(2)}, u32[]{:S(2)}) collective-permute-start(f32[8,120,128]{2,1,0:T(8,128)S(1)} %get-tuple-element.106), channel_id=1, source_target_pairs={{0,1},{1,0},{2,3},{3,2},{4,5},{5,4},{6,7},{7,6},{8,9},{9,8},{10,11... | collective-permute-start | bytes 1474568 | tf_op jit(solution)/shard_map/ppermute | solution.py:637
  158.8 46.3 %collective-permute-start.11 = (f32[8,120,128]{2,1,0:T(8,128)S(1)}, f32[8,120,128]{2,1,0:T(8,128)S(1)}, u32[]{:S(2)}, u32[]{:S(2)}) collective-permute-start(f32[8,120,128]{2,1,0:T(8,128)S(1)} %get-tuple-element.107), channel_id=1, source_target_pairs={{0,2},{1,3},{2,0},{3,1},{4,6},{5,7},{6,4},{7,5},{8,10},{9,11},{10,... | collective-permute-start | bytes 1474568 | tf_op jit(solution)/shard_map/ppermute | solution.py:637
  164.8 43.2 %collective-permute-start.12 = (f32[8,120,128]{2,1,0:T(8,128)S(1)}, f32[8,120,128]{2,1,0:T(8,128)S(1)}, u32[]{:S(2)}, u32[]{:S(2)}) collective-permute-start(f32[8,120,128]{2,1,0:T(8,128)S(1)} %get-tuple-element.108), channel_id=1, source_target_pairs={{0,3},{1,2},{2,1},{3,0},{4,7},{5,6},{6,5},{7,4},{8,11},{9,10},{10,... | collective-permute-start | bytes 1474568 | tf_op jit(solution)/shard_map/ppermute | solution.py:637
  201.5 21.6 %collective-permute-start.19 = (f32[8,120,128]{2,1,0:T(8,128)S(1)}, f32[8,120,128]{2,1,0:T(8,128)S(1)}, u32[]{:S(2)}, u32[]{:S(2)}) collective-permute-start(f32[8,120,128]{2,1,0:T(8,128)S(1)} %get-tuple-element.125), channel_id=1, source_target_pairs={{0,1},{1,0},{2,3},{3,2},{4,5},{5,4},{6,7},{7,6},{8,9},{9,8},{10,11... | collective-permute-start | bytes 1474568 | tf_op jit(solution)/shard_map/ppermute | solution.py:637
  202.4 22.1 %collective-permute-start.20 = (f32[8,120,128]{2,1,0:T(8,128)S(1)}, f32[8,120,128]{2,1,0:T(8,128)S(1)}, u32[]{:S(2)}, u32[]{:S(2)}) collective-permute-start(f32[8,120,128]{2,1,0:T(8,128)S(1)} %get-tuple-element.126), channel_id=1, source_target_pairs={{0,2},{1,3},{2,0},{3,1},{4,6},{5,7},{6,4},{7,5},{8,10},{9,11},{10,... | collective-permute-start | bytes 1474568 | tf_op jit(solution)/shard_map/ppermute | solution.py:637
  205.1 19.4 %collective-permute-start.21 = (f32[8,120,128]{2,1,0:T(8,128)S(1)}, f32[8,120,128]{2,1,0:T(8,128)S(1)}, u32[]{:S(2)}, u32[]{:S(2)}) collective-permute-start(f32[8,120,128]{2,1,0:T(8,128)S(1)} %get-tuple-element.127), channel_id=1, source_target_pairs={{0,3},{1,2},{2,1},{3,0},{4,7},{5,6},{6,5},{7,4},{8,11},{9,10},{10,... | collective-permute-start | bytes 1474568 | tf_op jit(solution)/shard_map/ppermute | solution.py:637
  212.7 19.2 %collective-permute-start.16 = (f32[608,128]{1,0:T(8,128)S(1)}, f32[608,128]{1,0:T(8,128)S(1)}, u32[]{:S(2)}, u32[]{:S(2)}) collective-permute-start(f32[608,128]{1,0:T(8,128)S(1)} %get-tuple-element.122), channel_id=1, source_target_pairs={{0,8},{4,12},{8,0},{12,4},{16,24},{20,28},{24,16},{28,20},{1,9},{5... | collective-permute-start | bytes 933896 | tf_op jit(solution)/shard_map/ppermute | solution.py:664
  222.0 19.9 %collective-permute-start.17 = (f32[608,128]{1,0:T(8,128)S(1)}, f32[608,128]{1,0:T(8,128)S(1)}, u32[]{:S(2)}, u32[]{:S(2)}) collective-permute-start(f32[608,128]{1,0:T(8,128)S(1)} %get-tuple-element.123), channel_id=1, source_target_pairs={{0,16},{4,20},{8,24},{12,28},{16,0},{20,4},{24,8},{28,12},{1,17},{... | collective-permute-start | bytes 933896 | tf_op jit(solution)/shard_map/ppermute | solution.py:664
  223.1 18.8 %collective-permute-start.18 = (f32[608,128]{1,0:T(8,128)S(1)}, f32[608,128]{1,0:T(8,128)S(1)}, u32[]{:S(2)}, u32[]{:S(2)}) collective-permute-start(f32[608,128]{1,0:T(8,128)S(1)} %get-tuple-element.124), channel_id=1, source_target_pairs={{0,24},{4,28},{8,16},{12,20},{16,8},{20,12},{24,0},{28,4},{1,25},{... | collective-permute-start | bytes 933896 | tf_op jit(solution)/shard_map/ppermute | solution.py:664
  231.9 36.9 %copy-start.7 = (f32[608,128]{1,0:T(8,128)}, f32[608,128]{1,0:T(8,128)S(1)}, u32[]{:S(2)}) copy-start(f32[608,128]{1,0:T(8,128)S(1)} %collective-permute-done.16.refs_1_) | copy-start | bytes 933892
  241.9 27.0 %copy-start.9 = (f32[608,128]{1,0:T(8,128)}, f32[608,128]{1,0:T(8,128)S(1)}, u32[]{:S(2)}) copy-start(f32[608,128]{1,0:T(8,128)S(1)} %collective-permute-done.18.refs_3_) | copy-start | bytes 933892
  241.9 12.1 %collective-permute-start.22 = (f32[608,128]{1,0:T(8,128)S(1)}, f32[608,128]{1,0:T(8,128)S(1)}, u32[]{:S(2)}, u32[]{:S(2)}) collective-permute-start(f32[608,128]{1,0:T(8,128)S(1)} %get-tuple-element.134), channel_id=1, source_target_pairs={{0,8},{4,12},{8,0},{12,4},{16,24},{20,28},{24,16},{28,20},{1,9},{5... | collective-permute-start | bytes 933896 | tf_op jit(solution)/shard_map/ppermute | solution.py:664
  245.8 23.0 %collective-permute-start.23 = (f32[608,128]{1,0:T(8,128)S(1)}, f32[608,128]{1,0:T(8,128)S(1)}, u32[]{:S(2)}, u32[]{:S(2)}) collective-permute-start(f32[608,128]{1,0:T(8,128)S(1)} %get-tuple-element.136), channel_id=1, source_target_pairs={{0,16},{4,20},{8,24},{12,28},{16,0},{20,4},{24,8},{28,12},{1,17},{... | collective-permute-start | bytes 933896 | tf_op jit(solution)/shard_map/ppermute | solution.py:664
  246.8 22.0 %collective-permute-start.24 = (f32[608,128]{1,0:T(8,128)S(1)}, f32[608,128]{1,0:T(8,128)S(1)}, u32[]{:S(2)}, u32[]{:S(2)}) collective-permute-start(f32[608,128]{1,0:T(8,128)S(1)} %get-tuple-element.138), channel_id=1, source_target_pairs={{0,24},{4,28},{8,16},{12,20},{16,8},{20,12},{24,0},{28,4},{1,25},{... | collective-permute-start | bytes 933896 | tf_op jit(solution)/shard_map/ppermute | solution.py:664
  274.9 3.7 %collective-permute-start.25 = (f32[160,2432]{1,0:T(8,128)}, f32[160,2432]{1,0:T(8,128)S(1)}, u32[]{:S(2)}, u32[]{:S(2)}) collective-permute-start(f32[160,2432]{1,0:T(8,128)} %get-tuple-element.140), channel_id=1, source_target_pairs={{0,4},{4,0},{8,12},{12,8},{16,20},{20,16},{24,28},{28,24},{1,5},{5... | collective-permute-start | bytes 4669448 | tf_op jit(solution)/shard_map/ppermute | solution.py:642
  (10 other events, 109.5 us)

commit v6 on v5

--- a/solution.py
+++ b/solution.py
@@ -116,90 +116,87 @@
     return pl.BlockSpec(array.shape, lambda *_: (0,) * rank)
 
 
-def first_synth_kernel(dims, place_ref, own_ref, other_ref, table_ref, *rest):
-    chunks, dests, xc = dims
-    outs = rest[: chunks * dests]
-    own_data, other_data, rows, held, sem, out_sem = rest[chunks * dests :]
-    _, ky_len, kz_len, _ = own_data.shape
+def first_synth_kernel(dims, place_ref, data_ref, table_ref, *rest):
+    chunks, dests, xc, own = dims
+    count = chunks * dests
+    outs = rest[-count - 5 : -5]
+    data, rows, held, sem, out_sem = rest[-5:]
+    _, ky_len, kz_len, _ = data.shape
     group = 5 * kz_len
-    half = rows.shape[0] // 2
+    size = held.shape[1]
     copies = [
-        pltpu.make_async_copy(ref.at[comp], data.at[comp], sem.at[side, comp])
-        for side, (ref, data) in enumerate(((own_ref, own_data), (other_ref, other_data)))
-        for comp in range(3)
+        pltpu.make_async_copy(data_ref.at[comp], data.at[comp], sem.at[comp]) for comp in range(3)
     ]
     for copy in copies:
         copy.start()
-    if ky_len * group < half:
-        for core in range(2):
-            rows[core * half + ky_len * group : (core + 1) * half, :] = jnp.zeros(
-                (half - ky_len * group, LANES), F32
-            )
+    if ky_len * group < rows.shape[0]:
+        rows[ky_len * group :, :] = jnp.zeros((rows.shape[0] - ky_len * group, LANES), F32)
     plain = jnp.concatenate([table_ref[0], table_ref[1]], axis=1)
     slope = jnp.concatenate([table_ref[2], table_ref[3]], axis=1)
     step = 4 if ky_len % 4 == 0 else 2
-
-    for side, data in enumerate((own_data, other_data)):
-        for copy in copies[3 * side : 3 * side + 3]:
-            copy.wait()
-        core = place_ref[1] if side == 0 else 1 - place_ref[1]
-
-        def body(idx, carry):
-            first = idx * step
-            lines = [[data[comp, first + k] for comp in range(3)] for k in range(step)]
-            found = both_passes(
-                jnp.concatenate([v for line in lines for v in line], axis=0), plain, table_ref[0]
-            )
-            sloped = both_passes(
-                jnp.concatenate([v for line in lines for v in line[1:]], axis=0), slope, table_ref[2]
-            )
-            for k in range(step):
-                base = core * half + (first + k) * group
-                rows[pl.ds(pl.multiple_of(base, 8), 3 * kz_len), :] = found[
-                    3 * k * kz_len : 3 * (k + 1) * kz_len
-                ]
-                rows[pl.ds(pl.multiple_of(base + 3 * kz_len, 8), 2 * kz_len), :] = sloped[
-                    2 * k * kz_len : 2 * (k + 1) * kz_len
-                ]
-            return carry
-
-        lax.fori_loop(0, ky_len // step, body, 0)
+    for copy in copies:
+        copy.wait()
+
+    def body(idx, carry):
+        first = idx * step
+        lines = [[data[comp, first + k] for comp in range(3)] for k in range(step)]
+        found = both_passes(
+            jnp.concatenate([v for line in lines for v in line], axis=0), plain, table_ref[0]
+        )
+        sloped = both_passes(
+            jnp.concatenate([v for line in lines for v in line[1:]], axis=0), slope, table_ref[2]
+        )
+        for k in range(step):
+            base = (first + k) * group
+            rows[pl.ds(pl.multiple_of(base, 8), 3 * kz_len), :] = found[
+                3 * k * kz_len : 3 * (k + 1) * kz_len
+            ]
+            rows[pl.ds(pl.multiple_of(base + 3 * kz_len, 8), 2 * kz_len), :] = sloped[
+                2 * k * kz_len : 2 * (k + 1) * kz_len
+            ]
+        return carry
+
+    lax.fori_loop(0, ky_len // step, body, 0)
 
     def flip(tile, carry):
         found = rows[pl.ds(pl.multiple_of(tile * LANES, LANES), LANES), :].T
-        for idx in range(chunks * dests):
+        for idx in range(count):
             held[idx, pl.ds(pl.multiple_of(tile * xc, 8), xc), :] = found[idx * xc : (idx + 1) * xc]
         return carry
 
-    lax.fori_loop(0, 2 * half // LANES, flip, 0, unroll=2)
-    copies = [pltpu.make_async_copy(held.at[k], out, out_sem.at[k]) for k, out in enumerate(outs)]
+    lax.fori_loop(0, rows.shape[0] // LANES, flip, 0, unroll=2)
+    core = place_ref[1] if own else 1 - place_ref[1]
+    spot = pl.ds(pl.multiple_of(core * size, 8), size)
+    copies = [
+        pltpu.make_async_copy(held.at[k], out.at[spot, :], out_sem.at[k]) for k, out in enumerate(outs)
+    ]
     for copy in copies:
         copy.start()
     for copy in copies:
         copy.wait()
 
 
-def first_synth(place, own, other, table, dims, lanes):
+def first_synth(place, coeffs, table, dims, lanes, half):
     chunks, dests, xc = dims
-    out = jax.ShapeDtypeStruct((2 * lanes // LANES * xc, LANES), F32)
-    found = pl.pallas_call(
-        functools.partial(first_synth_kernel, dims),
-        in_specs=[SMEM, ANY, ANY, VMEM],
-        out_specs=[HBM] * (chunks * dests),
-        out_shape=[out] * (chunks * dests),
+    size = lanes // LANES * xc
+    count = chunks * dests
+    return pl.pallas_call(
+        functools.partial(first_synth_kernel, (*dims, not half)),
+        in_specs=[SMEM, ANY, VMEM] + [HBM] * len(half),
+        out_specs=[HBM] * count,
+        out_shape=[jax.ShapeDtypeStruct((2 * size, LANES), F32)] * count,
+        input_output_aliases={3 + k: k for k in range(len(half))},
         scratch_shapes=[
-            pltpu.VMEM(own.shape, F32),
-            pltpu.VMEM(own.shape, F32),
-            pltpu.VMEM((2 * lanes, LANES), F32),
-            pltpu.VMEM((chunks * dests, *out.shape), F32),
-            pltpu.SemaphoreType.DMA((2, 3)),
-            pltpu.SemaphoreType.DMA((chunks * dests,)),
+            pltpu.VMEM(coeffs.shape, F32),
+            pltpu.VMEM((lanes, LANES), F32),
+            pltpu.VMEM((count, size, LANES), F32),
+            pltpu.SemaphoreType.DMA((3,)),
+            pltpu.SemaphoreType.DMA((count,)),
         ],
-        compiler_params=still(VMEM_MOST),
+        compiler_params=still(),
         cost_estimate=SHORT,
         name="first_synth",
-    )(place, own, other, table)
-    return [list(found[k * dests : (k + 1) * dests]) for k in range(chunks)]
+    )(place, coeffs, table, *half)
 
 
 def second_synth_kernel(dims, place_ref, *refs):
@@ -207,18 +204,21 @@
     groups = rows // 2
     parts, table_ref, out_refs = refs[:groups], refs[groups], refs[groups + 1 : -3]
     a_ref, held, sem = refs[-3:]
-    size = a_ref.shape[0] // groups
+    size = parts[0].shape[0] // 2
+    stride = a_ref.shape[0] // rows
     for k, part in enumerate(parts):
-        a_ref[pl.ds(pl.multiple_of((place_ref[0] ^ k) * size, 8), size), :] = part[...]
+        for core in range(2):
+            spot = pl.multiple_of(((place_ref[0] ^ k) * 2 + core) * stride, 8)
+            a_ref[pl.ds(spot, size), :] = part[core * size : (core + 1) * size, :]
     group = 5 * kz_len
     wide = round_up(group, LANES)
-    tiles = a_ref.shape[0] // (rows * xc)
+    tiles = size // xc
 
     def body(at, carry):
         turned = []
         for part in range(pack):
             line = [
-                a_ref[pl.ds(tile * xc + at * pack + part, rows, stride=tiles * xc), :]
+                a_ref[pl.ds(tile * xc + at * pack + part, rows, stride=stride), :]
                 for tile in range(tiles)
             ]
             found = []
@@ -267,7 +267,7 @@
         out_specs=[HBM] * cols,
         out_shape=[jax.ShapeDtypeStruct((packs, 6 * kz_len, LANES), F32)] * cols,
         scratch_shapes=[
-            pltpu.VMEM((len(arrived) * arrived[0].shape[0], LANES), F32),
+            pltpu.VMEM((rows * (arrived[0].shape[0] // 2 + 8), LANES), F32),
             pltpu.VMEM((cols, packs, 6 * kz_len, LANES), F32),
             pltpu.SemaphoreType.DMA((cols, packs)),
         ],
@@ -456,34 +456,35 @@
 
 
 def first_back_kernel(dims, place_ref, *refs):
-    count, xc = dims
-    parts, table_ref, outs = refs[:count], refs[count], refs[count + 1 : count + 3]
+    count, xc, own = dims
+    parts, table_ref, out_ref = refs[:count], refs[count], refs[count + 1]
     data, sem = refs[-2:]
-    copies = [pltpu.make_async_copy(part, data.at[k], sem.at[k]) for k, part in enumerate(parts)]
+    size = data.shape[1]
+    core = place_ref[1] if own else 1 - place_ref[1]
+    spot = pl.ds(pl.multiple_of(core * size, 8), size)
+    copies = [
+        pltpu.make_async_copy(part.at[spot, :], data.at[k], sem.at[k]) for k, part in enumerate(parts)
+    ]
     for copy in copies:
         copy.start()
     for copy in copies:
         copy.wait()
-    size = data.shape[1] // 2
-    for out_ref, core in zip(outs, (1 - place_ref[1], place_ref[1])):
-        for tile in range(size // xc):
-            spot = pl.ds(pl.multiple_of(core * size + tile * xc, 8), xc)
-            found = jnp.concatenate([data[k, spot, :] for k in range(count)], axis=0)
-            out_ref[:, tile * LANES : (tile + 1) * LANES] = dot_data_right(
-                table_ref[0], table_ref[1], found, NN
-            )
-
-
-def first_back(place, parts, table, xc):
+    for tile in range(size // xc):
+        found = jnp.concatenate([data[k, tile * xc : (tile + 1) * xc, :] for k in range(count)], axis=0)
+        out_ref[:, tile * LANES : (tile + 1) * LANES] = dot_data_right(
+            table_ref[0], table_ref[1], found, NN
+        )
+
+
+def first_back(place, parts, table, xc, own):
     count = len(parts)
-    size = parts[0].shape[0]
-    out = jax.ShapeDtypeStruct((table.shape[1], size // (2 * xc) * LANES), F32)
+    size = parts[0].shape[0] // 2
     return pl.pallas_call(
-        functools.partial(first_back_kernel, (count, xc)),
-        in_specs=[SMEM] + [ANY] * count + [VMEM],
-        out_shape=[out, out],
+        functools.partial(first_back_kernel, (count, xc, own)),
+        in_specs=[SMEM] + [HBM] * count + [VMEM],
+        out_shape=jax.ShapeDtypeStruct((table.shape[1], size // xc * LANES), F32),
         scratch_shapes=[pltpu.VMEM((count, size, LANES), F32), pltpu.SemaphoreType.DMA((count,))],
-        compiler_params=still(VMEM_MOST),
+        compiler_params=still(),
         cost_estimate=SHORT,
         name="first_back",
     )(place, *parts, table)
@@ -491,7 +492,7 @@
 
 def last_kernel(dims, *refs):
     kz_len, modes, scale = dims
-    wave_y_ref, own_ref, other_ref, wave_x_ref, wave_z_ref, out_ref, rows = refs
+    wave_y_ref, wave_x_ref, wave_z_ref, *sums, out_ref, rows = refs
     pair = 2 * 3 * kz_len
     at = pl.program_id(0)
 
@@ -499,7 +500,7 @@
     def _():
         for tile in range(rows.shape[0] // LANES):
             lanes = slice(tile * LANES, (tile + 1) * LANES)
-            rows[lanes, 0:modes] = (own_ref[:, lanes] + other_ref[:, lanes]).T
+            rows[lanes, 0:modes] = functools.reduce(jnp.add, [part[:, lanes] for part in sums]).T
 
     spec = rows[pl.ds(pl.multiple_of(at * pair, 8), pair), :]
     wide = spec.shape[1]
@@ -544,19 +545,19 @@
             out_ref[comp, y] = (found[comp] * scale)[:, :modes]
 
 
-def last(own, other, wave_y, wave_x, wave_z, ky_len, kz_len, scale):
-    modes, lanes = own.shape
+def last(sums, wave_y, wave_x, wave_z, ky_len, kz_len, scale):
+    modes, lanes = sums[0].shape
     return pl.pallas_call(
         functools.partial(last_kernel, (kz_len, modes, scale)),
         grid=(ky_len // 2,),
-        in_specs=[SMEM, *[whole(a) for a in (own, other, wave_x, wave_z)]],
+        in_specs=[SMEM, *[whole(a) for a in (wave_x, wave_z, *sums)]],
         out_specs=pl.BlockSpec((3, 2, kz_len, modes), lambda i: (0, i, 0, 0)),
         out_shape=jax.ShapeDtypeStruct((3, ky_len, kz_len, modes), F32),
         scratch_shapes=[pltpu.VMEM((lanes, wave_x.shape[1]), F32)],
         compiler_params=params(),
         cost_estimate=SHORT,
         name="last_projection",
-    )(wave_y, own, other, wave_x, wave_z)
+    )(wave_y, wave_x, wave_z, *sums)
 
 
 def after(value, *earlier_values):
@@ -642,7 +643,11 @@
         return lax.ppermute(value, "row", [(src, src ^ 1) for src in range(rows)])
 
     dims = (rows, xc, ky_len, kz_len, cols, y_len, pack)
-    sent = first_synth(place, coeffs, core_swap(coeffs), table_x, (chunks, groups, xc), lanes)
+    shape = (chunks, groups, xc)
+    other = core_swap(coeffs)
+    sent = first_synth(place, coeffs, table_x, shape, lanes, ())
+    sent = first_synth(place, other, table_x, shape, lanes, sent)
+    sent = [list(sent[k * groups : (k + 1) * groups]) for k in range(chunks)]
     latest = sent[0][0]
 
     def ordered(kernel, operands, *others):
@@ -683,8 +688,10 @@
         found = ordered(lambda values: second_back(place, values, table_y, dims), found)
         back[step] = z_exchange(found, *([back[step - 1]] if step else []))
     parts = [value for step in range(chunks) for value in back[step]]
-    away, home = first_back(place, parts, table_x, xc)
-    result = last(home, core_swap(away), wave_y, wave_x, wave_z, ky_len, kz_len, 1.0 / (orders + 1))
+    away = first_back(place, parts, table_x, xc, False)
+    home = first_back(place, parts, after(table_x, away), xc, True)
+    sums = [home, core_swap(away)]
+    result = last(sums, wave_y, wave_x, wave_z, ky_len, kz_len, 1.0 / (orders + 1))
     return result[:, :, :kz_own] if kz_len > kz_own else result
 
 

time: 289 us -> 290 us (level)
  local copies, waits for them, and re-layouts: 7.17 us -> 19.2 us
  starting transfers between devices: 52.8 us -> 44.9 us
    unnamed x32 -> x62, local copies, waits for them, and re-layouts: 4.39 us -> 17.1 us
    ppermute x12, waiting for transfers between devices: 28 us -> 38.2 us  [exchange(): lax.ppermute(value, axis, [(src, src ^ k << shift) for src in range(size)])]
    ppermute x12, starting transfers between devices: 37 us -> 29.2 us  [z_exchange(): lax.ppermute(value, 'row', [(src, src ^ 2 * k) for src in range(rows)])]
    ppermute x2, waiting for transfers between devices: 5.82 us -> 0.01 us  [core_swap(): return lax.ppermute(value, 'row', [(src, src ^ 1) for src in range(rows)])]
    ppermute x12, waiting for transfers between devices: 76.3 us -> 72.5 us  [z_exchange(): lax.ppermute(value, 'row', [(src, src ^ 2 * k) for src in range(rows)])]
    pallas_call x2 -> x4, Pallas kernels: 16.8 us -> 16.7 us  [the longest x2 10.7 us: first_synth(): pl.pallas_call(functools.partial(first_synth_kernel, (*dims, not half)),...]
  transfers between devices with their start and end apart: 26 -> 26, of which waited for: 13 -> 12; matrix products, arithmetic and copies ran while one was open for 1% -> 1% of each run, Pallas kernels for 27% -> 29%
where the time goes in v6:
time: 290 us
  Pallas kernels  114 us (39%)
  waiting for transfers between devices  111 us (38%)
  starting transfers between devices  44.9 us (15%)
  local copies, waits for them, and re-layouts  19.2 us (7%)
    ppermute x12, waiting for transfers between devices, z_exchange(): lax.ppermute(value, 'row', [(src, src ^ 2 * k) for src in range(rows)])  72.5 us
    ppermute x12, waiting for transfers between devices, exchange(): lax.ppermute(value, axis, [(src, src ^ k << shift) for src in range(size)])  38.2 us
    pallas_call x2, Pallas kernels, second_synth(): pl.pallas_call(functools.partial(second_synth_kernel, dims), in_specs=[SM...  29.4 us
    ppermute x12, starting transfers between devices, z_exchange(): lax.ppermute(value, 'row', [(src, src ^ 2 * k) for src in range(rows)])  29.2 us
    pallas_call x2, Pallas kernels, third(): pl.pallas_call(functools.partial(third_kernel, (chunk, *dims)), in_specs=...  29.1 us
    pallas_call x2, Pallas kernels, earlier(): pl.pallas_call(functools.partial(earlier_kernel, orders - 1), grid=(packs...  23.6 us
    unnamed x62, local copies, waits for them, and re-layouts  17.1 us
    ppermute x12, starting transfers between devices, exchange(): lax.ppermute(value, axis, [(src, src ^ k << shift) for src in range(size)])  15.2 us
  transfers between devices with their start and end apart: 26, of which 12 were waited for; matrix products, arithmetic and copies ran while one was open for 1% of the time, Pallas kernels for 29%

profile of v6, /device:TPU:0, one launch (start us, length us, event | category | flops | bytes accessed | tf_op | source)
XLA Modules:
  0.0 289.6 jit_solution(2219593565400544314)
XLA Ops:
  1.5 1.7 copy-done.2
  3.2 5.3 %first_synth.2 = (f32[1024,128]{1,0:T(8,128)S(1)}, f32[1024,128]{1,0:T(8,128)}, f32[1024,128]{1,0:T(8,128)}, f32[1024,128]{1,0:T(8,128)}, f32[1024,128]{1,0:T(8,...) custom-call(s32[3]{0:T(128)S(1)} %pad_add_fusion.place_ref, ...), custom_call_target="tpu_custom_call" | custom-call | flops 1024 | bytes 1024 | tf_op jit(solution)/shard_map/first_synth/pallas_call | solution.py:183
  8.5 5.4 %first_synth.3 = (f32[1024,128]{1,0:T(8,128)S(1)}, f32[1024,128]{1,0:T(8,128)}, f32[1024,128]{1,0:T(8,128)}, f32[1024,128]{1,0:T(8,128)}, f32[1024,128]{1,0:T(8,...) custom-call(s32[3]{0:T(128)S(1)} %pad_add_fusion.place_ref, ...), custom_call_target="tpu_custom_call", output_to_operand_aliasing={{0}: (3, {}), {1}: (4, {}), {2}: (5, {}), {3}: (6, {}), {4}... | custom-call | flops 1024 | bytes 1024 | tf_op jit(solution)/shard_map/first_synth/pallas_call | solution.py:183
  17.9 2.6 collective-permute-start.1
  20.5 2.6 collective-permute-start.2
  24.2 11.8 %earlier_orders.2.refs_6_ = f32[3,16,64,256]{3,2,1,0:T(8,128)S(1)} custom-call(f32[6,3,32,64,256]{4,3,2,1,0:T(8,128)} %refs_4_.5, f32[6,3,32,64,256]{4,3,2,1,0:T(8,128)} %refs_4_.5, f32[6,3,32,64,256]{4,3,2,1,0:T(8,128)} %refs_4_.5, f32[6,3,32,64,256]{4,3,2,1,0:T(8,128)} %refs_4_.5, f32[6,3,32,64,256]{4,3,2,1,0:T(8,128)} %refs_4_.5, ...), custom_call_target="tpu_custom_call" | custom-call | flops 1024 | bytes 1024 | tf_op jit(solution)/shard_map/earlier_orders/pallas_call | solution.py:318
  36.0 11.8 %earlier_orders.3.refs_6_ = f32[3,16,64,256]{3,2,1,0:T(8,128)S(1)} custom-call(f32[6,3,32,64,256]{4,3,2,1,0:T(8,128)} %refs_4_.5, f32[6,3,32,64,256]{4,3,2,1,0:T(8,128)} %refs_4_.5, f32[6,3,32,64,256]{4,3,2,1,0:T(8,128)} %refs_4_.5, f32[6,3,32,64,256]{4,3,2,1,0:T(8,128)} %refs_4_.5, f32[6,3,32,64,256]{4,3,2,1,0:T(8,128)} %refs_4_.5, ...), custom_call_target="tpu_custom_call" | custom-call | flops 1024 | bytes 1024 | tf_op jit(solution)/shard_map/earlier_orders/pallas_call | solution.py:318
  47.8 11.1 %collective-permute-done.2.refs_2_ = f32[1024,128]{1,0:T(8,128)} collective-permute-done((f32[1024,128]{1,0:T(8,128)}, f32[1024,128]{1,0:T(8,128)}, u32[]{:S(2)}, u32[]{:S(2)}) %collective-permute-start.2) | collective-permute-done | bytes 524320 | tf_op jit(solution)/shard_map/ppermute | solution.py:669
  59.0 15.1 %second_synth.2 = (f32[8,240,128]{2,1,0:T(8,128)S(1)}, f32[8,240,128]{2,1,0:T(8,128)S(1)}, f32[8,240,128]{2,1,0:T(8,128)S(1)}, f32[8,240,128]{2,1,0:T(8,128)S(1)}) custom-call(s32[3]{0:T(128)S(1)} %copy-done.30, f32[1024,128]{1,0:T(8,128)S(1)} %copy-done.4, f32[1024,128]{1,0:T(8,128)} %collective-permute-done.1.refs_1_, ...), custom_call_target="tpu_custom_call" | custom-call | flops 1024 | bytes 1024 | tf_op jit(solution)/shard_map/second_synth/pallas_call | solution.py:264
  75.7 2.5 collective-permute-start.9
  78.1 10.1 %collective-permute-start.8 = (f32[1024,128]{1,0:T(8,128)S(1)}, f32[1024,128]{1,0:T(8,128)S(1)}, u32[]{:S(2)}, u32[]{:S(2)}) collective-permute-start(f32[1024,128]{1,0:T(8,128)S(1)} %copy-done.26), channel_id=1, source_target_pairs={{0,16},{4,20},{8,24},{12,28},{16,0},{20,4},{24,8},{28,12},{1,17},{... | collective-permute-start | bytes 1572872 | tf_op jit(solution)/shard_map/ppermute | solution.py:669
  91.5 32.1 %collective-permute-done.8.refs_2_ = f32[1024,128]{1,0:T(8,128)S(1)} collective-permute-done((f32[1024,128]{1,0:T(8,128)S(1)}, f32[1024,128]{1,0:T(8,128)S(1)}, u32[]{:S(2)}, u32[]{:S(2)}) %collective-permute-start.8) | collective-permute-done | bytes 524320 | tf_op jit(solution)/shard_map/ppermute | solution.py:669
  123.6 14.3 %second_synth.3 = (f32[8,240,128]{2,1,0:T(8,128)S(1)}, f32[8,240,128]{2,1,0:T(8,128)S(1)}, f32[8,240,128]{2,1,0:T(8,128)S(1)}, f32[8,240,128]{2,1,0:T(8,128)S(1)}) custom-call(s32[3]{0:T(128)S(1)} %copy-done.30, f32[1024,128]{1,0:T(8,128)S(1)} %copy-done.6, f32[1024,128]{1,0:T(8,128)S(1)} %collective-permute-done.7.refs_1_, ...), custom_call_target="tpu_custom_call" | custom-call | flops 1024 | bytes 1024 | tf_op jit(solution)/shard_map/second_synth/pallas_call | solution.py:264
  141.4 14.6 %third_dimension.2 = (f32[8,120,128]{2,1,0:T(8,128)S(1)}, f32[8,120,128]{2,1,0:T(8,128)S(1)}, f32[8,120,128]{2,1,0:T(8,128)S(1)}, f32[8,120,128]{2,1,0:T(8,128)S(1)}) custom-call(s32[3]{0:T(128)S(1)} %copy-done.30, f32[8,240,128]{2,1,0:T(8,128)S(1)} %get-tuple-element.116.refs_0_, f32[8,240,128]{2,1,0:T(8,128)S(1)} %collective-permute-done.4.refs_1_, ...), custom_call_target="tpu_custom_call" | custom-call | flops 1024 | bytes 1024 | tf_op jit(solution)/shard_map/third_dimension/pallas_call | solution.py:388
  158.1 4.4 %collective-permute-done.13.refs_1_ = f32[8,240,128]{2,1,0:T(8,128)S(1)} collective-permute-done((f32[8,240,128]{2,1,0:T(8,128)S(1)}, f32[8,240,128]{2,1,0:T(8,128)S(1)}, u32[]{:S(2)}, u32[]{:S(2)}) %collective-permute-start.13) | collective-permute-done | bytes 983072 | tf_op jit(solution)/shard_map/ppermute | solution.py:638
  164.0 19.7 %collective-permute-done.14.refs_2_ = f32[8,240,128]{2,1,0:T(8,128)S(1)} collective-permute-done((f32[8,240,128]{2,1,0:T(8,128)S(1)}, f32[8,240,128]{2,1,0:T(8,128)S(1)}, u32[]{:S(2)}, u32[]{:S(2)}) %collective-permute-start.14) | collective-permute-done | bytes 983072 | tf_op jit(solution)/shard_map/ppermute | solution.py:638
  184.7 14.6 %third_dimension.3 = (f32[8,120,128]{2,1,0:T(8,128)S(1)}, f32[8,120,128]{2,1,0:T(8,128)S(1)}, f32[8,120,128]{2,1,0:T(8,128)S(1)}, f32[8,120,128]{2,1,0:T(8,128)S(1)}) custom-call(s32[3]{0:T(128)S(1)} %copy-done.30, f32[8,240,128]{2,1,0:T(8,128)S(1)} %get-tuple-element.127.refs_0_, f32[8,240,128]{2,1,0:T(8,128)S(1)} %collective-permute-done.13.refs_1_, ...), custom_call_target="tpu_custom_call" | custom-call | flops 1024 | bytes 1024 | tf_op jit(solution)/shard_map/third_dimension/pallas_call | solution.py:388
  202.8 3.0 %collective-permute-done.12.refs_3_ = f32[8,120,128]{2,1,0:T(8,128)S(1)} collective-permute-done((f32[8,120,128]{2,1,0:T(8,128)S(1)}, f32[8,120,128]{2,1,0:T(8,128)S(1)}, u32[]{:S(2)}, u32[]{:S(2)}) %collective-permute-start.12) | collective-permute-done | bytes 491552 | tf_op jit(solution)/shard_map/ppermute | solution.py:638
  205.8 4.7 %second_back.2 = (f32[608,128]{1,0:T(8,128)S(1)}, f32[608,128]{1,0:T(8,128)S(1)}, f32[608,128]{1,0:T(8,128)S(1)}, f32[608,128]{1,0:T(8,128)S(1)}) custom-call(s32[3]{0:T(128)S(1)} %copy-done.30, f32[8,120,128]{2,1,0:T(8,128)S(1)} %get-tuple-element.132.refs_0_, f32[8,120,128]{2,1,0:T(8,128)S(1)} %collective-permute-done.10.refs_1_, ...), custom_call_target="tpu_custom_call" | custom-call | flops 1024 | bytes 1024 | tf_op jit(solution)/shard_map/second_back/pallas_call | solution.py:446
  210.6 2.9 collective-permute-start.17
  213.4 1.9 collective-permute-done.19.refs_1_
  215.3 2.3 collective-permute-start.18
  217.6 8.3 %collective-permute-done.21.refs_3_ = f32[8,120,128]{2,1,0:T(8,128)S(1)} collective-permute-done((f32[8,120,128]{2,1,0:T(8,128)S(1)}, f32[8,120,128]{2,1,0:T(8,128)S(1)}, u32[]{:S(2)}, u32[]{:S(2)}) %collective-permute-start.21) | collective-permute-done | bytes 491552 | tf_op jit(solution)/shard_map/ppermute | solution.py:638
  225.9 4.7 %second_back.3 = (f32[608,128]{1,0:T(8,128)S(1)}, f32[608,128]{1,0:T(8,128)S(1)}, f32[608,128]{1,0:T(8,128)S(1)}, f32[608,128]{1,0:T(8,128)S(1)}) custom-call(s32[3]{0:T(128)S(1)} %copy-done.30, f32[8,120,128]{2,1,0:T(8,128)S(1)} %get-tuple-element.143.refs_0_, f32[8,120,128]{2,1,0:T(8,128)S(1)} %collective-permute-done.19.refs_1_, ...), custom_call_target="tpu_custom_call" | custom-call | flops 1024 | bytes 1024 | tf_op jit(solution)/shard_map/second_back/pallas_call | solution.py:446
  230.6 7.9 %collective-permute-done.17.refs_2_ = f32[608,128]{1,0:T(8,128)S(1)} collective-permute-done((f32[608,128]{1,0:T(8,128)S(1)}, f32[608,128]{1,0:T(8,128)S(1)}, u32[]{:S(2)}, u32[]{:S(2)}) %collective-permute-start.17) | collective-permute-done | bytes 311328 | tf_op jit(solution)/shard_map/ppermute | solution.py:669
  238.5 2.3 collective-permute-start.24
  240.8 3.6 %collective-permute-start.23 = (f32[608,128]{1,0:T(8,128)S(1)}, f32[608,128]{1,0:T(8,128)S(1)}, u32[]{:S(2)}, u32[]{:S(2)}) collective-permute-start(f32[608,128]{1,0:T(8,128)S(1)} %get-tuple-element.151), channel_id=1, source_target_pairs={{0,16},{4,20},{8,24},{12,28},{16,0},{20,4},{24,8},{28,12},{1,17},{... | collective-permute-start | bytes 933896 | tf_op jit(solution)/shard_map/ppermute | solution.py:669
  244.5 5.7 %collective-permute-done.24.refs_7_ = f32[608,128]{1,0:T(8,128)S(1)} collective-permute-done((f32[608,128]{1,0:T(8,128)S(1)}, f32[608,128]{1,0:T(8,128)S(1)}, u32[]{:S(2)}, u32[]{:S(2)}) %collective-permute-start.24) | collective-permute-done | bytes 311328 | tf_op jit(solution)/shard_map/ppermute | solution.py:669
  250.1 15.7 %collective-permute-done.23.refs_6_ = f32[608,128]{1,0:T(8,128)S(1)} collective-permute-done((f32[608,128]{1,0:T(8,128)S(1)}, f32[608,128]{1,0:T(8,128)S(1)}, u32[]{:S(2)}, u32[]{:S(2)}) %collective-permute-start.23) | collective-permute-done | bytes 311328 | tf_op jit(solution)/shard_map/ppermute | solution.py:669
  265.8 3.0 %first_back.2 = f32[160,2432]{1,0:T(8,128)S(1)} custom-call(s32[3]{0:T(128)S(1)} %copy-done.30, f32[608,128]{1,0:T(8,128)S(1)} %get-tuple-element.136.refs_0_, f32[608,128]{1,0:T(8,128)S(1)} %collective-permute-done.16.refs_1_, f32[608,128]{1,0:T(8,128)S(1)} %collective-permute-done.17.refs_2_, f32[608,128]{1,0:T(8,128)S(1)} %collective-permute-done.18.refs_3_, ...), custom_call_target="tpu_custom_call" | custom-call | flops 1024 | bytes 1024 | tf_op jit(solution)/shard_map/first_back/pallas_call | solution.py:482
  280.3 3.0 %first_back.3.refs_3_ = f32[160,2432]{1,0:T(8,128)S(1)} custom-call(s32[3]{0:T(128)S(1)} %copy-done.30, f32[608,128]{1,0:T(8,128)S(1)} %copy-done.8, f32[608,128]{1,0:T(8,128)S(1)} %copy-done.10, f32[608,128]{1,0:T(8,128)S(1)} %copy-done.12, f32[608,128]{1,0:T(8,128)S(1)} %copy-done.14, f32[608,128]{1,0:T(8,128)S(1)} %copy-done.16, ...), custom_call_target="tpu_custom_call" | custom-call | flops 1024 | bytes 1024 | tf_op jit(solution)/shard_map/first_back/pallas_call | solution.py:482
  283.4 6.2 %last_projection.1 = f32[3,20,40,160]{3,2,1,0:T(8,128)} custom-call(f32[10]{0:T(128)S(1)} %convert_multiply_fusion.1.refs_0_, f32[8,256]{1,0:T(8,128)S(1)} %broadcast_in_dim.9.refs_1_, f32[40,256]{1,0:T(8,128)S(1)} %broadcast_in_dim.18.refs_2_, f32[160,2432]{1,0:T(8,128)S(1)} %first_back.3.refs_3_, f32[160,2432]{1,0:T(8,128)S(1)} %collective-permute-done.25.refs_4_), custom_call_target="tpu_custom_call" | custom-call | flops 1024 | bytes 1024 | tf_op jit(solution)/shard_map/last_projection/pallas_call | solution.py:550
  (103 shorter events, 34.6 us)
Async XLA Ops:
  0.0 8.5 %collective-permute-start = (f32[3,20,40,160]{3,2,1,0:T(8,128)}, f32[3,20,40,160]{3,2,1,0:T(8,128)S(1)}, u32[]{:S(2)}, u32[]{:S(2)}) collective-permute-start(f32[3,20,40,160]{3,2,1,0:T(8,128)} %data_ref.1), channel_id=1, source_target_pairs={{0,4},{4,0},{8,12},{12,8},{16,20},{20,16},{24,28},{28,24},{1,5},{5... | collective-permute-start | bytes 4608008 | tf_op jit(solution)/shard_map/ppermute | solution.py:643
  17.9 29.9 %collective-permute-start.1 = (f32[1024,128]{1,0:T(8,128)}, f32[1024,128]{1,0:T(8,128)}, u32[]{:S(2)}, u32[]{:S(2)}) collective-permute-start(f32[1024,128]{1,0:T(8,128)} %get-tuple-element.89), channel_id=1, source_target_pairs={{0,8},{4,12},{8,0},{12,4},{16,24},{20,28},{24,16},{28,20},{1,9},{5... | collective-permute-start | bytes 1572872 | tf_op jit(solution)/shard_map/ppermute | solution.py:669
  20.5 38.5 %collective-permute-start.2 = (f32[1024,128]{1,0:T(8,128)}, f32[1024,128]{1,0:T(8,128)}, u32[]{:S(2)}, u32[]{:S(2)}) collective-permute-start(f32[1024,128]{1,0:T(8,128)} %get-tuple-element.90), channel_id=1, source_target_pairs={{0,16},{4,20},{8,24},{12,28},{16,0},{20,4},{24,8},{28,12},{1,17},{... | collective-permute-start | bytes 1572872 | tf_op jit(solution)/shard_map/ppermute | solution.py:669
  23.1 35.9 %collective-permute-start.3 = (f32[1024,128]{1,0:T(8,128)}, f32[1024,128]{1,0:T(8,128)}, u32[]{:S(2)}, u32[]{:S(2)}) collective-permute-start(f32[1024,128]{1,0:T(8,128)} %get-tuple-element.91), channel_id=1, source_target_pairs={{0,24},{4,28},{8,16},{12,20},{16,8},{20,12},{24,0},{28,4},{1,25},{... | collective-permute-start | bytes 1572872 | tf_op jit(solution)/shard_map/ppermute | solution.py:669
  47.8 27.9 %copy-start.28 = (f32[1024,128]{1,0:T(8,128)S(1)}, f32[1024,128]{1,0:T(8,128)}, u32[]{:S(2)}) copy-start(f32[1024,128]{1,0:T(8,128)} %copy-done.27) | copy-start | bytes 1572868
  47.8 30.3 %copy-start.26 = (f32[1024,128]{1,0:T(8,128)S(1)}, f32[1024,128]{1,0:T(8,128)}, u32[]{:S(2)}) copy-start(f32[1024,128]{1,0:T(8,128)} %copy-done.25) | copy-start | bytes 1572868
  47.8 40.4 %copy-start.24 = (f32[1024,128]{1,0:T(8,128)S(1)}, f32[1024,128]{1,0:T(8,128)}, u32[]{:S(2)}) copy-start(f32[1024,128]{1,0:T(8,128)} %copy-done.23) | copy-start | bytes 1572868
  47.8 75.8 %copy-start.6 = (f32[1024,128]{1,0:T(8,128)S(1)}, f32[1024,128]{1,0:T(8,128)}, u32[]{:S(2)}) copy-start(f32[1024,128]{1,0:T(8,128)} %copy-done.5) | copy-start | bytes 1572868
  74.1 65.9 %collective-permute-start.4 = (f32[8,240,128]{2,1,0:T(8,128)S(1)}, f32[8,240,128]{2,1,0:T(8,128)S(1)}, u32[]{:S(2)}, u32[]{:S(2)}) collective-permute-start(f32[8,240,128]{2,1,0:T(8,128)S(1)} %get-tuple-element.101), channel_id=1, source_target_pairs={{0,1},{1,0},{2,3},{3,2},{4,5},{5,4},{6,7},{7,6},{8,9},{9,8},{10,11... | collective-permute-start | bytes 2949128 | tf_op jit(solution)/shard_map/ppermute | solution.py:638
  75.7 14.4 %collective-permute-start.9 = (f32[1024,128]{1,0:T(8,128)S(1)}, f32[1024,128]{1,0:T(8,128)S(1)}, u32[]{:S(2)}, u32[]{:S(2)}) collective-permute-start(f32[1024,128]{1,0:T(8,128)S(1)} %copy-done.28), channel_id=1, source_target_pairs={{0,24},{4,28},{8,16},{12,20},{16,8},{20,12},{24,0},{28,4},{1,25},{... | collective-permute-start | bytes 1572872 | tf_op jit(solution)/shard_map/ppermute | solution.py:669
  78.1 45.4 %collective-permute-start.8 = (f32[1024,128]{1,0:T(8,128)S(1)}, f32[1024,128]{1,0:T(8,128)S(1)}, u32[]{:S(2)}, u32[]{:S(2)}) collective-permute-start(f32[1024,128]{1,0:T(8,128)S(1)} %copy-done.26), channel_id=1, source_target_pairs={{0,16},{4,20},{8,24},{12,28},{16,0},{20,4},{24,8},{28,12},{1,17},{... | collective-permute-start | bytes 1572872 | tf_op jit(solution)/shard_map/ppermute | solution.py:669
  88.2 35.3 %collective-permute-start.7 = (f32[1024,128]{1,0:T(8,128)S(1)}, f32[1024,128]{1,0:T(8,128)S(1)}, u32[]{:S(2)}, u32[]{:S(2)}) collective-permute-start(f32[1024,128]{1,0:T(8,128)S(1)} %copy-done.24), channel_id=1, source_target_pairs={{0,8},{4,12},{8,0},{12,4},{16,24},{20,28},{24,16},{28,20},{1,9},{5... | collective-permute-start | bytes 1572872 | tf_op jit(solution)/shard_map/ppermute | solution.py:669
  88.4 53.0 %collective-permute-start.5 = (f32[8,240,128]{2,1,0:T(8,128)S(1)}, f32[8,240,128]{2,1,0:T(8,128)S(1)}, u32[]{:S(2)}, u32[]{:S(2)}) collective-permute-start(f32[8,240,128]{2,1,0:T(8,128)S(1)} %get-tuple-element.102), channel_id=1, source_target_pairs={{0,2},{1,3},{2,0},{3,1},{4,6},{5,7},{6,4},{7,5},{8,10},{9,11},{10,... | collective-permute-start | bytes 2949128 | tf_op jit(solution)/shard_map/ppermute | solution.py:638
  90.0 51.4 %collective-permute-start.6 = (f32[8,240,128]{2,1,0:T(8,128)S(1)}, f32[8,240,128]{2,1,0:T(8,128)S(1)}, u32[]{:S(2)}, u32[]{:S(2)}) collective-permute-start(f32[8,240,128]{2,1,0:T(8,128)S(1)} %get-tuple-element.103), channel_id=1, source_target_pairs={{0,3},{1,2},{2,1},{3,0},{4,7},{5,6},{6,5},{7,4},{8,11},{9,10},{10,... | collective-permute-start | bytes 2949128 | tf_op jit(solution)/shard_map/ppermute | solution.py:638
  137.9 24.7 %collective-permute-start.13 = (f32[8,240,128]{2,1,0:T(8,128)S(1)}, f32[8,240,128]{2,1,0:T(8,128)S(1)}, u32[]{:S(2)}, u32[]{:S(2)}) collective-permute-start(f32[8,240,128]{2,1,0:T(8,128)S(1)} %get-tuple-element.124), channel_id=1, source_target_pairs={{0,1},{1,0},{2,3},{3,2},{4,5},{5,4},{6,7},{7,6},{8,9},{9,8},{10,11... | collective-permute-start | bytes 2949128 | tf_op jit(solution)/shard_map/ppermute | solution.py:638
  138.5 45.2 %collective-permute-start.14 = (f32[8,240,128]{2,1,0:T(8,128)S(1)}, f32[8,240,128]{2,1,0:T(8,128)S(1)}, u32[]{:S(2)}, u32[]{:S(2)}) collective-permute-start(f32[8,240,128]{2,1,0:T(8,128)S(1)} %get-tuple-element.125), channel_id=1, source_target_pairs={{0,2},{1,3},{2,0},{3,1},{4,6},{5,7},{6,4},{7,5},{8,10},{9,11},{10,... | collective-permute-start | bytes 2949128 | tf_op jit(solution)/shard_map/ppermute | solution.py:638
  140.0 44.7 %collective-permute-start.15 = (f32[8,240,128]{2,1,0:T(8,128)S(1)}, f32[8,240,128]{2,1,0:T(8,128)S(1)}, u32[]{:S(2)}, u32[]{:S(2)}) collective-permute-start(f32[8,240,128]{2,1,0:T(8,128)S(1)} %get-tuple-element.126), channel_id=1, source_target_pairs={{0,3},{1,2},{2,1},{3,0},{4,7},{5,6},{6,5},{7,4},{8,11},{9,10},{10,... | collective-permute-start | bytes 2949128 | tf_op jit(solution)/shard_map/ppermute | solution.py:638
  156.0 45.9 %collective-permute-start.10 = (f32[8,120,128]{2,1,0:T(8,128)S(1)}, f32[8,120,128]{2,1,0:T(8,128)S(1)}, u32[]{:S(2)}, u32[]{:S(2)}) collective-permute-start(f32[8,120,128]{2,1,0:T(8,128)S(1)} %get-tuple-element.121), channel_id=1, source_target_pairs={{0,1},{1,0},{2,3},{3,2},{4,5},{5,4},{6,7},{7,6},{8,9},{9,8},{10,11... | collective-permute-start | bytes 1474568 | tf_op jit(solution)/shard_map/ppermute | solution.py:638
  156.6 46.2 %collective-permute-start.11 = (f32[8,120,128]{2,1,0:T(8,128)S(1)}, f32[8,120,128]{2,1,0:T(8,128)S(1)}, u32[]{:S(2)}, u32[]{:S(2)}) collective-permute-start(f32[8,120,128]{2,1,0:T(8,128)S(1)} %get-tuple-element.122), channel_id=1, source_target_pairs={{0,2},{1,3},{2,0},{3,1},{4,6},{5,7},{6,4},{7,5},{8,10},{9,11},{10,... | collective-permute-start | bytes 1474568 | tf_op jit(solution)/shard_map/ppermute | solution.py:638
  162.6 43.2 %collective-permute-start.12 = (f32[8,120,128]{2,1,0:T(8,128)S(1)}, f32[8,120,128]{2,1,0:T(8,128)S(1)}, u32[]{:S(2)}, u32[]{:S(2)}) collective-permute-start(f32[8,120,128]{2,1,0:T(8,128)S(1)} %get-tuple-element.123), channel_id=1, source_target_pairs={{0,3},{1,2},{2,1},{3,0},{4,7},{5,6},{6,5},{7,4},{8,11},{9,10},{10,... | collective-permute-start | bytes 1474568 | tf_op jit(solution)/shard_map/ppermute | solution.py:638
  199.2 16.1 %collective-permute-start.19 = (f32[8,120,128]{2,1,0:T(8,128)S(1)}, f32[8,120,128]{2,1,0:T(8,128)S(1)}, u32[]{:S(2)}, u32[]{:S(2)}) collective-permute-start(f32[8,120,128]{2,1,0:T(8,128)S(1)} %get-tuple-element.140), channel_id=1, source_target_pairs={{0,1},{1,0},{2,3},{3,2},{4,5},{5,4},{6,7},{7,6},{8,9},{9,8},{10,11... | collective-permute-start | bytes 1474568 | tf_op jit(solution)/shard_map/ppermute | solution.py:638
  200.3 17.3 %collective-permute-start.20 = (f32[8,120,128]{2,1,0:T(8,128)S(1)}, f32[8,120,128]{2,1,0:T(8,128)S(1)}, u32[]{:S(2)}, u32[]{:S(2)}) collective-permute-start(f32[8,120,128]{2,1,0:T(8,128)S(1)} %get-tuple-element.141), channel_id=1, source_target_pairs={{0,2},{1,3},{2,0},{3,1},{4,6},{5,7},{6,4},{7,5},{8,10},{9,11},{10,... | collective-permute-start | bytes 1474568 | tf_op jit(solution)/shard_map/ppermute | solution.py:638
  201.9 24.0 %collective-permute-start.21 = (f32[8,120,128]{2,1,0:T(8,128)S(1)}, f32[8,120,128]{2,1,0:T(8,128)S(1)}, u32[]{:S(2)}, u32[]{:S(2)}) collective-permute-start(f32[8,120,128]{2,1,0:T(8,128)S(1)} %get-tuple-element.142), channel_id=1, source_target_pairs={{0,3},{1,2},{2,1},{3,0},{4,7},{5,6},{6,5},{7,4},{8,11},{9,10},{10,... | collective-permute-start | bytes 1474568 | tf_op jit(solution)/shard_map/ppermute | solution.py:638
  210.5 58.4 %copy-start.7 = (f32[608,128]{1,0:T(8,128)}, f32[608,128]{1,0:T(8,128)S(1)}, u32[]{:S(2)}) copy-start(f32[608,128]{1,0:T(8,128)S(1)} %get-tuple-element.136.refs_0_) | copy-start | bytes 933892
  210.5 55.3 %copy-start.1 = (bf16[4,160,128]{2,1,0:T(8,128)(2,1)S(1)}, bf16[4,160,128]{2,1,0:T(8,128)(2,1)}, u32[]{:S(2)}) copy-start(bf16[4,160,128]{2,1,0:T(8,128)(2,1)} %copy-done) | copy-start | bytes 491524
  210.5 20.1 %collective-permute-start.16 = (f32[608,128]{1,0:T(8,128)S(1)}, f32[608,128]{1,0:T(8,128)S(1)}, u32[]{:S(2)}, u32[]{:S(2)}) collective-permute-start(f32[608,128]{1,0:T(8,128)S(1)} %get-tuple-element.137), channel_id=1, source_target_pairs={{0,8},{4,12},{8,0},{12,4},{16,24},{20,28},{24,16},{28,20},{1,9},{5... | collective-permute-start | bytes 933896 | tf_op jit(solution)/shard_map/ppermute | solution.py:669
  210.6 27.9 %collective-permute-start.17 = (f32[608,128]{1,0:T(8,128)S(1)}, f32[608,128]{1,0:T(8,128)S(1)}, u32[]{:S(2)}, u32[]{:S(2)}) collective-permute-start(f32[608,128]{1,0:T(8,128)S(1)} %get-tuple-element.138), channel_id=1, source_target_pairs={{0,16},{4,20},{8,24},{12,28},{16,0},{20,4},{24,8},{28,12},{1,17},{... | collective-permute-start | bytes 933896 | tf_op jit(solution)/shard_map/ppermute | solution.py:669
  215.3 23.2 %collective-permute-start.18 = (f32[608,128]{1,0:T(8,128)S(1)}, f32[608,128]{1,0:T(8,128)S(1)}, u32[]{:S(2)}, u32[]{:S(2)}) collective-permute-start(f32[608,128]{1,0:T(8,128)S(1)} %get-tuple-element.139), channel_id=1, source_target_pairs={{0,24},{4,28},{8,16},{12,20},{16,8},{20,12},{24,0},{28,4},{1,25},{... | collective-permute-start | bytes 933896 | tf_op jit(solution)/shard_map/ppermute | solution.py:669
  238.5 11.6 %collective-permute-start.24 = (f32[608,128]{1,0:T(8,128)S(1)}, f32[608,128]{1,0:T(8,128)S(1)}, u32[]{:S(2)}, u32[]{:S(2)}) collective-permute-start(f32[608,128]{1,0:T(8,128)S(1)} %get-tuple-element.153), channel_id=1, source_target_pairs={{0,24},{4,28},{8,16},{12,20},{16,8},{20,12},{24,0},{28,4},{1,25},{... | collective-permute-start | bytes 933896 | tf_op jit(solution)/shard_map/ppermute | solution.py:669
  240.8 24.9 %collective-permute-start.23 = (f32[608,128]{1,0:T(8,128)S(1)}, f32[608,128]{1,0:T(8,128)S(1)}, u32[]{:S(2)}, u32[]{:S(2)}) collective-permute-start(f32[608,128]{1,0:T(8,128)S(1)} %get-tuple-element.151), channel_id=1, source_target_pairs={{0,16},{4,20},{8,24},{12,28},{16,0},{20,4},{24,8},{28,12},{1,17},{... | collective-permute-start | bytes 933896 | tf_op jit(solution)/shard_map/ppermute | solution.py:669
  244.5 21.3 %collective-permute-start.22 = (f32[608,128]{1,0:T(8,128)S(1)}, f32[608,128]{1,0:T(8,128)S(1)}, u32[]{:S(2)}, u32[]{:S(2)}) collective-permute-start(f32[608,128]{1,0:T(8,128)S(1)} %get-tuple-element.149), channel_id=1, source_target_pairs={{0,8},{4,12},{8,0},{12,4},{16,24},{20,28},{24,16},{28,20},{1,9},{5... | collective-permute-start | bytes 933896 | tf_op jit(solution)/shard_map/ppermute | solution.py:669
  272.5 10.8 %collective-permute-start.25 = (f32[160,2432]{1,0:T(8,128)S(1)}, f32[160,2432]{1,0:T(8,128)S(1)}, u32[]{:S(2)}, u32[]{:S(2)}) collective-permute-start(f32[160,2432]{1,0:T(8,128)S(1)} %first_back.2), channel_id=1, source_target_pairs={{0,4},{4,0},{8,12},{12,8},{16,20},{20,16},{24,28},{28,24},{1,5},{5... | collective-permute-start | bytes 4669448 | tf_op jit(solution)/shard_map/ppermute | solution.py:643
  (25 other events, 92.4 us)

commit v7 on v6

--- a/solution.py
+++ b/solution.py
@@ -11,7 +11,12 @@
 from jax.sharding import PartitionSpec as P
 
 LANES = 128
-XC = 16
+
+
+def chunk_sizes(x_len):
+    ends = 8
+    return [ends, x_len - 2 * ends, ends] if x_len > 3 * ends else [ends] * (x_len // ends)
+
 BF16 = jnp.bfloat16
 F32 = jnp.float32
 NN = (((1,), (0,)), ((), ()))
@@ -98,12 +103,6 @@
     return pltpu.CompilerParams(vmem_limit_bytes=limit)
 
 
-def finish(held, out_refs, sem):
-    for at in range(held.shape[1]):
-        for k, out in enumerate(out_refs):
-            pltpu.make_async_copy(held.at[k, at], out.at[at], sem.at[k, at]).wait()
-
-
 def both_passes(values, high_low, high):
     top, rest = pieces_of(values)
     wide = dot(top, high_low, NN)
@@ -117,13 +116,11 @@
 
 
 def first_synth_kernel(dims, place_ref, data_ref, table_ref, *rest):
-    chunks, dests, xc, own = dims
-    count = chunks * dests
-    outs = rest[-count - 5 : -5]
-    data, rows, held, sem, out_sem = rest[-5:]
+    sizes, chosen, dests, own = dims
+    outs = rest[-len(chosen) * dests - 3 : -3]
+    data, rows, sem = rest[-3:]
     _, ky_len, kz_len, _ = data.shape
     group = 5 * kz_len
-    size = held.shape[1]
     copies = [
         pltpu.make_async_copy(data_ref.at[comp], data.at[comp], sem.at[comp]) for comp in range(3)
     ]
@@ -158,40 +155,34 @@
 
     lax.fori_loop(0, ky_len // step, body, 0)
 
+    core = place_ref[1] if own else 1 - place_ref[1]
+
     def flip(tile, carry):
         found = rows[pl.ds(pl.multiple_of(tile * LANES, LANES), LANES), :].T
-        for idx in range(count):
-            held[idx, pl.ds(pl.multiple_of(tile * xc, 8), xc), :] = found[idx * xc : (idx + 1) * xc]
+        for idx, out in enumerate(outs):
+            chunk, k = chosen[idx // dests], idx % dests
+            xc = sizes[chunk]
+            at = sum(sizes[:chunk]) * dests + k * xc
+            spot = core * (out.shape[0] // 2) + tile * xc
+            out[pl.ds(pl.multiple_of(spot, 8), xc), :] = found[at : at + xc]
         return carry
 
     lax.fori_loop(0, rows.shape[0] // LANES, flip, 0, unroll=2)
-    core = place_ref[1] if own else 1 - place_ref[1]
-    spot = pl.ds(pl.multiple_of(core * size, 8), size)
-    copies = [
-        pltpu.make_async_copy(held.at[k], out.at[spot, :], out_sem.at[k]) for k, out in enumerate(outs)
-    ]
-    for copy in copies:
-        copy.start()
-    for copy in copies:
-        copy.wait()
-
-
-def first_synth(place, coeffs, table, dims, lanes, half):
-    chunks, dests, xc = dims
-    size = lanes // LANES * xc
-    count = chunks * dests
+
+
+def first_synth(place, coeffs, table, dims, chosen, lanes, half):
+    sizes, dests = dims
+    heights = [2 * (lanes // LANES) * sizes[chunk] for chunk in chosen for _ in range(dests)]
     return pl.pallas_call(
-        functools.partial(first_synth_kernel, (*dims, not half)),
-        in_specs=[SMEM, ANY, VMEM] + [HBM] * len(half),
-        out_specs=[HBM] * count,
-        out_shape=[jax.ShapeDtypeStruct((2 * size, LANES), F32)] * count,
+        functools.partial(first_synth_kernel, (sizes, chosen, dests, not half)),
+        in_specs=[SMEM, ANY, VMEM] + [ANY] * len(half),
+        out_specs=[VMEM] * len(heights),
+        out_shape=[jax.ShapeDtypeStruct((h, LANES), F32) for h in heights],
         input_output_aliases={3 + k: k for k in range(len(half))},
         scratch_shapes=[
             pltpu.VMEM(coeffs.shape, F32),
             pltpu.VMEM((lanes, LANES), F32),
-            pltpu.VMEM((count, size, LANES), F32),
             pltpu.SemaphoreType.DMA((3,)),
-            pltpu.SemaphoreType.DMA((count,)),
         ],
         compiler_params=still(),
         cost_estimate=SHORT,
@@ -202,8 +193,8 @@
 def second_synth_kernel(dims, place_ref, *refs):
     rows, xc, ky_len, kz_len, cols, y_len, pack = dims
     groups = rows // 2
-    parts, table_ref, out_refs = refs[:groups], refs[groups], refs[groups + 1 : -3]
-    a_ref, held, sem = refs[-3:]
+    parts, table_ref, out_refs = refs[:groups], refs[groups], refs[groups + 1 : -1]
+    a_ref = refs[-1]
     size = parts[0].shape[0] // 2
     stride = a_ref.shape[0] // rows
     for k, part in enumerate(parts):
@@ -248,14 +239,12 @@
             )
         for dest in range(cols):
             tile, off = divmod(dest * y_len, LANES)
-            held[dest, at] = lane_pack(
+            out_refs[dest][at] = lane_pack(
                 [f[:, tile * LANES : (tile + 1) * LANES] for f in fields], y_len, off
             )[0]
-            pltpu.make_async_copy(held.at[dest, at], out_refs[dest].at[at], sem.at[dest, at]).start()
         return carry
 
     lax.fori_loop(0, xc // pack, body, 0)
-    finish(held, out_refs, sem)
 
 
 def second_synth(place, arrived, table, dims):
@@ -264,12 +253,10 @@
     return pl.pallas_call(
         functools.partial(second_synth_kernel, dims),
         in_specs=[SMEM] + [VMEM] * (len(arrived) + 1),
-        out_specs=[HBM] * cols,
+        out_specs=[VMEM] * cols,
         out_shape=[jax.ShapeDtypeStruct((packs, 6 * kz_len, LANES), F32)] * cols,
         scratch_shapes=[
             pltpu.VMEM((rows * (arrived[0].shape[0] // 2 + 8), LANES), F32),
-            pltpu.VMEM((cols, packs, 6 * kz_len, LANES), F32),
-            pltpu.SemaphoreType.DMA((cols, packs)),
         ],
         compiler_params=still(),
         cost_estimate=SHORT,
@@ -305,13 +292,13 @@
         lax.fori_loop(0, y_len // 8, body, 0, unroll=2)
 
 
-def earlier(velocity, vorticity, chunk, xc, pack):
+def earlier(velocity, vorticity, start, xc, pack):
     orders, _, _, y_len, grid_len = velocity.shape
     packs = xc // pack
     block = (1, 3, pack, y_len, grid_len)
 
     def at(order):
-        return pl.BlockSpec(block, lambda i: (order, 0, chunk * packs + i, 0, 0))
+        return pl.BlockSpec(block, lambda i: (order, 0, start // pack + i, 0, 0))
 
     specs = [at(k) for k in range(1, orders)] + [at(orders - k) for k in range(1, orders)]
     size = xc * y_len * grid_len
@@ -328,17 +315,17 @@
 
 
 def third_kernel(dims, place_ref, *refs):
-    chunk, kz_len, cols, y_len, pack = dims
+    begin, kz_len, cols, y_len, pack = dims
     b_refs, stored_refs, table_ref = refs[:cols], refs[cols : cols + 3], refs[cols + 3]
-    data, sem, held, out_sem = refs[-4:]
-    out_refs = refs[-4 - cols : -4]
+    data, sem = refs[-2:]
+    out_refs = refs[-2 - cols : -2]
     grid_len = table_ref.shape[2]
     xc = data.shape[2]
     packs = xc // pack
 
     def copies(at):
         spot = pl.ds(at * pack, pack)
-        far = pl.ds(chunk * xc + at * pack, pack)
+        far = pl.ds(begin + at * pack, pack)
         sources = [ref.at[0, :, far] for ref in stored_refs[:2]] + [stored_refs[2].at[:, spot]]
         return [
             pltpu.make_async_copy(source, data.at[idx, :, spot], sem.at[idx, at])
@@ -371,30 +358,26 @@
         result = dot_data_right(table_ref[0], table_ref[1], jnp.concatenate(total, axis=0))
         for k in range(cols):
             for comp in range(3):
-                held[k, at, comp * kz_len : (comp + 1) * kz_len, :] = result[
+                out_refs[k][at, comp * kz_len : (comp + 1) * kz_len, :] = result[
                     k * kz_len : (k + 1) * kz_len, comp * LANES : (comp + 1) * LANES
                 ]
-            pltpu.make_async_copy(held.at[k, at], out_refs[k].at[at], out_sem.at[k, at]).start()
         return carry
 
     lax.fori_loop(0, packs, body, 0)
-    finish(held, out_refs, out_sem)
-
-
-def third(place, arrived, velocity, vorticity, base, table, chunk, dims):
+
+
+def third(place, arrived, velocity, vorticity, base, table, begin, dims):
     kz_len, cols, y_len, pack = dims
     packs = arrived[0].shape[0]
     grid_len = velocity.shape[-1]
     return pl.pallas_call(
-        functools.partial(third_kernel, (chunk, *dims)),
+        functools.partial(third_kernel, (begin, *dims)),
         in_specs=[SMEM] + [VMEM] * cols + [ANY] * 3 + [VMEM],
-        out_specs=[HBM] * cols,
+        out_specs=[VMEM] * cols,
         out_shape=[jax.ShapeDtypeStruct((packs, 3 * kz_len, LANES), F32)] * cols,
         scratch_shapes=[
             pltpu.VMEM((3, 3, packs * pack, y_len, grid_len), F32),
             pltpu.SemaphoreType.DMA((3, packs)),
-            pltpu.VMEM((cols, packs, 3 * kz_len, LANES), F32),
-            pltpu.SemaphoreType.DMA((cols, packs)),
         ],
         compiler_params=still(),
         cost_estimate=SHORT,
@@ -404,8 +387,7 @@
 
 def second_back_kernel(dims, place_ref, *refs):
     rows, xc, ky_len, kz_len, cols, y_len, pack = dims
-    c_refs, table_ref, outs = refs[:cols], refs[cols], refs[cols + 1 : -2]
-    all_ref, sem = refs[-2:]
+    c_refs, table_ref, outs, all_ref = refs[:cols], refs[cols], refs[cols + 1 : -1], refs[-1]
     width = 3 * kz_len
     high_pad = round_up(width, LANES)
 
@@ -429,14 +411,8 @@
 
     lax.fori_loop(0, xc // pack, body, 0)
     size = all_ref.shape[0] // len(outs)
-    copies = []
     for k, out in enumerate(outs):
-        spot = pl.multiple_of((place_ref[0] ^ k) * size, 8)
-        copies.append(pltpu.make_async_copy(all_ref.at[pl.ds(spot, size), :], out, sem.at[k]))
-    for copy in copies:
-        copy.start()
-    for copy in copies:
-        copy.wait()
+        out[...] = all_ref[pl.ds(pl.multiple_of((place_ref[0] ^ k) * size, 8), size), :]
 
 
 def second_back(place, arrived, table, dims):
@@ -446,9 +422,9 @@
     return pl.pallas_call(
         functools.partial(second_back_kernel, dims),
         in_specs=[SMEM] + [VMEM] * (cols + 1),
-        out_specs=[HBM] * groups,
+        out_specs=[VMEM] * groups,
         out_shape=[jax.ShapeDtypeStruct((2 * size, LANES), F32)] * groups,
-        scratch_shapes=[pltpu.VMEM((rows * size, LANES), F32), pltpu.SemaphoreType.DMA((groups,))],
+        scratch_shapes=[pltpu.VMEM((rows * size, LANES), F32)],
         compiler_params=still(),
         cost_estimate=SHORT,
         name="second_back",
@@ -456,34 +432,29 @@
 
 
 def first_back_kernel(dims, place_ref, *refs):
-    count, xc, own = dims
+    count, sizes, own = dims
     parts, table_ref, out_ref = refs[:count], refs[count], refs[count + 1]
-    data, sem = refs[-2:]
-    size = data.shape[1]
+    groups = count // len(sizes)
     core = place_ref[1] if own else 1 - place_ref[1]
-    spot = pl.ds(pl.multiple_of(core * size, 8), size)
-    copies = [
-        pltpu.make_async_copy(part.at[spot, :], data.at[k], sem.at[k]) for k, part in enumerate(parts)
-    ]
-    for copy in copies:
-        copy.start()
-    for copy in copies:
-        copy.wait()
-    for tile in range(size // xc):
-        found = jnp.concatenate([data[k, tile * xc : (tile + 1) * xc, :] for k in range(count)], axis=0)
+    for tile in range(out_ref.shape[1] // LANES):
+        found = []
+        for idx, part in enumerate(parts):
+            xc = sizes[idx // groups]
+            spot = pl.multiple_of(core * (part.shape[0] // 2) + tile * xc, 8)
+            found.append(part[pl.ds(spot, xc), :])
         out_ref[:, tile * LANES : (tile + 1) * LANES] = dot_data_right(
-            table_ref[0], table_ref[1], found, NN
+            table_ref[0], table_ref[1], jnp.concatenate(found, axis=0), NN
         )
 
 
-def first_back(place, parts, table, xc, own):
+def first_back(place, parts, table, sizes, own):
     count = len(parts)
-    size = parts[0].shape[0] // 2
+    tiles = parts[0].shape[0] // 2 // sizes[0]
     return pl.pallas_call(
-        functools.partial(first_back_kernel, (count, xc, own)),
-        in_specs=[SMEM] + [HBM] * count + [VMEM],
-        out_shape=jax.ShapeDtypeStruct((table.shape[1], size // xc * LANES), F32),
-        scratch_shapes=[pltpu.VMEM((count, size, LANES), F32), pltpu.SemaphoreType.DMA((count,))],
+        functools.partial(first_back_kernel, (count, tuple(sizes), own)),
+        in_specs=[SMEM] + [VMEM] * (count + 1),
+        out_specs=VMEM,
+        out_shape=jax.ShapeDtypeStruct((table.shape[1], tiles * LANES), F32),
         compiler_params=still(),
         cost_estimate=SHORT,
         name="first_back",
@@ -571,10 +542,10 @@
     orders, _, x_len, y_len, grid_len = stored_velocity.shape
     kz_len = round_up(kz_own, 8)
     kmax = modes // 2 - 1
-    xc = min(XC, x_len)
-    chunks = x_len // xc
+    sizes = chunk_sizes(x_len)
+    chunks = len(sizes)
+    begins = [sum(sizes[:k]) for k in range(chunks)]
     pack = LANES // y_len
-    packs = xc // pack
     wide = round_up(modes, LANES)
     group = 5 * kz_len
     lanes = round_up(ky_len * group, 256)
@@ -592,11 +563,12 @@
 
     def x_points(row):
         owner = np.array([row ^ (2 * k) for k in range(groups)])
-        return (
-            owner[None, :, None] * x_len
-            + np.arange(chunks)[:, None, None] * xc
-            + np.arange(xc)[None, None, :]
-        ).reshape(-1)
+        return np.concatenate(
+            [
+                (owner[:, None] * x_len + begin + np.arange(xc)[None, :]).reshape(-1)
+                for begin, xc in zip(begins, sizes)
+            ]
+        )
 
     def halves_of(plain, sloped):
         return np.stack([part for table in (plain, sloped) for part in halves(table)])
@@ -642,13 +614,22 @@
     def core_swap(value):
         return lax.ppermute(value, "row", [(src, src ^ 1) for src in range(rows)])
 
-    dims = (rows, xc, ky_len, kz_len, cols, y_len, pack)
-    shape = (chunks, groups, xc)
+    dims = [(rows, xc, ky_len, kz_len, cols, y_len, pack) for xc in sizes]
+    shape = (tuple(sizes), groups)
     other = core_swap(coeffs)
-    sent = first_synth(place, coeffs, table_x, shape, lanes, ())
-    sent = first_synth(place, other, table_x, shape, lanes, sent)
-    sent = [list(sent[k * groups : (k + 1) * groups]) for k in range(chunks)]
-    latest = sent[0][0]
+    small = (place, table_x, table_y, table_z, wave_x, wave_y, wave_z)
+    place, table_x, table_y, table_z, wave_x, wave_y, wave_z = lax.optimization_barrier(small)
+
+    def run_first(chosen, gate):
+        own = coeffs if gate is None else after(coeffs, gate)
+        found = first_synth(place, own, table_x, shape, chosen, lanes, ())
+        found = first_synth(place, other, table_x, shape, chosen, lanes, found)
+        return {chunk: list(found[k * groups : (k + 1) * groups]) for k, chunk in enumerate(chosen)}
+
+    sent = run_first((0,), None)
+    if chunks > 1:
+        sent.update(run_first(tuple(range(1, chunks)), sent[0][0]))
+    latest = sent[chunks - 1][0]
 
     def ordered(kernel, operands, *others):
         nonlocal latest
@@ -660,7 +641,7 @@
     stored = (stored_velocity, stored_vorticity)
 
     def run_earlier(chunk):
-        return ordered(lambda values: earlier(*values, chunk, xc, pack), stored)
+        return ordered(lambda values: earlier(*values, begins[chunk], sizes[chunk], pack), stored)
 
     def z_exchange(values, *gates):
         found = [values[0]]
@@ -670,26 +651,40 @@
         return found
 
     first, second, middle, back, base = {}, {}, {}, {}, {}
-    first[0] = z_exchange(sent[0])
-    for chunk in range(chunks):
-        base[chunk] = run_earlier(chunk)
     for step in range(chunks):
-        if step + 1 < chunks:
-            first[step + 1] = z_exchange(sent[step + 1], first[step])
-        found = ordered(lambda values: second_synth(place, values, table_y, dims), first[step])
-        second[step] = exchange(found, "col", 0, cols)
-    for step in range(chunks):
-        middle[step] = ordered(
-            lambda values: third(place, values, *stored, base[step], table_z, step, dims[3:]),
-            second[step],
+        first[step] = z_exchange(sent[step], *([first[step - 1]] if step else []))
+
+    def run_second(at):
+        found = ordered(lambda values: second_synth(place, values, table_y, dims[at]), first[at])
+        if at:
+            found = [found[0]] + [after(value, second[at - 1]) for value in found[1:]]
+        second[at] = exchange(found, "col", 0, cols)
+
+    def run_third(at):
+        found = ordered(
+            lambda values: third(
+                place, values, *stored, base[at], table_z, begins[at], dims[at][3:]
+            ),
+            second[at],
         )
-    for step in range(chunks):
-        found = exchange(middle[step], "col", 0, cols)
-        found = ordered(lambda values: second_back(place, values, table_y, dims), found)
-        back[step] = z_exchange(found, *([back[step - 1]] if step else []))
+        middle[at] = exchange(found, "col", 0, cols)
+
+    def run_back(at):
+        values = after(middle[at], back[at - 1]) if 0 < at < chunks - 1 else middle[at]
+        found = ordered(lambda values: second_back(place, values, table_y, dims[at]), values)
+        back[at] = z_exchange(found, *([back[at - 1]] if at else []))
+
+    def run_base(at):
+        base[at] = run_earlier(at)
+
+    plan = [(run_base, 0), (run_second, 0), (run_base, 1), (run_third, 0), (run_base, 2), (run_second, 1)]
+    plan += [(run_back, 0), (run_second, 2), (run_third, 1), (run_third, 2), (run_back, 1), (run_back, 2)]
+    for action, at in plan:
+        if at < chunks:
+            action(at)
     parts = [value for step in range(chunks) for value in back[step]]
-    away = first_back(place, parts, table_x, xc, False)
-    home = first_back(place, parts, after(table_x, away), xc, True)
+    away = first_back(place, parts, table_x, sizes, False)
+    home = first_back(place, parts, after(table_x, away), sizes, True)
     sums = [home, core_swap(away)]
     result = last(sums, wave_y, wave_x, wave_z, ky_len, kz_len, 1.0 / (orders + 1))
     return result[:, :, :kz_own] if kz_len > kz_own else result

time: 290 us -> 287 us (0.990)
  starting transfers between devices: 44.9 us -> 64.6 us
  local copies, waits for them, and re-layouts: 19.2 us -> 3.98 us
  Pallas kernels: 114 us -> 102 us
  waiting for transfers between devices: 111 us -> 114 us
    ppermute x12 -> x18, waiting for transfers between devices: 38.2 us -> 69 us  [exchange(): lax.ppermute(value, axis, [(src, src ^ k << shift) for src in range(size)])]
    ppermute x12 -> x18, waiting for transfers between devices: 72.5 us -> 42.7 us  [z_exchange(): lax.ppermute(value, 'row', [(src, src ^ 2 * k) for src in range(rows)])]
    unnamed x62 -> x32, local copies, waits for them, and re-layouts: 17.1 us -> 1.8 us
    pallas_call x2 -> x3, Pallas kernels: 29.4 us -> 15.1 us  [second_synth(): pl.pallas_call(functools.partial(second_synth_kernel, dims), in_specs=[SM...]
    ppermute x12 -> x18, starting transfers between devices: 29.2 us -> 40.6 us  [z_exchange(): lax.ppermute(value, 'row', [(src, src ^ 2 * k) for src in range(rows)])]
    ppermute x12 -> x18, starting transfers between devices: 15.2 us -> 23.4 us  [exchange(): lax.ppermute(value, axis, [(src, src ^ k << shift) for src in range(size)])]
    pallas_call x2 -> x3, Pallas kernels: 23.6 us -> 25 us  [earlier(): pl.pallas_call(functools.partial(earlier_kernel, orders - 1), grid=(packs...]
    pallas_call x6 -> x9, Pallas kernels: 45.8 us -> 46.6 us  [the longest x3 25 us: third(): pl.pallas_call(functools.partial(third_kernel, (begin, *dims)), in_specs=...]
  transfers between devices with their start and end apart: 26 -> 38, of which waited for: 12 -> 14; matrix products, arithmetic and copies ran while one was open for 1% -> 1% of each run, Pallas kernels for 29% -> 28%
where the time goes in v7:
time: 287 us; the launch traced here: 285 us
  waiting for transfers between devices  114 us (40%)
  Pallas kernels  102 us (36%)
  starting transfers between devices  64.6 us (23%)
  local copies, waits for them, and re-layouts  3.98 us (1%)
    ppermute x18, waiting for transfers between devices, exchange(): lax.ppermute(value, axis, [(src, src ^ k << shift) for src in range(size)])  69 us
    ppermute x18, waiting for transfers between devices, z_exchange(): lax.ppermute(value, 'row', [(src, src ^ 2 * k) for src in range(rows)])  42.7 us
    ppermute x18, starting transfers between devices, z_exchange(): lax.ppermute(value, 'row', [(src, src ^ 2 * k) for src in range(rows)])  40.6 us
    pallas_call x3, Pallas kernels, third(): pl.pallas_call(functools.partial(third_kernel, (begin, *dims)), in_specs=...  25 us
    pallas_call x3, Pallas kernels, earlier(): pl.pallas_call(functools.partial(earlier_kernel, orders - 1), grid=(packs...  25 us
    ppermute x18, starting transfers between devices, exchange(): lax.ppermute(value, axis, [(src, src ^ k << shift) for src in range(size)])  23.4 us
    pallas_call x4, Pallas kernels, first_synth(): pl.pallas_call(functools.partial(first_synth_kernel, (sizes, chosen, dest...  18.9 us
    pallas_call x3, Pallas kernels, second_synth(): pl.pallas_call(functools.partial(second_synth_kernel, dims), in_specs=[SM...  15.1 us
  transfers between devices with their start and end apart: 38, of which 14 were waited for; matrix products, arithmetic and copies ran while one was open for 1% of the time, Pallas kernels for 28%

profile of v7, /device:TPU:0, one launch (start us, length us, event | category | flops | bytes accessed | tf_op | source)
XLA Modules:
  0.0 285.3 jit_solution(2874125993750534807)
XLA Ops:
  4.5 4.0 %first_synth.4 = (f32[512,128]{1,0:T(8,128)S(1)}, f32[512,128]{1,0:T(8,128)S(1)}, f32[512,128]{1,0:T(8,128)S(1)}, f32[512,128]{1,0:T(8,128)S(1)}) custom-call(s32[3]{0:T(128)S(1)} %pad_add_fusion.place_ref, f32[3,20,40,160]{3,2,1,0:T(8,128)S(1)} %copy-done.2, bf16[4,160,128]{2,1,0:T(8,128)(2,1)S(1)} %dynamic-slice_bitcast_fusion.2.table_ref.refs_12_), custom_call_target="tpu_custom_call" | custom-call | flops 1024 | bytes 1024 | tf_op jit(solution)/shard_map/first_synth/pallas_call | solution.py:176
  8.5 4.0 %first_synth.5 = (f32[512,128]{1,0:T(8,128)S(1)}, f32[512,128]{1,0:T(8,128)S(1)}, f32[512,128]{1,0:T(8,128)S(1)}, f32[512,128]{1,0:T(8,128)S(1)}) custom-call(s32[3]{0:T(128)S(1)} %pad_add_fusion.place_ref, f32[3,20,40,160]{3,2,1,0:T(8,128)S(1)} %collective-permute-done.data_ref, ...), custom_call_target="tpu_custom_call", output_to_operand_aliasing={{0}: (3, {}), {1}: (4, {}), {2}: (5, {}), {3}: (6, {})} | custom-call | flops 1024 | bytes 1024 | tf_op jit(solution)/shard_map/first_synth/pallas_call | solution.py:176
  12.5 2.6 collective-permute-start.1
  17.7 5.5 %first_synth.6 = (f32[1024,128]{1,0:T(8,128)S(1)}, f32[1024,128]{1,0:T(8,128)}, f32[1024,128]{1,0:T(8,128)}, f32[1024,128]{1,0:T(8,128)}, f32[512,128]{1,0:T(8,1...) custom-call(s32[3]{0:T(128)S(1)} %pad_add_fusion.place_ref, ...), custom_call_target="tpu_custom_call" | custom-call | flops 1024 | bytes 1024 | tf_op jit(solution)/shard_map/first_synth/pallas_call | solution.py:176
  23.2 5.5 %first_synth.7 = (f32[1024,128]{1,0:T(8,128)S(1)}, f32[1024,128]{1,0:T(8,128)}, f32[1024,128]{1,0:T(8,128)}, f32[1024,128]{1,0:T(8,128)}, f32[512,128]{1,0:T(8,1...) custom-call(s32[3]{0:T(128)S(1)} %pad_add_fusion.place_ref, ...), custom_call_target="tpu_custom_call", output_to_operand_aliasing={{0}: (3, {}), {1}: (4, {}), {2}: (5, {}), {3}: (6, {}), {4}... | custom-call | flops 1024 | bytes 1024 | tf_op jit(solution)/shard_map/first_synth/pallas_call | solution.py:176
  28.8 6.9 %earlier_orders.3.refs_6_ = f32[3,8,64,256]{3,2,1,0:T(8,128)S(1)} custom-call(f32[6,3,32,64,256]{4,3,2,1,0:T(8,128)} %refs_4_.8, f32[6,3,32,64,256]{4,3,2,1,0:T(8,128)} %refs_4_.8, f32[6,3,32,64,256]{4,3,2,1,0:T(8,128)} %refs_4_.8, f32[6,3,32,64,256]{4,3,2,1,0:T(8,128)} %refs_4_.8, f32[6,3,32,64,256]{4,3,2,1,0:T(8,128)} %refs_4_.8, ...), custom_call_target="tpu_custom_call" | custom-call | flops 1024 | bytes 1024 | tf_op jit(solution)/shard_map/earlier_orders/pallas_call | solution.py:305
  36.4 3.7 %second_synth.3 = (f32[4,240,128]{2,1,0:T(8,128)S(1)}, f32[4,240,128]{2,1,0:T(8,128)S(1)}, f32[4,240,128]{2,1,0:T(8,128)S(1)}, f32[4,240,128]{2,1,0:T(8,128)S(1)}) custom-call(s32[3]{0:T(128)S(1)} %pad_add_fusion.place_ref, f32[512,128]{1,0:T(8,128)S(1)} %get-tuple-element.163.refs_0_, f32[512,128]{1,0:T(8,128)S(1)} %collective-permute-done.1.refs_1_, ...), custom_call_target="tpu_custom_call" | custom-call | flops 1024 | bytes 1024 | tf_op jit(solution)/shard_map/second_synth/pallas_call | solution.py:253
  41.7 3.1 %collective-permute-start.12 = (f32[1024,128]{1,0:T(8,128)}, f32[1024,128]{1,0:T(8,128)}, u32[]{:S(2)}, u32[]{:S(2)}) collective-permute-start(f32[1024,128]{1,0:T(8,128)} %get-tuple-element.189), channel_id=1, source_target_pairs={{0,24},{4,28},{8,16},{12,20},{16,8},{20,12},{24,0},{28,4},{1,25},{... | collective-permute-start | bytes 1572872 | tf_op jit(solution)/shard_map/ppermute | solution.py:650
  44.8 3.8 %collective-permute-start.11 = (f32[1024,128]{1,0:T(8,128)}, f32[1024,128]{1,0:T(8,128)}, u32[]{:S(2)}, u32[]{:S(2)}) collective-permute-start(f32[1024,128]{1,0:T(8,128)} %get-tuple-element.187), channel_id=1, source_target_pairs={{0,16},{4,20},{8,24},{12,28},{16,0},{20,4},{24,8},{28,12},{1,17},{... | collective-permute-start | bytes 1572872 | tf_op jit(solution)/shard_map/ppermute | solution.py:650
  55.0 11.7 %earlier_orders.4.refs_6_ = f32[3,16,64,256]{3,2,1,0:T(8,128)S(1)} custom-call(f32[6,3,32,64,256]{4,3,2,1,0:T(8,128)} %refs_4_.8, f32[6,3,32,64,256]{4,3,2,1,0:T(8,128)} %refs_4_.8, f32[6,3,32,64,256]{4,3,2,1,0:T(8,128)} %refs_4_.8, f32[6,3,32,64,256]{4,3,2,1,0:T(8,128)} %refs_4_.8, f32[6,3,32,64,256]{4,3,2,1,0:T(8,128)} %refs_4_.8, ...), custom_call_target="tpu_custom_call" | custom-call | flops 1024 | bytes 1024 | tf_op jit(solution)/shard_map/earlier_orders/pallas_call | solution.py:305
  66.8 4.2 %collective-permute-done.5.refs_2_ = f32[4,240,128]{2,1,0:T(8,128)S(1)} collective-permute-done((f32[4,240,128]{2,1,0:T(8,128)S(1)}, f32[4,240,128]{2,1,0:T(8,128)S(1)}, u32[]{:S(2)}, u32[]{:S(2)}) %collective-permute-start.5) | collective-permute-done | bytes 491552 | tf_op jit(solution)/shard_map/ppermute | solution.py:610
  71.0 6.4 %third_dimension.3 = (f32[4,120,128]{2,1,0:T(8,128)S(1)}, f32[4,120,128]{2,1,0:T(8,128)S(1)}, f32[4,120,128]{2,1,0:T(8,128)S(1)}, f32[4,120,128]{2,1,0:T(8,128)S(1)}) custom-call(s32[3]{0:T(128)S(1)} %pad_add_fusion.place_ref, f32[4,240,128]{2,1,0:T(8,128)S(1)} %get-tuple-element.174.refs_0_, f32[4,240,128]{2,1,0:T(8,128)S(1)} %collective-permute-done.4.refs_1_, ...), custom_call_target="tpu_custom_call" | custom-call | flops 1024 | bytes 1024 | tf_op jit(solution)/shard_map/third_dimension/pallas_call | solution.py:373
  77.5 6.5 %earlier_orders.5.refs_6_ = f32[3,8,64,256]{3,2,1,0:T(8,128)S(1)} custom-call(f32[6,3,32,64,256]{4,3,2,1,0:T(8,128)} %refs_4_.8, f32[6,3,32,64,256]{4,3,2,1,0:T(8,128)} %refs_4_.8, f32[6,3,32,64,256]{4,3,2,1,0:T(8,128)} %refs_4_.8, f32[6,3,32,64,256]{4,3,2,1,0:T(8,128)} %refs_4_.8, f32[6,3,32,64,256]{4,3,2,1,0:T(8,128)} %refs_4_.8, ...), custom_call_target="tpu_custom_call" | custom-call | flops 1024 | bytes 1024 | tf_op jit(solution)/shard_map/earlier_orders/pallas_call | solution.py:305
  84.0 6.4 %collective-permute-done.11.refs_2_ = f32[1024,128]{1,0:T(8,128)} collective-permute-done((f32[1024,128]{1,0:T(8,128)}, f32[1024,128]{1,0:T(8,128)}, u32[]{:S(2)}, u32[]{:S(2)}) %collective-permute-start.11) | collective-permute-done | bytes 524320 | tf_op jit(solution)/shard_map/ppermute | solution.py:650
  90.4 7.7 %second_synth.4 = (f32[8,240,128]{2,1,0:T(8,128)S(1)}, f32[8,240,128]{2,1,0:T(8,128)S(1)}, f32[8,240,128]{2,1,0:T(8,128)S(1)}, f32[8,240,128]{2,1,0:T(8,128)S(1)}) custom-call(s32[3]{0:T(128)S(1)} %pad_add_fusion.place_ref, f32[1024,128]{1,0:T(8,128)S(1)} %copy-done.7, f32[1024,128]{1,0:T(8,128)} %collective-permute-done.10.refs_1_, ...), custom_call_target="tpu_custom_call" | custom-call | flops 1024 | bytes 1024 | tf_op jit(solution)/shard_map/second_synth/pallas_call | solution.py:253
  103.7 45.5 %collective-permute-done.7.refs_1_ = f32[4,120,128]{2,1,0:T(8,128)S(1)} collective-permute-done((f32[4,120,128]{2,1,0:T(8,128)S(1)}, f32[4,120,128]{2,1,0:T(8,128)S(1)}, u32[]{:S(2)}, u32[]{:S(2)}) %collective-permute-start.7) | collective-permute-done | bytes 245792 | tf_op jit(solution)/shard_map/ppermute | solution.py:610
  150.6 7.3 %collective-permute-done.9.refs_3_ = f32[4,120,128]{2,1,0:T(8,128)S(1)} collective-permute-done((f32[4,120,128]{2,1,0:T(8,128)S(1)}, f32[4,120,128]{2,1,0:T(8,128)S(1)}, u32[]{:S(2)}, u32[]{:S(2)}) %collective-permute-start.9) | collective-permute-done | bytes 245792 | tf_op jit(solution)/shard_map/ppermute | solution.py:610
  157.9 3.1 %collective-permute-start.20 = (f32[512,128]{1,0:T(8,128)S(1)}, f32[512,128]{1,0:T(8,128)S(1)}, u32[]{:S(2)}, u32[]{:S(2)}) collective-permute-start(f32[512,128]{1,0:T(8,128)S(1)} %copy-done.13), channel_id=1, source_target_pairs={{0,16},{4,20},{8,24},{12,28},{16,0},{20,4},{24,8},{28,12},{1,17},{... | collective-permute-start | bytes 786440 | tf_op jit(solution)/shard_map/ppermute | solution.py:650
  163.9 14.3 %collective-permute-done.20.refs_2_ = f32[512,128]{1,0:T(8,128)S(1)} collective-permute-done((f32[512,128]{1,0:T(8,128)S(1)}, f32[512,128]{1,0:T(8,128)S(1)}, u32[]{:S(2)}, u32[]{:S(2)}) %collective-permute-start.20) | collective-permute-done | bytes 262176 | tf_op jit(solution)/shard_map/ppermute | solution.py:650
  178.2 3.7 %second_synth.5 = (f32[4,240,128]{2,1,0:T(8,128)S(1)}, f32[4,240,128]{2,1,0:T(8,128)S(1)}, f32[4,240,128]{2,1,0:T(8,128)S(1)}, f32[4,240,128]{2,1,0:T(8,128)S(1)}) custom-call(s32[3]{0:T(128)S(1)} %pad_add_fusion.place_ref, f32[512,128]{1,0:T(8,128)S(1)} %copy-done.9, f32[512,128]{1,0:T(8,128)S(1)} %collective-permute-done.19.refs_1_, ...), custom_call_target="tpu_custom_call" | custom-call | flops 1024 | bytes 1024 | tf_op jit(solution)/shard_map/second_synth/pallas_call | solution.py:253
  185.5 12.2 %third_dimension.4 = (f32[8,120,128]{2,1,0:T(8,128)S(1)}, f32[8,120,128]{2,1,0:T(8,128)S(1)}, f32[8,120,128]{2,1,0:T(8,128)S(1)}, f32[8,120,128]{2,1,0:T(8,128)S(1)}) custom-call(s32[3]{0:T(128)S(1)} %pad_add_fusion.place_ref, f32[8,240,128]{2,1,0:T(8,128)S(1)} %get-tuple-element.222.refs_0_, f32[8,240,128]{2,1,0:T(8,128)S(1)} %collective-permute-done.16.refs_1_, ...), custom_call_target="tpu_custom_call" | custom-call | flops 1024 | bytes 1024 | tf_op jit(solution)/shard_map/third_dimension/pallas_call | solution.py:373
  203.0 8.2 %collective-permute-start.13 = (f32[304,128]{1,0:T(8,128)S(1)}, f32[304,128]{1,0:T(8,128)S(1)}, u32[]{:S(2)}, u32[]{:S(2)}) collective-permute-start(f32[304,128]{1,0:T(8,128)S(1)} %get-tuple-element.202), channel_id=1, source_target_pairs={{0,8},{4,12},{8,0},{12,4},{16,24},{20,28},{24,16},{28,20},{1,9},{5... | collective-permute-start | bytes 466952 | tf_op jit(solution)/shard_map/ppermute | solution.py:650
  213.8 6.4 %third_dimension.5 = (f32[4,120,128]{2,1,0:T(8,128)S(1)}, f32[4,120,128]{2,1,0:T(8,128)S(1)}, f32[4,120,128]{2,1,0:T(8,128)S(1)}, f32[4,120,128]{2,1,0:T(8,128)S(1)}) custom-call(s32[3]{0:T(128)S(1)} %pad_add_fusion.place_ref, f32[4,240,128]{2,1,0:T(8,128)S(1)} %get-tuple-element.240.refs_0_, f32[4,240,128]{2,1,0:T(8,128)S(1)} %collective-permute-done.25.refs_1_, ...), custom_call_target="tpu_custom_call" | custom-call | flops 1024 | bytes 1024 | tf_op jit(solution)/shard_map/third_dimension/pallas_call | solution.py:373
  221.7 3.0 %collective-permute-start.15 = (f32[304,128]{1,0:T(8,128)S(1)}, f32[304,128]{1,0:T(8,128)S(1)}, u32[]{:S(2)}, u32[]{:S(2)}) collective-permute-start(f32[304,128]{1,0:T(8,128)S(1)} %get-tuple-element.204), channel_id=1, source_target_pairs={{0,24},{4,28},{8,16},{12,20},{16,8},{20,12},{24,0},{28,4},{1,25},{... | collective-permute-start | bytes 466952 | tf_op jit(solution)/shard_map/ppermute | solution.py:650
  224.8 4.1 %collective-permute-done.15.refs_3_ = f32[304,128]{1,0:T(8,128)S(1)} collective-permute-done((f32[304,128]{1,0:T(8,128)S(1)}, f32[304,128]{1,0:T(8,128)S(1)}, u32[]{:S(2)}, u32[]{:S(2)}) %collective-permute-start.15) | collective-permute-done | bytes 155680 | tf_op jit(solution)/shard_map/ppermute | solution.py:650
  228.9 4.4 %second_back.4 = (f32[608,128]{1,0:T(8,128)S(1)}, f32[608,128]{1,0:T(8,128)S(1)}, f32[608,128]{1,0:T(8,128)S(1)}, f32[608,128]{1,0:T(8,128)S(1)}) custom-call(s32[3]{0:T(128)S(1)} %pad_add_fusion.place_ref, f32[8,120,128]{2,1,0:T(8,128)S(1)} %get-tuple-element.245.refs_0_, f32[8,120,128]{2,1,0:T(8,128)S(1)} %collective-permute-done.22.refs_1_, ...), custom_call_target="tpu_custom_call" | custom-call | flops 1024 | bytes 1024 | tf_op jit(solution)/shard_map/second_back/pallas_call | solution.py:422
  233.3 3.0 %collective-permute-start.30 = (f32[608,128]{1,0:T(8,128)S(1)}, f32[608,128]{1,0:T(8,128)S(1)}, u32[]{:S(2)}, u32[]{:S(2)}) collective-permute-start(f32[608,128]{1,0:T(8,128)S(1)} %get-tuple-element.255), channel_id=1, source_target_pairs={{0,24},{4,28},{8,16},{12,20},{16,8},{20,12},{24,0},{28,4},{1,25},{... | collective-permute-start | bytes 933896 | tf_op jit(solution)/shard_map/ppermute | solution.py:650
  242.1 7.9 %collective-permute-done.32.refs_2_ = f32[4,120,128]{2,1,0:T(8,128)S(1)} collective-permute-done((f32[4,120,128]{2,1,0:T(8,128)S(1)}, f32[4,120,128]{2,1,0:T(8,128)S(1)}, u32[]{:S(2)}, u32[]{:S(2)}) %collective-permute-start.32) | collective-permute-done | bytes 245792 | tf_op jit(solution)/shard_map/ppermute | solution.py:610
  252.6 7.2 %collective-permute-done.29.refs_6_ = f32[608,128]{1,0:T(8,128)S(1)} collective-permute-done((f32[608,128]{1,0:T(8,128)S(1)}, f32[608,128]{1,0:T(8,128)S(1)}, u32[]{:S(2)}, u32[]{:S(2)}) %collective-permute-start.29) | collective-permute-done | bytes 311328 | tf_op jit(solution)/shard_map/ppermute | solution.py:650
  259.8 3.2 %collective-permute-start.35 = (f32[304,128]{1,0:T(8,128)S(1)}, f32[304,128]{1,0:T(8,128)S(1)}, u32[]{:S(2)}, u32[]{:S(2)}) collective-permute-start(f32[304,128]{1,0:T(8,128)S(1)} %get-tuple-element.267), channel_id=1, source_target_pairs={{0,16},{4,20},{8,24},{12,28},{16,0},{20,4},{24,8},{28,12},{1,17},{... | collective-permute-start | bytes 466952 | tf_op jit(solution)/shard_map/ppermute | solution.py:650
  266.3 7.9 %collective-permute-done.35.refs_10_ = f32[304,128]{1,0:T(8,128)S(1)} collective-permute-done((f32[304,128]{1,0:T(8,128)S(1)}, f32[304,128]{1,0:T(8,128)S(1)}, u32[]{:S(2)}, u32[]{:S(2)}) %collective-permute-start.35) | collective-permute-done | bytes 155680 | tf_op jit(solution)/shard_map/ppermute | solution.py:650
  279.0 6.2 %last_projection.1 = f32[3,20,40,160]{3,2,1,0:T(8,128)} custom-call(f32[10]{0:T(128)S(1)} %convert_multiply_fusion.1.refs_0_, f32[8,256]{1,0:T(8,128)S(1)} %broadcast_in_dim.9.refs_1_, f32[40,256]{1,0:T(8,128)S(1)} %broadcast_in_dim.18.refs_2_, f32[160,2432]{1,0:T(8,128)S(1)} %first_back.3.refs_3_, f32[160,2432]{1,0:T(8,128)S(1)} %collective-permute-done.37.refs_4_), custom_call_target="tpu_custom_call" | custom-call | flops 1024 | bytes 1024 | tf_op jit(solution)/shard_map/last_projection/pallas_call | solution.py:521
  (103 shorter events, 55.1 us)
Async XLA Ops:
  12.5 23.2 %collective-permute-start.1 = (f32[512,128]{1,0:T(8,128)S(1)}, f32[512,128]{1,0:T(8,128)S(1)}, u32[]{:S(2)}, u32[]{:S(2)}) collective-permute-start(f32[512,128]{1,0:T(8,128)S(1)} %get-tuple-element.148), channel_id=1, source_target_pairs={{0,8},{4,12},{8,0},{12,4},{16,24},{20,28},{24,16},{28,20},{1,9},{5... | collective-permute-start | bytes 786440 | tf_op jit(solution)/shard_map/ppermute | solution.py:650
  15.1 21.3 %collective-permute-start.2 = (f32[512,128]{1,0:T(8,128)S(1)}, f32[512,128]{1,0:T(8,128)S(1)}, u32[]{:S(2)}, u32[]{:S(2)}) collective-permute-start(f32[512,128]{1,0:T(8,128)S(1)} %get-tuple-element.149), channel_id=1, source_target_pairs={{0,16},{4,20},{8,24},{12,28},{16,0},{20,4},{24,8},{28,12},{1,17},{... | collective-permute-start | bytes 786440 | tf_op jit(solution)/shard_map/ppermute | solution.py:650
  17.7 18.7 %collective-permute-start.3 = (f32[512,128]{1,0:T(8,128)S(1)}, f32[512,128]{1,0:T(8,128)S(1)}, u32[]{:S(2)}, u32[]{:S(2)}) collective-permute-start(f32[512,128]{1,0:T(8,128)S(1)} %get-tuple-element.150), channel_id=1, source_target_pairs={{0,24},{4,28},{8,16},{12,20},{16,8},{20,12},{24,0},{28,4},{1,25},{... | collective-permute-start | bytes 786440 | tf_op jit(solution)/shard_map/ppermute | solution.py:650
  40.1 12.5 %collective-permute-start.4 = (f32[4,240,128]{2,1,0:T(8,128)S(1)}, f32[4,240,128]{2,1,0:T(8,128)S(1)}, u32[]{:S(2)}, u32[]{:S(2)}) collective-permute-start(f32[4,240,128]{2,1,0:T(8,128)S(1)} %get-tuple-element.169), channel_id=1, source_target_pairs={{0,1},{1,0},{2,3},{3,2},{4,5},{5,4},{6,7},{7,6},{8,9},{9,8},{10,11... | collective-permute-start | bytes 1474568 | tf_op jit(solution)/shard_map/ppermute | solution.py:610
  41.7 42.3 %collective-permute-start.12 = (f32[1024,128]{1,0:T(8,128)}, f32[1024,128]{1,0:T(8,128)}, u32[]{:S(2)}, u32[]{:S(2)}) collective-permute-start(f32[1024,128]{1,0:T(8,128)} %get-tuple-element.189), channel_id=1, source_target_pairs={{0,24},{4,28},{8,16},{12,20},{16,8},{20,12},{24,0},{28,4},{1,25},{... | collective-permute-start | bytes 1572872 | tf_op jit(solution)/shard_map/ppermute | solution.py:650
  44.8 45.5 %collective-permute-start.11 = (f32[1024,128]{1,0:T(8,128)}, f32[1024,128]{1,0:T(8,128)}, u32[]{:S(2)}, u32[]{:S(2)}) collective-permute-start(f32[1024,128]{1,0:T(8,128)} %get-tuple-element.187), channel_id=1, source_target_pairs={{0,16},{4,20},{8,24},{12,28},{16,0},{20,4},{24,8},{28,12},{1,17},{... | collective-permute-start | bytes 1572872 | tf_op jit(solution)/shard_map/ppermute | solution.py:650
  48.6 41.7 %collective-permute-start.10 = (f32[1024,128]{1,0:T(8,128)}, f32[1024,128]{1,0:T(8,128)}, u32[]{:S(2)}, u32[]{:S(2)}) collective-permute-start(f32[1024,128]{1,0:T(8,128)} %get-tuple-element.185), channel_id=1, source_target_pairs={{0,8},{4,12},{8,0},{12,4},{16,24},{20,28},{24,16},{28,20},{1,9},{5... | collective-permute-start | bytes 1572872 | tf_op jit(solution)/shard_map/ppermute | solution.py:650
  48.8 22.2 %collective-permute-start.5 = (f32[4,240,128]{2,1,0:T(8,128)S(1)}, f32[4,240,128]{2,1,0:T(8,128)S(1)}, u32[]{:S(2)}, u32[]{:S(2)}) collective-permute-start(f32[4,240,128]{2,1,0:T(8,128)S(1)} %get-tuple-element.170), channel_id=1, source_target_pairs={{0,2},{1,3},{2,0},{3,1},{4,6},{5,7},{6,4},{7,5},{8,10},{9,11},{10,... | collective-permute-start | bytes 1474568 | tf_op jit(solution)/shard_map/ppermute | solution.py:610
  52.6 18.4 %collective-permute-start.6 = (f32[4,240,128]{2,1,0:T(8,128)S(1)}, f32[4,240,128]{2,1,0:T(8,128)S(1)}, u32[]{:S(2)}, u32[]{:S(2)}) collective-permute-start(f32[4,240,128]{2,1,0:T(8,128)S(1)} %get-tuple-element.171), channel_id=1, source_target_pairs={{0,3},{1,2},{2,1},{3,0},{4,7},{5,6},{6,5},{7,4},{8,11},{9,10},{10,... | collective-permute-start | bytes 1474568 | tf_op jit(solution)/shard_map/ppermute | solution.py:610
  98.1 83.8 %collective-permute-start.18 = (f32[8,240,128]{2,1,0:T(8,128)S(1)}, f32[8,240,128]{2,1,0:T(8,128)S(1)}, u32[]{:S(2)}, u32[]{:S(2)}) collective-permute-start(f32[8,240,128]{2,1,0:T(8,128)S(1)} %get-tuple-element.210), channel_id=1, source_target_pairs={{0,3},{1,2},{2,1},{3,0},{4,7},{5,6},{6,5},{7,4},{8,11},{9,10},{10,... | collective-permute-start | bytes 2949128 | tf_op jit(solution)/shard_map/ppermute | solution.py:610
  99.7 82.3 %collective-permute-start.17 = (f32[8,240,128]{2,1,0:T(8,128)S(1)}, f32[8,240,128]{2,1,0:T(8,128)S(1)}, u32[]{:S(2)}, u32[]{:S(2)}) collective-permute-start(f32[8,240,128]{2,1,0:T(8,128)S(1)} %get-tuple-element.208), channel_id=1, source_target_pairs={{0,2},{1,3},{2,0},{3,1},{4,6},{5,7},{6,4},{7,5},{8,10},{9,11},{10,... | collective-permute-start | bytes 2949128 | tf_op jit(solution)/shard_map/ppermute | solution.py:610
  100.2 81.8 %collective-permute-start.16 = (f32[8,240,128]{2,1,0:T(8,128)S(1)}, f32[8,240,128]{2,1,0:T(8,128)S(1)}, u32[]{:S(2)}, u32[]{:S(2)}) collective-permute-start(f32[8,240,128]{2,1,0:T(8,128)S(1)} %get-tuple-element.206), channel_id=1, source_target_pairs={{0,1},{1,0},{2,3},{3,2},{4,5},{5,4},{6,7},{7,6},{8,9},{9,8},{10,11... | collective-permute-start | bytes 2949128 | tf_op jit(solution)/shard_map/ppermute | solution.py:610
  101.7 47.5 %collective-permute-start.7 = (f32[4,120,128]{2,1,0:T(8,128)S(1)}, f32[4,120,128]{2,1,0:T(8,128)S(1)}, u32[]{:S(2)}, u32[]{:S(2)}) collective-permute-start(f32[4,120,128]{2,1,0:T(8,128)S(1)} %get-tuple-element.180), channel_id=1, source_target_pairs={{0,1},{1,0},{2,3},{3,2},{4,5},{5,4},{6,7},{7,6},{8,9},{9,8},{10,11... | collective-permute-start | bytes 737288 | tf_op jit(solution)/shard_map/ppermute | solution.py:610
  102.2 47.7 %collective-permute-start.8 = (f32[4,120,128]{2,1,0:T(8,128)S(1)}, f32[4,120,128]{2,1,0:T(8,128)S(1)}, u32[]{:S(2)}, u32[]{:S(2)}) collective-permute-start(f32[4,120,128]{2,1,0:T(8,128)S(1)} %get-tuple-element.181), channel_id=1, source_target_pairs={{0,2},{1,3},{2,0},{3,1},{4,6},{5,7},{6,4},{7,5},{8,10},{9,11},{10,... | collective-permute-start | bytes 737288 | tf_op jit(solution)/shard_map/ppermute | solution.py:610
  149.2 11.8 %collective-permute-start.19 = (f32[512,128]{1,0:T(8,128)S(1)}, f32[512,128]{1,0:T(8,128)S(1)}, u32[]{:S(2)}, u32[]{:S(2)}) collective-permute-start(f32[512,128]{1,0:T(8,128)S(1)} %copy-done.11), channel_id=1, source_target_pairs={{0,8},{4,12},{8,0},{12,4},{16,24},{20,28},{24,16},{28,20},{1,9},{5... | collective-permute-start | bytes 786440 | tf_op jit(solution)/shard_map/ppermute | solution.py:650
  157.9 20.4 %collective-permute-start.20 = (f32[512,128]{1,0:T(8,128)S(1)}, f32[512,128]{1,0:T(8,128)S(1)}, u32[]{:S(2)}, u32[]{:S(2)}) collective-permute-start(f32[512,128]{1,0:T(8,128)S(1)} %copy-done.13), channel_id=1, source_target_pairs={{0,16},{4,20},{8,24},{12,28},{16,0},{20,4},{24,8},{28,12},{1,17},{... | collective-permute-start | bytes 786440 | tf_op jit(solution)/shard_map/ppermute | solution.py:650
  160.9 17.3 %collective-permute-start.21 = (f32[512,128]{1,0:T(8,128)S(1)}, f32[512,128]{1,0:T(8,128)S(1)}, u32[]{:S(2)}, u32[]{:S(2)}) collective-permute-start(f32[512,128]{1,0:T(8,128)S(1)} %copy-done.15), channel_id=1, source_target_pairs={{0,24},{4,28},{8,16},{12,20},{16,8},{20,12},{24,0},{28,4},{1,25},{... | collective-permute-start | bytes 786440 | tf_op jit(solution)/shard_map/ppermute | solution.py:650
  182.0 18.0 %collective-permute-start.25 = (f32[4,240,128]{2,1,0:T(8,128)S(1)}, f32[4,240,128]{2,1,0:T(8,128)S(1)}, u32[]{:S(2)}, u32[]{:S(2)}) collective-permute-start(f32[4,240,128]{2,1,0:T(8,128)S(1)} %get-tuple-element.235), channel_id=1, source_target_pairs={{0,1},{1,0},{2,3},{3,2},{4,5},{5,4},{6,7},{7,6},{8,9},{9,8},{10,11... | collective-permute-start | bytes 1474568 | tf_op jit(solution)/shard_map/ppermute | solution.py:610
  182.6 20.4 %collective-permute-start.26 = (f32[4,240,128]{2,1,0:T(8,128)S(1)}, f32[4,240,128]{2,1,0:T(8,128)S(1)}, u32[]{:S(2)}, u32[]{:S(2)}) collective-permute-start(f32[4,240,128]{2,1,0:T(8,128)S(1)} %get-tuple-element.237), channel_id=1, source_target_pairs={{0,2},{1,3},{2,0},{3,1},{4,6},{5,7},{6,4},{7,5},{8,10},{9,11},{10,... | collective-permute-start | bytes 1474568 | tf_op jit(solution)/shard_map/ppermute | solution.py:610
  184.3 26.9 %collective-permute-start.27 = (f32[4,240,128]{2,1,0:T(8,128)S(1)}, f32[4,240,128]{2,1,0:T(8,128)S(1)}, u32[]{:S(2)}, u32[]{:S(2)}) collective-permute-start(f32[4,240,128]{2,1,0:T(8,128)S(1)} %get-tuple-element.239), channel_id=1, source_target_pairs={{0,3},{1,2},{2,1},{3,0},{4,7},{5,6},{6,5},{7,4},{8,11},{9,10},{10,... | collective-permute-start | bytes 1474568 | tf_op jit(solution)/shard_map/ppermute | solution.py:610
  197.7 31.2 %collective-permute-start.22 = (f32[8,120,128]{2,1,0:T(8,128)S(1)}, f32[8,120,128]{2,1,0:T(8,128)S(1)}, u32[]{:S(2)}, u32[]{:S(2)}) collective-permute-start(f32[8,120,128]{2,1,0:T(8,128)S(1)} %get-tuple-element.227), channel_id=1, source_target_pairs={{0,1},{1,0},{2,3},{3,2},{4,5},{5,4},{6,7},{7,6},{8,9},{9,8},{10,11... | collective-permute-start | bytes 1474568 | tf_op jit(solution)/shard_map/ppermute | solution.py:610
  198.3 30.6 %collective-permute-start.23 = (f32[8,120,128]{2,1,0:T(8,128)S(1)}, f32[8,120,128]{2,1,0:T(8,128)S(1)}, u32[]{:S(2)}, u32[]{:S(2)}) collective-permute-start(f32[8,120,128]{2,1,0:T(8,128)S(1)} %get-tuple-element.228), channel_id=1, source_target_pairs={{0,2},{1,3},{2,0},{3,1},{4,6},{5,7},{6,4},{7,5},{8,10},{9,11},{10,... | collective-permute-start | bytes 1474568 | tf_op jit(solution)/shard_map/ppermute | solution.py:610
  200.0 28.8 %collective-permute-start.24 = (f32[8,120,128]{2,1,0:T(8,128)S(1)}, f32[8,120,128]{2,1,0:T(8,128)S(1)}, u32[]{:S(2)}, u32[]{:S(2)}) collective-permute-start(f32[8,120,128]{2,1,0:T(8,128)S(1)} %get-tuple-element.229), channel_id=1, source_target_pairs={{0,3},{1,2},{2,1},{3,0},{4,7},{5,6},{6,5},{7,4},{8,11},{9,10},{10,... | collective-permute-start | bytes 1474568 | tf_op jit(solution)/shard_map/ppermute | solution.py:610
  203.0 17.2 %collective-permute-start.13 = (f32[304,128]{1,0:T(8,128)S(1)}, f32[304,128]{1,0:T(8,128)S(1)}, u32[]{:S(2)}, u32[]{:S(2)}) collective-permute-start(f32[304,128]{1,0:T(8,128)S(1)} %get-tuple-element.202), channel_id=1, source_target_pairs={{0,8},{4,12},{8,0},{12,4},{16,24},{20,28},{24,16},{28,20},{1,9},{5... | collective-permute-start | bytes 466952 | tf_op jit(solution)/shard_map/ppermute | solution.py:650
  211.2 10.5 %collective-permute-start.14 = (f32[304,128]{1,0:T(8,128)S(1)}, f32[304,128]{1,0:T(8,128)S(1)}, u32[]{:S(2)}, u32[]{:S(2)}) collective-permute-start(f32[304,128]{1,0:T(8,128)S(1)} %get-tuple-element.203), channel_id=1, source_target_pairs={{0,16},{4,20},{8,24},{12,28},{16,0},{20,4},{24,8},{28,12},{1,17},{... | collective-permute-start | bytes 466952 | tf_op jit(solution)/shard_map/ppermute | solution.py:650
  220.2 20.7 %collective-permute-start.31 = (f32[4,120,128]{2,1,0:T(8,128)S(1)}, f32[4,120,128]{2,1,0:T(8,128)S(1)}, u32[]{:S(2)}, u32[]{:S(2)}) collective-permute-start(f32[4,120,128]{2,1,0:T(8,128)S(1)} %get-tuple-element.256), channel_id=1, source_target_pairs={{0,1},{1,0},{2,3},{3,2},{4,5},{5,4},{6,7},{7,6},{8,9},{9,8},{10,11... | collective-permute-start | bytes 737288 | tf_op jit(solution)/shard_map/ppermute | solution.py:610
  233.3 19.3 %collective-permute-start.30 = (f32[608,128]{1,0:T(8,128)S(1)}, f32[608,128]{1,0:T(8,128)S(1)}, u32[]{:S(2)}, u32[]{:S(2)}) collective-permute-start(f32[608,128]{1,0:T(8,128)S(1)} %get-tuple-element.255), channel_id=1, source_target_pairs={{0,24},{4,28},{8,16},{12,20},{16,8},{20,12},{24,0},{28,4},{1,25},{... | collective-permute-start | bytes 933896 | tf_op jit(solution)/shard_map/ppermute | solution.py:650
  236.3 23.5 %collective-permute-start.29 = (f32[608,128]{1,0:T(8,128)S(1)}, f32[608,128]{1,0:T(8,128)S(1)}, u32[]{:S(2)}, u32[]{:S(2)}) collective-permute-start(f32[608,128]{1,0:T(8,128)S(1)} %get-tuple-element.253), channel_id=1, source_target_pairs={{0,16},{4,20},{8,24},{12,28},{16,0},{20,4},{24,8},{28,12},{1,17},{... | collective-permute-start | bytes 933896 | tf_op jit(solution)/shard_map/ppermute | solution.py:650
  238.6 21.2 %collective-permute-start.28 = (f32[608,128]{1,0:T(8,128)S(1)}, f32[608,128]{1,0:T(8,128)S(1)}, u32[]{:S(2)}, u32[]{:S(2)}) collective-permute-start(f32[608,128]{1,0:T(8,128)S(1)} %get-tuple-element.251), channel_id=1, source_target_pairs={{0,8},{4,12},{8,0},{12,4},{16,24},{20,28},{24,16},{28,20},{1,9},{5... | collective-permute-start | bytes 933896 | tf_op jit(solution)/shard_map/ppermute | solution.py:650
  239.1 10.9 %collective-permute-start.32 = (f32[4,120,128]{2,1,0:T(8,128)S(1)}, f32[4,120,128]{2,1,0:T(8,128)S(1)}, u32[]{:S(2)}, u32[]{:S(2)}) collective-permute-start(f32[4,120,128]{2,1,0:T(8,128)S(1)} %get-tuple-element.257), channel_id=1, source_target_pairs={{0,2},{1,3},{2,0},{3,1},{4,6},{5,7},{6,4},{7,5},{8,10},{9,11},{10,... | collective-permute-start | bytes 737288 | tf_op jit(solution)/shard_map/ppermute | solution.py:610
  259.8 14.4 %collective-permute-start.35 = (f32[304,128]{1,0:T(8,128)S(1)}, f32[304,128]{1,0:T(8,128)S(1)}, u32[]{:S(2)}, u32[]{:S(2)}) collective-permute-start(f32[304,128]{1,0:T(8,128)S(1)} %get-tuple-element.267), channel_id=1, source_target_pairs={{0,16},{4,20},{8,24},{12,28},{16,0},{20,4},{24,8},{28,12},{1,17},{... | collective-permute-start | bytes 466952 | tf_op jit(solution)/shard_map/ppermute | solution.py:650
  263.0 11.2 %collective-permute-start.36 = (f32[304,128]{1,0:T(8,128)S(1)}, f32[304,128]{1,0:T(8,128)S(1)}, u32[]{:S(2)}, u32[]{:S(2)}) collective-permute-start(f32[304,128]{1,0:T(8,128)S(1)} %get-tuple-element.269), channel_id=1, source_target_pairs={{0,24},{4,28},{8,16},{12,20},{16,8},{20,12},{24,0},{28,4},{1,25},{... | collective-permute-start | bytes 466952 | tf_op jit(solution)/shard_map/ppermute | solution.py:650
  (22 other events, 518.7 us)

commit v8 on v7

--- a/solution.py
+++ b/solution.py
@@ -643,15 +643,17 @@
     def run_earlier(chunk):
         return ordered(lambda values: earlier(*values, begins[chunk], sizes[chunk], pack), stored)
 
-    def z_exchange(values, *gates):
+    def z_exchange(values, *gates, waves=True):
         found = [values[0]]
         for k in range(1, groups):
-            value = after(values[k], *gates) if gates else values[k]
+            value = values[k]
+            if gates:
+                value = after(value, found[1]) if waves and 2 * k > groups else after(value, *gates)
             found.append(lax.ppermute(value, "row", [(src, src ^ (2 * k)) for src in range(rows)]))
         return found
 
     first, second, middle, back, base = {}, {}, {}, {}, {}
-    for step in range(chunks):
+    for step in range(min(2, chunks)):
         first[step] = z_exchange(sent[step], *([first[step - 1]] if step else []))
 
     def run_second(at):
@@ -670,15 +672,16 @@
         middle[at] = exchange(found, "col", 0, cols)
 
     def run_back(at):
-        values = after(middle[at], back[at - 1]) if 0 < at < chunks - 1 else middle[at]
-        found = ordered(lambda values: second_back(place, values, table_y, dims[at]), values)
-        back[at] = z_exchange(found, *([back[at - 1]] if at else []))
+        found = ordered(lambda values: second_back(place, values, table_y, dims[at]), middle[at])
+        back[at] = z_exchange(found, back[at - 1] if at else first[min(1, chunks - 1)], waves=at == 0)
+        if at == 0 and chunks > 2:
+            first[2] = z_exchange(sent[2], back[0])
 
     def run_base(at):
         base[at] = run_earlier(at)
 
-    plan = [(run_base, 0), (run_second, 0), (run_base, 1), (run_third, 0), (run_base, 2), (run_second, 1)]
-    plan += [(run_back, 0), (run_second, 2), (run_third, 1), (run_third, 2), (run_back, 1), (run_back, 2)]
+    plan = [(run_base, 0), (run_second, 0), (run_base, 1), (run_third, 0), (run_base, 2), (run_back, 0)]
+    plan += [(run_second, 1), (run_second, 2), (run_third, 1), (run_third, 2), (run_back, 1), (run_back, 2)]
     for action, at in plan:
         if at < chunks:
             action(at)

time: 287 us -> 259 us (0.902)
  waiting for transfers between devices: 114 us -> 85.9 us
  local copies, waits for them, and re-layouts: 3.98 us -> 7.14 us
    ppermute x18, waiting for transfers between devices: 69 us -> 32.9 us  [exchange(): lax.ppermute(value, axis, [(src, src ^ k << shift) for src in range(size)])]
    ppermute x18, waiting for transfers between devices: 42.7 us -> 50.9 us  [z_exchange(): lax.ppermute(value, 'row', [(src, src ^ 2 * k) for src in range(rows)])]
    unnamed x32 -> x38, local copies, waits for them, and re-layouts: 1.8 us -> 4.96 us
  transfers between devices with their start and end apart: 38 -> 38, of which waited for: 14 -> 16; matrix products, arithmetic and copies ran while one was open for 1% -> 1% of each run, Pallas kernels for 28% -> 32%
where the time goes in v8:
time: 259 us; the launch traced here: 258 us
  Pallas kernels  101 us (39%)
  waiting for transfers between devices  85.9 us (33%)
  starting transfers between devices  63.2 us (24%)
  local copies, waits for them, and re-layouts  7.14 us (3%)
    ppermute x18, waiting for transfers between devices, z_exchange(): lax.ppermute(value, 'row', [(src, src ^ 2 * k) for src in range(rows)])  50.9 us
    ppermute x18, starting transfers between devices, z_exchange(): lax.ppermute(value, 'row', [(src, src ^ 2 * k) for src in range(rows)])  40.5 us
    ppermute x18, waiting for transfers between devices, exchange(): lax.ppermute(value, axis, [(src, src ^ k << shift) for src in range(size)])  32.9 us
    pallas_call x3, Pallas kernels, third(): pl.pallas_call(functools.partial(third_kernel, (begin, *dims)), in_specs=...  25 us
    pallas_call x3, Pallas kernels, earlier(): pl.pallas_call(functools.partial(earlier_kernel, orders - 1), grid=(packs...  24.5 us
    ppermute x18, starting transfers between devices, exchange(): lax.ppermute(value, axis, [(src, src ^ k << shift) for src in range(size)])  22.2 us
    pallas_call x4, Pallas kernels, first_synth(): pl.pallas_call(functools.partial(first_synth_kernel, (sizes, chosen, dest...  18.5 us
    pallas_call x3, Pallas kernels, second_synth(): pl.pallas_call(functools.partial(second_synth_kernel, dims), in_specs=[SM...  14.9 us
  transfers between devices with their start and end apart: 38, of which 16 were waited for; matrix products, arithmetic and copies ran while one was open for 1% of the time, Pallas kernels for 32%

profile of v8, /device:TPU:0, one launch (start us, length us, event | category | flops | bytes accessed | tf_op | source)
XLA Modules:
  0.0 258.0 jit_solution(816916626941561387)
XLA Ops:
  4.5 3.9 %first_synth.4 = (f32[512,128]{1,0:T(8,128)S(1)}, f32[512,128]{1,0:T(8,128)S(1)}, f32[512,128]{1,0:T(8,128)S(1)}, f32[512,128]{1,0:T(8,128)S(1)}) custom-call(s32[3]{0:T(128)S(1)} %pad_add_fusion.place_ref, f32[3,20,40,160]{3,2,1,0:T(8,128)S(1)} %copy-done.3, bf16[4,160,128]{2,1,0:T(8,128)(2,1)S(1)} %dynamic-slice_bitcast_fusion.2.table_ref.refs_12_), custom_call_target="tpu_custom_call" | custom-call | flops 1024 | bytes 1024 | tf_op jit(solution)/shard_map/first_synth/pallas_call | solution.py:176
  8.5 3.9 %first_synth.5 = (f32[512,128]{1,0:T(8,128)S(1)}, f32[512,128]{1,0:T(8,128)S(1)}, f32[512,128]{1,0:T(8,128)S(1)}, f32[512,128]{1,0:T(8,128)S(1)}) custom-call(s32[3]{0:T(128)S(1)} %pad_add_fusion.place_ref, f32[3,20,40,160]{3,2,1,0:T(8,128)S(1)} %collective-permute-done.data_ref, ...), custom_call_target="tpu_custom_call", output_to_operand_aliasing={{0}: (3, {}), {1}: (4, {}), {2}: (5, {}), {3}: (6, {})} | custom-call | flops 1024 | bytes 1024 | tf_op jit(solution)/shard_map/first_synth/pallas_call | solution.py:176
  12.4 2.6 %collective-permute-start.1 = (f32[512,128]{1,0:T(8,128)S(1)}, f32[512,128]{1,0:T(8,128)S(1)}, u32[]{:S(2)}, u32[]{:S(2)}) collective-permute-start(f32[512,128]{1,0:T(8,128)S(1)} %get-tuple-element.147), channel_id=1, source_target_pairs={{0,8},{4,12},{8,0},{12,4},{16,24},{20,28},{24,16},{28,20},{1,9},{5... | collective-permute-start | bytes 786440 | tf_op jit(solution)/shard_map/ppermute | solution.py:652
  17.7 5.3 %first_synth.6 = (f32[1024,128]{1,0:T(8,128)S(1)}, f32[1024,128]{1,0:T(8,128)S(1)}, f32[1024,128]{1,0:T(8,128)}, f32[1024,128]{1,0:T(8,128)}, f32[512,128]{1,0:T...) custom-call(s32[3]{0:T(128)S(1)} %pad_add_fusion.place_ref, ...), custom_call_target="tpu_custom_call" | custom-call | flops 1024 | bytes 1024 | tf_op jit(solution)/shard_map/first_synth/pallas_call | solution.py:176
  23.0 5.4 %first_synth.7 = (f32[1024,128]{1,0:T(8,128)S(1)}, f32[1024,128]{1,0:T(8,128)S(1)}, f32[1024,128]{1,0:T(8,128)}, f32[1024,128]{1,0:T(8,128)}, f32[512,128]{1,0:T...) custom-call(s32[3]{0:T(128)S(1)} %pad_add_fusion.place_ref, ...), custom_call_target="tpu_custom_call", output_to_operand_aliasing={{0}: (3, {}), {1}: (4, {}), {2}: (5, {}), {3}: (6, {}), {4}... | custom-call | flops 1024 | bytes 1024 | tf_op jit(solution)/shard_map/first_synth/pallas_call | solution.py:176
  30.6 5.8 %collective-permute-done.2.refs_2_ = f32[512,128]{1,0:T(8,128)S(1)} collective-permute-done((f32[512,128]{1,0:T(8,128)S(1)}, f32[512,128]{1,0:T(8,128)S(1)}, u32[]{:S(2)}, u32[]{:S(2)}) %collective-permute-start.2) | collective-permute-done | bytes 262176 | tf_op jit(solution)/shard_map/ppermute | solution.py:652
  36.4 5.5 %collective-permute-start.10 = (f32[1024,128]{1,0:T(8,128)S(1)}, f32[1024,128]{1,0:T(8,128)S(1)}, u32[]{:S(2)}, u32[]{:S(2)}) collective-permute-start(f32[1024,128]{1,0:T(8,128)S(1)} %get-tuple-element.192), channel_id=1, source_target_pairs={{0,8},{4,12},{8,0},{12,4},{16,24},{20,28},{24,16},{28,20},{1,9},{5... | collective-permute-start | bytes 1572872 | tf_op jit(solution)/shard_map/ppermute | solution.py:652
  41.9 6.4 %earlier_orders.3.refs_6_ = f32[3,8,64,256]{3,2,1,0:T(8,128)S(1)} custom-call(f32[6,3,32,64,256]{4,3,2,1,0:T(8,128)} %refs_4_.8, f32[6,3,32,64,256]{4,3,2,1,0:T(8,128)} %refs_4_.8, f32[6,3,32,64,256]{4,3,2,1,0:T(8,128)} %refs_4_.8, f32[6,3,32,64,256]{4,3,2,1,0:T(8,128)} %refs_4_.8, f32[6,3,32,64,256]{4,3,2,1,0:T(8,128)} %refs_4_.8, ...), custom_call_target="tpu_custom_call" | custom-call | flops 1024 | bytes 1024 | tf_op jit(solution)/shard_map/earlier_orders/pallas_call | solution.py:305
  48.3 3.7 %second_synth.3 = (f32[4,240,128]{2,1,0:T(8,128)S(1)}, f32[4,240,128]{2,1,0:T(8,128)S(1)}, f32[4,240,128]{2,1,0:T(8,128)S(1)}, f32[4,240,128]{2,1,0:T(8,128)S(1)}) custom-call(s32[3]{0:T(128)S(1)} %pad_add_fusion.place_ref, f32[512,128]{1,0:T(8,128)S(1)} %get-tuple-element.162.refs_0_, f32[512,128]{1,0:T(8,128)S(1)} %collective-permute-done.1.refs_1_, ...), custom_call_target="tpu_custom_call" | custom-call | flops 1024 | bytes 1024 | tf_op jit(solution)/shard_map/second_synth/pallas_call | solution.py:253
  58.1 11.7 %earlier_orders.4.refs_6_ = f32[3,16,64,256]{3,2,1,0:T(8,128)S(1)} custom-call(f32[6,3,32,64,256]{4,3,2,1,0:T(8,128)} %refs_4_.8, f32[6,3,32,64,256]{4,3,2,1,0:T(8,128)} %refs_4_.8, f32[6,3,32,64,256]{4,3,2,1,0:T(8,128)} %refs_4_.8, f32[6,3,32,64,256]{4,3,2,1,0:T(8,128)} %refs_4_.8, f32[6,3,32,64,256]{4,3,2,1,0:T(8,128)} %refs_4_.8, ...), custom_call_target="tpu_custom_call" | custom-call | flops 1024 | bytes 1024 | tf_op jit(solution)/shard_map/earlier_orders/pallas_call | solution.py:305
  69.8 6.2 %collective-permute-done.5.refs_2_ = f32[4,240,128]{2,1,0:T(8,128)S(1)} collective-permute-done((f32[4,240,128]{2,1,0:T(8,128)S(1)}, f32[4,240,128]{2,1,0:T(8,128)S(1)}, u32[]{:S(2)}, u32[]{:S(2)}) %collective-permute-start.5) | collective-permute-done | bytes 491552 | tf_op jit(solution)/shard_map/ppermute | solution.py:610
  76.1 6.4 %third_dimension.3 = (f32[4,120,128]{2,1,0:T(8,128)S(1)}, f32[4,120,128]{2,1,0:T(8,128)S(1)}, f32[4,120,128]{2,1,0:T(8,128)S(1)}, f32[4,120,128]{2,1,0:T(8,128)S(1)}) custom-call(s32[3]{0:T(128)S(1)} %pad_add_fusion.place_ref, f32[4,240,128]{2,1,0:T(8,128)S(1)} %get-tuple-element.173.refs_0_, f32[4,240,128]{2,1,0:T(8,128)S(1)} %collective-permute-done.4.refs_1_, ...), custom_call_target="tpu_custom_call" | custom-call | flops 1024 | bytes 1024 | tf_op jit(solution)/shard_map/third_dimension/pallas_call | solution.py:373
  86.1 6.4 %earlier_orders.5.refs_6_ = f32[3,8,64,256]{3,2,1,0:T(8,128)S(1)} custom-call(f32[6,3,32,64,256]{4,3,2,1,0:T(8,128)} %refs_4_.8, f32[6,3,32,64,256]{4,3,2,1,0:T(8,128)} %refs_4_.8, f32[6,3,32,64,256]{4,3,2,1,0:T(8,128)} %refs_4_.8, f32[6,3,32,64,256]{4,3,2,1,0:T(8,128)} %refs_4_.8, f32[6,3,32,64,256]{4,3,2,1,0:T(8,128)} %refs_4_.8, ...), custom_call_target="tpu_custom_call" | custom-call | flops 1024 | bytes 1024 | tf_op jit(solution)/shard_map/earlier_orders/pallas_call | solution.py:305
  98.4 7.5 %second_synth.4 = (f32[8,240,128]{2,1,0:T(8,128)S(1)}, f32[8,240,128]{2,1,0:T(8,128)S(1)}, f32[8,240,128]{2,1,0:T(8,128)S(1)}, f32[8,240,128]{2,1,0:T(8,128)S(1)}) custom-call(s32[3]{0:T(128)S(1)} %pad_add_fusion.place_ref, f32[1024,128]{1,0:T(8,128)S(1)} %copy-done.8, f32[1024,128]{1,0:T(8,128)S(1)} %copy-done.12, ...), custom_call_target="tpu_custom_call" | custom-call | flops 1024 | bytes 1024 | tf_op jit(solution)/shard_map/second_synth/pallas_call | solution.py:253
  109.5 5.6 %collective-permute-start.13 = (f32[304,128]{1,0:T(8,128)S(1)}, f32[304,128]{1,0:T(8,128)S(1)}, u32[]{:S(2)}, u32[]{:S(2)}) collective-permute-start(f32[304,128]{1,0:T(8,128)S(1)} %get-tuple-element.197), channel_id=1, source_target_pairs={{0,8},{4,12},{8,0},{12,4},{16,24},{20,28},{24,16},{28,20},{1,9},{5... | collective-permute-start | bytes 466952 | tf_op jit(solution)/shard_map/ppermute | solution.py:652
  116.0 4.5 %collective-permute-done.13.refs_1_ = f32[304,128]{1,0:T(8,128)S(1)} collective-permute-done((f32[304,128]{1,0:T(8,128)S(1)}, f32[304,128]{1,0:T(8,128)S(1)}, u32[]{:S(2)}, u32[]{:S(2)}) %collective-permute-start.13) | collective-permute-done | bytes 155680 | tf_op jit(solution)/shard_map/ppermute | solution.py:652
  122.1 6.6 %collective-permute-done.14.refs_2_ = f32[304,128]{1,0:T(8,128)S(1)} collective-permute-done((f32[304,128]{1,0:T(8,128)S(1)}, f32[304,128]{1,0:T(8,128)S(1)}, u32[]{:S(2)}, u32[]{:S(2)}) %collective-permute-start.14) | collective-permute-done | bytes 155680 | tf_op jit(solution)/shard_map/ppermute | solution.py:652
  128.7 2.7 %collective-permute-start.19 = (f32[512,128]{1,0:T(8,128)S(1)}, f32[512,128]{1,0:T(8,128)S(1)}, u32[]{:S(2)}, u32[]{:S(2)}) collective-permute-start(f32[512,128]{1,0:T(8,128)S(1)} %copy-done.14), channel_id=1, source_target_pairs={{0,8},{4,12},{8,0},{12,4},{16,24},{20,28},{24,16},{28,20},{1,9},{5... | collective-permute-start | bytes 786440 | tf_op jit(solution)/shard_map/ppermute | solution.py:652
  132.3 9.6 %collective-permute-done.19.refs_1_ = f32[512,128]{1,0:T(8,128)S(1)} collective-permute-done((f32[512,128]{1,0:T(8,128)S(1)}, f32[512,128]{1,0:T(8,128)S(1)}, u32[]{:S(2)}, u32[]{:S(2)}) %collective-permute-start.19) | collective-permute-done | bytes 262176 | tf_op jit(solution)/shard_map/ppermute | solution.py:652
  143.6 7.5 %collective-permute-done.20.refs_2_ = f32[512,128]{1,0:T(8,128)S(1)} collective-permute-done((f32[512,128]{1,0:T(8,128)S(1)}, f32[512,128]{1,0:T(8,128)S(1)}, u32[]{:S(2)}, u32[]{:S(2)}) %collective-permute-start.20) | collective-permute-done | bytes 262176 | tf_op jit(solution)/shard_map/ppermute | solution.py:652
  151.0 3.7 %second_synth.5 = (f32[4,240,128]{2,1,0:T(8,128)S(1)}, f32[4,240,128]{2,1,0:T(8,128)S(1)}, f32[4,240,128]{2,1,0:T(8,128)S(1)}, f32[4,240,128]{2,1,0:T(8,128)S(1)}) custom-call(s32[3]{0:T(128)S(1)} %pad_add_fusion.place_ref, f32[512,128]{1,0:T(8,128)S(1)} %copy-done.10, f32[512,128]{1,0:T(8,128)S(1)} %collective-permute-done.19.refs_1_, ...), custom_call_target="tpu_custom_call" | custom-call | flops 1024 | bytes 1024 | tf_op jit(solution)/shard_map/second_synth/pallas_call | solution.py:253
  158.3 12.1 %third_dimension.4 = (f32[8,120,128]{2,1,0:T(8,128)S(1)}, f32[8,120,128]{2,1,0:T(8,128)S(1)}, f32[8,120,128]{2,1,0:T(8,128)S(1)}, f32[8,120,128]{2,1,0:T(8,128)S(1)}) custom-call(s32[3]{0:T(128)S(1)} %pad_add_fusion.place_ref, f32[8,240,128]{2,1,0:T(8,128)S(1)} %get-tuple-element.224.refs_0_, f32[8,240,128]{2,1,0:T(8,128)S(1)} %collective-permute-done.16.refs_1_, ...), custom_call_target="tpu_custom_call" | custom-call | flops 1024 | bytes 1024 | tf_op jit(solution)/shard_map/third_dimension/pallas_call | solution.py:373
  174.1 6.5 %collective-permute-done.27.refs_3_ = f32[4,240,128]{2,1,0:T(8,128)S(1)} collective-permute-done((f32[4,240,128]{2,1,0:T(8,128)S(1)}, f32[4,240,128]{2,1,0:T(8,128)S(1)}, u32[]{:S(2)}, u32[]{:S(2)}) %collective-permute-start.27) | collective-permute-done | bytes 491552 | tf_op jit(solution)/shard_map/ppermute | solution.py:610
  180.5 6.4 %third_dimension.5 = (f32[4,120,128]{2,1,0:T(8,128)S(1)}, f32[4,120,128]{2,1,0:T(8,128)S(1)}, f32[4,120,128]{2,1,0:T(8,128)S(1)}, f32[4,120,128]{2,1,0:T(8,128)S(1)}) custom-call(s32[3]{0:T(128)S(1)} %pad_add_fusion.place_ref, f32[4,240,128]{2,1,0:T(8,128)S(1)} %get-tuple-element.238.refs_0_, f32[4,240,128]{2,1,0:T(8,128)S(1)} %collective-permute-done.25.refs_1_, ...), custom_call_target="tpu_custom_call" | custom-call | flops 1024 | bytes 1024 | tf_op jit(solution)/shard_map/third_dimension/pallas_call | solution.py:373
  192.2 7.1 %collective-permute-done.24.refs_3_ = f32[8,120,128]{2,1,0:T(8,128)S(1)} collective-permute-done((f32[8,120,128]{2,1,0:T(8,128)S(1)}, f32[8,120,128]{2,1,0:T(8,128)S(1)}, u32[]{:S(2)}, u32[]{:S(2)}) %collective-permute-start.24) | collective-permute-done | bytes 491552 | tf_op jit(solution)/shard_map/ppermute | solution.py:610
  199.3 4.4 %second_back.4 = (f32[608,128]{1,0:T(8,128)S(1)}, f32[608,128]{1,0:T(8,128)S(1)}, f32[608,128]{1,0:T(8,128)S(1)}, f32[608,128]{1,0:T(8,128)S(1)}) custom-call(s32[3]{0:T(128)S(1)} %pad_add_fusion.place_ref, f32[8,120,128]{2,1,0:T(8,128)S(1)} %get-tuple-element.243.refs_0_, f32[8,120,128]{2,1,0:T(8,128)S(1)} %collective-permute-done.22.refs_1_, ...), custom_call_target="tpu_custom_call" | custom-call | flops 1024 | bytes 1024 | tf_op jit(solution)/shard_map/second_back/pallas_call | solution.py:422
  205.4 7.8 %collective-permute-start.29 = (f32[608,128]{1,0:T(8,128)S(1)}, f32[608,128]{1,0:T(8,128)S(1)}, u32[]{:S(2)}, u32[]{:S(2)}) collective-permute-start(f32[608,128]{1,0:T(8,128)S(1)} %get-tuple-element.251), channel_id=1, source_target_pairs={{0,16},{4,20},{8,24},{12,28},{16,0},{20,4},{24,8},{28,12},{1,17},{... | collective-permute-start | bytes 933896 | tf_op jit(solution)/shard_map/ppermute | solution.py:652
  216.1 7.0 %collective-permute-done.32.refs_2_ = f32[4,120,128]{2,1,0:T(8,128)S(1)} collective-permute-done((f32[4,120,128]{2,1,0:T(8,128)S(1)}, f32[4,120,128]{2,1,0:T(8,128)S(1)}, u32[]{:S(2)}, u32[]{:S(2)}) %collective-permute-start.32) | collective-permute-done | bytes 245792 | tf_op jit(solution)/shard_map/ppermute | solution.py:610
  225.7 6.7 %collective-permute-done.29.refs_6_ = f32[608,128]{1,0:T(8,128)S(1)} collective-permute-done((f32[608,128]{1,0:T(8,128)S(1)}, f32[608,128]{1,0:T(8,128)S(1)}, u32[]{:S(2)}, u32[]{:S(2)}) %collective-permute-start.29) | collective-permute-done | bytes 311328 | tf_op jit(solution)/shard_map/ppermute | solution.py:652
  236.8 3.4 %collective-permute-done.34.refs_9_ = f32[304,128]{1,0:T(8,128)S(1)} collective-permute-done((f32[304,128]{1,0:T(8,128)S(1)}, f32[304,128]{1,0:T(8,128)S(1)}, u32[]{:S(2)}, u32[]{:S(2)}) %collective-permute-start.34) | collective-permute-done | bytes 155680 | tf_op jit(solution)/shard_map/ppermute | solution.py:652
  240.3 6.7 %collective-permute-done.35.refs_10_ = f32[304,128]{1,0:T(8,128)S(1)} collective-permute-done((f32[304,128]{1,0:T(8,128)S(1)}, f32[304,128]{1,0:T(8,128)S(1)}, u32[]{:S(2)}, u32[]{:S(2)}) %collective-permute-start.35) | collective-permute-done | bytes 155680 | tf_op jit(solution)/shard_map/ppermute | solution.py:652
  251.7 6.2 %last_projection.1 = f32[3,20,40,160]{3,2,1,0:T(8,128)} custom-call(f32[10]{0:T(128)S(1)} %convert_multiply_fusion.1.refs_0_, f32[8,256]{1,0:T(8,128)S(1)} %broadcast_in_dim.9.refs_1_, f32[40,256]{1,0:T(8,128)S(1)} %broadcast_in_dim.18.refs_2_, f32[160,2432]{1,0:T(8,128)S(1)} %first_back.3.refs_3_, f32[160,2432]{1,0:T(8,128)S(1)} %collective-permute-done.37.refs_4_), custom_call_target="tpu_custom_call" | custom-call | flops 1024 | bytes 1024 | tf_op jit(solution)/shard_map/last_projection/pallas_call | solution.py:521
  (109 shorter events, 62.1 us)
Async XLA Ops:
  12.4 18.1 %collective-permute-start.1 = (f32[512,128]{1,0:T(8,128)S(1)}, f32[512,128]{1,0:T(8,128)S(1)}, u32[]{:S(2)}, u32[]{:S(2)}) collective-permute-start(f32[512,128]{1,0:T(8,128)S(1)} %get-tuple-element.147), channel_id=1, source_target_pairs={{0,8},{4,12},{8,0},{12,4},{16,24},{20,28},{24,16},{28,20},{1,9},{5... | collective-permute-start | bytes 786440 | tf_op jit(solution)/shard_map/ppermute | solution.py:652
  15.1 21.3 %collective-permute-start.2 = (f32[512,128]{1,0:T(8,128)S(1)}, f32[512,128]{1,0:T(8,128)S(1)}, u32[]{:S(2)}, u32[]{:S(2)}) collective-permute-start(f32[512,128]{1,0:T(8,128)S(1)} %get-tuple-element.148), channel_id=1, source_target_pairs={{0,16},{4,20},{8,24},{12,28},{16,0},{20,4},{24,8},{28,12},{1,17},{... | collective-permute-start | bytes 786440 | tf_op jit(solution)/shard_map/ppermute | solution.py:652
  17.7 18.7 %collective-permute-start.3 = (f32[512,128]{1,0:T(8,128)S(1)}, f32[512,128]{1,0:T(8,128)S(1)}, u32[]{:S(2)}, u32[]{:S(2)}) collective-permute-start(f32[512,128]{1,0:T(8,128)S(1)} %get-tuple-element.149), channel_id=1, source_target_pairs={{0,24},{4,28},{8,16},{12,20},{16,8},{20,12},{24,0},{28,4},{1,25},{... | collective-permute-start | bytes 786440 | tf_op jit(solution)/shard_map/ppermute | solution.py:652
  36.4 20.2 %collective-permute-start.10 = (f32[1024,128]{1,0:T(8,128)S(1)}, f32[1024,128]{1,0:T(8,128)S(1)}, u32[]{:S(2)}, u32[]{:S(2)}) collective-permute-start(f32[1024,128]{1,0:T(8,128)S(1)} %get-tuple-element.192), channel_id=1, source_target_pairs={{0,8},{4,12},{8,0},{12,4},{16,24},{20,28},{24,16},{28,20},{1,9},{5... | collective-permute-start | bytes 1572872 | tf_op jit(solution)/shard_map/ppermute | solution.py:652
  52.0 17.8 %collective-permute-start.4 = (f32[4,240,128]{2,1,0:T(8,128)S(1)}, f32[4,240,128]{2,1,0:T(8,128)S(1)}, u32[]{:S(2)}, u32[]{:S(2)}) collective-permute-start(f32[4,240,128]{2,1,0:T(8,128)S(1)} %get-tuple-element.168), channel_id=1, source_target_pairs={{0,1},{1,0},{2,3},{3,2},{4,5},{5,4},{6,7},{7,6},{8,9},{9,8},{10,11... | collective-permute-start | bytes 1474568 | tf_op jit(solution)/shard_map/ppermute | solution.py:610
  53.6 22.5 %collective-permute-start.5 = (f32[4,240,128]{2,1,0:T(8,128)S(1)}, f32[4,240,128]{2,1,0:T(8,128)S(1)}, u32[]{:S(2)}, u32[]{:S(2)}) collective-permute-start(f32[4,240,128]{2,1,0:T(8,128)S(1)} %get-tuple-element.169), channel_id=1, source_target_pairs={{0,2},{1,3},{2,0},{3,1},{4,6},{5,7},{6,4},{7,5},{8,10},{9,11},{10,... | collective-permute-start | bytes 1474568 | tf_op jit(solution)/shard_map/ppermute | solution.py:610
  55.1 21.0 %collective-permute-start.6 = (f32[4,240,128]{2,1,0:T(8,128)S(1)}, f32[4,240,128]{2,1,0:T(8,128)S(1)}, u32[]{:S(2)}, u32[]{:S(2)}) collective-permute-start(f32[4,240,128]{2,1,0:T(8,128)S(1)} %get-tuple-element.170), channel_id=1, source_target_pairs={{0,3},{1,2},{2,1},{3,0},{4,7},{5,6},{6,5},{7,4},{8,11},{9,10},{10,... | collective-permute-start | bytes 1474568 | tf_op jit(solution)/shard_map/ppermute | solution.py:610
  55.6 41.8 %collective-permute-start.11 = (f32[1024,128]{1,0:T(8,128)}, f32[1024,128]{1,0:T(8,128)}, u32[]{:S(2)}, u32[]{:S(2)}) collective-permute-start(f32[1024,128]{1,0:T(8,128)} %get-tuple-element.194), channel_id=1, source_target_pairs={{0,16},{4,20},{8,24},{12,28},{16,0},{20,4},{24,8},{28,12},{1,17},{... | collective-permute-start | bytes 1572872 | tf_op jit(solution)/shard_map/ppermute | solution.py:652
  56.6 40.8 %collective-permute-start.12 = (f32[1024,128]{1,0:T(8,128)}, f32[1024,128]{1,0:T(8,128)}, u32[]{:S(2)}, u32[]{:S(2)}) collective-permute-start(f32[1024,128]{1,0:T(8,128)} %get-tuple-element.196), channel_id=1, source_target_pairs={{0,24},{4,28},{8,16},{12,20},{16,8},{20,12},{24,0},{28,4},{1,25},{... | collective-permute-start | bytes 1572872 | tf_op jit(solution)/shard_map/ppermute | solution.py:652
  82.5 10.0 %collective-permute-start.7 = (f32[4,120,128]{2,1,0:T(8,128)S(1)}, f32[4,120,128]{2,1,0:T(8,128)S(1)}, u32[]{:S(2)}, u32[]{:S(2)}) collective-permute-start(f32[4,120,128]{2,1,0:T(8,128)S(1)} %get-tuple-element.179), channel_id=1, source_target_pairs={{0,1},{1,0},{2,3},{3,2},{4,5},{5,4},{6,7},{7,6},{8,9},{9,8},{10,11... | collective-permute-start | bytes 737288 | tf_op jit(solution)/shard_map/ppermute | solution.py:610
  83.8 11.2 %collective-permute-start.8 = (f32[4,120,128]{2,1,0:T(8,128)S(1)}, f32[4,120,128]{2,1,0:T(8,128)S(1)}, u32[]{:S(2)}, u32[]{:S(2)}) collective-permute-start(f32[4,120,128]{2,1,0:T(8,128)S(1)} %get-tuple-element.180), channel_id=1, source_target_pairs={{0,2},{1,3},{2,0},{3,1},{4,6},{5,7},{6,4},{7,5},{8,10},{9,11},{10,... | collective-permute-start | bytes 737288 | tf_op jit(solution)/shard_map/ppermute | solution.py:610
  84.6 10.3 %collective-permute-start.9 = (f32[4,120,128]{2,1,0:T(8,128)S(1)}, f32[4,120,128]{2,1,0:T(8,128)S(1)}, u32[]{:S(2)}, u32[]{:S(2)}) collective-permute-start(f32[4,120,128]{2,1,0:T(8,128)S(1)} %get-tuple-element.181), channel_id=1, source_target_pairs={{0,3},{1,2},{2,1},{3,0},{4,7},{5,6},{6,5},{7,4},{8,11},{9,10},{10,... | collective-permute-start | bytes 737288 | tf_op jit(solution)/shard_map/ppermute | solution.py:610
  105.9 48.8 %collective-permute-start.18 = (f32[8,240,128]{2,1,0:T(8,128)S(1)}, f32[8,240,128]{2,1,0:T(8,128)S(1)}, u32[]{:S(2)}, u32[]{:S(2)}) collective-permute-start(f32[8,240,128]{2,1,0:T(8,128)S(1)} %get-tuple-element.212), channel_id=1, source_target_pairs={{0,3},{1,2},{2,1},{3,0},{4,7},{5,6},{6,5},{7,4},{8,11},{9,10},{10,... | collective-permute-start | bytes 2949128 | tf_op jit(solution)/shard_map/ppermute | solution.py:610
  107.6 47.2 %collective-permute-start.17 = (f32[8,240,128]{2,1,0:T(8,128)S(1)}, f32[8,240,128]{2,1,0:T(8,128)S(1)}, u32[]{:S(2)}, u32[]{:S(2)}) collective-permute-start(f32[8,240,128]{2,1,0:T(8,128)S(1)} %get-tuple-element.210), channel_id=1, source_target_pairs={{0,2},{1,3},{2,0},{3,1},{4,6},{5,7},{6,4},{7,5},{8,10},{9,11},{10,... | collective-permute-start | bytes 2949128 | tf_op jit(solution)/shard_map/ppermute | solution.py:610
  108.0 46.7 %collective-permute-start.16 = (f32[8,240,128]{2,1,0:T(8,128)S(1)}, f32[8,240,128]{2,1,0:T(8,128)S(1)}, u32[]{:S(2)}, u32[]{:S(2)}) collective-permute-start(f32[8,240,128]{2,1,0:T(8,128)S(1)} %get-tuple-element.208), channel_id=1, source_target_pairs={{0,1},{1,0},{2,3},{3,2},{4,5},{5,4},{6,7},{7,6},{8,9},{9,8},{10,11... | collective-permute-start | bytes 2949128 | tf_op jit(solution)/shard_map/ppermute | solution.py:610
  109.5 11.0 %collective-permute-start.13 = (f32[304,128]{1,0:T(8,128)S(1)}, f32[304,128]{1,0:T(8,128)S(1)}, u32[]{:S(2)}, u32[]{:S(2)}) collective-permute-start(f32[304,128]{1,0:T(8,128)S(1)} %get-tuple-element.197), channel_id=1, source_target_pairs={{0,8},{4,12},{8,0},{12,4},{16,24},{20,28},{24,16},{28,20},{1,9},{5... | collective-permute-start | bytes 466952 | tf_op jit(solution)/shard_map/ppermute | solution.py:652
  115.1 13.6 %collective-permute-start.14 = (f32[304,128]{1,0:T(8,128)S(1)}, f32[304,128]{1,0:T(8,128)S(1)}, u32[]{:S(2)}, u32[]{:S(2)}) collective-permute-start(f32[304,128]{1,0:T(8,128)S(1)} %get-tuple-element.199), channel_id=1, source_target_pairs={{0,16},{4,20},{8,24},{12,28},{16,0},{20,4},{24,8},{28,12},{1,17},{... | collective-permute-start | bytes 466952 | tf_op jit(solution)/shard_map/ppermute | solution.py:652
  128.7 13.3 %collective-permute-start.19 = (f32[512,128]{1,0:T(8,128)S(1)}, f32[512,128]{1,0:T(8,128)S(1)}, u32[]{:S(2)}, u32[]{:S(2)}) collective-permute-start(f32[512,128]{1,0:T(8,128)S(1)} %copy-done.14), channel_id=1, source_target_pairs={{0,8},{4,12},{8,0},{12,4},{16,24},{20,28},{24,16},{28,20},{1,9},{5... | collective-permute-start | bytes 786440 | tf_op jit(solution)/shard_map/ppermute | solution.py:652
  131.4 19.6 %collective-permute-start.20 = (f32[512,128]{1,0:T(8,128)S(1)}, f32[512,128]{1,0:T(8,128)S(1)}, u32[]{:S(2)}, u32[]{:S(2)}) collective-permute-start(f32[512,128]{1,0:T(8,128)S(1)} %copy-done.16), channel_id=1, source_target_pairs={{0,16},{4,20},{8,24},{12,28},{16,0},{20,4},{24,8},{28,12},{1,17},{... | collective-permute-start | bytes 786440 | tf_op jit(solution)/shard_map/ppermute | solution.py:652
  154.8 18.8 %collective-permute-start.25 = (f32[4,240,128]{2,1,0:T(8,128)S(1)}, f32[4,240,128]{2,1,0:T(8,128)S(1)}, u32[]{:S(2)}, u32[]{:S(2)}) collective-permute-start(f32[4,240,128]{2,1,0:T(8,128)S(1)} %get-tuple-element.233), channel_id=1, source_target_pairs={{0,1},{1,0},{2,3},{3,2},{4,5},{5,4},{6,7},{7,6},{8,9},{9,8},{10,11... | collective-permute-start | bytes 1474568 | tf_op jit(solution)/shard_map/ppermute | solution.py:610
  156.3 17.7 %collective-permute-start.26 = (f32[4,240,128]{2,1,0:T(8,128)S(1)}, f32[4,240,128]{2,1,0:T(8,128)S(1)}, u32[]{:S(2)}, u32[]{:S(2)}) collective-permute-start(f32[4,240,128]{2,1,0:T(8,128)S(1)} %get-tuple-element.235), channel_id=1, source_target_pairs={{0,2},{1,3},{2,0},{3,1},{4,6},{5,7},{6,4},{7,5},{8,10},{9,11},{10,... | collective-permute-start | bytes 1474568 | tf_op jit(solution)/shard_map/ppermute | solution.py:610
  157.8 22.7 %collective-permute-start.27 = (f32[4,240,128]{2,1,0:T(8,128)S(1)}, f32[4,240,128]{2,1,0:T(8,128)S(1)}, u32[]{:S(2)}, u32[]{:S(2)}) collective-permute-start(f32[4,240,128]{2,1,0:T(8,128)S(1)} %get-tuple-element.237), channel_id=1, source_target_pairs={{0,3},{1,2},{2,1},{3,0},{4,7},{5,6},{6,5},{7,4},{8,11},{9,10},{10,... | collective-permute-start | bytes 1474568 | tf_op jit(solution)/shard_map/ppermute | solution.py:610
  170.5 19.6 %collective-permute-start.22 = (f32[8,120,128]{2,1,0:T(8,128)S(1)}, f32[8,120,128]{2,1,0:T(8,128)S(1)}, u32[]{:S(2)}, u32[]{:S(2)}) collective-permute-start(f32[8,120,128]{2,1,0:T(8,128)S(1)} %get-tuple-element.229), channel_id=1, source_target_pairs={{0,1},{1,0},{2,3},{3,2},{4,5},{5,4},{6,7},{7,6},{8,9},{9,8},{10,11... | collective-permute-start | bytes 1474568 | tf_op jit(solution)/shard_map/ppermute | solution.py:610
  172.0 20.2 %collective-permute-start.23 = (f32[8,120,128]{2,1,0:T(8,128)S(1)}, f32[8,120,128]{2,1,0:T(8,128)S(1)}, u32[]{:S(2)}, u32[]{:S(2)}) collective-permute-start(f32[8,120,128]{2,1,0:T(8,128)S(1)} %get-tuple-element.230), channel_id=1, source_target_pairs={{0,2},{1,3},{2,0},{3,1},{4,6},{5,7},{6,4},{7,5},{8,10},{9,11},{10,... | collective-permute-start | bytes 1474568 | tf_op jit(solution)/shard_map/ppermute | solution.py:610
  173.6 25.7 %collective-permute-start.24 = (f32[8,120,128]{2,1,0:T(8,128)S(1)}, f32[8,120,128]{2,1,0:T(8,128)S(1)}, u32[]{:S(2)}, u32[]{:S(2)}) collective-permute-start(f32[8,120,128]{2,1,0:T(8,128)S(1)} %get-tuple-element.231), channel_id=1, source_target_pairs={{0,3},{1,2},{2,1},{3,0},{4,7},{5,6},{6,5},{7,4},{8,11},{9,10},{10,... | collective-permute-start | bytes 1474568 | tf_op jit(solution)/shard_map/ppermute | solution.py:610
  186.9 26.8 %collective-permute-start.31 = (f32[4,120,128]{2,1,0:T(8,128)S(1)}, f32[4,120,128]{2,1,0:T(8,128)S(1)}, u32[]{:S(2)}, u32[]{:S(2)}) collective-permute-start(f32[4,120,128]{2,1,0:T(8,128)S(1)} %get-tuple-element.254), channel_id=1, source_target_pairs={{0,1},{1,0},{2,3},{3,2},{4,5},{5,4},{6,7},{7,6},{8,9},{9,8},{10,11... | collective-permute-start | bytes 737288 | tf_op jit(solution)/shard_map/ppermute | solution.py:610
  203.7 22.0 %collective-permute-start.30 = (f32[608,128]{1,0:T(8,128)S(1)}, f32[608,128]{1,0:T(8,128)S(1)}, u32[]{:S(2)}, u32[]{:S(2)}) collective-permute-start(f32[608,128]{1,0:T(8,128)S(1)} %get-tuple-element.253), channel_id=1, source_target_pairs={{0,24},{4,28},{8,16},{12,20},{16,8},{20,12},{24,0},{28,4},{1,25},{... | collective-permute-start | bytes 933896 | tf_op jit(solution)/shard_map/ppermute | solution.py:652
  205.4 27.0 %collective-permute-start.29 = (f32[608,128]{1,0:T(8,128)S(1)}, f32[608,128]{1,0:T(8,128)S(1)}, u32[]{:S(2)}, u32[]{:S(2)}) collective-permute-start(f32[608,128]{1,0:T(8,128)S(1)} %get-tuple-element.251), channel_id=1, source_target_pairs={{0,16},{4,20},{8,24},{12,28},{16,0},{20,4},{24,8},{28,12},{1,17},{... | collective-permute-start | bytes 933896 | tf_op jit(solution)/shard_map/ppermute | solution.py:652
  213.2 19.2 %collective-permute-start.28 = (f32[608,128]{1,0:T(8,128)S(1)}, f32[608,128]{1,0:T(8,128)S(1)}, u32[]{:S(2)}, u32[]{:S(2)}) collective-permute-start(f32[608,128]{1,0:T(8,128)S(1)} %get-tuple-element.249), channel_id=1, source_target_pairs={{0,8},{4,12},{8,0},{12,4},{16,24},{20,28},{24,16},{28,20},{1,9},{5... | collective-permute-start | bytes 933896 | tf_op jit(solution)/shard_map/ppermute | solution.py:652
  213.2 9.9 %collective-permute-start.32 = (f32[4,120,128]{2,1,0:T(8,128)S(1)}, f32[4,120,128]{2,1,0:T(8,128)S(1)}, u32[]{:S(2)}, u32[]{:S(2)}) collective-permute-start(f32[4,120,128]{2,1,0:T(8,128)S(1)} %get-tuple-element.255), channel_id=1, source_target_pairs={{0,2},{1,3},{2,0},{3,1},{4,6},{5,7},{6,4},{7,5},{8,10},{9,11},{10,... | collective-permute-start | bytes 737288 | tf_op jit(solution)/shard_map/ppermute | solution.py:610
  232.4 14.5 %collective-permute-start.35 = (f32[304,128]{1,0:T(8,128)S(1)}, f32[304,128]{1,0:T(8,128)S(1)}, u32[]{:S(2)}, u32[]{:S(2)}) collective-permute-start(f32[304,128]{1,0:T(8,128)S(1)} %get-tuple-element.265), channel_id=1, source_target_pairs={{0,16},{4,20},{8,24},{12,28},{16,0},{20,4},{24,8},{28,12},{1,17},{... | collective-permute-start | bytes 466952 | tf_op jit(solution)/shard_map/ppermute | solution.py:652
  234.7 12.3 %collective-permute-start.36 = (f32[304,128]{1,0:T(8,128)S(1)}, f32[304,128]{1,0:T(8,128)S(1)}, u32[]{:S(2)}, u32[]{:S(2)}) collective-permute-start(f32[304,128]{1,0:T(8,128)S(1)} %get-tuple-element.267), channel_id=1, source_target_pairs={{0,24},{4,28},{8,16},{12,20},{16,8},{20,12},{24,0},{28,4},{1,25},{... | collective-permute-start | bytes 466952 | tf_op jit(solution)/shard_map/ppermute | solution.py:652
  (25 other events, 501.5 us)

commit v9 on v8

--- a/solution.py
+++ b/solution.py
@@ -115,24 +115,16 @@
     return pl.BlockSpec(array.shape, lambda *_: (0,) * rank)
 
 
-def first_synth_kernel(dims, place_ref, data_ref, table_ref, *rest):
+def first_synth_kernel(dims, place_ref, data, table_ref, *rest):
     sizes, chosen, dests, own = dims
-    outs = rest[-len(chosen) * dests - 3 : -3]
-    data, rows, sem = rest[-3:]
+    outs, rows = rest[-len(chosen) * dests - 1 : -1], rest[-1]
     _, ky_len, kz_len, _ = data.shape
     group = 5 * kz_len
-    copies = [
-        pltpu.make_async_copy(data_ref.at[comp], data.at[comp], sem.at[comp]) for comp in range(3)
-    ]
-    for copy in copies:
-        copy.start()
     if ky_len * group < rows.shape[0]:
         rows[ky_len * group :, :] = jnp.zeros((rows.shape[0] - ky_len * group, LANES), F32)
     plain = jnp.concatenate([table_ref[0], table_ref[1]], axis=1)
     slope = jnp.concatenate([table_ref[2], table_ref[3]], axis=1)
     step = 4 if ky_len % 4 == 0 else 2
-    for copy in copies:
-        copy.wait()
 
     def body(idx, carry):
         first = idx * step
@@ -175,15 +167,11 @@
     heights = [2 * (lanes // LANES) * sizes[chunk] for chunk in chosen for _ in range(dests)]
     return pl.pallas_call(
         functools.partial(first_synth_kernel, (sizes, chosen, dests, not half)),
-        in_specs=[SMEM, ANY, VMEM] + [ANY] * len(half),
+        in_specs=[SMEM, VMEM, VMEM] + [ANY] * len(half),
         out_specs=[VMEM] * len(heights),
         out_shape=[jax.ShapeDtypeStruct((h, LANES), F32) for h in heights],
         input_output_aliases={3 + k: k for k in range(len(half))},
-        scratch_shapes=[
-            pltpu.VMEM(coeffs.shape, F32),
-            pltpu.VMEM((lanes, LANES), F32),
-            pltpu.SemaphoreType.DMA((3,)),
-        ],
+        scratch_shapes=[pltpu.VMEM((lanes, LANES), F32)],
         compiler_params=still(),
         cost_estimate=SHORT,
         name="first_synth",
@@ -463,69 +451,86 @@
 
 def last_kernel(dims, *refs):
     kz_len, modes, scale = dims
-    wave_y_ref, wave_x_ref, wave_z_ref, *sums, out_ref, rows = refs
+    wave_y_ref, wave_x_ref, wave_z_ref, *sums, out_ref, rows, held, sem = refs
     pair = 2 * 3 * kz_len
-    at = pl.program_id(0)
-
-    @pl.when(at == 0)
-    def _():
-        for tile in range(rows.shape[0] // LANES):
-            lanes = slice(tile * LANES, (tile + 1) * LANES)
-            rows[lanes, 0:modes] = functools.reduce(jnp.add, [part[:, lanes] for part in sums]).T
-
-    spec = rows[pl.ds(pl.multiple_of(at * pair, 8), pair), :]
-    wide = spec.shape[1]
-    wave_x = jnp.broadcast_to(wave_x_ref[0:1, :], (kz_len, wide))
-    wave_z = wave_z_ref[...]
-    wave_y = wave_y_ref[at]
-    even_x = lax.broadcasted_iota(jnp.int32, (kz_len, wide), 1) % 2 == 0
-    even_z = lax.broadcasted_iota(jnp.int32, (kz_len, wide), 0) % 2 == 0
-
-    def slope_x(value):
-        return jnp.where(even_x, turn(value, -1), -turn(value, 1)) * wave_x
-
-    def slope_z(value):
-        return (
-            jnp.where(
-                even_z,
-                pltpu.roll(value, kz_len - 1, axis=0),
-                -pltpu.roll(value, 1, axis=0),
+    for tile in range(rows.shape[0] // LANES):
+        lanes = slice(tile * LANES, (tile + 1) * LANES)
+        rows[lanes, 0:modes] = functools.reduce(jnp.add, [part[:, lanes] for part in sums]).T
+
+    def copy(at):
+        spot = pl.ds(2 * at, 2)
+        return pltpu.make_async_copy(held.at[:, spot], out_ref.at[:, spot], sem.at[at])
+
+    def body(at, carry):
+        project(at)
+        copy(at).start()
+        return carry
+
+    def finish(at, carry):
+        copy(at).wait()
+        return carry
+
+    def project(at):
+        spec = rows[pl.ds(pl.multiple_of(at * pair, 8), pair), :]
+        wide = spec.shape[1]
+        wave_x = jnp.broadcast_to(wave_x_ref[0:1, :], (kz_len, wide))
+        wave_z = wave_z_ref[...]
+        wave_y = wave_y_ref[at]
+        even_x = lax.broadcasted_iota(jnp.int32, (kz_len, wide), 1) % 2 == 0
+        even_z = lax.broadcasted_iota(jnp.int32, (kz_len, wide), 0) % 2 == 0
+
+        def slope_x(value):
+            return jnp.where(even_x, turn(value, -1), -turn(value, 1)) * wave_x
+
+        def slope_z(value):
+            return (
+                jnp.where(
+                    even_z,
+                    pltpu.roll(value, kz_len - 1, axis=0),
+                    -pltpu.roll(value, 1, axis=0),
+                )
+                * wave_z
             )
-            * wave_z
-        )
-
-    s = [
-        [spec[(y * 3 + c) * kz_len : (y * 3 + c + 1) * kz_len] for c in range(3)] for y in range(2)
-    ]
-    square = wave_x * wave_x + wave_z * wave_z + wave_y * wave_y
-    positive = square > 0
-    safe = jnp.where(positive, square, 1.0)
-    potential = []
-    for y in range(2):
-        along_y = s[1 - y][1] * (wave_y if y == 0 else -wave_y)
-        divergence = slope_x(s[y][0]) + along_y + slope_z(s[y][2])
-        potential.append(jnp.where(positive, divergence / safe, 0.0))
-    for y in range(2):
-        along_y = potential[1 - y] * (wave_y if y == 0 else -wave_y)
-        found = [
-            s[y][0] + slope_x(potential[y]),
-            s[y][1] + along_y,
-            s[y][2] + slope_z(potential[y]),
+
+        s = [
+            [spec[(y * 3 + c) * kz_len : (y * 3 + c + 1) * kz_len] for c in range(3)] for y in range(2)
         ]
-        for comp in range(3):
-            out_ref[comp, y] = (found[comp] * scale)[:, :modes]
+        square = wave_x * wave_x + wave_z * wave_z + wave_y * wave_y
+        positive = square > 0
+        safe = jnp.where(positive, square, 1.0)
+        potential = []
+        for y in range(2):
+            along_y = s[1 - y][1] * (wave_y if y == 0 else -wave_y)
+            divergence = slope_x(s[y][0]) + along_y + slope_z(s[y][2])
+            potential.append(jnp.where(positive, divergence / safe, 0.0))
+        for y in range(2):
+            along_y = potential[1 - y] * (wave_y if y == 0 else -wave_y)
+            found = [
+                s[y][0] + slope_x(potential[y]),
+                s[y][1] + along_y,
+                s[y][2] + slope_z(potential[y]),
+            ]
+            for comp in range(3):
+                held[comp, 2 * at + y] = (found[comp] * scale)[:, :modes]
+
+    steps = held.shape[1] // 2
+    lax.fori_loop(0, steps, body, 0)
+    lax.fori_loop(0, steps, finish, 0)
 
 
 def last(sums, wave_y, wave_x, wave_z, ky_len, kz_len, scale):
     modes, lanes = sums[0].shape
     return pl.pallas_call(
         functools.partial(last_kernel, (kz_len, modes, scale)),
-        grid=(ky_len // 2,),
-        in_specs=[SMEM, *[whole(a) for a in (wave_x, wave_z, *sums)]],
-        out_specs=pl.BlockSpec((3, 2, kz_len, modes), lambda i: (0, i, 0, 0)),
+        in_specs=[SMEM] + [VMEM] * (2 + len(sums)),
+        out_specs=ANY,
         out_shape=jax.ShapeDtypeStruct((3, ky_len, kz_len, modes), F32),
-        scratch_shapes=[pltpu.VMEM((lanes, wave_x.shape[1]), F32)],
-        compiler_params=params(),
+        scratch_shapes=[
+            pltpu.VMEM((lanes, wave_x.shape[1]), F32),
+            pltpu.VMEM((3, ky_len, kz_len, modes), F32),
+            pltpu.SemaphoreType.DMA((ky_len // 2,)),
+        ],
+        compiler_params=still(),
         cost_estimate=SHORT,
         name="last_projection",
     )(wave_y, wave_x, wave_z, *sums)
@@ -680,7 +685,7 @@
     def run_base(at):
         base[at] = run_earlier(at)
 
-    plan = [(run_base, 0), (run_second, 0), (run_base, 1), (run_third, 0), (run_base, 2), (run_back, 0)]
+    plan = [(run_second, 0), (run_base, 0), (run_base, 1), (run_third, 0), (run_base, 2), (run_back, 0)]
     plan += [(run_second, 1), (run_second, 2), (run_third, 1), (run_third, 2), (run_back, 1), (run_back, 2)]
     for action, at in plan:
         if at < chunks:

time: 259 us -> 250 us (0.965)
  starting transfers between devices: 63.2 us -> 58.6 us
  waiting for transfers between devices: 85.9 us -> 82.6 us
    ppermute x18, waiting for transfers between devices: 32.9 us -> 26 us  [exchange(): lax.ppermute(value, axis, [(src, src ^ k << shift) for src in range(size)])]
    ppermute x18, starting transfers between devices: 40.5 us -> 34.9 us  [z_exchange(): lax.ppermute(value, 'row', [(src, src ^ 2 * k) for src in range(rows)])]
    ppermute x18, waiting for transfers between devices: 50.9 us -> 54.5 us  [z_exchange(): lax.ppermute(value, 'row', [(src, src ^ 2 * k) for src in range(rows)])]
    unnamed x38 -> x42, local copies, waits for them, and re-layouts: 4.96 us -> 5.6 us
  transfers between devices with their start and end apart: 38 -> 38, of which waited for: 16 -> 17; matrix products, arithmetic and copies ran while one was open for 1% -> 1% of each run, Pallas kernels for 32% -> 33%
where the time goes in v9:
time: 250 us
  Pallas kernels  100 us (40%)
  waiting for transfers between devices  82.6 us (33%)
  starting transfers between devices  58.6 us (23%)
  local copies, waits for them, and re-layouts  7.78 us (3%)
    ppermute x18, waiting for transfers between devices, z_exchange(): lax.ppermute(value, 'row', [(src, src ^ 2 * k) for src in range(rows)])  54.5 us
    ppermute x18, starting transfers between devices, z_exchange(): lax.ppermute(value, 'row', [(src, src ^ 2 * k) for src in range(rows)])  34.9 us
    ppermute x18, waiting for transfers between devices, exchange(): lax.ppermute(value, axis, [(src, src ^ k << shift) for src in range(size)])  26 us
    pallas_call x3, Pallas kernels, third(): pl.pallas_call(functools.partial(third_kernel, (begin, *dims)), in_specs=...  25.8 us
    pallas_call x3, Pallas kernels, earlier(): pl.pallas_call(functools.partial(earlier_kernel, orders - 1), grid=(packs...  24.6 us
    ppermute x18, starting transfers between devices, exchange(): lax.ppermute(value, axis, [(src, src ^ k << shift) for src in range(size)])  23.1 us
    pallas_call x4, Pallas kernels, first_synth(): pl.pallas_call(functools.partial(first_synth_kernel, (sizes, chosen, dest...  17.2 us
    pallas_call x3, Pallas kernels, second_synth(): pl.pallas_call(functools.partial(second_synth_kernel, dims), in_specs=[SM...  16.1 us
  transfers between devices with their start and end apart: 38, of which 17 were waited for; matrix products, arithmetic and copies ran while one was open for 1% of the time, Pallas kernels for 33%

profile of v9, /device:TPU:0, one launch (start us, length us, event | category | flops | bytes accessed | tf_op | source)
XLA Modules:
  0.0 249.7 jit_solution(4156680606639112506)
XLA Ops:
  4.5 3.6 %first_synth.4 = (f32[512,128]{1,0:T(8,128)S(1)}, f32[512,128]{1,0:T(8,128)S(1)}, f32[512,128]{1,0:T(8,128)S(1)}, f32[512,128]{1,0:T(8,128)S(1)}) custom-call(s32[3]{0:T(128)S(1)} %pad_add_fusion.place_ref, f32[3,20,40,160]{3,2,1,0:T(8,128)S(1)} %copy-done.3, bf16[4,160,128]{2,1,0:T(8,128)(2,1)S(1)} %dynamic-slice_bitcast_fusion.2.table_ref.refs_12_), custom_call_target="tpu_custom_call" | custom-call | flops 1024 | bytes 1024 | tf_op jit(solution)/shard_map/first_synth/pallas_call | solution.py:168
  8.2 3.6 %first_synth.5 = (f32[512,128]{1,0:T(8,128)S(1)}, f32[512,128]{1,0:T(8,128)S(1)}, f32[512,128]{1,0:T(8,128)S(1)}, f32[512,128]{1,0:T(8,128)S(1)}) custom-call(s32[3]{0:T(128)S(1)} %pad_add_fusion.place_ref, f32[3,20,40,160]{3,2,1,0:T(8,128)S(1)} %collective-permute-done.data, ...), custom_call_target="tpu_custom_call", output_to_operand_aliasing={{0}: (3, {}), {1}: (4, {}), {2}: (5, {}), {3}: (6, {})} | custom-call | flops 1024 | bytes 1024 | tf_op jit(solution)/shard_map/first_synth/pallas_call | solution.py:168
  17.0 5.0 %first_synth.6 = (f32[1024,128]{1,0:T(8,128)S(1)}, f32[1024,128]{1,0:T(8,128)S(1)}, f32[1024,128]{1,0:T(8,128)}, f32[1024,128]{1,0:T(8,128)}, f32[512,128]{1,0:T...) custom-call(s32[3]{0:T(128)S(1)} %pad_add_fusion.place_ref, ...), custom_call_target="tpu_custom_call" | custom-call | flops 1024 | bytes 1024 | tf_op jit(solution)/shard_map/first_synth/pallas_call | solution.py:168
  22.0 5.0 %first_synth.7 = (f32[1024,128]{1,0:T(8,128)S(1)}, f32[1024,128]{1,0:T(8,128)S(1)}, f32[1024,128]{1,0:T(8,128)}, f32[1024,128]{1,0:T(8,128)}, f32[512,128]{1,0:T...) custom-call(s32[3]{0:T(128)S(1)} %pad_add_fusion.place_ref, ...), custom_call_target="tpu_custom_call", output_to_operand_aliasing={{0}: (3, {}), {1}: (4, {}), {2}: (5, {}), {3}: (6, {}), {4}... | custom-call | flops 1024 | bytes 1024 | tf_op jit(solution)/shard_map/first_synth/pallas_call | solution.py:168
  29.2 6.5 %collective-permute-done.2.refs_2_ = f32[512,128]{1,0:T(8,128)S(1)} collective-permute-done((f32[512,128]{1,0:T(8,128)S(1)}, f32[512,128]{1,0:T(8,128)S(1)}, u32[]{:S(2)}, u32[]{:S(2)}) %collective-permute-start.2) | collective-permute-done | bytes 262176 | tf_op jit(solution)/shard_map/ppermute | solution.py:657
  35.7 5.5 %collective-permute-start.10 = (f32[1024,128]{1,0:T(8,128)S(1)}, f32[1024,128]{1,0:T(8,128)S(1)}, u32[]{:S(2)}, u32[]{:S(2)}) collective-permute-start(f32[1024,128]{1,0:T(8,128)S(1)} %get-tuple-element.192), channel_id=1, source_target_pairs={{0,8},{4,12},{8,0},{12,4},{16,24},{20,28},{24,16},{28,20},{1,9},{5... | collective-permute-start | bytes 1572872 | tf_op jit(solution)/shard_map/ppermute | solution.py:657
  41.2 4.8 %second_synth.3 = (f32[4,240,128]{2,1,0:T(8,128)S(1)}, f32[4,240,128]{2,1,0:T(8,128)}, f32[4,240,128]{2,1,0:T(8,128)}, f32[4,240,128]{2,1,0:T(8,128)}) custom-call(s32[3]{0:T(128)S(1)} %pad_add_fusion.place_ref, f32[512,128]{1,0:T(8,128)S(1)} %get-tuple-element.160.refs_0_, f32[512,128]{1,0:T(8,128)S(1)} %collective-permute-done.1.refs_1_, ...), custom_call_target="tpu_custom_call" | custom-call | flops 1024 | bytes 1024 | tf_op jit(solution)/shard_map/second_synth/pallas_call | solution.py:241
  50.5 5.0 %collective-permute-done.10.refs_1_ = f32[1024,128]{1,0:T(8,128)S(1)} collective-permute-done((f32[1024,128]{1,0:T(8,128)S(1)}, f32[1024,128]{1,0:T(8,128)S(1)}, u32[]{:S(2)}, u32[]{:S(2)}) %collective-permute-start.10) | collective-permute-done | bytes 524320 | tf_op jit(solution)/shard_map/ppermute | solution.py:657
  57.0 6.4 %earlier_orders.3.refs_6_ = f32[3,8,64,256]{3,2,1,0:T(8,128)S(1)} custom-call(f32[6,3,32,64,256]{4,3,2,1,0:T(8,128)} %refs_4_.8, f32[6,3,32,64,256]{4,3,2,1,0:T(8,128)} %refs_4_.8, f32[6,3,32,64,256]{4,3,2,1,0:T(8,128)} %refs_4_.8, f32[6,3,32,64,256]{4,3,2,1,0:T(8,128)} %refs_4_.8, f32[6,3,32,64,256]{4,3,2,1,0:T(8,128)} %refs_4_.8, ...), custom_call_target="tpu_custom_call" | custom-call | flops 1024 | bytes 1024 | tf_op jit(solution)/shard_map/earlier_orders/pallas_call | solution.py:293
  63.4 11.7 %earlier_orders.4.refs_6_ = f32[3,16,64,256]{3,2,1,0:T(8,128)S(1)} custom-call(f32[6,3,32,64,256]{4,3,2,1,0:T(8,128)} %refs_4_.8, f32[6,3,32,64,256]{4,3,2,1,0:T(8,128)} %refs_4_.8, f32[6,3,32,64,256]{4,3,2,1,0:T(8,128)} %refs_4_.8, f32[6,3,32,64,256]{4,3,2,1,0:T(8,128)} %refs_4_.8, f32[6,3,32,64,256]{4,3,2,1,0:T(8,128)} %refs_4_.8, ...), custom_call_target="tpu_custom_call" | custom-call | flops 1024 | bytes 1024 | tf_op jit(solution)/shard_map/earlier_orders/pallas_call | solution.py:293
  75.2 7.2 %third_dimension.3 = (f32[4,120,128]{2,1,0:T(8,128)S(1)}, f32[4,120,128]{2,1,0:T(8,128)S(1)}, f32[4,120,128]{2,1,0:T(8,128)S(1)}, f32[4,120,128]{2,1,0:T(8,128)S(1)}) custom-call(s32[3]{0:T(128)S(1)} %pad_add_fusion.place_ref, f32[4,240,128]{2,1,0:T(8,128)S(1)} %get-tuple-element.173.refs_0_, f32[4,240,128]{2,1,0:T(8,128)} %collective-permute-done.4.refs_1_, ...), custom_call_target="tpu_custom_call" | custom-call | flops 1024 | bytes 1024 | tf_op jit(solution)/shard_map/third_dimension/pallas_call | solution.py:361
  86.0 6.4 %earlier_orders.5.refs_6_ = f32[3,8,64,256]{3,2,1,0:T(8,128)S(1)} custom-call(f32[6,3,32,64,256]{4,3,2,1,0:T(8,128)} %refs_4_.8, f32[6,3,32,64,256]{4,3,2,1,0:T(8,128)} %refs_4_.8, f32[6,3,32,64,256]{4,3,2,1,0:T(8,128)} %refs_4_.8, f32[6,3,32,64,256]{4,3,2,1,0:T(8,128)} %refs_4_.8, f32[6,3,32,64,256]{4,3,2,1,0:T(8,128)} %refs_4_.8, ...), custom_call_target="tpu_custom_call" | custom-call | flops 1024 | bytes 1024 | tf_op jit(solution)/shard_map/earlier_orders/pallas_call | solution.py:293
  97.7 7.5 %second_synth.4 = (f32[8,240,128]{2,1,0:T(8,128)S(1)}, f32[8,240,128]{2,1,0:T(8,128)S(1)}, f32[8,240,128]{2,1,0:T(8,128)S(1)}, f32[8,240,128]{2,1,0:T(8,128)S(1)}) custom-call(s32[3]{0:T(128)S(1)} %copy-done.20, f32[1024,128]{1,0:T(8,128)S(1)} %copy-done.8, f32[1024,128]{1,0:T(8,128)S(1)} %copy-done.12, f32[1024,128]{1,0:T(8,128)} %collective-permute-done.11.refs_2_, ...), custom_call_target="tpu_custom_call" | custom-call | flops 1024 | bytes 1024 | tf_op jit(solution)/shard_map/second_synth/pallas_call | solution.py:241
  110.9 3.8 %collective-permute-done.13.refs_1_ = f32[304,128]{1,0:T(8,128)S(1)} collective-permute-done((f32[304,128]{1,0:T(8,128)S(1)}, f32[304,128]{1,0:T(8,128)S(1)}, u32[]{:S(2)}, u32[]{:S(2)}) %collective-permute-start.13) | collective-permute-done | bytes 155680 | tf_op jit(solution)/shard_map/ppermute | solution.py:657
  117.6 4.5 %collective-permute-done.14.refs_2_ = f32[304,128]{1,0:T(8,128)S(1)} collective-permute-done((f32[304,128]{1,0:T(8,128)S(1)}, f32[304,128]{1,0:T(8,128)S(1)}, u32[]{:S(2)}, u32[]{:S(2)}) %collective-permute-start.14) | collective-permute-done | bytes 155680 | tf_op jit(solution)/shard_map/ppermute | solution.py:657
  125.5 6.0 %collective-permute-done.19.refs_1_ = f32[512,128]{1,0:T(8,128)S(1)} collective-permute-done((f32[512,128]{1,0:T(8,128)S(1)}, f32[512,128]{1,0:T(8,128)S(1)}, u32[]{:S(2)}, u32[]{:S(2)}) %collective-permute-start.19) | collective-permute-done | bytes 262176 | tf_op jit(solution)/shard_map/ppermute | solution.py:657
  134.1 9.3 %collective-permute-done.20.refs_2_ = f32[512,128]{1,0:T(8,128)S(1)} collective-permute-done((f32[512,128]{1,0:T(8,128)S(1)}, f32[512,128]{1,0:T(8,128)S(1)}, u32[]{:S(2)}, u32[]{:S(2)}) %collective-permute-start.20) | collective-permute-done | bytes 262176 | tf_op jit(solution)/shard_map/ppermute | solution.py:657
  143.5 3.7 %second_synth.5 = (f32[4,240,128]{2,1,0:T(8,128)S(1)}, f32[4,240,128]{2,1,0:T(8,128)S(1)}, f32[4,240,128]{2,1,0:T(8,128)S(1)}, f32[4,240,128]{2,1,0:T(8,128)S(1)}) custom-call(s32[3]{0:T(128)S(1)} %copy-done.20, f32[512,128]{1,0:T(8,128)S(1)} %copy-done.10, f32[512,128]{1,0:T(8,128)S(1)} %collective-permute-done.19.refs_1_, ...), custom_call_target="tpu_custom_call" | custom-call | flops 1024 | bytes 1024 | tf_op jit(solution)/shard_map/second_synth/pallas_call | solution.py:241
  150.8 12.1 %third_dimension.4 = (f32[8,120,128]{2,1,0:T(8,128)S(1)}, f32[8,120,128]{2,1,0:T(8,128)S(1)}, f32[8,120,128]{2,1,0:T(8,128)S(1)}, f32[8,120,128]{2,1,0:T(8,128)S(1)}) custom-call(s32[3]{0:T(128)S(1)} %copy-done.20, f32[8,240,128]{2,1,0:T(8,128)S(1)} %get-tuple-element.224.refs_0_, f32[8,240,128]{2,1,0:T(8,128)S(1)} %collective-permute-done.16.refs_1_, ...), custom_call_target="tpu_custom_call" | custom-call | flops 1024 | bytes 1024 | tf_op jit(solution)/shard_map/third_dimension/pallas_call | solution.py:361
  166.5 3.2 %collective-permute-done.26.refs_2_ = f32[4,240,128]{2,1,0:T(8,128)S(1)} collective-permute-done((f32[4,240,128]{2,1,0:T(8,128)S(1)}, f32[4,240,128]{2,1,0:T(8,128)S(1)}, u32[]{:S(2)}, u32[]{:S(2)}) %collective-permute-start.26) | collective-permute-done | bytes 491552 | tf_op jit(solution)/shard_map/ppermute | solution.py:615
  169.6 3.2 %collective-permute-done.27.refs_3_ = f32[4,240,128]{2,1,0:T(8,128)S(1)} collective-permute-done((f32[4,240,128]{2,1,0:T(8,128)S(1)}, f32[4,240,128]{2,1,0:T(8,128)S(1)}, u32[]{:S(2)}, u32[]{:S(2)}) %collective-permute-start.27) | collective-permute-done | bytes 491552 | tf_op jit(solution)/shard_map/ppermute | solution.py:615
  172.8 6.4 %third_dimension.5 = (f32[4,120,128]{2,1,0:T(8,128)S(1)}, f32[4,120,128]{2,1,0:T(8,128)S(1)}, f32[4,120,128]{2,1,0:T(8,128)S(1)}, f32[4,120,128]{2,1,0:T(8,128)S(1)}) custom-call(s32[3]{0:T(128)S(1)} %copy-done.20, f32[4,240,128]{2,1,0:T(8,128)S(1)} %get-tuple-element.238.refs_0_, f32[4,240,128]{2,1,0:T(8,128)S(1)} %collective-permute-done.25.refs_1_, ...), custom_call_target="tpu_custom_call" | custom-call | flops 1024 | bytes 1024 | tf_op jit(solution)/shard_map/third_dimension/pallas_call | solution.py:361
  182.5 7.9 %collective-permute-done.23.refs_2_ = f32[8,120,128]{2,1,0:T(8,128)S(1)} collective-permute-done((f32[8,120,128]{2,1,0:T(8,128)S(1)}, f32[8,120,128]{2,1,0:T(8,128)S(1)}, u32[]{:S(2)}, u32[]{:S(2)}) %collective-permute-start.23) | collective-permute-done | bytes 491552 | tf_op jit(solution)/shard_map/ppermute | solution.py:615
  190.4 3.5 %collective-permute-done.24.refs_3_ = f32[8,120,128]{2,1,0:T(8,128)S(1)} collective-permute-done((f32[8,120,128]{2,1,0:T(8,128)S(1)}, f32[8,120,128]{2,1,0:T(8,128)S(1)}, u32[]{:S(2)}, u32[]{:S(2)}) %collective-permute-start.24) | collective-permute-done | bytes 491552 | tf_op jit(solution)/shard_map/ppermute | solution.py:615
  193.9 4.4 %second_back.4 = (f32[608,128]{1,0:T(8,128)S(1)}, f32[608,128]{1,0:T(8,128)S(1)}, f32[608,128]{1,0:T(8,128)S(1)}, f32[608,128]{1,0:T(8,128)S(1)}) custom-call(s32[3]{0:T(128)S(1)} %copy-done.20, f32[8,120,128]{2,1,0:T(8,128)S(1)} %get-tuple-element.243.refs_0_, f32[8,120,128]{2,1,0:T(8,128)S(1)} %collective-permute-done.22.refs_1_, ...), custom_call_target="tpu_custom_call" | custom-call | flops 1024 | bytes 1024 | tf_op jit(solution)/shard_map/second_back/pallas_call | solution.py:410
  200.0 4.7 %collective-permute-start.29 = (f32[608,128]{1,0:T(8,128)S(1)}, f32[608,128]{1,0:T(8,128)S(1)}, u32[]{:S(2)}, u32[]{:S(2)}) collective-permute-start(f32[608,128]{1,0:T(8,128)S(1)} %get-tuple-element.251), channel_id=1, source_target_pairs={{0,16},{4,20},{8,24},{12,28},{16,0},{20,4},{24,8},{28,12},{1,17},{... | collective-permute-start | bytes 933896 | tf_op jit(solution)/shard_map/ppermute | solution.py:657
  208.2 5.8 %collective-permute-done.32.refs_2_ = f32[4,120,128]{2,1,0:T(8,128)S(1)} collective-permute-done((f32[4,120,128]{2,1,0:T(8,128)S(1)}, f32[4,120,128]{2,1,0:T(8,128)S(1)}, u32[]{:S(2)}, u32[]{:S(2)}) %collective-permute-start.32) | collective-permute-done | bytes 245792 | tf_op jit(solution)/shard_map/ppermute | solution.py:615
  216.6 9.3 %collective-permute-done.29.refs_6_ = f32[608,128]{1,0:T(8,128)S(1)} collective-permute-done((f32[608,128]{1,0:T(8,128)S(1)}, f32[608,128]{1,0:T(8,128)S(1)}, u32[]{:S(2)}, u32[]{:S(2)}) %collective-permute-start.29) | collective-permute-done | bytes 311328 | tf_op jit(solution)/shard_map/ppermute | solution.py:657
  227.0 3.2 %collective-permute-start.36 = (f32[304,128]{1,0:T(8,128)S(1)}, f32[304,128]{1,0:T(8,128)S(1)}, u32[]{:S(2)}, u32[]{:S(2)}) collective-permute-start(f32[304,128]{1,0:T(8,128)S(1)} %get-tuple-element.267), channel_id=1, source_target_pairs={{0,24},{4,28},{8,16},{12,20},{16,8},{20,12},{24,0},{28,4},{1,25},{... | collective-permute-start | bytes 466952 | tf_op jit(solution)/shard_map/ppermute | solution.py:657
  230.2 3.1 %collective-permute-done.34.refs_9_ = f32[304,128]{1,0:T(8,128)S(1)} collective-permute-done((f32[304,128]{1,0:T(8,128)S(1)}, f32[304,128]{1,0:T(8,128)S(1)}, u32[]{:S(2)}, u32[]{:S(2)}) %collective-permute-start.34) | collective-permute-done | bytes 155680 | tf_op jit(solution)/shard_map/ppermute | solution.py:657
  233.3 7.0 %collective-permute-done.35.refs_10_ = f32[304,128]{1,0:T(8,128)S(1)} collective-permute-done((f32[304,128]{1,0:T(8,128)S(1)}, f32[304,128]{1,0:T(8,128)S(1)}, u32[]{:S(2)}, u32[]{:S(2)}) %collective-permute-start.35) | collective-permute-done | bytes 155680 | tf_op jit(solution)/shard_map/ppermute | solution.py:657
  245.1 4.5 %last_projection.1 = f32[3,20,40,160]{3,2,1,0:T(8,128)} custom-call(f32[10]{0:T(128)S(1)} %convert_multiply_fusion.1.refs_0_, f32[8,256]{1,0:T(8,128)S(1)} %broadcast_in_dim.9.refs_1_, f32[40,256]{1,0:T(8,128)S(1)} %broadcast_in_dim.18.refs_2_, f32[160,2432]{1,0:T(8,128)S(1)} %first_back.3.refs_3_, f32[160,2432]{1,0:T(8,128)S(1)} %collective-permute-done.37.refs_4_), custom_call_target="tpu_custom_call" | custom-call | flops 1024 | bytes 1024 | tf_op jit(solution)/shard_map/last_projection/pallas_call | solution.py:523
  (113 shorter events, 65.3 us)
Async XLA Ops:
  11.8 17.5 %collective-permute-start.1 = (f32[512,128]{1,0:T(8,128)S(1)}, f32[512,128]{1,0:T(8,128)S(1)}, u32[]{:S(2)}, u32[]{:S(2)}) collective-permute-start(f32[512,128]{1,0:T(8,128)S(1)} %get-tuple-element.147), channel_id=1, source_target_pairs={{0,8},{4,12},{8,0},{12,4},{16,24},{20,28},{24,16},{28,20},{1,9},{5... | collective-permute-start | bytes 786440 | tf_op jit(solution)/shard_map/ppermute | solution.py:657
  14.4 21.3 %collective-permute-start.2 = (f32[512,128]{1,0:T(8,128)S(1)}, f32[512,128]{1,0:T(8,128)S(1)}, u32[]{:S(2)}, u32[]{:S(2)}) collective-permute-start(f32[512,128]{1,0:T(8,128)S(1)} %get-tuple-element.148), channel_id=1, source_target_pairs={{0,16},{4,20},{8,24},{12,28},{16,0},{20,4},{24,8},{28,12},{1,17},{... | collective-permute-start | bytes 786440 | tf_op jit(solution)/shard_map/ppermute | solution.py:657
  17.0 18.7 %collective-permute-start.3 = (f32[512,128]{1,0:T(8,128)S(1)}, f32[512,128]{1,0:T(8,128)S(1)}, u32[]{:S(2)}, u32[]{:S(2)}) collective-permute-start(f32[512,128]{1,0:T(8,128)S(1)} %get-tuple-element.149), channel_id=1, source_target_pairs={{0,24},{4,28},{8,16},{12,20},{16,8},{20,12},{24,0},{28,4},{1,25},{... | collective-permute-start | bytes 786440 | tf_op jit(solution)/shard_map/ppermute | solution.py:657
  35.7 19.8 %collective-permute-start.10 = (f32[1024,128]{1,0:T(8,128)S(1)}, f32[1024,128]{1,0:T(8,128)S(1)}, u32[]{:S(2)}, u32[]{:S(2)}) collective-permute-start(f32[1024,128]{1,0:T(8,128)S(1)} %get-tuple-element.192), channel_id=1, source_target_pairs={{0,8},{4,12},{8,0},{12,4},{16,24},{20,28},{24,16},{28,20},{1,9},{5... | collective-permute-start | bytes 1572872 | tf_op jit(solution)/shard_map/ppermute | solution.py:657
  46.0 29.2 %collective-permute-start.4 = (f32[4,240,128]{2,1,0:T(8,128)}, f32[4,240,128]{2,1,0:T(8,128)}, u32[]{:S(2)}, u32[]{:S(2)}) collective-permute-start(f32[4,240,128]{2,1,0:T(8,128)} %get-tuple-element.166), channel_id=1, source_target_pairs={{0,1},{1,0},{2,3},{3,2},{4,5},{5,4},{6,7},{7,6},{8,9},{9,8},{10,11... | collective-permute-start | bytes 1474568 | tf_op jit(solution)/shard_map/ppermute | solution.py:615
  47.5 27.7 %collective-permute-start.5 = (f32[4,240,128]{2,1,0:T(8,128)}, f32[4,240,128]{2,1,0:T(8,128)}, u32[]{:S(2)}, u32[]{:S(2)}) collective-permute-start(f32[4,240,128]{2,1,0:T(8,128)} %get-tuple-element.167), channel_id=1, source_target_pairs={{0,2},{1,3},{2,0},{3,1},{4,6},{5,7},{6,4},{7,5},{8,10},{9,11},{10,... | collective-permute-start | bytes 1474568 | tf_op jit(solution)/shard_map/ppermute | solution.py:615
  49.0 26.2 %collective-permute-start.6 = (f32[4,240,128]{2,1,0:T(8,128)}, f32[4,240,128]{2,1,0:T(8,128)}, u32[]{:S(2)}, u32[]{:S(2)}) collective-permute-start(f32[4,240,128]{2,1,0:T(8,128)} %get-tuple-element.168), channel_id=1, source_target_pairs={{0,3},{1,2},{2,1},{3,0},{4,7},{5,6},{6,5},{7,4},{8,11},{9,10},{10,... | collective-permute-start | bytes 1474568 | tf_op jit(solution)/shard_map/ppermute | solution.py:615
  49.5 46.6 %collective-permute-start.11 = (f32[1024,128]{1,0:T(8,128)}, f32[1024,128]{1,0:T(8,128)}, u32[]{:S(2)}, u32[]{:S(2)}) collective-permute-start(f32[1024,128]{1,0:T(8,128)} %get-tuple-element.194), channel_id=1, source_target_pairs={{0,16},{4,20},{8,24},{12,28},{16,0},{20,4},{24,8},{28,12},{1,17},{... | collective-permute-start | bytes 1572872 | tf_op jit(solution)/shard_map/ppermute | solution.py:657
  55.5 40.5 %collective-permute-start.12 = (f32[1024,128]{1,0:T(8,128)}, f32[1024,128]{1,0:T(8,128)}, u32[]{:S(2)}, u32[]{:S(2)}) collective-permute-start(f32[1024,128]{1,0:T(8,128)} %get-tuple-element.196), channel_id=1, source_target_pairs={{0,24},{4,28},{8,16},{12,20},{16,8},{20,12},{24,0},{28,4},{1,25},{... | collective-permute-start | bytes 1572872 | tf_op jit(solution)/shard_map/ppermute | solution.py:657
  82.4 10.0 %collective-permute-start.7 = (f32[4,120,128]{2,1,0:T(8,128)S(1)}, f32[4,120,128]{2,1,0:T(8,128)S(1)}, u32[]{:S(2)}, u32[]{:S(2)}) collective-permute-start(f32[4,120,128]{2,1,0:T(8,128)S(1)} %get-tuple-element.179), channel_id=1, source_target_pairs={{0,1},{1,0},{2,3},{3,2},{4,5},{5,4},{6,7},{7,6},{8,9},{9,8},{10,11... | collective-permute-start | bytes 737288 | tf_op jit(solution)/shard_map/ppermute | solution.py:615
  84.0 9.6 %collective-permute-start.8 = (f32[4,120,128]{2,1,0:T(8,128)S(1)}, f32[4,120,128]{2,1,0:T(8,128)S(1)}, u32[]{:S(2)}, u32[]{:S(2)}) collective-permute-start(f32[4,120,128]{2,1,0:T(8,128)S(1)} %get-tuple-element.180), channel_id=1, source_target_pairs={{0,2},{1,3},{2,0},{3,1},{4,6},{5,7},{6,4},{7,5},{8,10},{9,11},{10,... | collective-permute-start | bytes 737288 | tf_op jit(solution)/shard_map/ppermute | solution.py:615
  105.2 41.9 %collective-permute-start.18 = (f32[8,240,128]{2,1,0:T(8,128)S(1)}, f32[8,240,128]{2,1,0:T(8,128)S(1)}, u32[]{:S(2)}, u32[]{:S(2)}) collective-permute-start(f32[8,240,128]{2,1,0:T(8,128)S(1)} %get-tuple-element.212), channel_id=1, source_target_pairs={{0,3},{1,2},{2,1},{3,0},{4,7},{5,6},{6,5},{7,4},{8,11},{9,10},{10,... | collective-permute-start | bytes 2949128 | tf_op jit(solution)/shard_map/ppermute | solution.py:615
  106.8 40.4 %collective-permute-start.17 = (f32[8,240,128]{2,1,0:T(8,128)S(1)}, f32[8,240,128]{2,1,0:T(8,128)S(1)}, u32[]{:S(2)}, u32[]{:S(2)}) collective-permute-start(f32[8,240,128]{2,1,0:T(8,128)S(1)} %get-tuple-element.210), channel_id=1, source_target_pairs={{0,2},{1,3},{2,0},{3,1},{4,6},{5,7},{6,4},{7,5},{8,10},{9,11},{10,... | collective-permute-start | bytes 2949128 | tf_op jit(solution)/shard_map/ppermute | solution.py:615
  108.0 39.2 %collective-permute-start.16 = (f32[8,240,128]{2,1,0:T(8,128)S(1)}, f32[8,240,128]{2,1,0:T(8,128)S(1)}, u32[]{:S(2)}, u32[]{:S(2)}) collective-permute-start(f32[8,240,128]{2,1,0:T(8,128)S(1)} %get-tuple-element.208), channel_id=1, source_target_pairs={{0,1},{1,0},{2,3},{3,2},{4,5},{5,4},{6,7},{7,6},{8,9},{9,8},{10,11... | collective-permute-start | bytes 2949128 | tf_op jit(solution)/shard_map/ppermute | solution.py:615
  109.8 12.2 %collective-permute-start.14 = (f32[304,128]{1,0:T(8,128)S(1)}, f32[304,128]{1,0:T(8,128)S(1)}, u32[]{:S(2)}, u32[]{:S(2)}) collective-permute-start(f32[304,128]{1,0:T(8,128)S(1)} %get-tuple-element.199), channel_id=1, source_target_pairs={{0,16},{4,20},{8,24},{12,28},{16,0},{20,4},{24,8},{28,12},{1,17},{... | collective-permute-start | bytes 466952 | tf_op jit(solution)/shard_map/ppermute | solution.py:657
  122.1 9.4 %collective-permute-start.19 = (f32[512,128]{1,0:T(8,128)S(1)}, f32[512,128]{1,0:T(8,128)S(1)}, u32[]{:S(2)}, u32[]{:S(2)}) collective-permute-start(f32[512,128]{1,0:T(8,128)S(1)} %copy-done.14), channel_id=1, source_target_pairs={{0,8},{4,12},{8,0},{12,4},{16,24},{20,28},{24,16},{28,20},{1,9},{5... | collective-permute-start | bytes 786440 | tf_op jit(solution)/shard_map/ppermute | solution.py:657
  124.3 19.2 %collective-permute-start.20 = (f32[512,128]{1,0:T(8,128)S(1)}, f32[512,128]{1,0:T(8,128)S(1)}, u32[]{:S(2)}, u32[]{:S(2)}) collective-permute-start(f32[512,128]{1,0:T(8,128)S(1)} %copy-done.16), channel_id=1, source_target_pairs={{0,16},{4,20},{8,24},{12,28},{16,0},{20,4},{24,8},{28,12},{1,17},{... | collective-permute-start | bytes 786440 | tf_op jit(solution)/shard_map/ppermute | solution.py:657
  131.5 12.0 %collective-permute-start.21 = (f32[512,128]{1,0:T(8,128)S(1)}, f32[512,128]{1,0:T(8,128)S(1)}, u32[]{:S(2)}, u32[]{:S(2)}) collective-permute-start(f32[512,128]{1,0:T(8,128)S(1)} %copy-done.18), channel_id=1, source_target_pairs={{0,24},{4,28},{8,16},{12,20},{16,8},{20,12},{24,0},{28,4},{1,25},{... | collective-permute-start | bytes 786440 | tf_op jit(solution)/shard_map/ppermute | solution.py:657
  147.2 19.0 %collective-permute-start.25 = (f32[4,240,128]{2,1,0:T(8,128)S(1)}, f32[4,240,128]{2,1,0:T(8,128)S(1)}, u32[]{:S(2)}, u32[]{:S(2)}) collective-permute-start(f32[4,240,128]{2,1,0:T(8,128)S(1)} %get-tuple-element.233), channel_id=1, source_target_pairs={{0,1},{1,0},{2,3},{3,2},{4,5},{5,4},{6,7},{7,6},{8,9},{9,8},{10,11... | collective-permute-start | bytes 1474568 | tf_op jit(solution)/shard_map/ppermute | solution.py:615
  149.0 20.6 %collective-permute-start.26 = (f32[4,240,128]{2,1,0:T(8,128)S(1)}, f32[4,240,128]{2,1,0:T(8,128)S(1)}, u32[]{:S(2)}, u32[]{:S(2)}) collective-permute-start(f32[4,240,128]{2,1,0:T(8,128)S(1)} %get-tuple-element.235), channel_id=1, source_target_pairs={{0,2},{1,3},{2,0},{3,1},{4,6},{5,7},{6,4},{7,5},{8,10},{9,11},{10,... | collective-permute-start | bytes 1474568 | tf_op jit(solution)/shard_map/ppermute | solution.py:615
  150.5 22.3 %collective-permute-start.27 = (f32[4,240,128]{2,1,0:T(8,128)S(1)}, f32[4,240,128]{2,1,0:T(8,128)S(1)}, u32[]{:S(2)}, u32[]{:S(2)}) collective-permute-start(f32[4,240,128]{2,1,0:T(8,128)S(1)} %get-tuple-element.237), channel_id=1, source_target_pairs={{0,3},{1,2},{2,1},{3,0},{4,7},{5,6},{6,5},{7,4},{8,11},{9,10},{10,... | collective-permute-start | bytes 1474568 | tf_op jit(solution)/shard_map/ppermute | solution.py:615
  162.9 19.6 %collective-permute-start.22 = (f32[8,120,128]{2,1,0:T(8,128)S(1)}, f32[8,120,128]{2,1,0:T(8,128)S(1)}, u32[]{:S(2)}, u32[]{:S(2)}) collective-permute-start(f32[8,120,128]{2,1,0:T(8,128)S(1)} %get-tuple-element.229), channel_id=1, source_target_pairs={{0,1},{1,0},{2,3},{3,2},{4,5},{5,4},{6,7},{7,6},{8,9},{9,8},{10,11... | collective-permute-start | bytes 1474568 | tf_op jit(solution)/shard_map/ppermute | solution.py:615
  164.7 25.7 %collective-permute-start.23 = (f32[8,120,128]{2,1,0:T(8,128)S(1)}, f32[8,120,128]{2,1,0:T(8,128)S(1)}, u32[]{:S(2)}, u32[]{:S(2)}) collective-permute-start(f32[8,120,128]{2,1,0:T(8,128)S(1)} %get-tuple-element.230), channel_id=1, source_target_pairs={{0,2},{1,3},{2,0},{3,1},{4,6},{5,7},{6,4},{7,5},{8,10},{9,11},{10,... | collective-permute-start | bytes 1474568 | tf_op jit(solution)/shard_map/ppermute | solution.py:615
  166.2 27.7 %collective-permute-start.24 = (f32[8,120,128]{2,1,0:T(8,128)S(1)}, f32[8,120,128]{2,1,0:T(8,128)S(1)}, u32[]{:S(2)}, u32[]{:S(2)}) collective-permute-start(f32[8,120,128]{2,1,0:T(8,128)S(1)} %get-tuple-element.231), channel_id=1, source_target_pairs={{0,3},{1,2},{2,1},{3,0},{4,7},{5,6},{6,5},{7,4},{8,11},{9,10},{10,... | collective-permute-start | bytes 1474568 | tf_op jit(solution)/shard_map/ppermute | solution.py:615
  179.3 26.1 %collective-permute-start.31 = (f32[4,120,128]{2,1,0:T(8,128)S(1)}, f32[4,120,128]{2,1,0:T(8,128)S(1)}, u32[]{:S(2)}, u32[]{:S(2)}) collective-permute-start(f32[4,120,128]{2,1,0:T(8,128)S(1)} %get-tuple-element.254), channel_id=1, source_target_pairs={{0,1},{1,0},{2,3},{3,2},{4,5},{5,4},{6,7},{7,6},{8,9},{9,8},{10,11... | collective-permute-start | bytes 737288 | tf_op jit(solution)/shard_map/ppermute | solution.py:615
  198.3 18.2 %collective-permute-start.30 = (f32[608,128]{1,0:T(8,128)S(1)}, f32[608,128]{1,0:T(8,128)S(1)}, u32[]{:S(2)}, u32[]{:S(2)}) collective-permute-start(f32[608,128]{1,0:T(8,128)S(1)} %get-tuple-element.253), channel_id=1, source_target_pairs={{0,24},{4,28},{8,16},{12,20},{16,8},{20,12},{24,0},{28,4},{1,25},{... | collective-permute-start | bytes 933896 | tf_op jit(solution)/shard_map/ppermute | solution.py:657
  200.0 25.8 %collective-permute-start.29 = (f32[608,128]{1,0:T(8,128)S(1)}, f32[608,128]{1,0:T(8,128)S(1)}, u32[]{:S(2)}, u32[]{:S(2)}) collective-permute-start(f32[608,128]{1,0:T(8,128)S(1)} %get-tuple-element.251), channel_id=1, source_target_pairs={{0,16},{4,20},{8,24},{12,28},{16,0},{20,4},{24,8},{28,12},{1,17},{... | collective-permute-start | bytes 933896 | tf_op jit(solution)/shard_map/ppermute | solution.py:657
  204.7 21.1 %collective-permute-start.28 = (f32[608,128]{1,0:T(8,128)S(1)}, f32[608,128]{1,0:T(8,128)S(1)}, u32[]{:S(2)}, u32[]{:S(2)}) collective-permute-start(f32[608,128]{1,0:T(8,128)S(1)} %get-tuple-element.249), channel_id=1, source_target_pairs={{0,8},{4,12},{8,0},{12,4},{16,24},{20,28},{24,16},{28,20},{1,9},{5... | collective-permute-start | bytes 933896 | tf_op jit(solution)/shard_map/ppermute | solution.py:657
  204.7 9.2 %collective-permute-start.32 = (f32[4,120,128]{2,1,0:T(8,128)S(1)}, f32[4,120,128]{2,1,0:T(8,128)S(1)}, u32[]{:S(2)}, u32[]{:S(2)}) collective-permute-start(f32[4,120,128]{2,1,0:T(8,128)S(1)} %get-tuple-element.255), channel_id=1, source_target_pairs={{0,2},{1,3},{2,0},{3,1},{4,6},{5,7},{6,4},{7,5},{8,10},{9,11},{10,... | collective-permute-start | bytes 737288 | tf_op jit(solution)/shard_map/ppermute | solution.py:615
  205.4 8.6 %collective-permute-start.33 = (f32[4,120,128]{2,1,0:T(8,128)S(1)}, f32[4,120,128]{2,1,0:T(8,128)S(1)}, u32[]{:S(2)}, u32[]{:S(2)}) collective-permute-start(f32[4,120,128]{2,1,0:T(8,128)S(1)} %get-tuple-element.256), channel_id=1, source_target_pairs={{0,3},{1,2},{2,1},{3,0},{4,7},{5,6},{6,5},{7,4},{8,11},{9,10},{10,... | collective-permute-start | bytes 737288 | tf_op jit(solution)/shard_map/ppermute | solution.py:615
  225.9 14.5 %collective-permute-start.35 = (f32[304,128]{1,0:T(8,128)S(1)}, f32[304,128]{1,0:T(8,128)S(1)}, u32[]{:S(2)}, u32[]{:S(2)}) collective-permute-start(f32[304,128]{1,0:T(8,128)S(1)} %get-tuple-element.265), channel_id=1, source_target_pairs={{0,16},{4,20},{8,24},{12,28},{16,0},{20,4},{24,8},{28,12},{1,17},{... | collective-permute-start | bytes 466952 | tf_op jit(solution)/shard_map/ppermute | solution.py:657
  227.0 13.3 %collective-permute-start.36 = (f32[304,128]{1,0:T(8,128)S(1)}, f32[304,128]{1,0:T(8,128)S(1)}, u32[]{:S(2)}, u32[]{:S(2)}) collective-permute-start(f32[304,128]{1,0:T(8,128)S(1)} %get-tuple-element.267), channel_id=1, source_target_pairs={{0,24},{4,28},{8,16},{12,20},{16,8},{20,12},{24,0},{28,4},{1,25},{... | collective-permute-start | bytes 466952 | tf_op jit(solution)/shard_map/ppermute | solution.py:657
  (27 other events, 574.9 us)

commit v10 on v9

--- a/solution.py
+++ b/solution.py
@@ -14,8 +14,8 @@
 
 
 def chunk_sizes(x_len):
-    ends = 8
-    return [ends, x_len - 2 * ends, ends] if x_len > 3 * ends else [ends] * (x_len // ends)
+    short = 8
+    return [short, short, x_len - 2 * short] if x_len > 3 * short else [short] * (x_len // short)
 
 BF16 = jnp.bfloat16
 F32 = jnp.float32
@@ -653,18 +653,19 @@
         for k in range(1, groups):
             value = values[k]
             if gates:
-                value = after(value, found[1]) if waves and 2 * k > groups else after(value, *gates)
+                value = after(value, found[groups // 2]) if waves and 2 * k > groups else after(value, *gates)
             found.append(lax.ppermute(value, "row", [(src, src ^ (2 * k)) for src in range(rows)]))
         return found
 
     first, second, middle, back, base = {}, {}, {}, {}, {}
-    for step in range(min(2, chunks)):
-        first[step] = z_exchange(sent[step], *([first[step - 1]] if step else []))
+    for step in range(chunks):
+        first[step] = z_exchange(sent[step], *([first[step - 1]] if step else []), waves=step > 1)
 
     def run_second(at):
         found = ordered(lambda values: second_synth(place, values, table_y, dims[at]), first[at])
         if at:
-            found = [found[0]] + [after(value, second[at - 1]) for value in found[1:]]
+            gates = [second[at - 1]] + ([middle[at - 1]] if at - 1 in middle else [])
+            found = [found[0]] + [after(value, *gates) for value in found[1:]]
         second[at] = exchange(found, "col", 0, cols)
 
     def run_third(at):
@@ -677,16 +678,16 @@
         middle[at] = exchange(found, "col", 0, cols)
 
     def run_back(at):
-        found = ordered(lambda values: second_back(place, values, table_y, dims[at]), middle[at])
-        back[at] = z_exchange(found, back[at - 1] if at else first[min(1, chunks - 1)], waves=at == 0)
-        if at == 0 and chunks > 2:
-            first[2] = z_exchange(sent[2], back[0])
+        values = after(middle[at], back[0]) if at == 1 else middle[at]
+        found = ordered(lambda values: second_back(place, values, table_y, dims[at]), values)
+        gate = back[at - 1] if at else first[chunks - 1]
+        back[at] = z_exchange(found, gate, waves=at == 0)
 
     def run_base(at):
         base[at] = run_earlier(at)
 
-    plan = [(run_second, 0), (run_base, 0), (run_base, 1), (run_third, 0), (run_base, 2), (run_back, 0)]
-    plan += [(run_second, 1), (run_second, 2), (run_third, 1), (run_third, 2), (run_back, 1), (run_back, 2)]
+    plan = [(run_second, 0), (run_base, 0), (run_second, 1), (run_third, 0), (run_base, 1), (run_base, 2)]
+    plan += [(run_third, 1), (run_back, 0), (run_second, 2), (run_back, 1), (run_third, 2), (run_back, 2)]
     for action, at in plan:
         if at < chunks:
             action(at)

time: 250 us -> 269 us (1.076)
  waiting for transfers between devices: 82.6 us -> 106 us
  starting transfers between devices: 58.6 us -> 54.2 us
    ppermute x18, waiting for transfers between devices: 26 us -> 39.2 us  [exchange(): lax.ppermute(value, axis, [(src, src ^ k << shift) for src in range(size)])]
    ppermute x18, waiting for transfers between devices: 54.5 us -> 64.8 us  [z_exchange(): lax.ppermute(value, 'row', [(src, src ^ 2 * k) for src in range(rows)])]
  transfers between devices with their start and end apart: 38 -> 38, of which waited for: 17 -> 13; matrix products, arithmetic and copies ran while one was open for 1% -> 1% of each run, Pallas kernels for 33% -> 29%
where the time goes in v10:
time: 269 us
  waiting for transfers between devices  106 us (39%)
  Pallas kernels  99.9 us (37%)
  starting transfers between devices  54.2 us (20%)
  local copies, waits for them, and re-layouts  8.24 us (3%)
    ppermute x18, waiting for transfers between devices, z_exchange(): lax.ppermute(value, 'row', [(src, src ^ 2 * k) for src in range(rows)])  64.8 us
    ppermute x18, waiting for transfers between devices, exchange(): lax.ppermute(value, axis, [(src, src ^ k << shift) for src in range(size)])  39.2 us
    ppermute x18, starting transfers between devices, z_exchange(): lax.ppermute(value, 'row', [(src, src ^ 2 * k) for src in range(rows)])  32.4 us
    pallas_call x3, Pallas kernels, third(): pl.pallas_call(functools.partial(third_kernel, (begin, *dims)), in_specs=...  25.8 us
    pallas_call x3, Pallas kernels, earlier(): pl.pallas_call(functools.partial(earlier_kernel, orders - 1), grid=(packs...  24.7 us
    ppermute x18, starting transfers between devices, exchange(): lax.ppermute(value, axis, [(src, src ^ k << shift) for src in range(size)])  21.3 us
    pallas_call x4, Pallas kernels, first_synth(): pl.pallas_call(functools.partial(first_synth_kernel, (sizes, chosen, dest...  17.3 us
    pallas_call x3, Pallas kernels, second_synth(): pl.pallas_call(functools.partial(second_synth_kernel, dims), in_specs=[SM...  15 us
  transfers between devices with their start and end apart: 38, of which 13 were waited for; matrix products, arithmetic and copies ran while one was open for 1% of the time, Pallas kernels for 29%

profile of v10, /device:TPU:0, one launch (start us, length us, event | category | flops | bytes accessed | tf_op | source)
XLA Modules:
  0.0 269.1 jit_solution(5182498735727754489)
XLA Ops:
  4.6 3.6 %first_synth.4 = (f32[512,128]{1,0:T(8,128)S(1)}, f32[512,128]{1,0:T(8,128)S(1)}, f32[512,128]{1,0:T(8,128)S(1)}, f32[512,128]{1,0:T(8,128)S(1)}) custom-call(s32[3]{0:T(128)S(1)} %pad_add_fusion.place_ref, f32[3,20,40,160]{3,2,1,0:T(8,128)S(1)} %copy-done.3, bf16[4,160,128]{2,1,0:T(8,128)(2,1)S(1)} %dynamic-slice_bitcast_fusion.2.table_ref.refs_12_), custom_call_target="tpu_custom_call" | custom-call | flops 1024 | bytes 1024 | tf_op jit(solution)/shard_map/first_synth/pallas_call | solution.py:168
  8.3 3.6 %first_synth.5 = (f32[512,128]{1,0:T(8,128)S(1)}, f32[512,128]{1,0:T(8,128)S(1)}, f32[512,128]{1,0:T(8,128)S(1)}, f32[512,128]{1,0:T(8,128)S(1)}) custom-call(s32[3]{0:T(128)S(1)} %pad_add_fusion.place_ref, f32[3,20,40,160]{3,2,1,0:T(8,128)S(1)} %collective-permute-done.data, ...), custom_call_target="tpu_custom_call", output_to_operand_aliasing={{0}: (3, {}), {1}: (4, {}), {2}: (5, {}), {3}: (6, {})} | custom-call | flops 1024 | bytes 1024 | tf_op jit(solution)/shard_map/first_synth/pallas_call | solution.py:168
  11.9 2.6 collective-permute-start.1
  14.5 2.6 collective-permute-start.2
  17.1 5.0 %first_synth.6 = (f32[512,128]{1,0:T(8,128)S(1)}, f32[512,128]{1,0:T(8,128)S(1)}, f32[512,128]{1,0:T(8,128)S(1)}, f32[512,128]{1,0:T(8,128)S(1)}, f32[1024,128]{...) custom-call(s32[3]{0:T(128)S(1)} %pad_add_fusion.place_ref, ...), custom_call_target="tpu_custom_call" | custom-call | flops 1024 | bytes 1024 | tf_op jit(solution)/shard_map/first_synth/pallas_call | solution.py:168
  22.1 5.0 %first_synth.7 = (f32[512,128]{1,0:T(8,128)S(1)}, f32[512,128]{1,0:T(8,128)S(1)}, f32[512,128]{1,0:T(8,128)S(1)}, f32[512,128]{1,0:T(8,128)S(1)}, f32[1024,128]{...) custom-call(s32[3]{0:T(128)S(1)} %pad_add_fusion.place_ref, ...), custom_call_target="tpu_custom_call", output_to_operand_aliasing={{0}: (3, {}), {1}: (4, {}), {2}: (5, {}), {3}: (6, {}), {4}... | custom-call | flops 1024 | bytes 1024 | tf_op jit(solution)/shard_map/first_synth/pallas_call | solution.py:168
  27.2 8.7 %collective-permute-done.2.refs_2_ = f32[512,128]{1,0:T(8,128)S(1)} collective-permute-done((f32[512,128]{1,0:T(8,128)S(1)}, f32[512,128]{1,0:T(8,128)S(1)}, u32[]{:S(2)}, u32[]{:S(2)}) %collective-permute-start.2) | collective-permute-done | bytes 262176 | tf_op jit(solution)/shard_map/ppermute | solution.py:657
  38.3 3.7 %second_synth.3 = (f32[4,240,128]{2,1,0:T(8,128)S(1)}, f32[4,240,128]{2,1,0:T(8,128)S(1)}, f32[4,240,128]{2,1,0:T(8,128)S(1)}, f32[4,240,128]{2,1,0:T(8,128)S(1)}) custom-call(s32[3]{0:T(128)S(1)} %pad_add_fusion.place_ref, f32[512,128]{1,0:T(8,128)S(1)} %get-tuple-element.164.refs_0_, f32[512,128]{1,0:T(8,128)S(1)} %collective-permute-done.1.refs_1_, ...), custom_call_target="tpu_custom_call" | custom-call | flops 1024 | bytes 1024 | tf_op jit(solution)/shard_map/second_synth/pallas_call | solution.py:241
  45.6 10.1 %collective-permute-start.8 = (f32[512,128]{1,0:T(8,128)S(1)}, f32[512,128]{1,0:T(8,128)S(1)}, u32[]{:S(2)}, u32[]{:S(2)}) collective-permute-start(f32[512,128]{1,0:T(8,128)S(1)} %get-tuple-element.177), channel_id=1, source_target_pairs={{0,16},{4,20},{8,24},{12,28},{16,0},{20,4},{24,8},{28,12},{1,17},{... | collective-permute-start | bytes 786440 | tf_op jit(solution)/shard_map/ppermute | solution.py:657
  55.8 10.3 %collective-permute-done.8.refs_2_ = f32[512,128]{1,0:T(8,128)S(1)} collective-permute-done((f32[512,128]{1,0:T(8,128)S(1)}, f32[512,128]{1,0:T(8,128)S(1)}, u32[]{:S(2)}, u32[]{:S(2)}) %collective-permute-start.8) | collective-permute-done | bytes 262176 | tf_op jit(solution)/shard_map/ppermute | solution.py:657
  66.1 2.8 %collective-permute-start.17 = (f32[1024,128]{1,0:T(8,128)S(1)}, f32[1024,128]{1,0:T(8,128)S(1)}, u32[]{:S(2)}, u32[]{:S(2)}) collective-permute-start(f32[1024,128]{1,0:T(8,128)S(1)} %get-tuple-element.220), channel_id=1, source_target_pairs={{0,16},{4,20},{8,24},{12,28},{16,0},{20,4},{24,8},{28,12},{1,17},{... | collective-permute-start | bytes 1572872 | tf_op jit(solution)/shard_map/ppermute | solution.py:657
  68.9 6.4 %earlier_orders.3.refs_6_ = f32[3,8,64,256]{3,2,1,0:T(8,128)S(1)} custom-call(f32[6,3,32,64,256]{4,3,2,1,0:T(8,128)} %refs_4_.8, f32[6,3,32,64,256]{4,3,2,1,0:T(8,128)} %refs_4_.8, f32[6,3,32,64,256]{4,3,2,1,0:T(8,128)} %refs_4_.8, f32[6,3,32,64,256]{4,3,2,1,0:T(8,128)} %refs_4_.8, f32[6,3,32,64,256]{4,3,2,1,0:T(8,128)} %refs_4_.8, ...), custom_call_target="tpu_custom_call" | custom-call | flops 1024 | bytes 1024 | tf_op jit(solution)/shard_map/earlier_orders/pallas_call | solution.py:293
  75.3 3.7 %second_synth.4 = (f32[4,240,128]{2,1,0:T(8,128)S(1)}, f32[4,240,128]{2,1,0:T(8,128)S(1)}, f32[4,240,128]{2,1,0:T(8,128)S(1)}, f32[4,240,128]{2,1,0:T(8,128)S(1)}) custom-call(s32[3]{0:T(128)S(1)} %pad_add_fusion.place_ref, f32[512,128]{1,0:T(8,128)S(1)} %get-tuple-element.182.refs_0_, f32[512,128]{1,0:T(8,128)S(1)} %collective-permute-done.7.refs_1_, ...), custom_call_target="tpu_custom_call" | custom-call | flops 1024 | bytes 1024 | tf_op jit(solution)/shard_map/second_synth/pallas_call | solution.py:241
  83.1 6.6 %collective-permute-done.17.refs_2_ = f32[1024,128]{1,0:T(8,128)S(1)} collective-permute-done((f32[1024,128]{1,0:T(8,128)S(1)}, f32[1024,128]{1,0:T(8,128)S(1)}, u32[]{:S(2)}, u32[]{:S(2)}) %collective-permute-start.17) | collective-permute-done | bytes 524320 | tf_op jit(solution)/shard_map/ppermute | solution.py:657
  90.5 3.5 %collective-permute-start.18 = (f32[1024,128]{1,0:T(8,128)}, f32[1024,128]{1,0:T(8,128)}, u32[]{:S(2)}, u32[]{:S(2)}) collective-permute-start(f32[1024,128]{1,0:T(8,128)} %get-tuple-element.222), channel_id=1, source_target_pairs={{0,24},{4,28},{8,16},{12,20},{16,8},{20,12},{24,0},{28,4},{1,25},{... | collective-permute-start | bytes 1572872 | tf_op jit(solution)/shard_map/ppermute | solution.py:657
  94.0 7.3 %third_dimension.3 = (f32[4,120,128]{2,1,0:T(8,128)S(1)}, f32[4,120,128]{2,1,0:T(8,128)}, f32[4,120,128]{2,1,0:T(8,128)}, f32[4,120,128]{2,1,0:T(8,128)}) custom-call(s32[3]{0:T(128)S(1)} %pad_add_fusion.place_ref, f32[4,240,128]{2,1,0:T(8,128)S(1)} %get-tuple-element.187.refs_0_, f32[4,240,128]{2,1,0:T(8,128)S(1)} %collective-permute-done.4.refs_1_, ...), custom_call_target="tpu_custom_call" | custom-call | flops 1024 | bytes 1024 | tf_op jit(solution)/shard_map/third_dimension/pallas_call | solution.py:361
  107.2 6.4 %earlier_orders.4.refs_6_ = f32[3,8,64,256]{3,2,1,0:T(8,128)S(1)} custom-call(f32[6,3,32,64,256]{4,3,2,1,0:T(8,128)} %refs_4_.8, f32[6,3,32,64,256]{4,3,2,1,0:T(8,128)} %refs_4_.8, f32[6,3,32,64,256]{4,3,2,1,0:T(8,128)} %refs_4_.8, f32[6,3,32,64,256]{4,3,2,1,0:T(8,128)} %refs_4_.8, f32[6,3,32,64,256]{4,3,2,1,0:T(8,128)} %refs_4_.8, ...), custom_call_target="tpu_custom_call" | custom-call | flops 1024 | bytes 1024 | tf_op jit(solution)/shard_map/earlier_orders/pallas_call | solution.py:293
  113.6 11.9 %earlier_orders.5.refs_6_ = f32[3,16,64,256]{3,2,1,0:T(8,128)S(1)} custom-call(f32[6,3,32,64,256]{4,3,2,1,0:T(8,128)} %refs_4_.8, f32[6,3,32,64,256]{4,3,2,1,0:T(8,128)} %refs_4_.8, f32[6,3,32,64,256]{4,3,2,1,0:T(8,128)} %refs_4_.8, f32[6,3,32,64,256]{4,3,2,1,0:T(8,128)} %refs_4_.8, f32[6,3,32,64,256]{4,3,2,1,0:T(8,128)} %refs_4_.8, ...), custom_call_target="tpu_custom_call" | custom-call | flops 1024 | bytes 1024 | tf_op jit(solution)/shard_map/earlier_orders/pallas_call | solution.py:293
  125.6 6.4 %third_dimension.4 = (f32[4,120,128]{2,1,0:T(8,128)S(1)}, f32[4,120,128]{2,1,0:T(8,128)S(1)}, f32[4,120,128]{2,1,0:T(8,128)S(1)}, f32[4,120,128]{2,1,0:T(8,128)S(1)}) custom-call(s32[3]{0:T(128)S(1)} %copy-done.20, f32[4,240,128]{2,1,0:T(8,128)S(1)} %get-tuple-element.206.refs_0_, f32[4,240,128]{2,1,0:T(8,128)S(1)} %copy-done.18, ...), custom_call_target="tpu_custom_call" | custom-call | flops 1024 | bytes 1024 | tf_op jit(solution)/shard_map/third_dimension/pallas_call | solution.py:361
  135.7 3.1 %second_back.3 = (f32[304,128]{1,0:T(8,128)S(1)}, f32[304,128]{1,0:T(8,128)S(1)}, f32[304,128]{1,0:T(8,128)S(1)}, f32[304,128]{1,0:T(8,128)S(1)}) custom-call(s32[3]{0:T(128)S(1)} %copy-done.20, f32[4,120,128]{2,1,0:T(8,128)S(1)} %get-tuple-element.211.refs_0_, f32[4,120,128]{2,1,0:T(8,128)} %collective-permute-done.10.refs_1_, ...), custom_call_target="tpu_custom_call" | custom-call | flops 1024 | bytes 1024 | tf_op jit(solution)/shard_map/second_back/pallas_call | solution.py:410
  139.7 7.6 %second_synth.5 = (f32[8,240,128]{2,1,0:T(8,128)S(1)}, f32[8,240,128]{2,1,0:T(8,128)S(1)}, f32[8,240,128]{2,1,0:T(8,128)S(1)}, f32[8,240,128]{2,1,0:T(8,128)S(1)}) custom-call(s32[3]{0:T(128)S(1)} %copy-done.20, f32[1024,128]{1,0:T(8,128)S(1)} %copy-done.10, f32[1024,128]{1,0:T(8,128)} %collective-permute-done.16.refs_1_, f32[1024,128]{1,0:T(8,128)S(1)} %copy-done.12, ...), custom_call_target="tpu_custom_call" | custom-call | flops 1024 | bytes 1024 | tf_op jit(solution)/shard_map/second_synth/pallas_call | solution.py:241
  151.8 9.7 %collective-permute-done.20.refs_2_ = f32[304,128]{1,0:T(8,128)S(1)} collective-permute-done((f32[304,128]{1,0:T(8,128)S(1)}, f32[304,128]{1,0:T(8,128)S(1)}, u32[]{:S(2)}, u32[]{:S(2)}) %collective-permute-start.20) | collective-permute-done | bytes 155680 | tf_op jit(solution)/shard_map/ppermute | solution.py:657
  161.5 7.0 %collective-permute-done.21.refs_3_ = f32[304,128]{1,0:T(8,128)S(1)} collective-permute-done((f32[304,128]{1,0:T(8,128)S(1)}, f32[304,128]{1,0:T(8,128)S(1)}, u32[]{:S(2)}, u32[]{:S(2)}) %collective-permute-start.21) | collective-permute-done | bytes 155680 | tf_op jit(solution)/shard_map/ppermute | solution.py:657
  173.0 18.0 %collective-permute-done.29.refs_2_ = f32[8,240,128]{2,1,0:T(8,128)S(1)} collective-permute-done((f32[8,240,128]{2,1,0:T(8,128)S(1)}, f32[8,240,128]{2,1,0:T(8,128)S(1)}, u32[]{:S(2)}, u32[]{:S(2)}) %collective-permute-start.29) | collective-permute-done | bytes 983072 | tf_op jit(solution)/shard_map/ppermute | solution.py:615
  191.1 12.1 %third_dimension.5 = (f32[8,120,128]{2,1,0:T(8,128)S(1)}, f32[8,120,128]{2,1,0:T(8,128)S(1)}, f32[8,120,128]{2,1,0:T(8,128)S(1)}, f32[8,120,128]{2,1,0:T(8,128)S(1)}) custom-call(s32[3]{0:T(128)S(1)} %copy-done.20, f32[8,240,128]{2,1,0:T(8,128)S(1)} %get-tuple-element.257.refs_0_, f32[8,240,128]{2,1,0:T(8,128)S(1)} %collective-permute-done.28.refs_1_, ...), custom_call_target="tpu_custom_call" | custom-call | flops 1024 | bytes 1024 | tf_op jit(solution)/shard_map/third_dimension/pallas_call | solution.py:361
  208.7 8.7 %collective-permute-done.31.refs_1_ = f32[8,120,128]{2,1,0:T(8,128)S(1)} collective-permute-done((f32[8,120,128]{2,1,0:T(8,128)S(1)}, f32[8,120,128]{2,1,0:T(8,128)S(1)}, u32[]{:S(2)}, u32[]{:S(2)}) %collective-permute-start.31) | collective-permute-done | bytes 491552 | tf_op jit(solution)/shard_map/ppermute | solution.py:615
  217.9 10.3 %collective-permute-done.32.refs_2_ = f32[8,120,128]{2,1,0:T(8,128)S(1)} collective-permute-done((f32[8,120,128]{2,1,0:T(8,128)S(1)}, f32[8,120,128]{2,1,0:T(8,128)S(1)}, u32[]{:S(2)}, u32[]{:S(2)}) %collective-permute-start.32) | collective-permute-done | bytes 491552 | tf_op jit(solution)/shard_map/ppermute | solution.py:615
  228.1 4.6 %second_back.5 = (f32[608,128]{1,0:T(8,128)S(1)}, f32[608,128]{1,0:T(8,128)S(1)}, f32[608,128]{1,0:T(8,128)S(1)}, f32[608,128]{1,0:T(8,128)S(1)}) custom-call(s32[3]{0:T(128)S(1)} %copy-done.20, f32[8,120,128]{2,1,0:T(8,128)S(1)} %get-tuple-element.265.refs_0_, f32[8,120,128]{2,1,0:T(8,128)S(1)} %collective-permute-done.31.refs_1_, ...), custom_call_target="tpu_custom_call" | custom-call | flops 1024 | bytes 1024 | tf_op jit(solution)/shard_map/second_back/pallas_call | solution.py:410
  233.9 3.3 %collective-permute-start.34 = (f32[608,128]{1,0:T(8,128)S(1)}, f32[608,128]{1,0:T(8,128)S(1)}, u32[]{:S(2)}, u32[]{:S(2)}) collective-permute-start(f32[608,128]{1,0:T(8,128)S(1)} %get-tuple-element.271), channel_id=1, source_target_pairs={{0,8},{4,12},{8,0},{12,4},{16,24},{20,28},{24,16},{28,20},{1,9},{5... | collective-permute-start | bytes 933896 | tf_op jit(solution)/shard_map/ppermute | solution.py:657
  237.2 7.8 %collective-permute-done.36.refs_11_ = f32[608,128]{1,0:T(8,128)S(1)} collective-permute-done((f32[608,128]{1,0:T(8,128)S(1)}, f32[608,128]{1,0:T(8,128)S(1)}, u32[]{:S(2)}, u32[]{:S(2)}) %collective-permute-start.36) | collective-permute-done | bytes 311328 | tf_op jit(solution)/shard_map/ppermute | solution.py:657
  245.0 14.7 %collective-permute-done.35.refs_10_ = f32[608,128]{1,0:T(8,128)S(1)} collective-permute-done((f32[608,128]{1,0:T(8,128)S(1)}, f32[608,128]{1,0:T(8,128)S(1)}, u32[]{:S(2)}, u32[]{:S(2)}) %collective-permute-start.35) | collective-permute-done | bytes 311328 | tf_op jit(solution)/shard_map/ppermute | solution.py:657
  264.5 4.5 %last_projection.1 = f32[3,20,40,160]{3,2,1,0:T(8,128)} custom-call(f32[10]{0:T(128)S(1)} %convert_multiply_fusion.1.refs_0_, f32[8,256]{1,0:T(8,128)S(1)} %broadcast_in_dim.9.refs_1_, f32[40,256]{1,0:T(8,128)S(1)} %broadcast_in_dim.18.refs_2_, f32[160,2432]{1,0:T(8,128)S(1)} %first_back.3.refs_3_, f32[160,2432]{1,0:T(8,128)S(1)} %collective-permute-done.37.refs_4_), custom_call_target="tpu_custom_call" | custom-call | flops 1024 | bytes 1024 | tf_op jit(solution)/shard_map/last_projection/pallas_call | solution.py:523
  (113 shorter events, 46.9 us)
Async XLA Ops:
  11.9 15.2 %collective-permute-start.1 = (f32[512,128]{1,0:T(8,128)S(1)}, f32[512,128]{1,0:T(8,128)S(1)}, u32[]{:S(2)}, u32[]{:S(2)}) collective-permute-start(f32[512,128]{1,0:T(8,128)S(1)} %get-tuple-element.151), channel_id=1, source_target_pairs={{0,8},{4,12},{8,0},{12,4},{16,24},{20,28},{24,16},{28,20},{1,9},{5... | collective-permute-start | bytes 786440 | tf_op jit(solution)/shard_map/ppermute | solution.py:657
  14.5 21.3 %collective-permute-start.2 = (f32[512,128]{1,0:T(8,128)S(1)}, f32[512,128]{1,0:T(8,128)S(1)}, u32[]{:S(2)}, u32[]{:S(2)}) collective-permute-start(f32[512,128]{1,0:T(8,128)S(1)} %get-tuple-element.152), channel_id=1, source_target_pairs={{0,16},{4,20},{8,24},{12,28},{16,0},{20,4},{24,8},{28,12},{1,17},{... | collective-permute-start | bytes 786440 | tf_op jit(solution)/shard_map/ppermute | solution.py:657
  17.1 18.7 %collective-permute-start.3 = (f32[512,128]{1,0:T(8,128)S(1)}, f32[512,128]{1,0:T(8,128)S(1)}, u32[]{:S(2)}, u32[]{:S(2)}) collective-permute-start(f32[512,128]{1,0:T(8,128)S(1)} %get-tuple-element.153), channel_id=1, source_target_pairs={{0,24},{4,28},{8,16},{12,20},{16,8},{20,12},{24,0},{28,4},{1,25},{... | collective-permute-start | bytes 786440 | tf_op jit(solution)/shard_map/ppermute | solution.py:657
  35.9 19.8 %collective-permute-start.9 = (f32[512,128]{1,0:T(8,128)S(1)}, f32[512,128]{1,0:T(8,128)S(1)}, u32[]{:S(2)}, u32[]{:S(2)}) collective-permute-start(f32[512,128]{1,0:T(8,128)S(1)} %get-tuple-element.179), channel_id=1, source_target_pairs={{0,24},{4,28},{8,16},{12,20},{16,8},{20,12},{24,0},{28,4},{1,25},{... | collective-permute-start | bytes 786440 | tf_op jit(solution)/shard_map/ppermute | solution.py:657
  42.1 36.9 %collective-permute-start.4 = (f32[4,240,128]{2,1,0:T(8,128)S(1)}, f32[4,240,128]{2,1,0:T(8,128)S(1)}, u32[]{:S(2)}, u32[]{:S(2)}) collective-permute-start(f32[4,240,128]{2,1,0:T(8,128)S(1)} %get-tuple-element.170), channel_id=1, source_target_pairs={{0,1},{1,0},{2,3},{3,2},{4,5},{5,4},{6,7},{7,6},{8,9},{9,8},{10,11... | collective-permute-start | bytes 1474568 | tf_op jit(solution)/shard_map/ppermute | solution.py:615
  43.6 35.4 %collective-permute-start.5 = (f32[4,240,128]{2,1,0:T(8,128)S(1)}, f32[4,240,128]{2,1,0:T(8,128)S(1)}, u32[]{:S(2)}, u32[]{:S(2)}) collective-permute-start(f32[4,240,128]{2,1,0:T(8,128)S(1)} %get-tuple-element.171), channel_id=1, source_target_pairs={{0,2},{1,3},{2,0},{3,1},{4,6},{5,7},{6,4},{7,5},{8,10},{9,11},{10,... | collective-permute-start | bytes 1474568 | tf_op jit(solution)/shard_map/ppermute | solution.py:615
  45.1 33.9 %collective-permute-start.6 = (f32[4,240,128]{2,1,0:T(8,128)S(1)}, f32[4,240,128]{2,1,0:T(8,128)S(1)}, u32[]{:S(2)}, u32[]{:S(2)}) collective-permute-start(f32[4,240,128]{2,1,0:T(8,128)S(1)} %get-tuple-element.172), channel_id=1, source_target_pairs={{0,3},{1,2},{2,1},{3,0},{4,7},{5,6},{6,5},{7,4},{8,11},{9,10},{10,... | collective-permute-start | bytes 1474568 | tf_op jit(solution)/shard_map/ppermute | solution.py:615
  45.6 20.5 %collective-permute-start.8 = (f32[512,128]{1,0:T(8,128)S(1)}, f32[512,128]{1,0:T(8,128)S(1)}, u32[]{:S(2)}, u32[]{:S(2)}) collective-permute-start(f32[512,128]{1,0:T(8,128)S(1)} %get-tuple-element.177), channel_id=1, source_target_pairs={{0,16},{4,20},{8,24},{12,28},{16,0},{20,4},{24,8},{28,12},{1,17},{... | collective-permute-start | bytes 786440 | tf_op jit(solution)/shard_map/ppermute | solution.py:657
  66.1 23.6 %collective-permute-start.17 = (f32[1024,128]{1,0:T(8,128)S(1)}, f32[1024,128]{1,0:T(8,128)S(1)}, u32[]{:S(2)}, u32[]{:S(2)}) collective-permute-start(f32[1024,128]{1,0:T(8,128)S(1)} %get-tuple-element.220), channel_id=1, source_target_pairs={{0,16},{4,20},{8,24},{12,28},{16,0},{20,4},{24,8},{28,12},{1,17},{... | collective-permute-start | bytes 1572872 | tf_op jit(solution)/shard_map/ppermute | solution.py:657
  79.0 22.3 %collective-permute-start.15 = (f32[4,240,128]{2,1,0:T(8,128)S(1)}, f32[4,240,128]{2,1,0:T(8,128)S(1)}, u32[]{:S(2)}, u32[]{:S(2)}) collective-permute-start(f32[4,240,128]{2,1,0:T(8,128)S(1)} %get-tuple-element.201), channel_id=1, source_target_pairs={{0,3},{1,2},{2,1},{3,0},{4,7},{5,6},{6,5},{7,4},{8,11},{9,10},{10,... | collective-permute-start | bytes 1474568 | tf_op jit(solution)/shard_map/ppermute | solution.py:615
  81.5 22.1 %collective-permute-start.14 = (f32[4,240,128]{2,1,0:T(8,128)S(1)}, f32[4,240,128]{2,1,0:T(8,128)S(1)}, u32[]{:S(2)}, u32[]{:S(2)}) collective-permute-start(f32[4,240,128]{2,1,0:T(8,128)S(1)} %get-tuple-element.199), channel_id=1, source_target_pairs={{0,2},{1,3},{2,0},{3,1},{4,6},{5,7},{6,4},{7,5},{8,10},{9,11},{10,... | collective-permute-start | bytes 1474568 | tf_op jit(solution)/shard_map/ppermute | solution.py:615
  82.0 23.9 %collective-permute-start.13 = (f32[4,240,128]{2,1,0:T(8,128)S(1)}, f32[4,240,128]{2,1,0:T(8,128)S(1)}, u32[]{:S(2)}, u32[]{:S(2)}) collective-permute-start(f32[4,240,128]{2,1,0:T(8,128)S(1)} %get-tuple-element.197), channel_id=1, source_target_pairs={{0,1},{1,0},{2,3},{3,2},{4,5},{5,4},{6,7},{7,6},{8,9},{9,8},{10,11... | collective-permute-start | bytes 1474568 | tf_op jit(solution)/shard_map/ppermute | solution.py:615
  82.6 56.2 %collective-permute-start.16 = (f32[1024,128]{1,0:T(8,128)}, f32[1024,128]{1,0:T(8,128)}, u32[]{:S(2)}, u32[]{:S(2)}) collective-permute-start(f32[1024,128]{1,0:T(8,128)} %get-tuple-element.218), channel_id=1, source_target_pairs={{0,8},{4,12},{8,0},{12,4},{16,24},{20,28},{24,16},{28,20},{1,9},{5... | collective-permute-start | bytes 1572872 | tf_op jit(solution)/shard_map/ppermute | solution.py:657
  90.5 48.2 %collective-permute-start.18 = (f32[1024,128]{1,0:T(8,128)}, f32[1024,128]{1,0:T(8,128)}, u32[]{:S(2)}, u32[]{:S(2)}) collective-permute-start(f32[1024,128]{1,0:T(8,128)} %get-tuple-element.222), channel_id=1, source_target_pairs={{0,24},{4,28},{8,16},{12,20},{16,8},{20,12},{24,0},{28,4},{1,25},{... | collective-permute-start | bytes 1572872 | tf_op jit(solution)/shard_map/ppermute | solution.py:657
  102.1 30.0 %collective-permute-start.10 = (f32[4,120,128]{2,1,0:T(8,128)}, f32[4,120,128]{2,1,0:T(8,128)}, u32[]{:S(2)}, u32[]{:S(2)}) collective-permute-start(f32[4,120,128]{2,1,0:T(8,128)} %get-tuple-element.193), channel_id=1, source_target_pairs={{0,1},{1,0},{2,3},{3,2},{4,5},{5,4},{6,7},{7,6},{8,9},{9,8},{10,11... | collective-permute-start | bytes 737288 | tf_op jit(solution)/shard_map/ppermute | solution.py:615
  104.4 29.2 %collective-permute-start.11 = (f32[4,120,128]{2,1,0:T(8,128)}, f32[4,120,128]{2,1,0:T(8,128)}, u32[]{:S(2)}, u32[]{:S(2)}) collective-permute-start(f32[4,120,128]{2,1,0:T(8,128)} %get-tuple-element.194), channel_id=1, source_target_pairs={{0,2},{1,3},{2,0},{3,1},{4,6},{5,7},{6,4},{7,5},{8,10},{9,11},{10,... | collective-permute-start | bytes 737288 | tf_op jit(solution)/shard_map/ppermute | solution.py:615
  106.8 28.4 %collective-permute-start.12 = (f32[4,120,128]{2,1,0:T(8,128)}, f32[4,120,128]{2,1,0:T(8,128)}, u32[]{:S(2)}, u32[]{:S(2)}) collective-permute-start(f32[4,120,128]{2,1,0:T(8,128)} %get-tuple-element.195), channel_id=1, source_target_pairs={{0,3},{1,2},{2,1},{3,0},{4,7},{5,6},{6,5},{7,4},{8,11},{9,10},{10,... | collective-permute-start | bytes 737288 | tf_op jit(solution)/shard_map/ppermute | solution.py:615
  132.1 15.2 %collective-permute-start.22 = (f32[4,120,128]{2,1,0:T(8,128)S(1)}, f32[4,120,128]{2,1,0:T(8,128)S(1)}, u32[]{:S(2)}, u32[]{:S(2)}) collective-permute-start(f32[4,120,128]{2,1,0:T(8,128)S(1)} %get-tuple-element.228), channel_id=1, source_target_pairs={{0,1},{1,0},{2,3},{3,2},{4,5},{5,4},{6,7},{7,6},{8,9},{9,8},{10,11... | collective-permute-start | bytes 737288 | tf_op jit(solution)/shard_map/ppermute | solution.py:615
  133.7 13.7 %collective-permute-start.23 = (f32[4,120,128]{2,1,0:T(8,128)S(1)}, f32[4,120,128]{2,1,0:T(8,128)S(1)}, u32[]{:S(2)}, u32[]{:S(2)}) collective-permute-start(f32[4,120,128]{2,1,0:T(8,128)S(1)} %get-tuple-element.229), channel_id=1, source_target_pairs={{0,2},{1,3},{2,0},{3,1},{4,6},{5,7},{6,4},{7,5},{8,10},{9,11},{10,... | collective-permute-start | bytes 737288 | tf_op jit(solution)/shard_map/ppermute | solution.py:615
  135.2 12.2 %collective-permute-start.24 = (f32[4,120,128]{2,1,0:T(8,128)S(1)}, f32[4,120,128]{2,1,0:T(8,128)S(1)}, u32[]{:S(2)}, u32[]{:S(2)}) collective-permute-start(f32[4,120,128]{2,1,0:T(8,128)S(1)} %get-tuple-element.230), channel_id=1, source_target_pairs={{0,3},{1,2},{2,1},{3,0},{4,7},{5,6},{6,5},{7,4},{8,11},{9,10},{10,... | collective-permute-start | bytes 737288 | tf_op jit(solution)/shard_map/ppermute | solution.py:615
  147.4 25.7 %collective-permute-start.30 = (f32[8,240,128]{2,1,0:T(8,128)S(1)}, f32[8,240,128]{2,1,0:T(8,128)S(1)}, u32[]{:S(2)}, u32[]{:S(2)}) collective-permute-start(f32[8,240,128]{2,1,0:T(8,128)S(1)} %get-tuple-element.256), channel_id=1, source_target_pairs={{0,3},{1,2},{2,1},{3,0},{4,7},{5,6},{6,5},{7,4},{8,11},{9,10},{10,... | collective-permute-start | bytes 2949128 | tf_op jit(solution)/shard_map/ppermute | solution.py:615
  149.9 41.2 %collective-permute-start.29 = (f32[8,240,128]{2,1,0:T(8,128)S(1)}, f32[8,240,128]{2,1,0:T(8,128)S(1)}, u32[]{:S(2)}, u32[]{:S(2)}) collective-permute-start(f32[8,240,128]{2,1,0:T(8,128)S(1)} %get-tuple-element.254), channel_id=1, source_target_pairs={{0,2},{1,3},{2,0},{3,1},{4,6},{5,7},{6,4},{7,5},{8,10},{9,11},{10,... | collective-permute-start | bytes 2949128 | tf_op jit(solution)/shard_map/ppermute | solution.py:615
  150.4 40.8 %collective-permute-start.28 = (f32[8,240,128]{2,1,0:T(8,128)S(1)}, f32[8,240,128]{2,1,0:T(8,128)S(1)}, u32[]{:S(2)}, u32[]{:S(2)}) collective-permute-start(f32[8,240,128]{2,1,0:T(8,128)S(1)} %get-tuple-element.252), channel_id=1, source_target_pairs={{0,1},{1,0},{2,3},{3,2},{4,5},{5,4},{6,7},{7,6},{8,9},{9,8},{10,11... | collective-permute-start | bytes 2949128 | tf_op jit(solution)/shard_map/ppermute | solution.py:615
  203.3 14.2 %collective-permute-start.31 = (f32[8,120,128]{2,1,0:T(8,128)S(1)}, f32[8,120,128]{2,1,0:T(8,128)S(1)}, u32[]{:S(2)}, u32[]{:S(2)}) collective-permute-start(f32[8,120,128]{2,1,0:T(8,128)S(1)} %get-tuple-element.262), channel_id=1, source_target_pairs={{0,1},{1,0},{2,3},{3,2},{4,5},{5,4},{6,7},{7,6},{8,9},{9,8},{10,11... | collective-permute-start | bytes 1474568 | tf_op jit(solution)/shard_map/ppermute | solution.py:615
  204.8 23.3 %collective-permute-start.32 = (f32[8,120,128]{2,1,0:T(8,128)S(1)}, f32[8,120,128]{2,1,0:T(8,128)S(1)}, u32[]{:S(2)}, u32[]{:S(2)}) collective-permute-start(f32[8,120,128]{2,1,0:T(8,128)S(1)} %get-tuple-element.263), channel_id=1, source_target_pairs={{0,2},{1,3},{2,0},{3,1},{4,6},{5,7},{6,4},{7,5},{8,10},{9,11},{10,... | collective-permute-start | bytes 1474568 | tf_op jit(solution)/shard_map/ppermute | solution.py:615
  205.6 22.6 %collective-permute-start.33 = (f32[8,120,128]{2,1,0:T(8,128)S(1)}, f32[8,120,128]{2,1,0:T(8,128)S(1)}, u32[]{:S(2)}, u32[]{:S(2)}) collective-permute-start(f32[8,120,128]{2,1,0:T(8,128)S(1)} %get-tuple-element.264), channel_id=1, source_target_pairs={{0,3},{1,2},{2,1},{3,0},{4,7},{5,6},{6,5},{7,4},{8,11},{9,10},{10,... | collective-permute-start | bytes 1474568 | tf_op jit(solution)/shard_map/ppermute | solution.py:615
  206.8 25.9 %collective-permute-start.27 = (f32[304,128]{1,0:T(8,128)S(1)}, f32[304,128]{1,0:T(8,128)S(1)}, u32[]{:S(2)}, u32[]{:S(2)}) collective-permute-start(f32[304,128]{1,0:T(8,128)S(1)} %get-tuple-element.250), channel_id=1, source_target_pairs={{0,24},{4,28},{8,16},{12,20},{16,8},{20,12},{24,0},{28,4},{1,25},{... | collective-permute-start | bytes 466952 | tf_op jit(solution)/shard_map/ppermute | solution.py:657
  207.1 25.6 %collective-permute-start.26 = (f32[304,128]{1,0:T(8,128)S(1)}, f32[304,128]{1,0:T(8,128)S(1)}, u32[]{:S(2)}, u32[]{:S(2)}) collective-permute-start(f32[304,128]{1,0:T(8,128)S(1)} %get-tuple-element.248), channel_id=1, source_target_pairs={{0,16},{4,20},{8,24},{12,28},{16,0},{20,4},{24,8},{28,12},{1,17},{... | collective-permute-start | bytes 466952 | tf_op jit(solution)/shard_map/ppermute | solution.py:657
  217.5 15.3 %collective-permute-start.25 = (f32[304,128]{1,0:T(8,128)S(1)}, f32[304,128]{1,0:T(8,128)S(1)}, u32[]{:S(2)}, u32[]{:S(2)}) collective-permute-start(f32[304,128]{1,0:T(8,128)S(1)} %get-tuple-element.246), channel_id=1, source_target_pairs={{0,8},{4,12},{8,0},{12,4},{16,24},{20,28},{24,16},{28,20},{1,9},{5... | collective-permute-start | bytes 466952 | tf_op jit(solution)/shard_map/ppermute | solution.py:657
  232.8 12.3 %collective-permute-start.36 = (f32[608,128]{1,0:T(8,128)S(1)}, f32[608,128]{1,0:T(8,128)S(1)}, u32[]{:S(2)}, u32[]{:S(2)}) collective-permute-start(f32[608,128]{1,0:T(8,128)S(1)} %get-tuple-element.275), channel_id=1, source_target_pairs={{0,24},{4,28},{8,16},{12,20},{16,8},{20,12},{24,0},{28,4},{1,25},{... | collective-permute-start | bytes 933896 | tf_op jit(solution)/shard_map/ppermute | solution.py:657
  233.1 26.6 %collective-permute-start.35 = (f32[608,128]{1,0:T(8,128)S(1)}, f32[608,128]{1,0:T(8,128)S(1)}, u32[]{:S(2)}, u32[]{:S(2)}) collective-permute-start(f32[608,128]{1,0:T(8,128)S(1)} %get-tuple-element.273), channel_id=1, source_target_pairs={{0,16},{4,20},{8,24},{12,28},{16,0},{20,4},{24,8},{28,12},{1,17},{... | collective-permute-start | bytes 933896 | tf_op jit(solution)/shard_map/ppermute | solution.py:657
  233.9 25.8 %collective-permute-start.34 = (f32[608,128]{1,0:T(8,128)S(1)}, f32[608,128]{1,0:T(8,128)S(1)}, u32[]{:S(2)}, u32[]{:S(2)}) collective-permute-start(f32[608,128]{1,0:T(8,128)S(1)} %get-tuple-element.271), channel_id=1, source_target_pairs={{0,8},{4,12},{8,0},{12,4},{16,24},{20,28},{24,16},{28,20},{1,9},{5... | collective-permute-start | bytes 933896 | tf_op jit(solution)/shard_map/ppermute | solution.py:657
  (27 other events, 689.3 us)

commit v11 on v9

--- a/solution.py
+++ b/solution.py
@@ -648,18 +648,18 @@
     def run_earlier(chunk):
         return ordered(lambda values: earlier(*values, begins[chunk], sizes[chunk], pack), stored)
 
-    def z_exchange(values, *gates, waves=True):
+    def z_exchange(values, *gates, waves=True, lead=1):
         found = [values[0]]
         for k in range(1, groups):
             value = values[k]
             if gates:
-                value = after(value, found[1]) if waves and 2 * k > groups else after(value, *gates)
+                value = after(value, found[lead]) if waves and 2 * k > groups else after(value, *gates)
             found.append(lax.ppermute(value, "row", [(src, src ^ (2 * k)) for src in range(rows)]))
         return found
 
     first, second, middle, back, base = {}, {}, {}, {}, {}
     for step in range(min(2, chunks)):
-        first[step] = z_exchange(sent[step], *([first[step - 1]] if step else []))
+        first[step] = z_exchange(sent[step], *([first[step - 1]] if step else []), lead=groups // 2)
 
     def run_second(at):
         found = ordered(lambda values: second_synth(place, values, table_y, dims[at]), first[at])
@@ -679,14 +679,14 @@
     def run_back(at):
         found = ordered(lambda values: second_back(place, values, table_y, dims[at]), middle[at])
         back[at] = z_exchange(found, back[at - 1] if at else first[min(1, chunks - 1)], waves=at == 0)
-        if at == 0 and chunks > 2:
-            first[2] = z_exchange(sent[2], back[0])
 
     def run_base(at):
         base[at] = run_earlier(at)
-
-    plan = [(run_second, 0), (run_base, 0), (run_base, 1), (run_third, 0), (run_base, 2), (run_back, 0)]
-    plan += [(run_second, 1), (run_second, 2), (run_third, 1), (run_third, 2), (run_back, 1), (run_back, 2)]
+        if at == 1 and chunks > 2:
+            first[2] = z_exchange(sent[2], back[0], base[1])
+
+    plan = [(run_second, 0), (run_base, 0), (run_third, 0), (run_back, 0), (run_second, 1), (run_base, 1)]
+    plan += [(run_base, 2), (run_second, 2), (run_third, 1), (run_third, 2), (run_back, 1), (run_back, 2)]
     for action, at in plan:
         if at < chunks:
             action(at)

time: 250 us -> 246 us (0.984)
    ppermute x18, starting transfers between devices: 34.9 us -> 31.4 us  [z_exchange(): lax.ppermute(value, 'row', [(src, src ^ 2 * k) for src in range(rows)])]
    unnamed x42 -> x48, local copies, waits for them, and re-layouts: 5.6 us -> 3.27 us
where the time goes in v11:
time: 246 us; the launch traced here: 245 us
  Pallas kernels  98.5 us (40%)
  waiting for transfers between devices  83.5 us (34%)
  starting transfers between devices  56.6 us (23%)
  local copies, waits for them, and re-layouts  5.45 us (2%)
    ppermute x18, waiting for transfers between devices, z_exchange(): lax.ppermute(value, 'row', [(src, src ^ 2 * k) for src in range(rows)])  53.2 us
    ppermute x18, starting transfers between devices, z_exchange(): lax.ppermute(value, 'row', [(src, src ^ 2 * k) for src in range(rows)])  31.4 us
    ppermute x18, waiting for transfers between devices, exchange(): lax.ppermute(value, axis, [(src, src ^ k << shift) for src in range(size)])  28.3 us
    pallas_call x3, Pallas kernels, third(): pl.pallas_call(functools.partial(third_kernel, (begin, *dims)), in_specs=...  26.3 us
    ppermute x18, starting transfers between devices, exchange(): lax.ppermute(value, axis, [(src, src ^ k << shift) for src in range(size)])  24.7 us
    pallas_call x3, Pallas kernels, earlier(): pl.pallas_call(functools.partial(earlier_kernel, orders - 1), grid=(packs...  24.5 us
    pallas_call x3, Pallas kernels, second_synth(): pl.pallas_call(functools.partial(second_synth_kernel, dims), in_specs=[SM...  15.8 us
    pallas_call x4, Pallas kernels, first_synth(): pl.pallas_call(functools.partial(first_synth_kernel, (sizes, chosen, dest...  15.3 us
  transfers between devices with their start and end apart: 38, of which 17 were waited for; matrix products, arithmetic and copies ran while one was open for 1% of the time, Pallas kernels for 33%

profile of v11, /device:TPU:0, one launch (start us, length us, event | category | flops | bytes accessed | tf_op | source)
XLA Modules:
  0.0 244.9 jit_solution(919952412635655303)
XLA Ops:
  4.6 3.6 %first_synth.4 = (f32[512,128]{1,0:T(8,128)S(1)}, f32[512,128]{1,0:T(8,128)S(1)}, f32[512,128]{1,0:T(8,128)S(1)}, f32[512,128]{1,0:T(8,128)S(1)}) custom-call(s32[3]{0:T(128)S(1)} %pad_add_fusion.place_ref, f32[3,20,40,160]{3,2,1,0:T(8,128)S(1)} %copy-done.2, bf16[4,160,128]{2,1,0:T(8,128)(2,1)S(1)} %dynamic-slice_bitcast_fusion.2.table_ref.refs_12_), custom_call_target="tpu_custom_call" | custom-call | flops 1024 | bytes 1024 | tf_op jit(solution)/shard_map/first_synth/pallas_call | solution.py:168
  8.3 3.6 %first_synth.5 = (f32[512,128]{1,0:T(8,128)S(1)}, f32[512,128]{1,0:T(8,128)S(1)}, f32[512,128]{1,0:T(8,128)S(1)}, f32[512,128]{1,0:T(8,128)S(1)}) custom-call(s32[3]{0:T(128)S(1)} %pad_add_fusion.place_ref, f32[3,20,40,160]{3,2,1,0:T(8,128)S(1)} %collective-permute-done.data, ...), custom_call_target="tpu_custom_call", output_to_operand_aliasing={{0}: (3, {}), {1}: (4, {}), {2}: (5, {}), {3}: (6, {})} | custom-call | flops 1024 | bytes 1024 | tf_op jit(solution)/shard_map/first_synth/pallas_call | solution.py:168
  11.9 2.6 %collective-permute-start.1 = (f32[512,128]{1,0:T(8,128)S(1)}, f32[512,128]{1,0:T(8,128)S(1)}, u32[]{:S(2)}, u32[]{:S(2)}) collective-permute-start(f32[512,128]{1,0:T(8,128)S(1)} %get-tuple-element.147), channel_id=1, source_target_pairs={{0,8},{4,12},{8,0},{12,4},{16,24},{20,28},{24,16},{28,20},{1,9},{5... | collective-permute-start | bytes 786440 | tf_op jit(solution)/shard_map/ppermute | solution.py:657
  17.1 4.0 %first_synth.6 = (f32[1024,128]{1,0:T(8,128)S(1)}, f32[1024,128]{1,0:T(8,128)S(1)}, f32[1024,128]{1,0:T(8,128)S(1)}, f32[1024,128]{1,0:T(8,128)S(1)}, f32[512,12...) custom-call(s32[3]{0:T(128)S(1)} %pad_add_fusion.place_ref, ...), custom_call_target="tpu_custom_call" | custom-call | flops 1024 | bytes 1024 | tf_op jit(solution)/shard_map/first_synth/pallas_call | solution.py:168
  21.1 4.1 %first_synth.7 = (f32[1024,128]{1,0:T(8,128)S(1)}, f32[1024,128]{1,0:T(8,128)S(1)}, f32[1024,128]{1,0:T(8,128)S(1)}, f32[1024,128]{1,0:T(8,128)S(1)}, f32[512,12...) custom-call(s32[3]{0:T(128)S(1)} %pad_add_fusion.place_ref, ...), custom_call_target="tpu_custom_call", output_to_operand_aliasing={{0}: (3, {}), {1}: (4, {}), {2}: (5, {}), {3}: (6, {}), {4}... | custom-call | flops 1024 | bytes 1024 | tf_op jit(solution)/shard_map/first_synth/pallas_call | solution.py:168
  26.7 9.1 %collective-permute-done.2.refs_2_ = f32[512,128]{1,0:T(8,128)S(1)} collective-permute-done((f32[512,128]{1,0:T(8,128)S(1)}, f32[512,128]{1,0:T(8,128)S(1)}, u32[]{:S(2)}, u32[]{:S(2)}) %collective-permute-start.2) | collective-permute-done | bytes 262176 | tf_op jit(solution)/shard_map/ppermute | solution.py:657
  35.8 6.5 %collective-permute-start.11 = (f32[1024,128]{1,0:T(8,128)S(1)}, f32[1024,128]{1,0:T(8,128)S(1)}, u32[]{:S(2)}, u32[]{:S(2)}) collective-permute-start(f32[1024,128]{1,0:T(8,128)S(1)} %get-tuple-element.190), channel_id=1, source_target_pairs={{0,16},{4,20},{8,24},{12,28},{16,0},{20,4},{24,8},{28,12},{1,17},{... | collective-permute-start | bytes 1572872 | tf_op jit(solution)/shard_map/ppermute | solution.py:657
  42.3 3.7 %second_synth.3 = (f32[4,240,128]{2,1,0:T(8,128)S(1)}, f32[4,240,128]{2,1,0:T(8,128)S(1)}, f32[4,240,128]{2,1,0:T(8,128)S(1)}, f32[4,240,128]{2,1,0:T(8,128)S(1)}) custom-call(s32[3]{0:T(128)S(1)} %pad_add_fusion.place_ref, f32[512,128]{1,0:T(8,128)S(1)} %get-tuple-element.160.refs_0_, f32[512,128]{1,0:T(8,128)S(1)} %collective-permute-done.1.refs_1_, ...), custom_call_target="tpu_custom_call" | custom-call | flops 1024 | bytes 1024 | tf_op jit(solution)/shard_map/second_synth/pallas_call | solution.py:241
  49.6 16.1 %collective-permute-done.11.refs_2_ = f32[1024,128]{1,0:T(8,128)S(1)} collective-permute-done((f32[1024,128]{1,0:T(8,128)S(1)}, f32[1024,128]{1,0:T(8,128)S(1)}, u32[]{:S(2)}, u32[]{:S(2)}) %collective-permute-start.11) | collective-permute-done | bytes 524320 | tf_op jit(solution)/shard_map/ppermute | solution.py:657
  66.5 6.4 %earlier_orders.3.refs_6_ = f32[3,8,64,256]{3,2,1,0:T(8,128)S(1)} custom-call(f32[6,3,32,64,256]{4,3,2,1,0:T(8,128)} %refs_4_.8, f32[6,3,32,64,256]{4,3,2,1,0:T(8,128)} %refs_4_.8, f32[6,3,32,64,256]{4,3,2,1,0:T(8,128)} %refs_4_.8, f32[6,3,32,64,256]{4,3,2,1,0:T(8,128)} %refs_4_.8, f32[6,3,32,64,256]{4,3,2,1,0:T(8,128)} %refs_4_.8, ...), custom_call_target="tpu_custom_call" | custom-call | flops 1024 | bytes 1024 | tf_op jit(solution)/shard_map/earlier_orders/pallas_call | solution.py:293
  73.0 6.4 %third_dimension.3 = (f32[4,120,128]{2,1,0:T(8,128)S(1)}, f32[4,120,128]{2,1,0:T(8,128)S(1)}, f32[4,120,128]{2,1,0:T(8,128)S(1)}, f32[4,120,128]{2,1,0:T(8,128)S(1)}) custom-call(s32[3]{0:T(128)S(1)} %pad_add_fusion.place_ref, f32[4,240,128]{2,1,0:T(8,128)S(1)} %get-tuple-element.171.refs_0_, f32[4,240,128]{2,1,0:T(8,128)S(1)} %collective-permute-done.4.refs_1_, ...), custom_call_target="tpu_custom_call" | custom-call | flops 1024 | bytes 1024 | tf_op jit(solution)/shard_map/third_dimension/pallas_call | solution.py:361
  83.0 5.4 %collective-permute-done.7.refs_1_ = f32[4,120,128]{2,1,0:T(8,128)S(1)} collective-permute-done((f32[4,120,128]{2,1,0:T(8,128)S(1)}, f32[4,120,128]{2,1,0:T(8,128)S(1)}, u32[]{:S(2)}, u32[]{:S(2)}) %collective-permute-start.7) | collective-permute-done | bytes 245792 | tf_op jit(solution)/shard_map/ppermute | solution.py:615
  88.4 3.9 %collective-permute-done.8.refs_2_ = f32[4,120,128]{2,1,0:T(8,128)S(1)} collective-permute-done((f32[4,120,128]{2,1,0:T(8,128)S(1)}, f32[4,120,128]{2,1,0:T(8,128)S(1)}, u32[]{:S(2)}, u32[]{:S(2)}) %collective-permute-start.8) | collective-permute-done | bytes 245792 | tf_op jit(solution)/shard_map/ppermute | solution.py:615
  94.7 8.5 %second_synth.4 = (f32[8,240,128]{2,1,0:T(8,128)S(1)}, f32[8,240,128]{2,1,0:T(8,128)}, f32[8,240,128]{2,1,0:T(8,128)}, f32[8,240,128]{2,1,0:T(8,128)}) custom-call(s32[3]{0:T(128)S(1)} %pad_add_fusion.place_ref, f32[1024,128]{1,0:T(8,128)S(1)} %get-tuple-element.198.refs_0_, f32[1024,128]{1,0:T(8,128)S(1)} %collective-permute-done.10.refs_1_, ...), custom_call_target="tpu_custom_call" | custom-call | flops 1024 | bytes 1024 | tf_op jit(solution)/shard_map/second_synth/pallas_call | solution.py:241
  106.7 3.1 %collective-permute-start.14 = (f32[304,128]{1,0:T(8,128)S(1)}, f32[304,128]{1,0:T(8,128)S(1)}, u32[]{:S(2)}, u32[]{:S(2)}) collective-permute-start(f32[304,128]{1,0:T(8,128)S(1)} %get-tuple-element.195), channel_id=1, source_target_pairs={{0,16},{4,20},{8,24},{12,28},{16,0},{20,4},{24,8},{28,12},{1,17},{... | collective-permute-start | bytes 466952 | tf_op jit(solution)/shard_map/ppermute | solution.py:657
  109.8 2.6 %collective-permute-done.13.refs_1_ = f32[304,128]{1,0:T(8,128)S(1)} collective-permute-done((f32[304,128]{1,0:T(8,128)S(1)}, f32[304,128]{1,0:T(8,128)S(1)}, u32[]{:S(2)}, u32[]{:S(2)}) %collective-permute-start.13) | collective-permute-done | bytes 155680 | tf_op jit(solution)/shard_map/ppermute | solution.py:657
  112.5 4.0 %collective-permute-start.15 = (f32[304,128]{1,0:T(8,128)S(1)}, f32[304,128]{1,0:T(8,128)S(1)}, u32[]{:S(2)}, u32[]{:S(2)}) collective-permute-start(f32[304,128]{1,0:T(8,128)S(1)} %get-tuple-element.197), channel_id=1, source_target_pairs={{0,24},{4,28},{8,16},{12,20},{16,8},{20,12},{24,0},{28,4},{1,25},{... | collective-permute-start | bytes 466952 | tf_op jit(solution)/shard_map/ppermute | solution.py:657
  116.5 11.8 %earlier_orders.4.refs_6_ = f32[3,16,64,256]{3,2,1,0:T(8,128)S(1)} custom-call(f32[6,3,32,64,256]{4,3,2,1,0:T(8,128)} %refs_4_.8, f32[6,3,32,64,256]{4,3,2,1,0:T(8,128)} %refs_4_.8, f32[6,3,32,64,256]{4,3,2,1,0:T(8,128)} %refs_4_.8, f32[6,3,32,64,256]{4,3,2,1,0:T(8,128)} %refs_4_.8, f32[6,3,32,64,256]{4,3,2,1,0:T(8,128)} %refs_4_.8, ...), custom_call_target="tpu_custom_call" | custom-call | flops 1024 | bytes 1024 | tf_op jit(solution)/shard_map/earlier_orders/pallas_call | solution.py:293
  130.2 7.4 %collective-permute-done.19.refs_1_ = f32[512,128]{1,0:T(8,128)S(1)} collective-permute-done((f32[512,128]{1,0:T(8,128)S(1)}, f32[512,128]{1,0:T(8,128)S(1)}, u32[]{:S(2)}, u32[]{:S(2)}) %collective-permute-start.19) | collective-permute-done | bytes 262176 | tf_op jit(solution)/shard_map/ppermute | solution.py:657
  139.4 6.4 %earlier_orders.5.refs_6_ = f32[3,8,64,256]{3,2,1,0:T(8,128)S(1)} custom-call(f32[6,3,32,64,256]{4,3,2,1,0:T(8,128)} %refs_4_.8, f32[6,3,32,64,256]{4,3,2,1,0:T(8,128)} %refs_4_.8, f32[6,3,32,64,256]{4,3,2,1,0:T(8,128)} %refs_4_.8, f32[6,3,32,64,256]{4,3,2,1,0:T(8,128)} %refs_4_.8, f32[6,3,32,64,256]{4,3,2,1,0:T(8,128)} %refs_4_.8, ...), custom_call_target="tpu_custom_call" | custom-call | flops 1024 | bytes 1024 | tf_op jit(solution)/shard_map/earlier_orders/pallas_call | solution.py:293
  146.9 3.7 %second_synth.5 = (f32[4,240,128]{2,1,0:T(8,128)S(1)}, f32[4,240,128]{2,1,0:T(8,128)S(1)}, f32[4,240,128]{2,1,0:T(8,128)S(1)}, f32[4,240,128]{2,1,0:T(8,128)S(1)}) custom-call(s32[3]{0:T(128)S(1)} %copy-done.23, f32[512,128]{1,0:T(8,128)S(1)} %copy-done.9, f32[512,128]{1,0:T(8,128)S(1)} %collective-permute-done.19.refs_1_, ...), custom_call_target="tpu_custom_call" | custom-call | flops 1024 | bytes 1024 | tf_op jit(solution)/shard_map/second_synth/pallas_call | solution.py:241
  155.1 13.4 %third_dimension.4 = (f32[8,120,128]{2,1,0:T(8,128)S(1)}, f32[8,120,128]{2,1,0:T(8,128)S(1)}, f32[8,120,128]{2,1,0:T(8,128)S(1)}, f32[8,120,128]{2,1,0:T(8,128)S(1)}) custom-call(s32[3]{0:T(128)S(1)} %copy-done.23, f32[8,240,128]{2,1,0:T(8,128)S(1)} %get-tuple-element.224.refs_0_, f32[8,240,128]{2,1,0:T(8,128)} %collective-permute-done.16.refs_1_, ...), custom_call_target="tpu_custom_call" | custom-call | flops 1024 | bytes 1024 | tf_op jit(solution)/shard_map/third_dimension/pallas_call | solution.py:361
  172.1 2.8 %collective-permute-done.25.refs_1_ = f32[4,240,128]{2,1,0:T(8,128)S(1)} collective-permute-done((f32[4,240,128]{2,1,0:T(8,128)S(1)}, f32[4,240,128]{2,1,0:T(8,128)S(1)}, u32[]{:S(2)}, u32[]{:S(2)}) %collective-permute-start.25) | collective-permute-done | bytes 491552 | tf_op jit(solution)/shard_map/ppermute | solution.py:615
  174.9 6.4 %third_dimension.5 = (f32[4,120,128]{2,1,0:T(8,128)S(1)}, f32[4,120,128]{2,1,0:T(8,128)S(1)}, f32[4,120,128]{2,1,0:T(8,128)S(1)}, f32[4,120,128]{2,1,0:T(8,128)S(1)}) custom-call(s32[3]{0:T(128)S(1)} %copy-done.23, f32[4,240,128]{2,1,0:T(8,128)S(1)} %get-tuple-element.238.refs_0_, f32[4,240,128]{2,1,0:T(8,128)S(1)} %collective-permute-done.25.refs_1_, ...), custom_call_target="tpu_custom_call" | custom-call | flops 1024 | bytes 1024 | tf_op jit(solution)/shard_map/third_dimension/pallas_call | solution.py:361
  186.7 8.0 %collective-permute-done.24.refs_3_ = f32[8,120,128]{2,1,0:T(8,128)S(1)} collective-permute-done((f32[8,120,128]{2,1,0:T(8,128)S(1)}, f32[8,120,128]{2,1,0:T(8,128)S(1)}, u32[]{:S(2)}, u32[]{:S(2)}) %collective-permute-start.24) | collective-permute-done | bytes 491552 | tf_op jit(solution)/shard_map/ppermute | solution.py:615
  194.8 4.4 %second_back.4 = (f32[608,128]{1,0:T(8,128)S(1)}, f32[608,128]{1,0:T(8,128)S(1)}, f32[608,128]{1,0:T(8,128)S(1)}, f32[608,128]{1,0:T(8,128)S(1)}) custom-call(s32[3]{0:T(128)S(1)} %copy-done.23, f32[8,120,128]{2,1,0:T(8,128)S(1)} %get-tuple-element.243.refs_0_, f32[8,120,128]{2,1,0:T(8,128)S(1)} %collective-permute-done.22.refs_1_, ...), custom_call_target="tpu_custom_call" | custom-call | flops 1024 | bytes 1024 | tf_op jit(solution)/shard_map/second_back/pallas_call | solution.py:410
  205.6 2.6 %collective-permute-start.33 = (f32[4,120,128]{2,1,0:T(8,128)S(1)}, f32[4,120,128]{2,1,0:T(8,128)S(1)}, u32[]{:S(2)}, u32[]{:S(2)}) collective-permute-start(f32[4,120,128]{2,1,0:T(8,128)S(1)} %get-tuple-element.256), channel_id=1, source_target_pairs={{0,3},{1,2},{2,1},{3,0},{4,7},{5,6},{6,5},{7,4},{8,11},{9,10},{10,... | collective-permute-start | bytes 737288 | tf_op jit(solution)/shard_map/ppermute | solution.py:615
  208.3 4.7 %collective-permute-done.32.refs_2_ = f32[4,120,128]{2,1,0:T(8,128)S(1)} collective-permute-done((f32[4,120,128]{2,1,0:T(8,128)S(1)}, f32[4,120,128]{2,1,0:T(8,128)S(1)}, u32[]{:S(2)}, u32[]{:S(2)}) %collective-permute-start.32) | collective-permute-done | bytes 245792 | tf_op jit(solution)/shard_map/ppermute | solution.py:615
  213.0 2.6 %second_back.5 = (f32[304,128]{1,0:T(8,128)S(1)}, f32[304,128]{1,0:T(8,128)S(1)}, f32[304,128]{1,0:T(8,128)S(1)}, f32[304,128]{1,0:T(8,128)S(1)}) custom-call(s32[3]{0:T(128)S(1)} %copy-done.23, f32[4,120,128]{2,1,0:T(8,128)S(1)} %get-tuple-element.257.refs_0_, f32[4,120,128]{2,1,0:T(8,128)S(1)} %collective-permute-done.31.refs_1_, ...), custom_call_target="tpu_custom_call" | custom-call | flops 1024 | bytes 1024 | tf_op jit(solution)/shard_map/second_back/pallas_call | solution.py:410
  215.6 6.9 %collective-permute-done.29.refs_6_ = f32[608,128]{1,0:T(8,128)S(1)} collective-permute-done((f32[608,128]{1,0:T(8,128)S(1)}, f32[608,128]{1,0:T(8,128)S(1)}, u32[]{:S(2)}, u32[]{:S(2)}) %collective-permute-start.29) | collective-permute-done | bytes 311328 | tf_op jit(solution)/shard_map/ppermute | solution.py:657
  229.5 5.9 %collective-permute-done.35.refs_10_ = f32[304,128]{1,0:T(8,128)S(1)} collective-permute-done((f32[304,128]{1,0:T(8,128)S(1)}, f32[304,128]{1,0:T(8,128)S(1)}, u32[]{:S(2)}, u32[]{:S(2)}) %collective-permute-start.35) | collective-permute-done | bytes 155680 | tf_op jit(solution)/shard_map/ppermute | solution.py:657
  240.2 4.5 %last_projection.1 = f32[3,20,40,160]{3,2,1,0:T(8,128)} custom-call(f32[10]{0:T(128)S(1)} %convert_multiply_fusion.1.refs_0_, f32[8,256]{1,0:T(8,128)S(1)} %broadcast_in_dim.9.refs_1_, f32[40,256]{1,0:T(8,128)S(1)} %broadcast_in_dim.18.refs_2_, f32[160,2432]{1,0:T(8,128)S(1)} %first_back.3.refs_3_, f32[160,2432]{1,0:T(8,128)S(1)} %collective-permute-done.37.refs_4_), custom_call_target="tpu_custom_call" | custom-call | flops 1024 | bytes 1024 | tf_op jit(solution)/shard_map/last_projection/pallas_call | solution.py:523
  (119 shorter events, 59.0 us)
Async XLA Ops:
  11.9 14.8 %collective-permute-start.1 = (f32[512,128]{1,0:T(8,128)S(1)}, f32[512,128]{1,0:T(8,128)S(1)}, u32[]{:S(2)}, u32[]{:S(2)}) collective-permute-start(f32[512,128]{1,0:T(8,128)S(1)} %get-tuple-element.147), channel_id=1, source_target_pairs={{0,8},{4,12},{8,0},{12,4},{16,24},{20,28},{24,16},{28,20},{1,9},{5... | collective-permute-start | bytes 786440 | tf_op jit(solution)/shard_map/ppermute | solution.py:657
  14.5 21.3 %collective-permute-start.2 = (f32[512,128]{1,0:T(8,128)S(1)}, f32[512,128]{1,0:T(8,128)S(1)}, u32[]{:S(2)}, u32[]{:S(2)}) collective-permute-start(f32[512,128]{1,0:T(8,128)S(1)} %get-tuple-element.148), channel_id=1, source_target_pairs={{0,16},{4,20},{8,24},{12,28},{16,0},{20,4},{24,8},{28,12},{1,17},{... | collective-permute-start | bytes 786440 | tf_op jit(solution)/shard_map/ppermute | solution.py:657
  17.1 18.7 %collective-permute-start.3 = (f32[512,128]{1,0:T(8,128)S(1)}, f32[512,128]{1,0:T(8,128)S(1)}, u32[]{:S(2)}, u32[]{:S(2)}) collective-permute-start(f32[512,128]{1,0:T(8,128)S(1)} %get-tuple-element.149), channel_id=1, source_target_pairs={{0,24},{4,28},{8,16},{12,20},{16,8},{20,12},{24,0},{28,4},{1,25},{... | collective-permute-start | bytes 786440 | tf_op jit(solution)/shard_map/ppermute | solution.py:657
  35.8 29.8 %collective-permute-start.11 = (f32[1024,128]{1,0:T(8,128)S(1)}, f32[1024,128]{1,0:T(8,128)S(1)}, u32[]{:S(2)}, u32[]{:S(2)}) collective-permute-start(f32[1024,128]{1,0:T(8,128)S(1)} %get-tuple-element.190), channel_id=1, source_target_pairs={{0,16},{4,20},{8,24},{12,28},{16,0},{20,4},{24,8},{28,12},{1,17},{... | collective-permute-start | bytes 1572872 | tf_op jit(solution)/shard_map/ppermute | solution.py:657
  46.0 26.9 %collective-permute-start.4 = (f32[4,240,128]{2,1,0:T(8,128)S(1)}, f32[4,240,128]{2,1,0:T(8,128)S(1)}, u32[]{:S(2)}, u32[]{:S(2)}) collective-permute-start(f32[4,240,128]{2,1,0:T(8,128)S(1)} %get-tuple-element.166), channel_id=1, source_target_pairs={{0,1},{1,0},{2,3},{3,2},{4,5},{5,4},{6,7},{7,6},{8,9},{9,8},{10,11... | collective-permute-start | bytes 1474568 | tf_op jit(solution)/shard_map/ppermute | solution.py:615
  47.6 25.4 %collective-permute-start.5 = (f32[4,240,128]{2,1,0:T(8,128)S(1)}, f32[4,240,128]{2,1,0:T(8,128)S(1)}, u32[]{:S(2)}, u32[]{:S(2)}) collective-permute-start(f32[4,240,128]{2,1,0:T(8,128)S(1)} %get-tuple-element.167), channel_id=1, source_target_pairs={{0,2},{1,3},{2,0},{3,1},{4,6},{5,7},{6,4},{7,5},{8,10},{9,11},{10,... | collective-permute-start | bytes 1474568 | tf_op jit(solution)/shard_map/ppermute | solution.py:615
  49.1 23.8 %collective-permute-start.6 = (f32[4,240,128]{2,1,0:T(8,128)S(1)}, f32[4,240,128]{2,1,0:T(8,128)S(1)}, u32[]{:S(2)}, u32[]{:S(2)}) collective-permute-start(f32[4,240,128]{2,1,0:T(8,128)S(1)} %get-tuple-element.168), channel_id=1, source_target_pairs={{0,3},{1,2},{2,1},{3,0},{4,7},{5,6},{6,5},{7,4},{8,11},{9,10},{10,... | collective-permute-start | bytes 1474568 | tf_op jit(solution)/shard_map/ppermute | solution.py:615
  49.6 45.2 %collective-permute-start.10 = (f32[1024,128]{1,0:T(8,128)S(1)}, f32[1024,128]{1,0:T(8,128)S(1)}, u32[]{:S(2)}, u32[]{:S(2)}) collective-permute-start(f32[1024,128]{1,0:T(8,128)S(1)} %get-tuple-element.188), channel_id=1, source_target_pairs={{0,8},{4,12},{8,0},{12,4},{16,24},{20,28},{24,16},{28,20},{1,9},{5... | collective-permute-start | bytes 1572872 | tf_op jit(solution)/shard_map/ppermute | solution.py:657
  65.7 29.1 %collective-permute-start.12 = (f32[1024,128]{1,0:T(8,128)S(1)}, f32[1024,128]{1,0:T(8,128)S(1)}, u32[]{:S(2)}, u32[]{:S(2)}) collective-permute-start(f32[1024,128]{1,0:T(8,128)S(1)} %get-tuple-element.192), channel_id=1, source_target_pairs={{0,24},{4,28},{8,16},{12,20},{16,8},{20,12},{24,0},{28,4},{1,25},{... | collective-permute-start | bytes 1572872 | tf_op jit(solution)/shard_map/ppermute | solution.py:657
  79.4 9.0 %collective-permute-start.7 = (f32[4,120,128]{2,1,0:T(8,128)S(1)}, f32[4,120,128]{2,1,0:T(8,128)S(1)}, u32[]{:S(2)}, u32[]{:S(2)}) collective-permute-start(f32[4,120,128]{2,1,0:T(8,128)S(1)} %get-tuple-element.177), channel_id=1, source_target_pairs={{0,1},{1,0},{2,3},{3,2},{4,5},{5,4},{6,7},{7,6},{8,9},{9,8},{10,11... | collective-permute-start | bytes 737288 | tf_op jit(solution)/shard_map/ppermute | solution.py:615
  81.0 11.3 %collective-permute-start.8 = (f32[4,120,128]{2,1,0:T(8,128)S(1)}, f32[4,120,128]{2,1,0:T(8,128)S(1)}, u32[]{:S(2)}, u32[]{:S(2)}) collective-permute-start(f32[4,120,128]{2,1,0:T(8,128)S(1)} %get-tuple-element.178), channel_id=1, source_target_pairs={{0,2},{1,3},{2,0},{3,1},{4,6},{5,7},{6,4},{7,5},{8,10},{9,11},{10,... | collective-permute-start | bytes 737288 | tf_op jit(solution)/shard_map/ppermute | solution.py:615
  82.5 9.8 %collective-permute-start.9 = (f32[4,120,128]{2,1,0:T(8,128)S(1)}, f32[4,120,128]{2,1,0:T(8,128)S(1)}, u32[]{:S(2)}, u32[]{:S(2)}) collective-permute-start(f32[4,120,128]{2,1,0:T(8,128)S(1)} %get-tuple-element.179), channel_id=1, source_target_pairs={{0,3},{1,2},{2,1},{3,0},{4,7},{5,6},{6,5},{7,4},{8,11},{9,10},{10,... | collective-permute-start | bytes 737288 | tf_op jit(solution)/shard_map/ppermute | solution.py:615
  103.2 47.4 %collective-permute-start.18 = (f32[8,240,128]{2,1,0:T(8,128)}, f32[8,240,128]{2,1,0:T(8,128)}, u32[]{:S(2)}, u32[]{:S(2)}) collective-permute-start(f32[8,240,128]{2,1,0:T(8,128)} %get-tuple-element.208), channel_id=1, source_target_pairs={{0,3},{1,2},{2,1},{3,0},{4,7},{5,6},{6,5},{7,4},{8,11},{9,10},{10,... | collective-permute-start | bytes 2949128 | tf_op jit(solution)/shard_map/ppermute | solution.py:615
  104.7 45.9 %collective-permute-start.17 = (f32[8,240,128]{2,1,0:T(8,128)}, f32[8,240,128]{2,1,0:T(8,128)}, u32[]{:S(2)}, u32[]{:S(2)}) collective-permute-start(f32[8,240,128]{2,1,0:T(8,128)} %get-tuple-element.206), channel_id=1, source_target_pairs={{0,2},{1,3},{2,0},{3,1},{4,6},{5,7},{6,4},{7,5},{8,10},{9,11},{10,... | collective-permute-start | bytes 2949128 | tf_op jit(solution)/shard_map/ppermute | solution.py:615
  105.9 44.7 %collective-permute-start.16 = (f32[8,240,128]{2,1,0:T(8,128)}, f32[8,240,128]{2,1,0:T(8,128)}, u32[]{:S(2)}, u32[]{:S(2)}) collective-permute-start(f32[8,240,128]{2,1,0:T(8,128)} %get-tuple-element.204), channel_id=1, source_target_pairs={{0,1},{1,0},{2,3},{3,2},{4,5},{5,4},{6,7},{7,6},{8,9},{9,8},{10,11... | collective-permute-start | bytes 2949128 | tf_op jit(solution)/shard_map/ppermute | solution.py:615
  106.7 21.6 %collective-permute-start.14 = (f32[304,128]{1,0:T(8,128)S(1)}, f32[304,128]{1,0:T(8,128)S(1)}, u32[]{:S(2)}, u32[]{:S(2)}) collective-permute-start(f32[304,128]{1,0:T(8,128)S(1)} %get-tuple-element.195), channel_id=1, source_target_pairs={{0,16},{4,20},{8,24},{12,28},{16,0},{20,4},{24,8},{28,12},{1,17},{... | collective-permute-start | bytes 466952 | tf_op jit(solution)/shard_map/ppermute | solution.py:657
  112.5 16.5 %collective-permute-start.15 = (f32[304,128]{1,0:T(8,128)S(1)}, f32[304,128]{1,0:T(8,128)S(1)}, u32[]{:S(2)}, u32[]{:S(2)}) collective-permute-start(f32[304,128]{1,0:T(8,128)S(1)} %get-tuple-element.197), channel_id=1, source_target_pairs={{0,24},{4,28},{8,16},{12,20},{16,8},{20,12},{24,0},{28,4},{1,25},{... | collective-permute-start | bytes 466952 | tf_op jit(solution)/shard_map/ppermute | solution.py:657
  129.6 17.2 %collective-permute-start.20 = (f32[512,128]{1,0:T(8,128)S(1)}, f32[512,128]{1,0:T(8,128)S(1)}, u32[]{:S(2)}, u32[]{:S(2)}) collective-permute-start(f32[512,128]{1,0:T(8,128)S(1)} %copy-done.19), channel_id=1, source_target_pairs={{0,16},{4,20},{8,24},{12,28},{16,0},{20,4},{24,8},{28,12},{1,17},{... | collective-permute-start | bytes 786440 | tf_op jit(solution)/shard_map/ppermute | solution.py:657
  137.6 9.2 %collective-permute-start.21 = (f32[512,128]{1,0:T(8,128)S(1)}, f32[512,128]{1,0:T(8,128)S(1)}, u32[]{:S(2)}, u32[]{:S(2)}) collective-permute-start(f32[512,128]{1,0:T(8,128)S(1)} %copy-done.21), channel_id=1, source_target_pairs={{0,24},{4,28},{8,16},{12,20},{16,8},{20,12},{24,0},{28,4},{1,25},{... | collective-permute-start | bytes 786440 | tf_op jit(solution)/shard_map/ppermute | solution.py:657
  150.6 20.1 %collective-permute-start.27 = (f32[4,240,128]{2,1,0:T(8,128)S(1)}, f32[4,240,128]{2,1,0:T(8,128)S(1)}, u32[]{:S(2)}, u32[]{:S(2)}) collective-permute-start(f32[4,240,128]{2,1,0:T(8,128)S(1)} %get-tuple-element.237), channel_id=1, source_target_pairs={{0,3},{1,2},{2,1},{3,0},{4,7},{5,6},{6,5},{7,4},{8,11},{9,10},{10,... | collective-permute-start | bytes 1474568 | tf_op jit(solution)/shard_map/ppermute | solution.py:615
  152.1 20.0 %collective-permute-start.26 = (f32[4,240,128]{2,1,0:T(8,128)S(1)}, f32[4,240,128]{2,1,0:T(8,128)S(1)}, u32[]{:S(2)}, u32[]{:S(2)}) collective-permute-start(f32[4,240,128]{2,1,0:T(8,128)S(1)} %get-tuple-element.235), channel_id=1, source_target_pairs={{0,2},{1,3},{2,0},{3,1},{4,6},{5,7},{6,4},{7,5},{8,10},{9,11},{10,... | collective-permute-start | bytes 1474568 | tf_op jit(solution)/shard_map/ppermute | solution.py:615
  153.9 21.1 %collective-permute-start.25 = (f32[4,240,128]{2,1,0:T(8,128)S(1)}, f32[4,240,128]{2,1,0:T(8,128)S(1)}, u32[]{:S(2)}, u32[]{:S(2)}) collective-permute-start(f32[4,240,128]{2,1,0:T(8,128)S(1)} %get-tuple-element.233), channel_id=1, source_target_pairs={{0,1},{1,0},{2,3},{3,2},{4,5},{5,4},{6,7},{7,6},{8,9},{9,8},{10,11... | collective-permute-start | bytes 1474568 | tf_op jit(solution)/shard_map/ppermute | solution.py:615
  168.6 16.9 %collective-permute-start.22 = (f32[8,120,128]{2,1,0:T(8,128)S(1)}, f32[8,120,128]{2,1,0:T(8,128)S(1)}, u32[]{:S(2)}, u32[]{:S(2)}) collective-permute-start(f32[8,120,128]{2,1,0:T(8,128)S(1)} %get-tuple-element.229), channel_id=1, source_target_pairs={{0,1},{1,0},{2,3},{3,2},{4,5},{5,4},{6,7},{7,6},{8,9},{9,8},{10,11... | collective-permute-start | bytes 1474568 | tf_op jit(solution)/shard_map/ppermute | solution.py:615
  169.4 17.3 %collective-permute-start.23 = (f32[8,120,128]{2,1,0:T(8,128)S(1)}, f32[8,120,128]{2,1,0:T(8,128)S(1)}, u32[]{:S(2)}, u32[]{:S(2)}) collective-permute-start(f32[8,120,128]{2,1,0:T(8,128)S(1)} %get-tuple-element.230), channel_id=1, source_target_pairs={{0,2},{1,3},{2,0},{3,1},{4,6},{5,7},{6,4},{7,5},{8,10},{9,11},{10,... | collective-permute-start | bytes 1474568 | tf_op jit(solution)/shard_map/ppermute | solution.py:615
  170.7 24.0 %collective-permute-start.24 = (f32[8,120,128]{2,1,0:T(8,128)S(1)}, f32[8,120,128]{2,1,0:T(8,128)S(1)}, u32[]{:S(2)}, u32[]{:S(2)}) collective-permute-start(f32[8,120,128]{2,1,0:T(8,128)S(1)} %get-tuple-element.231), channel_id=1, source_target_pairs={{0,3},{1,2},{2,1},{3,0},{4,7},{5,6},{6,5},{7,4},{8,11},{9,10},{10,... | collective-permute-start | bytes 1474568 | tf_op jit(solution)/shard_map/ppermute | solution.py:615
  181.4 24.3 %collective-permute-start.31 = (f32[4,120,128]{2,1,0:T(8,128)S(1)}, f32[4,120,128]{2,1,0:T(8,128)S(1)}, u32[]{:S(2)}, u32[]{:S(2)}) collective-permute-start(f32[4,120,128]{2,1,0:T(8,128)S(1)} %get-tuple-element.254), channel_id=1, source_target_pairs={{0,1},{1,0},{2,3},{3,2},{4,5},{5,4},{6,7},{7,6},{8,9},{9,8},{10,11... | collective-permute-start | bytes 737288 | tf_op jit(solution)/shard_map/ppermute | solution.py:615
  199.2 16.5 %collective-permute-start.30 = (f32[608,128]{1,0:T(8,128)S(1)}, f32[608,128]{1,0:T(8,128)S(1)}, u32[]{:S(2)}, u32[]{:S(2)}) collective-permute-start(f32[608,128]{1,0:T(8,128)S(1)} %get-tuple-element.253), channel_id=1, source_target_pairs={{0,24},{4,28},{8,16},{12,20},{16,8},{20,12},{24,0},{28,4},{1,25},{... | collective-permute-start | bytes 933896 | tf_op jit(solution)/shard_map/ppermute | solution.py:657
  201.1 21.4 %collective-permute-start.29 = (f32[608,128]{1,0:T(8,128)S(1)}, f32[608,128]{1,0:T(8,128)S(1)}, u32[]{:S(2)}, u32[]{:S(2)}) collective-permute-start(f32[608,128]{1,0:T(8,128)S(1)} %get-tuple-element.251), channel_id=1, source_target_pairs={{0,16},{4,20},{8,24},{12,28},{16,0},{20,4},{24,8},{28,12},{1,17},{... | collective-permute-start | bytes 933896 | tf_op jit(solution)/shard_map/ppermute | solution.py:657
  203.7 18.9 %collective-permute-start.28 = (f32[608,128]{1,0:T(8,128)S(1)}, f32[608,128]{1,0:T(8,128)S(1)}, u32[]{:S(2)}, u32[]{:S(2)}) collective-permute-start(f32[608,128]{1,0:T(8,128)S(1)} %get-tuple-element.249), channel_id=1, source_target_pairs={{0,8},{4,12},{8,0},{12,4},{16,24},{20,28},{24,16},{28,20},{1,9},{5... | collective-permute-start | bytes 933896 | tf_op jit(solution)/shard_map/ppermute | solution.py:657
  204.1 8.8 %collective-permute-start.32 = (f32[4,120,128]{2,1,0:T(8,128)S(1)}, f32[4,120,128]{2,1,0:T(8,128)S(1)}, u32[]{:S(2)}, u32[]{:S(2)}) collective-permute-start(f32[4,120,128]{2,1,0:T(8,128)S(1)} %get-tuple-element.255), channel_id=1, source_target_pairs={{0,2},{1,3},{2,0},{3,1},{4,6},{5,7},{6,4},{7,5},{8,10},{9,11},{10,... | collective-permute-start | bytes 737288 | tf_op jit(solution)/shard_map/ppermute | solution.py:615
  222.5 12.9 %collective-permute-start.35 = (f32[304,128]{1,0:T(8,128)S(1)}, f32[304,128]{1,0:T(8,128)S(1)}, u32[]{:S(2)}, u32[]{:S(2)}) collective-permute-start(f32[304,128]{1,0:T(8,128)S(1)} %get-tuple-element.265), channel_id=1, source_target_pairs={{0,16},{4,20},{8,24},{12,28},{16,0},{20,4},{24,8},{28,12},{1,17},{... | collective-permute-start | bytes 466952 | tf_op jit(solution)/shard_map/ppermute | solution.py:657
  224.7 10.8 %collective-permute-start.36 = (f32[304,128]{1,0:T(8,128)S(1)}, f32[304,128]{1,0:T(8,128)S(1)}, u32[]{:S(2)}, u32[]{:S(2)}) collective-permute-start(f32[304,128]{1,0:T(8,128)S(1)} %get-tuple-element.267), channel_id=1, source_target_pairs={{0,24},{4,28},{8,16},{12,20},{16,8},{20,12},{24,0},{28,4},{1,25},{... | collective-permute-start | bytes 466952 | tf_op jit(solution)/shard_map/ppermute | solution.py:657
  (30 other events, 844.5 us)

commit v12 on v11

--- a/solution.py
+++ b/solution.py
@@ -648,18 +648,18 @@
     def run_earlier(chunk):
         return ordered(lambda values: earlier(*values, begins[chunk], sizes[chunk], pack), stored)
 
-    def z_exchange(values, *gates, waves=True, lead=1):
+    def z_exchange(values, *gates, waves=True):
         found = [values[0]]
         for k in range(1, groups):
             value = values[k]
             if gates:
-                value = after(value, found[lead]) if waves and 2 * k > groups else after(value, *gates)
+                value = after(value, found[1]) if waves and 2 * k > groups else after(value, *gates)
             found.append(lax.ppermute(value, "row", [(src, src ^ (2 * k)) for src in range(rows)]))
         return found
 
     first, second, middle, back, base = {}, {}, {}, {}, {}
     for step in range(min(2, chunks)):
-        first[step] = z_exchange(sent[step], *([first[step - 1]] if step else []), lead=groups // 2)
+        first[step] = z_exchange(sent[step], *([first[step - 1]] if step else []))
 
     def run_second(at):
         found = ordered(lambda values: second_synth(place, values, table_y, dims[at]), first[at])
@@ -678,7 +678,8 @@
 
     def run_back(at):
         found = ordered(lambda values: second_back(place, values, table_y, dims[at]), middle[at])
-        back[at] = z_exchange(found, back[at - 1] if at else first[min(1, chunks - 1)], waves=at == 0)
+        gates = [back[0] if at else first[min(1, chunks - 1)]] if at < 2 else []
+        back[at] = z_exchange(found, *gates, waves=at == 0)
 
     def run_base(at):
         base[at] = run_earlier(at)

time: 246 us -> 242 us (0.984)
  waiting for transfers between devices: 83.5 us -> 73.7 us
  starting transfers between devices: 56.6 us -> 61.1 us
    ppermute x18, waiting for transfers between devices: 53.2 us -> 44.7 us  [z_exchange(): lax.ppermute(value, 'row', [(src, src ^ 2 * k) for src in range(rows)])]
    ppermute x18, starting transfers between devices: 31.4 us -> 38.4 us  [z_exchange(): lax.ppermute(value, 'row', [(src, src ^ 2 * k) for src in range(rows)])]
    ppermute x18, starting transfers between devices: 24.7 us -> 22.2 us  [exchange(): lax.ppermute(value, axis, [(src, src ^ k << shift) for src in range(size)])]
  transfers between devices with their start and end apart: 38 -> 38, of which waited for: 17 -> 15; matrix products, arithmetic and copies ran while one was open for 1% -> 1% of each run, Pallas kernels for 33% -> 33%
where the time goes in v12:
time: 242 us
  Pallas kernels  98.6 us (41%)
  waiting for transfers between devices  73.7 us (30%)
  starting transfers between devices  61.1 us (25%)
  local copies, waits for them, and re-layouts  7.51 us (3%)
    ppermute x18, waiting for transfers between devices, z_exchange(): lax.ppermute(value, 'row', [(src, src ^ 2 * k) for src in range(rows)])  44.7 us
    ppermute x18, starting transfers between devices, z_exchange(): lax.ppermute(value, 'row', [(src, src ^ 2 * k) for src in range(rows)])  38.4 us
    ppermute x18, waiting for transfers between devices, exchange(): lax.ppermute(value, axis, [(src, src ^ k << shift) for src in range(size)])  26.9 us
    pallas_call x3, Pallas kernels, third(): pl.pallas_call(functools.partial(third_kernel, (begin, *dims)), in_specs=...  26.3 us
    pallas_call x3, Pallas kernels, earlier(): pl.pallas_call(functools.partial(earlier_kernel, orders - 1), grid=(packs...  24.6 us
    ppermute x18, starting transfers between devices, exchange(): lax.ppermute(value, axis, [(src, src ^ k << shift) for src in range(size)])  22.2 us
    pallas_call x3, Pallas kernels, second_synth(): pl.pallas_call(functools.partial(second_synth_kernel, dims), in_specs=[SM...  15.9 us
    pallas_call x4, Pallas kernels, first_synth(): pl.pallas_call(functools.partial(first_synth_kernel, (sizes, chosen, dest...  15.3 us
  transfers between devices with their start and end apart: 38, of which 15 were waited for; matrix products, arithmetic and copies ran while one was open for 1% of the time, Pallas kernels for 33%

profile of v12, /device:TPU:0, one launch (start us, length us, event | category | flops | bytes accessed | tf_op | source)
XLA Modules:
  0.0 241.6 jit_solution(10148944376176655219)
XLA Ops:
  4.6 3.6 %first_synth.4 = (f32[512,128]{1,0:T(8,128)S(1)}, f32[512,128]{1,0:T(8,128)S(1)}, f32[512,128]{1,0:T(8,128)S(1)}, f32[512,128]{1,0:T(8,128)S(1)}) custom-call(s32[3]{0:T(128)S(1)} %pad_add_fusion.place_ref, f32[3,20,40,160]{3,2,1,0:T(8,128)S(1)} %copy-done.2, bf16[4,160,128]{2,1,0:T(8,128)(2,1)S(1)} %dynamic-slice_bitcast_fusion.2.table_ref.refs_12_), custom_call_target="tpu_custom_call" | custom-call | flops 1024 | bytes 1024 | tf_op jit(solution)/shard_map/first_synth/pallas_call | solution.py:168
  8.3 3.6 %first_synth.5 = (f32[512,128]{1,0:T(8,128)S(1)}, f32[512,128]{1,0:T(8,128)S(1)}, f32[512,128]{1,0:T(8,128)S(1)}, f32[512,128]{1,0:T(8,128)S(1)}) custom-call(s32[3]{0:T(128)S(1)} %pad_add_fusion.place_ref, f32[3,20,40,160]{3,2,1,0:T(8,128)S(1)} %collective-permute-done.data, ...), custom_call_target="tpu_custom_call", output_to_operand_aliasing={{0}: (3, {}), {1}: (4, {}), {2}: (5, {}), {3}: (6, {})} | custom-call | flops 1024 | bytes 1024 | tf_op jit(solution)/shard_map/first_synth/pallas_call | solution.py:168
  11.9 2.6 %collective-permute-start.1 = (f32[512,128]{1,0:T(8,128)S(1)}, f32[512,128]{1,0:T(8,128)S(1)}, u32[]{:S(2)}, u32[]{:S(2)}) collective-permute-start(f32[512,128]{1,0:T(8,128)S(1)} %get-tuple-element.144), channel_id=1, source_target_pairs={{0,8},{4,12},{8,0},{12,4},{16,24},{20,28},{24,16},{28,20},{1,9},{5... | collective-permute-start | bytes 786440 | tf_op jit(solution)/shard_map/ppermute | solution.py:657
  14.5 2.6 %collective-permute-start.2 = (f32[512,128]{1,0:T(8,128)S(1)}, f32[512,128]{1,0:T(8,128)S(1)}, u32[]{:S(2)}, u32[]{:S(2)}) collective-permute-start(f32[512,128]{1,0:T(8,128)S(1)} %get-tuple-element.145), channel_id=1, source_target_pairs={{0,16},{4,20},{8,24},{12,28},{16,0},{20,4},{24,8},{28,12},{1,17},{... | collective-permute-start | bytes 786440 | tf_op jit(solution)/shard_map/ppermute | solution.py:657
  17.1 4.0 %first_synth.6 = (f32[1024,128]{1,0:T(8,128)S(1)}, f32[1024,128]{1,0:T(8,128)S(1)}, f32[1024,128]{1,0:T(8,128)S(1)}, f32[1024,128]{1,0:T(8,128)S(1)}, f32[512,12...) custom-call(s32[3]{0:T(128)S(1)} %pad_add_fusion.place_ref, ...), custom_call_target="tpu_custom_call" | custom-call | flops 1024 | bytes 1024 | tf_op jit(solution)/shard_map/first_synth/pallas_call | solution.py:168
  21.2 4.1 %first_synth.7 = (f32[1024,128]{1,0:T(8,128)S(1)}, f32[1024,128]{1,0:T(8,128)S(1)}, f32[1024,128]{1,0:T(8,128)S(1)}, f32[1024,128]{1,0:T(8,128)S(1)}, f32[512,12...) custom-call(s32[3]{0:T(128)S(1)} %pad_add_fusion.place_ref, ...), custom_call_target="tpu_custom_call", output_to_operand_aliasing={{0}: (3, {}), {1}: (4, {}), {2}: (5, {}), {3}: (6, {}), {4}... | custom-call | flops 1024 | bytes 1024 | tf_op jit(solution)/shard_map/first_synth/pallas_call | solution.py:168
  26.7 9.1 %collective-permute-done.2.refs_2_ = f32[512,128]{1,0:T(8,128)S(1)} collective-permute-done((f32[512,128]{1,0:T(8,128)S(1)}, f32[512,128]{1,0:T(8,128)S(1)}, u32[]{:S(2)}, u32[]{:S(2)}) %collective-permute-start.2) | collective-permute-done | bytes 262176 | tf_op jit(solution)/shard_map/ppermute | solution.py:657
  35.9 5.5 %collective-permute-start.10 = (f32[1024,128]{1,0:T(8,128)S(1)}, f32[1024,128]{1,0:T(8,128)S(1)}, u32[]{:S(2)}, u32[]{:S(2)}) collective-permute-start(f32[1024,128]{1,0:T(8,128)S(1)} %get-tuple-element.185), channel_id=1, source_target_pairs={{0,8},{4,12},{8,0},{12,4},{16,24},{20,28},{24,16},{28,20},{1,9},{5... | collective-permute-start | bytes 1572872 | tf_op jit(solution)/shard_map/ppermute | solution.py:657
  41.3 3.7 %second_synth.3 = (f32[4,240,128]{2,1,0:T(8,128)S(1)}, f32[4,240,128]{2,1,0:T(8,128)S(1)}, f32[4,240,128]{2,1,0:T(8,128)S(1)}, f32[4,240,128]{2,1,0:T(8,128)S(1)}) custom-call(s32[3]{0:T(128)S(1)} %pad_add_fusion.place_ref, f32[512,128]{1,0:T(8,128)S(1)} %get-tuple-element.157.refs_0_, f32[512,128]{1,0:T(8,128)S(1)} %collective-permute-done.1.refs_1_, ...), custom_call_target="tpu_custom_call" | custom-call | flops 1024 | bytes 1024 | tf_op jit(solution)/shard_map/second_synth/pallas_call | solution.py:241
  49.6 7.9 %collective-permute-done.10.refs_1_ = f32[1024,128]{1,0:T(8,128)S(1)} collective-permute-done((f32[1024,128]{1,0:T(8,128)S(1)}, f32[1024,128]{1,0:T(8,128)S(1)}, u32[]{:S(2)}, u32[]{:S(2)}) %collective-permute-start.10) | collective-permute-done | bytes 524320 | tf_op jit(solution)/shard_map/ppermute | solution.py:657
  58.9 6.4 %earlier_orders.3.refs_6_ = f32[3,8,64,256]{3,2,1,0:T(8,128)S(1)} custom-call(f32[6,3,32,64,256]{4,3,2,1,0:T(8,128)} %refs_4_.8, f32[6,3,32,64,256]{4,3,2,1,0:T(8,128)} %refs_4_.8, f32[6,3,32,64,256]{4,3,2,1,0:T(8,128)} %refs_4_.8, f32[6,3,32,64,256]{4,3,2,1,0:T(8,128)} %refs_4_.8, f32[6,3,32,64,256]{4,3,2,1,0:T(8,128)} %refs_4_.8, ...), custom_call_target="tpu_custom_call" | custom-call | flops 1024 | bytes 1024 | tf_op jit(solution)/shard_map/earlier_orders/pallas_call | solution.py:293
  65.3 3.8 %collective-permute-done.5.refs_2_ = f32[4,240,128]{2,1,0:T(8,128)S(1)} collective-permute-done((f32[4,240,128]{2,1,0:T(8,128)S(1)}, f32[4,240,128]{2,1,0:T(8,128)S(1)}, u32[]{:S(2)}, u32[]{:S(2)}) %collective-permute-start.5) | collective-permute-done | bytes 491552 | tf_op jit(solution)/shard_map/ppermute | solution.py:615
  69.1 6.4 %third_dimension.3 = (f32[4,120,128]{2,1,0:T(8,128)S(1)}, f32[4,120,128]{2,1,0:T(8,128)S(1)}, f32[4,120,128]{2,1,0:T(8,128)S(1)}, f32[4,120,128]{2,1,0:T(8,128)S(1)}) custom-call(s32[3]{0:T(128)S(1)} %pad_add_fusion.place_ref, f32[4,240,128]{2,1,0:T(8,128)S(1)} %get-tuple-element.168.refs_0_, f32[4,240,128]{2,1,0:T(8,128)S(1)} %collective-permute-done.4.refs_1_, ...), custom_call_target="tpu_custom_call" | custom-call | flops 1024 | bytes 1024 | tf_op jit(solution)/shard_map/third_dimension/pallas_call | solution.py:361
  79.1 5.0 %collective-permute-done.7.refs_1_ = f32[4,120,128]{2,1,0:T(8,128)S(1)} collective-permute-done((f32[4,120,128]{2,1,0:T(8,128)S(1)}, f32[4,120,128]{2,1,0:T(8,128)S(1)}, u32[]{:S(2)}, u32[]{:S(2)}) %collective-permute-start.7) | collective-permute-done | bytes 245792 | tf_op jit(solution)/shard_map/ppermute | solution.py:615
  84.1 3.8 %collective-permute-done.8.refs_2_ = f32[4,120,128]{2,1,0:T(8,128)S(1)} collective-permute-done((f32[4,120,128]{2,1,0:T(8,128)S(1)}, f32[4,120,128]{2,1,0:T(8,128)S(1)}, u32[]{:S(2)}, u32[]{:S(2)}) %collective-permute-start.8) | collective-permute-done | bytes 245792 | tf_op jit(solution)/shard_map/ppermute | solution.py:615
  90.3 8.5 %second_synth.4 = (f32[8,240,128]{2,1,0:T(8,128)S(1)}, f32[8,240,128]{2,1,0:T(8,128)}, f32[8,240,128]{2,1,0:T(8,128)}, f32[8,240,128]{2,1,0:T(8,128)}) custom-call(s32[3]{0:T(128)S(1)} %pad_add_fusion.place_ref, f32[1024,128]{1,0:T(8,128)S(1)} %get-tuple-element.195.refs_0_, f32[1024,128]{1,0:T(8,128)S(1)} %collective-permute-done.10.refs_1_, ...), custom_call_target="tpu_custom_call" | custom-call | flops 1024 | bytes 1024 | tf_op jit(solution)/shard_map/second_synth/pallas_call | solution.py:241
  102.3 5.6 %collective-permute-start.13 = (f32[304,128]{1,0:T(8,128)S(1)}, f32[304,128]{1,0:T(8,128)S(1)}, u32[]{:S(2)}, u32[]{:S(2)}) collective-permute-start(f32[304,128]{1,0:T(8,128)S(1)} %get-tuple-element.190), channel_id=1, source_target_pairs={{0,8},{4,12},{8,0},{12,4},{16,24},{20,28},{24,16},{28,20},{1,9},{5... | collective-permute-start | bytes 466952 | tf_op jit(solution)/shard_map/ppermute | solution.py:657
  111.1 4.8 %collective-permute-start.15 = (f32[304,128]{1,0:T(8,128)S(1)}, f32[304,128]{1,0:T(8,128)S(1)}, u32[]{:S(2)}, u32[]{:S(2)}) collective-permute-start(f32[304,128]{1,0:T(8,128)S(1)} %get-tuple-element.194), channel_id=1, source_target_pairs={{0,24},{4,28},{8,16},{12,20},{16,8},{20,12},{24,0},{28,4},{1,25},{... | collective-permute-start | bytes 466952 | tf_op jit(solution)/shard_map/ppermute | solution.py:657
  115.9 11.8 %earlier_orders.4.refs_6_ = f32[3,16,64,256]{3,2,1,0:T(8,128)S(1)} custom-call(f32[6,3,32,64,256]{4,3,2,1,0:T(8,128)} %refs_4_.8, f32[6,3,32,64,256]{4,3,2,1,0:T(8,128)} %refs_4_.8, f32[6,3,32,64,256]{4,3,2,1,0:T(8,128)} %refs_4_.8, f32[6,3,32,64,256]{4,3,2,1,0:T(8,128)} %refs_4_.8, f32[6,3,32,64,256]{4,3,2,1,0:T(8,128)} %refs_4_.8, ...), custom_call_target="tpu_custom_call" | custom-call | flops 1024 | bytes 1024 | tf_op jit(solution)/shard_map/earlier_orders/pallas_call | solution.py:293
  129.7 8.0 %collective-permute-done.19.refs_1_ = f32[512,128]{1,0:T(8,128)S(1)} collective-permute-done((f32[512,128]{1,0:T(8,128)S(1)}, f32[512,128]{1,0:T(8,128)S(1)}, u32[]{:S(2)}, u32[]{:S(2)}) %collective-permute-start.19) | collective-permute-done | bytes 262176 | tf_op jit(solution)/shard_map/ppermute | solution.py:657
  137.7 6.4 %earlier_orders.5.refs_6_ = f32[3,8,64,256]{3,2,1,0:T(8,128)S(1)} custom-call(f32[6,3,32,64,256]{4,3,2,1,0:T(8,128)} %refs_4_.8, f32[6,3,32,64,256]{4,3,2,1,0:T(8,128)} %refs_4_.8, f32[6,3,32,64,256]{4,3,2,1,0:T(8,128)} %refs_4_.8, f32[6,3,32,64,256]{4,3,2,1,0:T(8,128)} %refs_4_.8, f32[6,3,32,64,256]{4,3,2,1,0:T(8,128)} %refs_4_.8, ...), custom_call_target="tpu_custom_call" | custom-call | flops 1024 | bytes 1024 | tf_op jit(solution)/shard_map/earlier_orders/pallas_call | solution.py:293
  146.4 3.7 %second_synth.5 = (f32[4,240,128]{2,1,0:T(8,128)S(1)}, f32[4,240,128]{2,1,0:T(8,128)S(1)}, f32[4,240,128]{2,1,0:T(8,128)S(1)}, f32[4,240,128]{2,1,0:T(8,128)S(1)}) custom-call(s32[3]{0:T(128)S(1)} %pad_add_fusion.place_ref, f32[512,128]{1,0:T(8,128)S(1)} %copy-done.9, f32[512,128]{1,0:T(8,128)S(1)} %collective-permute-done.19.refs_1_, ...), custom_call_target="tpu_custom_call" | custom-call | flops 1024 | bytes 1024 | tf_op jit(solution)/shard_map/second_synth/pallas_call | solution.py:241
  154.4 13.4 %third_dimension.4 = (f32[8,120,128]{2,1,0:T(8,128)S(1)}, f32[8,120,128]{2,1,0:T(8,128)S(1)}, f32[8,120,128]{2,1,0:T(8,128)S(1)}, f32[8,120,128]{2,1,0:T(8,128)S(1)}) custom-call(s32[3]{0:T(128)S(1)} %copy-done.23, f32[8,240,128]{2,1,0:T(8,128)S(1)} %get-tuple-element.221.refs_0_, f32[8,240,128]{2,1,0:T(8,128)} %collective-permute-done.16.refs_1_, ...), custom_call_target="tpu_custom_call" | custom-call | flops 1024 | bytes 1024 | tf_op jit(solution)/shard_map/third_dimension/pallas_call | solution.py:361
  173.3 6.4 %third_dimension.5 = (f32[4,120,128]{2,1,0:T(8,128)S(1)}, f32[4,120,128]{2,1,0:T(8,128)S(1)}, f32[4,120,128]{2,1,0:T(8,128)S(1)}, f32[4,120,128]{2,1,0:T(8,128)S(1)}) custom-call(s32[3]{0:T(128)S(1)} %copy-done.23, f32[4,240,128]{2,1,0:T(8,128)S(1)} %get-tuple-element.235.refs_0_, f32[4,240,128]{2,1,0:T(8,128)S(1)} %collective-permute-done.25.refs_1_, ...), custom_call_target="tpu_custom_call" | custom-call | flops 1024 | bytes 1024 | tf_op jit(solution)/shard_map/third_dimension/pallas_call | solution.py:361
  183.8 8.0 %collective-permute-done.24.refs_3_ = f32[8,120,128]{2,1,0:T(8,128)S(1)} collective-permute-done((f32[8,120,128]{2,1,0:T(8,128)S(1)}, f32[8,120,128]{2,1,0:T(8,128)S(1)}, u32[]{:S(2)}, u32[]{:S(2)}) %collective-permute-start.24) | collective-permute-done | bytes 491552 | tf_op jit(solution)/shard_map/ppermute | solution.py:615
  191.8 4.4 %second_back.4 = (f32[608,128]{1,0:T(8,128)S(1)}, f32[608,128]{1,0:T(8,128)S(1)}, f32[608,128]{1,0:T(8,128)S(1)}, f32[608,128]{1,0:T(8,128)S(1)}) custom-call(s32[3]{0:T(128)S(1)} %copy-done.23, f32[8,120,128]{2,1,0:T(8,128)S(1)} %get-tuple-element.240.refs_0_, f32[8,120,128]{2,1,0:T(8,128)S(1)} %collective-permute-done.22.refs_1_, ...), custom_call_target="tpu_custom_call" | custom-call | flops 1024 | bytes 1024 | tf_op jit(solution)/shard_map/second_back/pallas_call | solution.py:410
  196.2 2.8 %collective-permute-start.30 = (f32[608,128]{1,0:T(8,128)S(1)}, f32[608,128]{1,0:T(8,128)S(1)}, u32[]{:S(2)}, u32[]{:S(2)}) collective-permute-start(f32[608,128]{1,0:T(8,128)S(1)} %get-tuple-element.250), channel_id=1, source_target_pairs={{0,24},{4,28},{8,16},{12,20},{16,8},{20,12},{24,0},{28,4},{1,25},{... | collective-permute-start | bytes 933896 | tf_op jit(solution)/shard_map/ppermute | solution.py:657
  201.9 3.5 %collective-permute-start.29 = (f32[608,128]{1,0:T(8,128)S(1)}, f32[608,128]{1,0:T(8,128)S(1)}, u32[]{:S(2)}, u32[]{:S(2)}) collective-permute-start(f32[608,128]{1,0:T(8,128)S(1)} %get-tuple-element.248), channel_id=1, source_target_pairs={{0,16},{4,20},{8,24},{12,28},{16,0},{20,4},{24,8},{28,12},{1,17},{... | collective-permute-start | bytes 933896 | tf_op jit(solution)/shard_map/ppermute | solution.py:657
  207.8 2.6 %second_back.5 = (f32[304,128]{1,0:T(8,128)S(1)}, f32[304,128]{1,0:T(8,128)S(1)}, f32[304,128]{1,0:T(8,128)S(1)}, f32[304,128]{1,0:T(8,128)S(1)}) custom-call(s32[3]{0:T(128)S(1)} %copy-done.23, f32[4,120,128]{2,1,0:T(8,128)S(1)} %get-tuple-element.254.refs_0_, f32[4,120,128]{2,1,0:T(8,128)S(1)} %collective-permute-done.31.refs_1_, ...), custom_call_target="tpu_custom_call" | custom-call | flops 1024 | bytes 1024 | tf_op jit(solution)/shard_map/second_back/pallas_call | solution.py:410
  210.4 4.1 %collective-permute-start.34 = (f32[304,128]{1,0:T(8,128)S(1)}, f32[304,128]{1,0:T(8,128)S(1)}, u32[]{:S(2)}, u32[]{:S(2)}) collective-permute-start(f32[304,128]{1,0:T(8,128)S(1)} %get-tuple-element.259), channel_id=1, source_target_pairs={{0,8},{4,12},{8,0},{12,4},{16,24},{20,28},{24,16},{28,20},{1,9},{5... | collective-permute-start | bytes 466952 | tf_op jit(solution)/shard_map/ppermute | solution.py:657
  216.9 13.5 %collective-permute-done.29.refs_6_ = f32[608,128]{1,0:T(8,128)S(1)} collective-permute-done((f32[608,128]{1,0:T(8,128)S(1)}, f32[608,128]{1,0:T(8,128)S(1)}, u32[]{:S(2)}, u32[]{:S(2)}) %collective-permute-start.29) | collective-permute-done | bytes 311328 | tf_op jit(solution)/shard_map/ppermute | solution.py:657
  236.9 4.5 %last_projection.1 = f32[3,20,40,160]{3,2,1,0:T(8,128)} custom-call(f32[10]{0:T(128)S(1)} %convert_multiply_fusion.1.refs_0_, f32[8,256]{1,0:T(8,128)S(1)} %broadcast_in_dim.9.refs_1_, f32[40,256]{1,0:T(8,128)S(1)} %broadcast_in_dim.18.refs_2_, f32[160,2432]{1,0:T(8,128)S(1)} %first_back.3.refs_3_, f32[160,2432]{1,0:T(8,128)S(1)} %collective-permute-done.37.refs_4_), custom_call_target="tpu_custom_call" | custom-call | flops 1024 | bytes 1024 | tf_op jit(solution)/shard_map/last_projection/pallas_call | solution.py:523
  (119 shorter events, 56.9 us)
Async XLA Ops:
  11.9 14.8 %collective-permute-start.1 = (f32[512,128]{1,0:T(8,128)S(1)}, f32[512,128]{1,0:T(8,128)S(1)}, u32[]{:S(2)}, u32[]{:S(2)}) collective-permute-start(f32[512,128]{1,0:T(8,128)S(1)} %get-tuple-element.144), channel_id=1, source_target_pairs={{0,8},{4,12},{8,0},{12,4},{16,24},{20,28},{24,16},{28,20},{1,9},{5... | collective-permute-start | bytes 786440 | tf_op jit(solution)/shard_map/ppermute | solution.py:657
  14.5 21.3 %collective-permute-start.2 = (f32[512,128]{1,0:T(8,128)S(1)}, f32[512,128]{1,0:T(8,128)S(1)}, u32[]{:S(2)}, u32[]{:S(2)}) collective-permute-start(f32[512,128]{1,0:T(8,128)S(1)} %get-tuple-element.145), channel_id=1, source_target_pairs={{0,16},{4,20},{8,24},{12,28},{16,0},{20,4},{24,8},{28,12},{1,17},{... | collective-permute-start | bytes 786440 | tf_op jit(solution)/shard_map/ppermute | solution.py:657
  17.1 18.7 %collective-permute-start.3 = (f32[512,128]{1,0:T(8,128)S(1)}, f32[512,128]{1,0:T(8,128)S(1)}, u32[]{:S(2)}, u32[]{:S(2)}) collective-permute-start(f32[512,128]{1,0:T(8,128)S(1)} %get-tuple-element.146), channel_id=1, source_target_pairs={{0,24},{4,28},{8,16},{12,20},{16,8},{20,12},{24,0},{28,4},{1,25},{... | collective-permute-start | bytes 786440 | tf_op jit(solution)/shard_map/ppermute | solution.py:657
  35.9 21.7 %collective-permute-start.10 = (f32[1024,128]{1,0:T(8,128)S(1)}, f32[1024,128]{1,0:T(8,128)S(1)}, u32[]{:S(2)}, u32[]{:S(2)}) collective-permute-start(f32[1024,128]{1,0:T(8,128)S(1)} %get-tuple-element.185), channel_id=1, source_target_pairs={{0,8},{4,12},{8,0},{12,4},{16,24},{20,28},{24,16},{28,20},{1,9},{5... | collective-permute-start | bytes 1572872 | tf_op jit(solution)/shard_map/ppermute | solution.py:657
  45.0 20.2 %collective-permute-start.4 = (f32[4,240,128]{2,1,0:T(8,128)S(1)}, f32[4,240,128]{2,1,0:T(8,128)S(1)}, u32[]{:S(2)}, u32[]{:S(2)}) collective-permute-start(f32[4,240,128]{2,1,0:T(8,128)S(1)} %get-tuple-element.163), channel_id=1, source_target_pairs={{0,1},{1,0},{2,3},{3,2},{4,5},{5,4},{6,7},{7,6},{8,9},{9,8},{10,11... | collective-permute-start | bytes 1474568 | tf_op jit(solution)/shard_map/ppermute | solution.py:615
  46.6 22.5 %collective-permute-start.5 = (f32[4,240,128]{2,1,0:T(8,128)S(1)}, f32[4,240,128]{2,1,0:T(8,128)S(1)}, u32[]{:S(2)}, u32[]{:S(2)}) collective-permute-start(f32[4,240,128]{2,1,0:T(8,128)S(1)} %get-tuple-element.164), channel_id=1, source_target_pairs={{0,2},{1,3},{2,0},{3,1},{4,6},{5,7},{6,4},{7,5},{8,10},{9,11},{10,... | collective-permute-start | bytes 1474568 | tf_op jit(solution)/shard_map/ppermute | solution.py:615
  48.1 21.0 %collective-permute-start.6 = (f32[4,240,128]{2,1,0:T(8,128)S(1)}, f32[4,240,128]{2,1,0:T(8,128)S(1)}, u32[]{:S(2)}, u32[]{:S(2)}) collective-permute-start(f32[4,240,128]{2,1,0:T(8,128)S(1)} %get-tuple-element.165), channel_id=1, source_target_pairs={{0,3},{1,2},{2,1},{3,0},{4,7},{5,6},{6,5},{7,4},{8,11},{9,10},{10,... | collective-permute-start | bytes 1474568 | tf_op jit(solution)/shard_map/ppermute | solution.py:615
  48.6 41.7 %collective-permute-start.11 = (f32[1024,128]{1,0:T(8,128)S(1)}, f32[1024,128]{1,0:T(8,128)S(1)}, u32[]{:S(2)}, u32[]{:S(2)}) collective-permute-start(f32[1024,128]{1,0:T(8,128)S(1)} %get-tuple-element.187), channel_id=1, source_target_pairs={{0,16},{4,20},{8,24},{12,28},{16,0},{20,4},{24,8},{28,12},{1,17},{... | collective-permute-start | bytes 1572872 | tf_op jit(solution)/shard_map/ppermute | solution.py:657
  57.5 32.8 %collective-permute-start.12 = (f32[1024,128]{1,0:T(8,128)S(1)}, f32[1024,128]{1,0:T(8,128)S(1)}, u32[]{:S(2)}, u32[]{:S(2)}) collective-permute-start(f32[1024,128]{1,0:T(8,128)S(1)} %get-tuple-element.189), channel_id=1, source_target_pairs={{0,24},{4,28},{8,16},{12,20},{16,8},{20,12},{24,0},{28,4},{1,25},{... | collective-permute-start | bytes 1572872 | tf_op jit(solution)/shard_map/ppermute | solution.py:657
  76.9 11.0 %collective-permute-start.8 = (f32[4,120,128]{2,1,0:T(8,128)S(1)}, f32[4,120,128]{2,1,0:T(8,128)S(1)}, u32[]{:S(2)}, u32[]{:S(2)}) collective-permute-start(f32[4,120,128]{2,1,0:T(8,128)S(1)} %get-tuple-element.175), channel_id=1, source_target_pairs={{0,2},{1,3},{2,0},{3,1},{4,6},{5,7},{6,4},{7,5},{8,10},{9,11},{10,... | collective-permute-start | bytes 737288 | tf_op jit(solution)/shard_map/ppermute | solution.py:615
  77.7 10.2 %collective-permute-start.9 = (f32[4,120,128]{2,1,0:T(8,128)S(1)}, f32[4,120,128]{2,1,0:T(8,128)S(1)}, u32[]{:S(2)}, u32[]{:S(2)}) collective-permute-start(f32[4,120,128]{2,1,0:T(8,128)S(1)} %get-tuple-element.176), channel_id=1, source_target_pairs={{0,3},{1,2},{2,1},{3,0},{4,7},{5,6},{6,5},{7,4},{8,11},{9,10},{10,... | collective-permute-start | bytes 737288 | tf_op jit(solution)/shard_map/ppermute | solution.py:615
  98.8 51.3 %collective-permute-start.18 = (f32[8,240,128]{2,1,0:T(8,128)}, f32[8,240,128]{2,1,0:T(8,128)}, u32[]{:S(2)}, u32[]{:S(2)}) collective-permute-start(f32[8,240,128]{2,1,0:T(8,128)} %get-tuple-element.205), channel_id=1, source_target_pairs={{0,3},{1,2},{2,1},{3,0},{4,7},{5,6},{6,5},{7,4},{8,11},{9,10},{10,... | collective-permute-start | bytes 2949128 | tf_op jit(solution)/shard_map/ppermute | solution.py:615
  100.4 49.7 %collective-permute-start.17 = (f32[8,240,128]{2,1,0:T(8,128)}, f32[8,240,128]{2,1,0:T(8,128)}, u32[]{:S(2)}, u32[]{:S(2)}) collective-permute-start(f32[8,240,128]{2,1,0:T(8,128)} %get-tuple-element.203), channel_id=1, source_target_pairs={{0,2},{1,3},{2,0},{3,1},{4,6},{5,7},{6,4},{7,5},{8,10},{9,11},{10,... | collective-permute-start | bytes 2949128 | tf_op jit(solution)/shard_map/ppermute | solution.py:615
  100.9 49.3 %collective-permute-start.16 = (f32[8,240,128]{2,1,0:T(8,128)}, f32[8,240,128]{2,1,0:T(8,128)}, u32[]{:S(2)}, u32[]{:S(2)}) collective-permute-start(f32[8,240,128]{2,1,0:T(8,128)} %get-tuple-element.201), channel_id=1, source_target_pairs={{0,1},{1,0},{2,3},{3,2},{4,5},{5,4},{6,7},{7,6},{8,9},{9,8},{10,11... | collective-permute-start | bytes 2949128 | tf_op jit(solution)/shard_map/ppermute | solution.py:615
  102.3 8.8 %collective-permute-start.13 = (f32[304,128]{1,0:T(8,128)S(1)}, f32[304,128]{1,0:T(8,128)S(1)}, u32[]{:S(2)}, u32[]{:S(2)}) collective-permute-start(f32[304,128]{1,0:T(8,128)S(1)} %get-tuple-element.190), channel_id=1, source_target_pairs={{0,8},{4,12},{8,0},{12,4},{16,24},{20,28},{24,16},{28,20},{1,9},{5... | collective-permute-start | bytes 466952 | tf_op jit(solution)/shard_map/ppermute | solution.py:657
  107.9 19.9 %collective-permute-start.14 = (f32[304,128]{1,0:T(8,128)S(1)}, f32[304,128]{1,0:T(8,128)S(1)}, u32[]{:S(2)}, u32[]{:S(2)}) collective-permute-start(f32[304,128]{1,0:T(8,128)S(1)} %get-tuple-element.192), channel_id=1, source_target_pairs={{0,16},{4,20},{8,24},{12,28},{16,0},{20,4},{24,8},{28,12},{1,17},{... | collective-permute-start | bytes 466952 | tf_op jit(solution)/shard_map/ppermute | solution.py:657
  111.1 17.3 %collective-permute-start.15 = (f32[304,128]{1,0:T(8,128)S(1)}, f32[304,128]{1,0:T(8,128)S(1)}, u32[]{:S(2)}, u32[]{:S(2)}) collective-permute-start(f32[304,128]{1,0:T(8,128)S(1)} %get-tuple-element.194), channel_id=1, source_target_pairs={{0,24},{4,28},{8,16},{12,20},{16,8},{20,12},{24,0},{28,4},{1,25},{... | collective-permute-start | bytes 466952 | tf_op jit(solution)/shard_map/ppermute | solution.py:657
  129.2 17.2 %collective-permute-start.20 = (f32[512,128]{1,0:T(8,128)S(1)}, f32[512,128]{1,0:T(8,128)S(1)}, u32[]{:S(2)}, u32[]{:S(2)}) collective-permute-start(f32[512,128]{1,0:T(8,128)S(1)} %copy-done.19), channel_id=1, source_target_pairs={{0,16},{4,20},{8,24},{12,28},{16,0},{20,4},{24,8},{28,12},{1,17},{... | collective-permute-start | bytes 786440 | tf_op jit(solution)/shard_map/ppermute | solution.py:657
  150.1 20.7 %collective-permute-start.27 = (f32[4,240,128]{2,1,0:T(8,128)S(1)}, f32[4,240,128]{2,1,0:T(8,128)S(1)}, u32[]{:S(2)}, u32[]{:S(2)}) collective-permute-start(f32[4,240,128]{2,1,0:T(8,128)S(1)} %get-tuple-element.234), channel_id=1, source_target_pairs={{0,3},{1,2},{2,1},{3,0},{4,7},{5,6},{6,5},{7,4},{8,11},{9,10},{10,... | collective-permute-start | bytes 1474568 | tf_op jit(solution)/shard_map/ppermute | solution.py:615
  152.6 18.8 %collective-permute-start.26 = (f32[4,240,128]{2,1,0:T(8,128)S(1)}, f32[4,240,128]{2,1,0:T(8,128)S(1)}, u32[]{:S(2)}, u32[]{:S(2)}) collective-permute-start(f32[4,240,128]{2,1,0:T(8,128)S(1)} %get-tuple-element.232), channel_id=1, source_target_pairs={{0,2},{1,3},{2,0},{3,1},{4,6},{5,7},{6,4},{7,5},{8,10},{9,11},{10,... | collective-permute-start | bytes 1474568 | tf_op jit(solution)/shard_map/ppermute | solution.py:615
  153.1 20.1 %collective-permute-start.25 = (f32[4,240,128]{2,1,0:T(8,128)S(1)}, f32[4,240,128]{2,1,0:T(8,128)S(1)}, u32[]{:S(2)}, u32[]{:S(2)}) collective-permute-start(f32[4,240,128]{2,1,0:T(8,128)S(1)} %get-tuple-element.230), channel_id=1, source_target_pairs={{0,1},{1,0},{2,3},{3,2},{4,5},{5,4},{6,7},{7,6},{8,9},{9,8},{10,11... | collective-permute-start | bytes 1474568 | tf_op jit(solution)/shard_map/ppermute | solution.py:615
  167.8 16.0 %collective-permute-start.22 = (f32[8,120,128]{2,1,0:T(8,128)S(1)}, f32[8,120,128]{2,1,0:T(8,128)S(1)}, u32[]{:S(2)}, u32[]{:S(2)}) collective-permute-start(f32[8,120,128]{2,1,0:T(8,128)S(1)} %get-tuple-element.226), channel_id=1, source_target_pairs={{0,1},{1,0},{2,3},{3,2},{4,5},{5,4},{6,7},{7,6},{8,9},{9,8},{10,11... | collective-permute-start | bytes 1474568 | tf_op jit(solution)/shard_map/ppermute | solution.py:615
  169.3 14.4 %collective-permute-start.23 = (f32[8,120,128]{2,1,0:T(8,128)S(1)}, f32[8,120,128]{2,1,0:T(8,128)S(1)}, u32[]{:S(2)}, u32[]{:S(2)}) collective-permute-start(f32[8,120,128]{2,1,0:T(8,128)S(1)} %get-tuple-element.227), channel_id=1, source_target_pairs={{0,2},{1,3},{2,0},{3,1},{4,6},{5,7},{6,4},{7,5},{8,10},{9,11},{10,... | collective-permute-start | bytes 1474568 | tf_op jit(solution)/shard_map/ppermute | solution.py:615
  170.9 20.9 %collective-permute-start.24 = (f32[8,120,128]{2,1,0:T(8,128)S(1)}, f32[8,120,128]{2,1,0:T(8,128)S(1)}, u32[]{:S(2)}, u32[]{:S(2)}) collective-permute-start(f32[8,120,128]{2,1,0:T(8,128)S(1)} %get-tuple-element.228), channel_id=1, source_target_pairs={{0,3},{1,2},{2,1},{3,0},{4,7},{5,6},{6,5},{7,4},{8,11},{9,10},{10,... | collective-permute-start | bytes 1474568 | tf_op jit(solution)/shard_map/ppermute | solution.py:615
  179.7 25.7 %collective-permute-start.31 = (f32[4,120,128]{2,1,0:T(8,128)S(1)}, f32[4,120,128]{2,1,0:T(8,128)S(1)}, u32[]{:S(2)}, u32[]{:S(2)}) collective-permute-start(f32[4,120,128]{2,1,0:T(8,128)S(1)} %get-tuple-element.251), channel_id=1, source_target_pairs={{0,1},{1,0},{2,3},{3,2},{4,5},{5,4},{6,7},{7,6},{8,9},{9,8},{10,11... | collective-permute-start | bytes 737288 | tf_op jit(solution)/shard_map/ppermute | solution.py:615
  196.2 18.3 %collective-permute-start.30 = (f32[608,128]{1,0:T(8,128)S(1)}, f32[608,128]{1,0:T(8,128)S(1)}, u32[]{:S(2)}, u32[]{:S(2)}) collective-permute-start(f32[608,128]{1,0:T(8,128)S(1)} %get-tuple-element.250), channel_id=1, source_target_pairs={{0,24},{4,28},{8,16},{12,20},{16,8},{20,12},{24,0},{28,4},{1,25},{... | collective-permute-start | bytes 933896 | tf_op jit(solution)/shard_map/ppermute | solution.py:657
  198.9 8.8 %collective-permute-start.32 = (f32[4,120,128]{2,1,0:T(8,128)S(1)}, f32[4,120,128]{2,1,0:T(8,128)S(1)}, u32[]{:S(2)}, u32[]{:S(2)}) collective-permute-start(f32[4,120,128]{2,1,0:T(8,128)S(1)} %get-tuple-element.252), channel_id=1, source_target_pairs={{0,2},{1,3},{2,0},{3,1},{4,6},{5,7},{6,4},{7,5},{8,10},{9,11},{10,... | collective-permute-start | bytes 737288 | tf_op jit(solution)/shard_map/ppermute | solution.py:615
  201.9 28.5 %collective-permute-start.29 = (f32[608,128]{1,0:T(8,128)S(1)}, f32[608,128]{1,0:T(8,128)S(1)}, u32[]{:S(2)}, u32[]{:S(2)}) collective-permute-start(f32[608,128]{1,0:T(8,128)S(1)} %get-tuple-element.248), channel_id=1, source_target_pairs={{0,16},{4,20},{8,24},{12,28},{16,0},{20,4},{24,8},{28,12},{1,17},{... | collective-permute-start | bytes 933896 | tf_op jit(solution)/shard_map/ppermute | solution.py:657
  205.4 25.0 %collective-permute-start.28 = (f32[608,128]{1,0:T(8,128)S(1)}, f32[608,128]{1,0:T(8,128)S(1)}, u32[]{:S(2)}, u32[]{:S(2)}) collective-permute-start(f32[608,128]{1,0:T(8,128)S(1)} %get-tuple-element.246), channel_id=1, source_target_pairs={{0,8},{4,12},{8,0},{12,4},{16,24},{20,28},{24,16},{28,20},{1,9},{5... | collective-permute-start | bytes 933896 | tf_op jit(solution)/shard_map/ppermute | solution.py:657
  210.4 20.1 %collective-permute-start.34 = (f32[304,128]{1,0:T(8,128)S(1)}, f32[304,128]{1,0:T(8,128)S(1)}, u32[]{:S(2)}, u32[]{:S(2)}) collective-permute-start(f32[304,128]{1,0:T(8,128)S(1)} %get-tuple-element.259), channel_id=1, source_target_pairs={{0,8},{4,12},{8,0},{12,4},{16,24},{20,28},{24,16},{28,20},{1,9},{5... | collective-permute-start | bytes 466952 | tf_op jit(solution)/shard_map/ppermute | solution.py:657
  214.4 17.7 %collective-permute-start.35 = (f32[304,128]{1,0:T(8,128)S(1)}, f32[304,128]{1,0:T(8,128)S(1)}, u32[]{:S(2)}, u32[]{:S(2)}) collective-permute-start(f32[304,128]{1,0:T(8,128)S(1)} %get-tuple-element.260), channel_id=1, source_target_pairs={{0,16},{4,20},{8,24},{12,28},{16,0},{20,4},{24,8},{28,12},{1,17},{... | collective-permute-start | bytes 466952 | tf_op jit(solution)/shard_map/ppermute | solution.py:657
  214.4 17.7 %collective-permute-start.36 = (f32[304,128]{1,0:T(8,128)S(1)}, f32[304,128]{1,0:T(8,128)S(1)}, u32[]{:S(2)}, u32[]{:S(2)}) collective-permute-start(f32[304,128]{1,0:T(8,128)S(1)} %get-tuple-element.261), channel_id=1, source_target_pairs={{0,24},{4,28},{8,16},{12,20},{16,8},{20,12},{24,0},{28,4},{1,25},{... | collective-permute-start | bytes 466952 | tf_op jit(solution)/shard_map/ppermute | solution.py:657
  (30 other events, 774.7 us)

commit v13 on v12

--- a/solution.py
+++ b/solution.py
@@ -658,13 +658,14 @@
         return found
 
     first, second, middle, back, base = {}, {}, {}, {}, {}
-    for step in range(min(2, chunks)):
+    for step in range(chunks):
         first[step] = z_exchange(sent[step], *([first[step - 1]] if step else []))
 
     def run_second(at):
         found = ordered(lambda values: second_synth(place, values, table_y, dims[at]), first[at])
         if at:
-            found = [found[0]] + [after(value, second[at - 1]) for value in found[1:]]
+            gates = [second[at - 1]] + ([back[0]] if at == 2 else [])
+            found = [found[0]] + [after(value, *gates) for value in found[1:]]
         second[at] = exchange(found, "col", 0, cols)
 
     def run_third(at):
@@ -678,16 +679,16 @@
 
     def run_back(at):
         found = ordered(lambda values: second_back(place, values, table_y, dims[at]), middle[at])
-        gates = [back[0] if at else first[min(1, chunks - 1)]] if at < 2 else []
-        back[at] = z_exchange(found, *gates, waves=at == 0)
+        gates = [back[0] if at else first[chunks - 1]] if at < 2 else []
+        back[at] = found if at == 0 and chunks > 2 else z_exchange(found, *gates, waves=at == 0)
 
     def run_base(at):
         base[at] = run_earlier(at)
         if at == 1 and chunks > 2:
-            first[2] = z_exchange(sent[2], back[0], base[1])
-
-    plan = [(run_second, 0), (run_base, 0), (run_third, 0), (run_back, 0), (run_second, 1), (run_base, 1)]
-    plan += [(run_base, 2), (run_second, 2), (run_third, 1), (run_third, 2), (run_back, 1), (run_back, 2)]
+            back[0] = z_exchange(back[0], first[2], base[1])
+
+    plan = [(run_second, 0), (run_base, 0), (run_third, 0), (run_base, 2), (run_back, 0), (run_second, 1)]
+    plan += [(run_base, 1), (run_second, 2), (run_third, 1), (run_third, 2), (run_back, 1), (run_back, 2)]
     for action, at in plan:
         if at < chunks:
             action(at)

time: 242 us -> 243 us (level)
  starting transfers between devices: 61.1 us -> 69.4 us
  waiting for transfers between devices: 73.7 us -> 66.1 us
    ppermute x18, starting transfers between devices: 38.4 us -> 46.7 us  [z_exchange(): lax.ppermute(value, 'row', [(src, src ^ 2 * k) for src in range(rows)])]
    ppermute x18, waiting for transfers between devices: 44.7 us -> 40 us  [z_exchange(): lax.ppermute(value, 'row', [(src, src ^ 2 * k) for src in range(rows)])]
    ppermute x18, waiting for transfers between devices: 26.9 us -> 24.1 us  [exchange(): lax.ppermute(value, axis, [(src, src ^ k << shift) for src in range(size)])]
    unnamed x48 -> x42, local copies, waits for them, and re-layouts: 5.33 us -> 5.09 us
  transfers between devices with their start and end apart: 38 -> 38, of which waited for: 15 -> 15; matrix products, arithmetic and copies ran while one was open for 1% -> 1% of each run, Pallas kernels for 33% -> 34%
where the time goes in v13:
time: 243 us; the launch traced here: 242 us
  Pallas kernels  98.2 us (40%)
  starting transfers between devices  69.4 us (29%)
  waiting for transfers between devices  66.1 us (27%)
  local copies, waits for them, and re-layouts  7.28 us (3%)
    ppermute x18, starting transfers between devices, z_exchange(): lax.ppermute(value, 'row', [(src, src ^ 2 * k) for src in range(rows)])  46.7 us
    ppermute x18, waiting for transfers between devices, z_exchange(): lax.ppermute(value, 'row', [(src, src ^ 2 * k) for src in range(rows)])  40 us
    pallas_call x3, Pallas kernels, third(): pl.pallas_call(functools.partial(third_kernel, (begin, *dims)), in_specs=...  25 us
    pallas_call x3, Pallas kernels, earlier(): pl.pallas_call(functools.partial(earlier_kernel, orders - 1), grid=(packs...  24.6 us
    ppermute x18, waiting for transfers between devices, exchange(): lax.ppermute(value, axis, [(src, src ^ k << shift) for src in range(size)])  24.1 us
    ppermute x18, starting transfers between devices, exchange(): lax.ppermute(value, axis, [(src, src ^ k << shift) for src in range(size)])  22.2 us
    pallas_call x4, Pallas kernels, first_synth(): pl.pallas_call(functools.partial(first_synth_kernel, (sizes, chosen, dest...  17.2 us
    pallas_call x3, Pallas kernels, second_synth(): pl.pallas_call(functools.partial(second_synth_kernel, dims), in_specs=[SM...  14.9 us
  transfers between devices with their start and end apart: 38, of which 15 were waited for; matrix products, arithmetic and copies ran while one was open for 1% of the time, Pallas kernels for 34%

profile of v13, /device:TPU:0, one launch (start us, length us, event | category | flops | bytes accessed | tf_op | source)
XLA Modules:
  0.0 241.7 jit_solution(7972941256406970081)
XLA Ops:
  4.6 3.6 %first_synth.4 = (f32[512,128]{1,0:T(8,128)S(1)}, f32[512,128]{1,0:T(8,128)S(1)}, f32[512,128]{1,0:T(8,128)S(1)}, f32[512,128]{1,0:T(8,128)S(1)}) custom-call(s32[3]{0:T(128)S(1)} %pad_add_fusion.place_ref, f32[3,20,40,160]{3,2,1,0:T(8,128)S(1)} %copy-done.3, bf16[4,160,128]{2,1,0:T(8,128)(2,1)S(1)} %dynamic-slice_bitcast_fusion.2.table_ref.refs_12_), custom_call_target="tpu_custom_call" | custom-call | flops 1024 | bytes 1024 | tf_op jit(solution)/shard_map/first_synth/pallas_call | solution.py:168
  8.3 3.6 %first_synth.5 = (f32[512,128]{1,0:T(8,128)S(1)}, f32[512,128]{1,0:T(8,128)S(1)}, f32[512,128]{1,0:T(8,128)S(1)}, f32[512,128]{1,0:T(8,128)S(1)}) custom-call(s32[3]{0:T(128)S(1)} %pad_add_fusion.place_ref, f32[3,20,40,160]{3,2,1,0:T(8,128)S(1)} %collective-permute-done.data, ...), custom_call_target="tpu_custom_call", output_to_operand_aliasing={{0}: (3, {}), {1}: (4, {}), {2}: (5, {}), {3}: (6, {})} | custom-call | flops 1024 | bytes 1024 | tf_op jit(solution)/shard_map/first_synth/pallas_call | solution.py:168
  11.9 2.6 %collective-permute-start.1 = (f32[512,128]{1,0:T(8,128)S(1)}, f32[512,128]{1,0:T(8,128)S(1)}, u32[]{:S(2)}, u32[]{:S(2)}) collective-permute-start(f32[512,128]{1,0:T(8,128)S(1)} %get-tuple-element.144), channel_id=1, source_target_pairs={{0,8},{4,12},{8,0},{12,4},{16,24},{20,28},{24,16},{28,20},{1,9},{5... | collective-permute-start | bytes 786440 | tf_op jit(solution)/shard_map/ppermute | solution.py:657
  17.1 5.0 %first_synth.6 = (f32[1024,128]{1,0:T(8,128)S(1)}, f32[1024,128]{1,0:T(8,128)S(1)}, f32[1024,128]{1,0:T(8,128)}, f32[1024,128]{1,0:T(8,128)}, f32[512,128]{1,0:T...) custom-call(s32[3]{0:T(128)S(1)} %pad_add_fusion.place_ref, ...), custom_call_target="tpu_custom_call" | custom-call | flops 1024 | bytes 1024 | tf_op jit(solution)/shard_map/first_synth/pallas_call | solution.py:168
  22.1 5.0 %first_synth.7 = (f32[1024,128]{1,0:T(8,128)S(1)}, f32[1024,128]{1,0:T(8,128)S(1)}, f32[1024,128]{1,0:T(8,128)}, f32[1024,128]{1,0:T(8,128)}, f32[512,128]{1,0:T...) custom-call(s32[3]{0:T(128)S(1)} %pad_add_fusion.place_ref, ...), custom_call_target="tpu_custom_call", output_to_operand_aliasing={{0}: (3, {}), {1}: (4, {}), {2}: (5, {}), {3}: (6, {}), {4}... | custom-call | flops 1024 | bytes 1024 | tf_op jit(solution)/shard_map/first_synth/pallas_call | solution.py:168
  29.3 6.5 %collective-permute-done.2.refs_2_ = f32[512,128]{1,0:T(8,128)S(1)} collective-permute-done((f32[512,128]{1,0:T(8,128)S(1)}, f32[512,128]{1,0:T(8,128)S(1)}, u32[]{:S(2)}, u32[]{:S(2)}) %collective-permute-start.2) | collective-permute-done | bytes 262176 | tf_op jit(solution)/shard_map/ppermute | solution.py:657
  35.8 5.5 %collective-permute-start.10 = (f32[1024,128]{1,0:T(8,128)S(1)}, f32[1024,128]{1,0:T(8,128)S(1)}, u32[]{:S(2)}, u32[]{:S(2)}) collective-permute-start(f32[1024,128]{1,0:T(8,128)S(1)} %get-tuple-element.188), channel_id=1, source_target_pairs={{0,8},{4,12},{8,0},{12,4},{16,24},{20,28},{24,16},{28,20},{1,9},{5... | collective-permute-start | bytes 1572872 | tf_op jit(solution)/shard_map/ppermute | solution.py:657
  41.3 3.7 %second_synth.3 = (f32[4,240,128]{2,1,0:T(8,128)S(1)}, f32[4,240,128]{2,1,0:T(8,128)S(1)}, f32[4,240,128]{2,1,0:T(8,128)S(1)}, f32[4,240,128]{2,1,0:T(8,128)S(1)}) custom-call(s32[3]{0:T(128)S(1)} %pad_add_fusion.place_ref, f32[512,128]{1,0:T(8,128)S(1)} %get-tuple-element.157.refs_0_, f32[512,128]{1,0:T(8,128)S(1)} %collective-permute-done.1.refs_1_, ...), custom_call_target="tpu_custom_call" | custom-call | flops 1024 | bytes 1024 | tf_op jit(solution)/shard_map/second_synth/pallas_call | solution.py:241
  49.6 7.7 %collective-permute-done.10.refs_1_ = f32[1024,128]{1,0:T(8,128)S(1)} collective-permute-done((f32[1024,128]{1,0:T(8,128)S(1)}, f32[1024,128]{1,0:T(8,128)S(1)}, u32[]{:S(2)}, u32[]{:S(2)}) %collective-permute-start.10) | collective-permute-done | bytes 524320 | tf_op jit(solution)/shard_map/ppermute | solution.py:657
  58.6 6.4 %earlier_orders.3.refs_6_ = f32[3,8,64,256]{3,2,1,0:T(8,128)S(1)} custom-call(f32[6,3,32,64,256]{4,3,2,1,0:T(8,128)} %refs_4_.8, f32[6,3,32,64,256]{4,3,2,1,0:T(8,128)} %refs_4_.8, f32[6,3,32,64,256]{4,3,2,1,0:T(8,128)} %refs_4_.8, f32[6,3,32,64,256]{4,3,2,1,0:T(8,128)} %refs_4_.8, f32[6,3,32,64,256]{4,3,2,1,0:T(8,128)} %refs_4_.8, ...), custom_call_target="tpu_custom_call" | custom-call | flops 1024 | bytes 1024 | tf_op jit(solution)/shard_map/earlier_orders/pallas_call | solution.py:293
  65.1 4.0 %collective-permute-done.5.refs_2_ = f32[4,240,128]{2,1,0:T(8,128)S(1)} collective-permute-done((f32[4,240,128]{2,1,0:T(8,128)S(1)}, f32[4,240,128]{2,1,0:T(8,128)S(1)}, u32[]{:S(2)}, u32[]{:S(2)}) %collective-permute-start.5) | collective-permute-done | bytes 491552 | tf_op jit(solution)/shard_map/ppermute | solution.py:615
  69.1 6.4 %third_dimension.3 = (f32[4,120,128]{2,1,0:T(8,128)S(1)}, f32[4,120,128]{2,1,0:T(8,128)S(1)}, f32[4,120,128]{2,1,0:T(8,128)S(1)}, f32[4,120,128]{2,1,0:T(8,128)S(1)}) custom-call(s32[3]{0:T(128)S(1)} %pad_add_fusion.place_ref, f32[4,240,128]{2,1,0:T(8,128)S(1)} %get-tuple-element.168.refs_0_, f32[4,240,128]{2,1,0:T(8,128)S(1)} %collective-permute-done.4.refs_1_, ...), custom_call_target="tpu_custom_call" | custom-call | flops 1024 | bytes 1024 | tf_op jit(solution)/shard_map/third_dimension/pallas_call | solution.py:361
  79.1 6.4 %earlier_orders.4.refs_6_ = f32[3,8,64,256]{3,2,1,0:T(8,128)S(1)} custom-call(f32[6,3,32,64,256]{4,3,2,1,0:T(8,128)} %refs_4_.8, f32[6,3,32,64,256]{4,3,2,1,0:T(8,128)} %refs_4_.8, f32[6,3,32,64,256]{4,3,2,1,0:T(8,128)} %refs_4_.8, f32[6,3,32,64,256]{4,3,2,1,0:T(8,128)} %refs_4_.8, f32[6,3,32,64,256]{4,3,2,1,0:T(8,128)} %refs_4_.8, ...), custom_call_target="tpu_custom_call" | custom-call | flops 1024 | bytes 1024 | tf_op jit(solution)/shard_map/earlier_orders/pallas_call | solution.py:293
  91.4 7.5 %second_synth.4 = (f32[8,240,128]{2,1,0:T(8,128)S(1)}, f32[8,240,128]{2,1,0:T(8,128)S(1)}, f32[8,240,128]{2,1,0:T(8,128)S(1)}, f32[8,240,128]{2,1,0:T(8,128)S(1)}) custom-call(s32[3]{0:T(128)S(1)} %pad_add_fusion.place_ref, f32[1024,128]{1,0:T(8,128)S(1)} %copy-done.10, f32[1024,128]{1,0:T(8,128)S(1)} %copy-done.14, ...), custom_call_target="tpu_custom_call" | custom-call | flops 1024 | bytes 1024 | tf_op jit(solution)/shard_map/second_synth/pallas_call | solution.py:241
  102.5 5.8 %collective-permute-start.13 = (f32[512,128]{1,0:T(8,128)S(1)}, f32[512,128]{1,0:T(8,128)S(1)}, u32[]{:S(2)}, u32[]{:S(2)}) collective-permute-start(f32[512,128]{1,0:T(8,128)S(1)} %copy-done.16), channel_id=1, source_target_pairs={{0,8},{4,12},{8,0},{12,4},{16,24},{20,28},{24,16},{28,20},{1,9},{5... | collective-permute-start | bytes 786440 | tf_op jit(solution)/shard_map/ppermute | solution.py:657
  109.4 5.3 %collective-permute-done.13.refs_1_ = f32[512,128]{1,0:T(8,128)S(1)} collective-permute-done((f32[512,128]{1,0:T(8,128)S(1)}, f32[512,128]{1,0:T(8,128)S(1)}, u32[]{:S(2)}, u32[]{:S(2)}) %collective-permute-start.13) | collective-permute-done | bytes 262176 | tf_op jit(solution)/shard_map/ppermute | solution.py:657
  114.7 4.1 %collective-permute-start.15 = (f32[512,128]{1,0:T(8,128)S(1)}, f32[512,128]{1,0:T(8,128)S(1)}, u32[]{:S(2)}, u32[]{:S(2)}) collective-permute-start(f32[512,128]{1,0:T(8,128)S(1)} %copy-done.20), channel_id=1, source_target_pairs={{0,24},{4,28},{8,16},{12,20},{16,8},{20,12},{24,0},{28,4},{1,25},{... | collective-permute-start | bytes 786440 | tf_op jit(solution)/shard_map/ppermute | solution.py:657
  118.8 11.8 %earlier_orders.5.refs_6_ = f32[3,16,64,256]{3,2,1,0:T(8,128)S(1)} custom-call(f32[6,3,32,64,256]{4,3,2,1,0:T(8,128)} %refs_4_.8, f32[6,3,32,64,256]{4,3,2,1,0:T(8,128)} %refs_4_.8, f32[6,3,32,64,256]{4,3,2,1,0:T(8,128)} %refs_4_.8, f32[6,3,32,64,256]{4,3,2,1,0:T(8,128)} %refs_4_.8, f32[6,3,32,64,256]{4,3,2,1,0:T(8,128)} %refs_4_.8, ...), custom_call_target="tpu_custom_call" | custom-call | flops 1024 | bytes 1024 | tf_op jit(solution)/shard_map/earlier_orders/pallas_call | solution.py:293
  132.7 3.2 %collective-permute-done.16.refs_1_ = f32[304,128]{1,0:T(8,128)S(1)} collective-permute-done((f32[304,128]{1,0:T(8,128)S(1)}, f32[304,128]{1,0:T(8,128)S(1)}, u32[]{:S(2)}, u32[]{:S(2)}) %collective-permute-start.16) | collective-permute-done | bytes 155680 | tf_op jit(solution)/shard_map/ppermute | solution.py:657
  135.9 3.2 %collective-permute-start.18 = (f32[304,128]{1,0:T(8,128)S(1)}, f32[304,128]{1,0:T(8,128)S(1)}, u32[]{:S(2)}, u32[]{:S(2)}) collective-permute-start(f32[304,128]{1,0:T(8,128)S(1)} %get-tuple-element.209), channel_id=1, source_target_pairs={{0,24},{4,28},{8,16},{12,20},{16,8},{20,12},{24,0},{28,4},{1,25},{... | collective-permute-start | bytes 466952 | tf_op jit(solution)/shard_map/ppermute | solution.py:657
  139.1 3.7 %second_synth.5 = (f32[4,240,128]{2,1,0:T(8,128)S(1)}, f32[4,240,128]{2,1,0:T(8,128)S(1)}, f32[4,240,128]{2,1,0:T(8,128)S(1)}, f32[4,240,128]{2,1,0:T(8,128)S(1)}) custom-call(s32[3]{0:T(128)S(1)} %pad_add_fusion.place_ref, f32[512,128]{1,0:T(8,128)S(1)} %copy-done.12, f32[512,128]{1,0:T(8,128)S(1)} %collective-permute-done.13.refs_1_, ...), custom_call_target="tpu_custom_call" | custom-call | flops 1024 | bytes 1024 | tf_op jit(solution)/shard_map/second_synth/pallas_call | solution.py:241
  148.4 12.1 %third_dimension.4 = (f32[8,120,128]{2,1,0:T(8,128)S(1)}, f32[8,120,128]{2,1,0:T(8,128)S(1)}, f32[8,120,128]{2,1,0:T(8,128)S(1)}, f32[8,120,128]{2,1,0:T(8,128)S(1)}) custom-call(s32[3]{0:T(128)S(1)} %pad_add_fusion.place_ref, f32[8,240,128]{2,1,0:T(8,128)S(1)} %get-tuple-element.221.refs_0_, f32[8,240,128]{2,1,0:T(8,128)S(1)} %collective-permute-done.19.refs_1_, ...), custom_call_target="tpu_custom_call" | custom-call | flops 1024 | bytes 1024 | tf_op jit(solution)/shard_map/third_dimension/pallas_call | solution.py:361
  166.0 4.5 %collective-permute-done.25.refs_1_ = f32[4,240,128]{2,1,0:T(8,128)S(1)} collective-permute-done((f32[4,240,128]{2,1,0:T(8,128)S(1)}, f32[4,240,128]{2,1,0:T(8,128)S(1)}, u32[]{:S(2)}, u32[]{:S(2)}) %collective-permute-start.25) | collective-permute-done | bytes 491552 | tf_op jit(solution)/shard_map/ppermute | solution.py:615
  170.5 6.4 %third_dimension.5 = (f32[4,120,128]{2,1,0:T(8,128)S(1)}, f32[4,120,128]{2,1,0:T(8,128)S(1)}, f32[4,120,128]{2,1,0:T(8,128)S(1)}, f32[4,120,128]{2,1,0:T(8,128)S(1)}) custom-call(s32[3]{0:T(128)S(1)} %pad_add_fusion.place_ref, f32[4,240,128]{2,1,0:T(8,128)S(1)} %get-tuple-element.235.refs_0_, f32[4,240,128]{2,1,0:T(8,128)S(1)} %collective-permute-done.25.refs_1_, ...), custom_call_target="tpu_custom_call" | custom-call | flops 1024 | bytes 1024 | tf_op jit(solution)/shard_map/third_dimension/pallas_call | solution.py:361
  181.0 7.9 %collective-permute-done.24.refs_3_ = f32[8,120,128]{2,1,0:T(8,128)S(1)} collective-permute-done((f32[8,120,128]{2,1,0:T(8,128)S(1)}, f32[8,120,128]{2,1,0:T(8,128)S(1)}, u32[]{:S(2)}, u32[]{:S(2)}) %collective-permute-start.24) | collective-permute-done | bytes 491552 | tf_op jit(solution)/shard_map/ppermute | solution.py:615
  189.0 4.4 %second_back.4 = (f32[608,128]{1,0:T(8,128)S(1)}, f32[608,128]{1,0:T(8,128)S(1)}, f32[608,128]{1,0:T(8,128)S(1)}, f32[608,128]{1,0:T(8,128)S(1)}) custom-call(s32[3]{0:T(128)S(1)} %pad_add_fusion.place_ref, f32[8,120,128]{2,1,0:T(8,128)S(1)} %get-tuple-element.240.refs_0_, f32[8,120,128]{2,1,0:T(8,128)S(1)} %collective-permute-done.22.refs_1_, ...), custom_call_target="tpu_custom_call" | custom-call | flops 1024 | bytes 1024 | tf_op jit(solution)/shard_map/second_back/pallas_call | solution.py:410
  198.9 4.7 %collective-permute-start.29 = (f32[608,128]{1,0:T(8,128)S(1)}, f32[608,128]{1,0:T(8,128)S(1)}, u32[]{:S(2)}, u32[]{:S(2)}) collective-permute-start(f32[608,128]{1,0:T(8,128)S(1)} %get-tuple-element.248), channel_id=1, source_target_pairs={{0,16},{4,20},{8,24},{12,28},{16,0},{20,4},{24,8},{28,12},{1,17},{... | collective-permute-start | bytes 933896 | tf_op jit(solution)/shard_map/ppermute | solution.py:657
  204.8 2.6 %second_back.5 = (f32[304,128]{1,0:T(8,128)S(1)}, f32[304,128]{1,0:T(8,128)S(1)}, f32[304,128]{1,0:T(8,128)S(1)}, f32[304,128]{1,0:T(8,128)S(1)}) custom-call(s32[3]{0:T(128)S(1)} %pad_add_fusion.place_ref, f32[4,120,128]{2,1,0:T(8,128)S(1)} %get-tuple-element.254.refs_0_, f32[4,120,128]{2,1,0:T(8,128)S(1)} %collective-permute-done.31.refs_1_, ...), custom_call_target="tpu_custom_call" | custom-call | flops 1024 | bytes 1024 | tf_op jit(solution)/shard_map/second_back/pallas_call | solution.py:410
  207.4 7.3 %collective-permute-start.34 = (f32[304,128]{1,0:T(8,128)S(1)}, f32[304,128]{1,0:T(8,128)S(1)}, u32[]{:S(2)}, u32[]{:S(2)}) collective-permute-start(f32[304,128]{1,0:T(8,128)S(1)} %get-tuple-element.259), channel_id=1, source_target_pairs={{0,8},{4,12},{8,0},{12,4},{16,24},{20,28},{24,16},{28,20},{1,9},{5... | collective-permute-start | bytes 466952 | tf_op jit(solution)/shard_map/ppermute | solution.py:657
  217.1 11.8 %collective-permute-done.29.refs_6_ = f32[608,128]{1,0:T(8,128)S(1)} collective-permute-done((f32[608,128]{1,0:T(8,128)S(1)}, f32[608,128]{1,0:T(8,128)S(1)}, u32[]{:S(2)}, u32[]{:S(2)}) %collective-permute-start.29) | collective-permute-done | bytes 311328 | tf_op jit(solution)/shard_map/ppermute | solution.py:657
  229.0 3.3 %collective-permute-done.35.refs_10_ = f32[304,128]{1,0:T(8,128)S(1)} collective-permute-done((f32[304,128]{1,0:T(8,128)S(1)}, f32[304,128]{1,0:T(8,128)S(1)}, u32[]{:S(2)}, u32[]{:S(2)}) %collective-permute-start.35) | collective-permute-done | bytes 155680 | tf_op jit(solution)/shard_map/ppermute | solution.py:657
  237.1 4.5 %last_projection.1 = f32[3,20,40,160]{3,2,1,0:T(8,128)} custom-call(f32[10]{0:T(128)S(1)} %convert_multiply_fusion.1.refs_0_, f32[8,256]{1,0:T(8,128)S(1)} %broadcast_in_dim.9.refs_1_, f32[40,256]{1,0:T(8,128)S(1)} %broadcast_in_dim.18.refs_2_, f32[160,2432]{1,0:T(8,128)S(1)} %first_back.3.refs_3_, f32[160,2432]{1,0:T(8,128)S(1)} %collective-permute-done.37.refs_4_), custom_call_target="tpu_custom_call" | custom-call | flops 1024 | bytes 1024 | tf_op jit(solution)/shard_map/last_projection/pallas_call | solution.py:523
  (113 shorter events, 60.5 us)
Async XLA Ops:
  11.9 17.4 %collective-permute-start.1 = (f32[512,128]{1,0:T(8,128)S(1)}, f32[512,128]{1,0:T(8,128)S(1)}, u32[]{:S(2)}, u32[]{:S(2)}) collective-permute-start(f32[512,128]{1,0:T(8,128)S(1)} %get-tuple-element.144), channel_id=1, source_target_pairs={{0,8},{4,12},{8,0},{12,4},{16,24},{20,28},{24,16},{28,20},{1,9},{5... | collective-permute-start | bytes 786440 | tf_op jit(solution)/shard_map/ppermute | solution.py:657
  14.5 21.3 %collective-permute-start.2 = (f32[512,128]{1,0:T(8,128)S(1)}, f32[512,128]{1,0:T(8,128)S(1)}, u32[]{:S(2)}, u32[]{:S(2)}) collective-permute-start(f32[512,128]{1,0:T(8,128)S(1)} %get-tuple-element.145), channel_id=1, source_target_pairs={{0,16},{4,20},{8,24},{12,28},{16,0},{20,4},{24,8},{28,12},{1,17},{... | collective-permute-start | bytes 786440 | tf_op jit(solution)/shard_map/ppermute | solution.py:657
  17.1 18.7 %collective-permute-start.3 = (f32[512,128]{1,0:T(8,128)S(1)}, f32[512,128]{1,0:T(8,128)S(1)}, u32[]{:S(2)}, u32[]{:S(2)}) collective-permute-start(f32[512,128]{1,0:T(8,128)S(1)} %get-tuple-element.146), channel_id=1, source_target_pairs={{0,24},{4,28},{8,16},{12,20},{16,8},{20,12},{24,0},{28,4},{1,25},{... | collective-permute-start | bytes 786440 | tf_op jit(solution)/shard_map/ppermute | solution.py:657
  35.8 21.5 %collective-permute-start.10 = (f32[1024,128]{1,0:T(8,128)S(1)}, f32[1024,128]{1,0:T(8,128)S(1)}, u32[]{:S(2)}, u32[]{:S(2)}) collective-permute-start(f32[1024,128]{1,0:T(8,128)S(1)} %get-tuple-element.188), channel_id=1, source_target_pairs={{0,8},{4,12},{8,0},{12,4},{16,24},{20,28},{24,16},{28,20},{1,9},{5... | collective-permute-start | bytes 1572872 | tf_op jit(solution)/shard_map/ppermute | solution.py:657
  45.0 20.0 %collective-permute-start.4 = (f32[4,240,128]{2,1,0:T(8,128)S(1)}, f32[4,240,128]{2,1,0:T(8,128)S(1)}, u32[]{:S(2)}, u32[]{:S(2)}) collective-permute-start(f32[4,240,128]{2,1,0:T(8,128)S(1)} %get-tuple-element.163), channel_id=1, source_target_pairs={{0,1},{1,0},{2,3},{3,2},{4,5},{5,4},{6,7},{7,6},{8,9},{9,8},{10,11... | collective-permute-start | bytes 1474568 | tf_op jit(solution)/shard_map/ppermute | solution.py:615
  46.6 22.5 %collective-permute-start.5 = (f32[4,240,128]{2,1,0:T(8,128)S(1)}, f32[4,240,128]{2,1,0:T(8,128)S(1)}, u32[]{:S(2)}, u32[]{:S(2)}) collective-permute-start(f32[4,240,128]{2,1,0:T(8,128)S(1)} %get-tuple-element.164), channel_id=1, source_target_pairs={{0,2},{1,3},{2,0},{3,1},{4,6},{5,7},{6,4},{7,5},{8,10},{9,11},{10,... | collective-permute-start | bytes 1474568 | tf_op jit(solution)/shard_map/ppermute | solution.py:615
  48.1 21.0 %collective-permute-start.6 = (f32[4,240,128]{2,1,0:T(8,128)S(1)}, f32[4,240,128]{2,1,0:T(8,128)S(1)}, u32[]{:S(2)}, u32[]{:S(2)}) collective-permute-start(f32[4,240,128]{2,1,0:T(8,128)S(1)} %get-tuple-element.165), channel_id=1, source_target_pairs={{0,3},{1,2},{2,1},{3,0},{4,7},{5,6},{6,5},{7,4},{8,11},{9,10},{10,... | collective-permute-start | bytes 1474568 | tf_op jit(solution)/shard_map/ppermute | solution.py:615
  48.6 41.8 %collective-permute-start.11 = (f32[1024,128]{1,0:T(8,128)}, f32[1024,128]{1,0:T(8,128)}, u32[]{:S(2)}, u32[]{:S(2)}) collective-permute-start(f32[1024,128]{1,0:T(8,128)} %get-tuple-element.190), channel_id=1, source_target_pairs={{0,16},{4,20},{8,24},{12,28},{16,0},{20,4},{24,8},{28,12},{1,17},{... | collective-permute-start | bytes 1572872 | tf_op jit(solution)/shard_map/ppermute | solution.py:657
  57.3 33.1 %collective-permute-start.12 = (f32[1024,128]{1,0:T(8,128)}, f32[1024,128]{1,0:T(8,128)}, u32[]{:S(2)}, u32[]{:S(2)}) collective-permute-start(f32[1024,128]{1,0:T(8,128)} %get-tuple-element.192), channel_id=1, source_target_pairs={{0,24},{4,28},{8,16},{12,20},{16,8},{20,12},{24,0},{28,4},{1,25},{... | collective-permute-start | bytes 1572872 | tf_op jit(solution)/shard_map/ppermute | solution.py:657
  75.5 10.0 %collective-permute-start.7 = (f32[4,120,128]{2,1,0:T(8,128)S(1)}, f32[4,120,128]{2,1,0:T(8,128)S(1)}, u32[]{:S(2)}, u32[]{:S(2)}) collective-permute-start(f32[4,120,128]{2,1,0:T(8,128)S(1)} %get-tuple-element.174), channel_id=1, source_target_pairs={{0,1},{1,0},{2,3},{3,2},{4,5},{5,4},{6,7},{7,6},{8,9},{9,8},{10,11... | collective-permute-start | bytes 737288 | tf_op jit(solution)/shard_map/ppermute | solution.py:615
  76.8 11.2 %collective-permute-start.8 = (f32[4,120,128]{2,1,0:T(8,128)S(1)}, f32[4,120,128]{2,1,0:T(8,128)S(1)}, u32[]{:S(2)}, u32[]{:S(2)}) collective-permute-start(f32[4,120,128]{2,1,0:T(8,128)S(1)} %get-tuple-element.175), channel_id=1, source_target_pairs={{0,2},{1,3},{2,0},{3,1},{4,6},{5,7},{6,4},{7,5},{8,10},{9,11},{10,... | collective-permute-start | bytes 737288 | tf_op jit(solution)/shard_map/ppermute | solution.py:615
  77.6 10.3 %collective-permute-start.9 = (f32[4,120,128]{2,1,0:T(8,128)S(1)}, f32[4,120,128]{2,1,0:T(8,128)S(1)}, u32[]{:S(2)}, u32[]{:S(2)}) collective-permute-start(f32[4,120,128]{2,1,0:T(8,128)S(1)} %get-tuple-element.176), channel_id=1, source_target_pairs={{0,3},{1,2},{2,1},{3,0},{4,7},{5,6},{6,5},{7,4},{8,11},{9,10},{10,... | collective-permute-start | bytes 737288 | tf_op jit(solution)/shard_map/ppermute | solution.py:615
  99.0 45.8 %collective-permute-start.21 = (f32[8,240,128]{2,1,0:T(8,128)S(1)}, f32[8,240,128]{2,1,0:T(8,128)S(1)}, u32[]{:S(2)}, u32[]{:S(2)}) collective-permute-start(f32[8,240,128]{2,1,0:T(8,128)S(1)} %get-tuple-element.215), channel_id=1, source_target_pairs={{0,3},{1,2},{2,1},{3,0},{4,7},{5,6},{6,5},{7,4},{8,11},{9,10},{10,... | collective-permute-start | bytes 2949128 | tf_op jit(solution)/shard_map/ppermute | solution.py:615
  100.6 44.2 %collective-permute-start.20 = (f32[8,240,128]{2,1,0:T(8,128)S(1)}, f32[8,240,128]{2,1,0:T(8,128)S(1)}, u32[]{:S(2)}, u32[]{:S(2)}) collective-permute-start(f32[8,240,128]{2,1,0:T(8,128)S(1)} %get-tuple-element.213), channel_id=1, source_target_pairs={{0,2},{1,3},{2,0},{3,1},{4,6},{5,7},{6,4},{7,5},{8,10},{9,11},{10,... | collective-permute-start | bytes 2949128 | tf_op jit(solution)/shard_map/ppermute | solution.py:615
  101.0 43.8 %collective-permute-start.19 = (f32[8,240,128]{2,1,0:T(8,128)S(1)}, f32[8,240,128]{2,1,0:T(8,128)S(1)}, u32[]{:S(2)}, u32[]{:S(2)}) collective-permute-start(f32[8,240,128]{2,1,0:T(8,128)S(1)} %get-tuple-element.211), channel_id=1, source_target_pairs={{0,1},{1,0},{2,3},{3,2},{4,5},{5,4},{6,7},{7,6},{8,9},{9,8},{10,11... | collective-permute-start | bytes 2949128 | tf_op jit(solution)/shard_map/ppermute | solution.py:615
  102.5 12.2 %collective-permute-start.13 = (f32[512,128]{1,0:T(8,128)S(1)}, f32[512,128]{1,0:T(8,128)S(1)}, u32[]{:S(2)}, u32[]{:S(2)}) collective-permute-start(f32[512,128]{1,0:T(8,128)S(1)} %copy-done.16), channel_id=1, source_target_pairs={{0,8},{4,12},{8,0},{12,4},{16,24},{20,28},{24,16},{28,20},{1,9},{5... | collective-permute-start | bytes 786440 | tf_op jit(solution)/shard_map/ppermute | solution.py:657
  108.3 22.3 %collective-permute-start.14 = (f32[512,128]{1,0:T(8,128)S(1)}, f32[512,128]{1,0:T(8,128)S(1)}, u32[]{:S(2)}, u32[]{:S(2)}) collective-permute-start(f32[512,128]{1,0:T(8,128)S(1)} %copy-done.18), channel_id=1, source_target_pairs={{0,16},{4,20},{8,24},{12,28},{16,0},{20,4},{24,8},{28,12},{1,17},{... | collective-permute-start | bytes 786440 | tf_op jit(solution)/shard_map/ppermute | solution.py:657
  114.7 15.9 %collective-permute-start.15 = (f32[512,128]{1,0:T(8,128)S(1)}, f32[512,128]{1,0:T(8,128)S(1)}, u32[]{:S(2)}, u32[]{:S(2)}) collective-permute-start(f32[512,128]{1,0:T(8,128)S(1)} %copy-done.20), channel_id=1, source_target_pairs={{0,24},{4,28},{8,16},{12,20},{16,8},{20,12},{24,0},{28,4},{1,25},{... | collective-permute-start | bytes 786440 | tf_op jit(solution)/shard_map/ppermute | solution.py:657
  131.6 13.2 %collective-permute-start.17 = (f32[304,128]{1,0:T(8,128)S(1)}, f32[304,128]{1,0:T(8,128)S(1)}, u32[]{:S(2)}, u32[]{:S(2)}) collective-permute-start(f32[304,128]{1,0:T(8,128)S(1)} %get-tuple-element.207), channel_id=1, source_target_pairs={{0,16},{4,20},{8,24},{12,28},{16,0},{20,4},{24,8},{28,12},{1,17},{... | collective-permute-start | bytes 466952 | tf_op jit(solution)/shard_map/ppermute | solution.py:657
  144.8 18.7 %collective-permute-start.27 = (f32[4,240,128]{2,1,0:T(8,128)S(1)}, f32[4,240,128]{2,1,0:T(8,128)S(1)}, u32[]{:S(2)}, u32[]{:S(2)}) collective-permute-start(f32[4,240,128]{2,1,0:T(8,128)S(1)} %get-tuple-element.234), channel_id=1, source_target_pairs={{0,3},{1,2},{2,1},{3,0},{4,7},{5,6},{6,5},{7,4},{8,11},{9,10},{10,... | collective-permute-start | bytes 1474568 | tf_op jit(solution)/shard_map/ppermute | solution.py:615
  147.3 18.7 %collective-permute-start.26 = (f32[4,240,128]{2,1,0:T(8,128)S(1)}, f32[4,240,128]{2,1,0:T(8,128)S(1)}, u32[]{:S(2)}, u32[]{:S(2)}) collective-permute-start(f32[4,240,128]{2,1,0:T(8,128)S(1)} %get-tuple-element.232), channel_id=1, source_target_pairs={{0,2},{1,3},{2,0},{3,1},{4,6},{5,7},{6,4},{7,5},{8,10},{9,11},{10,... | collective-permute-start | bytes 1474568 | tf_op jit(solution)/shard_map/ppermute | solution.py:615
  147.8 22.7 %collective-permute-start.25 = (f32[4,240,128]{2,1,0:T(8,128)S(1)}, f32[4,240,128]{2,1,0:T(8,128)S(1)}, u32[]{:S(2)}, u32[]{:S(2)}) collective-permute-start(f32[4,240,128]{2,1,0:T(8,128)S(1)} %get-tuple-element.230), channel_id=1, source_target_pairs={{0,1},{1,0},{2,3},{3,2},{4,5},{5,4},{6,7},{7,6},{8,9},{9,8},{10,11... | collective-permute-start | bytes 1474568 | tf_op jit(solution)/shard_map/ppermute | solution.py:615
  160.5 20.5 %collective-permute-start.22 = (f32[8,120,128]{2,1,0:T(8,128)S(1)}, f32[8,120,128]{2,1,0:T(8,128)S(1)}, u32[]{:S(2)}, u32[]{:S(2)}) collective-permute-start(f32[8,120,128]{2,1,0:T(8,128)S(1)} %get-tuple-element.226), channel_id=1, source_target_pairs={{0,1},{1,0},{2,3},{3,2},{4,5},{5,4},{6,7},{7,6},{8,9},{9,8},{10,11... | collective-permute-start | bytes 1474568 | tf_op jit(solution)/shard_map/ppermute | solution.py:615
  162.1 19.0 %collective-permute-start.23 = (f32[8,120,128]{2,1,0:T(8,128)S(1)}, f32[8,120,128]{2,1,0:T(8,128)S(1)}, u32[]{:S(2)}, u32[]{:S(2)}) collective-permute-start(f32[8,120,128]{2,1,0:T(8,128)S(1)} %get-tuple-element.227), channel_id=1, source_target_pairs={{0,2},{1,3},{2,0},{3,1},{4,6},{5,7},{6,4},{7,5},{8,10},{9,11},{10,... | collective-permute-start | bytes 1474568 | tf_op jit(solution)/shard_map/ppermute | solution.py:615
  163.5 25.4 %collective-permute-start.24 = (f32[8,120,128]{2,1,0:T(8,128)S(1)}, f32[8,120,128]{2,1,0:T(8,128)S(1)}, u32[]{:S(2)}, u32[]{:S(2)}) collective-permute-start(f32[8,120,128]{2,1,0:T(8,128)S(1)} %get-tuple-element.228), channel_id=1, source_target_pairs={{0,3},{1,2},{2,1},{3,0},{4,7},{5,6},{6,5},{7,4},{8,11},{9,10},{10,... | collective-permute-start | bytes 1474568 | tf_op jit(solution)/shard_map/ppermute | solution.py:615
  176.9 26.6 %collective-permute-start.31 = (f32[4,120,128]{2,1,0:T(8,128)S(1)}, f32[4,120,128]{2,1,0:T(8,128)S(1)}, u32[]{:S(2)}, u32[]{:S(2)}) collective-permute-start(f32[4,120,128]{2,1,0:T(8,128)S(1)} %get-tuple-element.251), channel_id=1, source_target_pairs={{0,1},{1,0},{2,3},{3,2},{4,5},{5,4},{6,7},{7,6},{8,9},{9,8},{10,11... | collective-permute-start | bytes 737288 | tf_op jit(solution)/shard_map/ppermute | solution.py:615
  193.4 21.3 %collective-permute-start.30 = (f32[608,128]{1,0:T(8,128)S(1)}, f32[608,128]{1,0:T(8,128)S(1)}, u32[]{:S(2)}, u32[]{:S(2)}) collective-permute-start(f32[608,128]{1,0:T(8,128)S(1)} %get-tuple-element.250), channel_id=1, source_target_pairs={{0,24},{4,28},{8,16},{12,20},{16,8},{20,12},{24,0},{28,4},{1,25},{... | collective-permute-start | bytes 933896 | tf_op jit(solution)/shard_map/ppermute | solution.py:657
  198.9 30.1 %collective-permute-start.29 = (f32[608,128]{1,0:T(8,128)S(1)}, f32[608,128]{1,0:T(8,128)S(1)}, u32[]{:S(2)}, u32[]{:S(2)}) collective-permute-start(f32[608,128]{1,0:T(8,128)S(1)} %get-tuple-element.248), channel_id=1, source_target_pairs={{0,16},{4,20},{8,24},{12,28},{16,0},{20,4},{24,8},{28,12},{1,17},{... | collective-permute-start | bytes 933896 | tf_op jit(solution)/shard_map/ppermute | solution.py:657
  203.6 25.4 %collective-permute-start.28 = (f32[608,128]{1,0:T(8,128)S(1)}, f32[608,128]{1,0:T(8,128)S(1)}, u32[]{:S(2)}, u32[]{:S(2)}) collective-permute-start(f32[608,128]{1,0:T(8,128)S(1)} %get-tuple-element.246), channel_id=1, source_target_pairs={{0,8},{4,12},{8,0},{12,4},{16,24},{20,28},{24,16},{28,20},{1,9},{5... | collective-permute-start | bytes 933896 | tf_op jit(solution)/shard_map/ppermute | solution.py:657
  207.4 21.6 %collective-permute-start.34 = (f32[304,128]{1,0:T(8,128)S(1)}, f32[304,128]{1,0:T(8,128)S(1)}, u32[]{:S(2)}, u32[]{:S(2)}) collective-permute-start(f32[304,128]{1,0:T(8,128)S(1)} %get-tuple-element.259), channel_id=1, source_target_pairs={{0,8},{4,12},{8,0},{12,4},{16,24},{20,28},{24,16},{28,20},{1,9},{5... | collective-permute-start | bytes 466952 | tf_op jit(solution)/shard_map/ppermute | solution.py:657
  214.7 17.6 %collective-permute-start.35 = (f32[304,128]{1,0:T(8,128)S(1)}, f32[304,128]{1,0:T(8,128)S(1)}, u32[]{:S(2)}, u32[]{:S(2)}) collective-permute-start(f32[304,128]{1,0:T(8,128)S(1)} %get-tuple-element.260), channel_id=1, source_target_pairs={{0,16},{4,20},{8,24},{12,28},{16,0},{20,4},{24,8},{28,12},{1,17},{... | collective-permute-start | bytes 466952 | tf_op jit(solution)/shard_map/ppermute | solution.py:657
  214.7 17.6 %collective-permute-start.36 = (f32[304,128]{1,0:T(8,128)S(1)}, f32[304,128]{1,0:T(8,128)S(1)}, u32[]{:S(2)}, u32[]{:S(2)}) collective-permute-start(f32[304,128]{1,0:T(8,128)S(1)} %get-tuple-element.261), channel_id=1, source_target_pairs={{0,24},{4,28},{8,16},{12,20},{16,8},{20,12},{24,0},{28,4},{1,25},{... | collective-permute-start | bytes 466952 | tf_op jit(solution)/shard_map/ppermute | solution.py:657
  (27 other events, 494.2 us)
